TPU v7x, 32 devices: a whole 2x2x4 slice. The times are simulated.
32 devices in a mesh: dp: 16 (over z, x, core), tensor: 2 (over y).
Axes of the slice: x: 2, y: 2, z: 4, core: 2. Of those that a mesh axis runs over, the one named last changes fastest.
Arguments:
- frames: bfloat16 [19200, 512], P('dp', 'tensor'), may hold values from -6 to 6
- resets: int32 [19200], P('dp'), may hold values 0 or 1
- first_gain: float32 [512], replicated, may hold values from 0.5 to 1.5
- first_shift: float32 [512], replicated, may hold values from -1 to 1
- qkv_weight: bfloat16 [3, 512, 512], P(None, None, 'tensor'), may hold values from -0.375 to 0.375
- out_weight: bfloat16 [512, 512], P('tensor'), may hold values from -0.75 to 0.75
- out_bias: float32 [512], replicated, may hold values from -1 to 1
- second_gain: float32 [512], replicated, may hold values from 0.5 to 1.5
- second_shift: float32 [512], replicated, may hold values from -1 to 1
- up_weight: bfloat16 [512, 2048], P(None, 'tensor'), may hold values from -0.25 to 0.25
- up_bias: float32 [2048], P('tensor'), may hold values from -1 to 1
- down_weight: bfloat16 [2048, 512], P('tensor'), may hold values from -0.125 to 0.125
- down_bias: float32 [512], replicated, may hold values from -1 to 1
- prior_gain: float32 [512], replicated, may hold values from 0.5 to 1.5
- prior_shift: float32 [512], replicated, may hold values from -1 to 1
- prior_weight: bfloat16 [512, 1024], P(None, 'tensor'), may hold values from -0.25 to 0.25
- prior_bias: float32 [1024], P('tensor'), may hold values from -2.5 to 2.5
- out_cotangent: bfloat16 [19200, 512], P('dp', 'tensor'), may hold values from -6 to 6
- logit_cotangent: bfloat16 [19200, 1024], P('dp', 'tensor'), may hold values from -6 to 6
Outputs:
- block_out: bfloat16 [19200, 512], P('dp', 'tensor')
- logits: float32 [19200, 1024], P('dp', 'tensor')
- grad_frames: float32 [19200, 512], P('dp', 'tensor')
- grad_first_gain: float32 [512], replicated
- grad_first_shift: float32 [512], replicated
- grad_qkv: float32 [3, 512, 512], P(None, None, 'tensor')
- grad_out_weight: float32 [512, 512], P('tensor')
- grad_out_bias: float32 [512], replicated
- grad_second_gain: float32 [512], replicated
- grad_second_shift: float32 [512], replicated
- grad_up_weight: float32 [512, 2048], P(None, 'tensor')
- grad_up_bias: float32 [2048], P('tensor')
- grad_down_weight: float32 [2048, 512], P('tensor')
- grad_down_bias: float32 [512], replicated
- grad_prior_gain: float32 [512], replicated
- grad_prior_shift: float32 [512], replicated
- grad_prior_weight: float32 [512, 1024], P(None, 'tensor')
- grad_prior_bias: float32 [1024], P('tensor')
All inputs are finite; a program needn't handle non-finite values. No bound on the sum of `resets` on one device may be relied on, other than what follows from the above.
Results may differ from a plain program's by a relative error of at most 0.012.
The roundings to bfloat16 on the way count: a program that leaves them out, or rounds other values in their place, can miss the bound.
Values may be sent and summed in bfloat16 or wider, within the bound.
No kernel may reach another device: no remote copies, remote signals or barrier semaphores. Data moves between devices by JAX's collectives and lax.ppermute only.
A program may use at most 128 MiB of HBM per device.

v0:
```python
import functools
import math

import jax
import jax.numpy as jnp
from jax import lax
from jax.experimental import pallas as pl
from jax.experimental.pallas import tpu as pltpu
from jax.sharding import PartitionSpec as P

HEAD_DIM = 64
SEQ_LEN = 50
BLOCK = 4 * SEQ_LEN
PAD = -(-BLOCK // 16) * 16
EPS = 1e-05
NEG = -1e30
GELU_C = 0.7978845608028654
GELU_A = 0.044715
SPILL = 8 * 1024 * 1024
GROUP, GROUP_BACK = 4, 6
COST = 1e8
FOLD = 100.0
BF = jnp.bfloat16
F32 = jnp.float32
FIRST_GAIN, FIRST_SHIFT, OUT_BIAS, SECOND_GAIN, SECOND_SHIFT, DOWN_BIAS, PRIOR_GAIN, PRIOR_SHIFT, UP_BIAS, PRIOR_BIAS = range(10)


def mm(a, b):
    return lax.dot_general(a, b, (((1,), (0,)), ((), ())), preferred_element_type=F32)


def mm_bt(a, b):
    return lax.dot_general(a, b, (((1,), (1,)), ((), ())), preferred_element_type=F32)


def mm_at(a, b):
    return lax.dot_general(a, b, (((0,), (0,)), ((), ())), preferred_element_type=F32)


def norm_of(value):
    centre = value - jnp.mean(value, axis=-1, keepdims=True)
    factor = lax.rsqrt(jnp.mean(centre * centre, axis=-1, keepdims=True) + EPS)
    return centre * factor, factor


def norm_back(grad, unit, factor, gain):
    scaled = grad * gain
    first = jnp.mean(scaled, axis=-1, keepdims=True)
    second = jnp.mean(scaled * unit, axis=-1, keepdims=True)
    return factor * (scaled - first - unit * second)


def col_sum(value):
    return jnp.sum(value, axis=0, keepdims=True)


def whole_rows(here, own, other):
    low = jnp.where(here == 0, own[...], other[...])
    high = jnp.where(here == 0, other[...], own[...])
    return jnp.concatenate([low, high], axis=1).astype(F32)


def allowed_pairs(resets):
    place = lax.broadcasted_iota(jnp.int32, (1, PAD), 1)
    starts = jnp.where((resets == 1) | (lax.rem(place, SEQ_LEN) == 0) | (place >= BLOCK), place, 0)
    row = lax.broadcasted_iota(jnp.int32, (PAD, PAD), 0)
    col = lax.broadcasted_iota(jnp.int32, (PAD, PAD), 1)
    seg = jnp.max(jnp.where(col <= row, starts, 0).astype(F32), axis=-1, keepdims=True).astype(jnp.int32)
    seg2 = jnp.concatenate([seg, seg], axis=0)
    row = lax.broadcasted_iota(jnp.int32, (2 * PAD, PAD), 0)
    row = jnp.where(row >= PAD, row - PAD, row)
    col = lax.broadcasted_iota(jnp.int32, (2 * PAD, PAD), 1)
    return (col <= row) & (col >= seg2)


def two_heads(value):
    first = lax.broadcasted_iota(jnp.int32, value.shape, 1) < HEAD_DIM
    none = jnp.zeros_like(value)
    return jnp.concatenate([jnp.where(first, value, none), jnp.where(first, none, value)], axis=0)


def one_pair(value):
    first = lax.broadcasted_iota(jnp.int32, (PAD, 2 * HEAD_DIM), 1) < HEAD_DIM
    return jnp.where(first, value[:PAD], value[PAD:])


def softmax_of(scores, allowed):
    scores = jnp.where(allowed, scores, NEG)
    expo = jnp.exp(scores - jnp.max(scores, axis=-1, keepdims=True))
    return expo * (1.0 / jnp.sum(expo, axis=-1, keepdims=True))


def vector(small, index, n):
    return small[index : index + 1, :n]


def blocks_in(ref):
    return [slice(i * PAD, i * PAD + PAD) for i in range(ref.shape[0] // PAD)]


def add_up(sums, values):
    return [v if s is None else s + v for s, v in zip(sums, values, strict=True)]


def split_rows(half, source, own, sent, wide_rows):
    rows, n = source.shape
    wide_rows[0:rows, 0:n] = source[...].astype(F32)
    for which, target in ((half, own), (1 - half, sent)):
        for block, at in enumerate(blocks_in(target)):
            start = pl.multiple_of(which * (rows // 2) + block * BLOCK, 8)
            part = wide_rows[pl.ds(start, PAD), 0:n]
            inside = lax.broadcasted_iota(jnp.int32, part.shape, 0) < BLOCK
            target[at, :] = jnp.where(inside, part, 0.0).astype(BF)


def tiles_of(ref, start, n, count):
    return jnp.concatenate([ref[start + t * n : start + t * n + n, :] for t in range(count)], axis=1)


class Packed:
    def __init__(self, refs, n, q, o):
        self.one, self.two = refs
        self.n, self.q, self.o = n, q, o

    def up(self):
        return tiles_of(self.one, 0, self.n, 2)

    def out(self):
        return tiles_of(self.one, 2 * self.n, self.o, 4)

    def bias(self):
        start = 2 * self.n + 4 * self.o
        parts = [self.one[start + 16 * k : start + 16 * k + 16, :].astype(F32) for k in range(3)]
        return (parts[2] + parts[1] + parts[0])[:3]

    def down(self):
        return tiles_of(self.two, 0, self.q, 4)

    def prior(self):
        return self.two[4 * self.q : 4 * self.q + self.n, :]


def put_tiles(target, start, part):
    for t in range(part.shape[-1] // 128):
        target[start : start + part.shape[0], :] = part[:, t * 128 : t * 128 + 128]
        start += part.shape[0]
    return start


def first_kernel(s, frames, qkv, up, out, down, prior, resets, *refs):
    smalls, refs = refs[:-9], refs[-9:]
    sent_ref, one_ref, two_ref, own_ref, small_ref, resets_ref, wide_rows, rows, other = refs
    resets_ref[...] = resets[...]
    split_rows(s[0], frames, own_ref, other, wide_rows)
    start = put_tiles(sent_ref, 0, other)
    for c in range(3):
        start = put_tiles(sent_ref, start, qkv.get().at[c])
    start = put_tiles(one_ref, put_tiles(one_ref, 0, up), out)
    for i, ref in enumerate(smalls):
        small_ref[i : i + 1, : ref.shape[1]] = ref[...]
    rows[...] = jnp.zeros_like(rows)
    for t in range(2):
        rows[t : t + 1, :] = smalls[UP_BIAS][:, pl.ds(pl.multiple_of(s[1] * 256 + t * 128, 128), 128)]
    rows[2:3, :] = smalls[PRIOR_BIAS][:, pl.ds(pl.multiple_of(s[1] * 128, 128), 128)]
    left = rows[...]
    for k in range(3):
        term = left.astype(BF)
        one_ref[start : start + 16, :] = term
        left = left - term.astype(F32)
        start += 16
    put_tiles(two_ref, put_tiles(two_ref, 0, down), prior)


def cut_kernel(s, got, qkv_ref):
    qkv_ref[...] = got[got.shape[0] - qkv_ref.shape[0] :, :]


def cotangents_kernel(s, logit, out, sent, logit_own, out_own, wide_rows, logit_sent, out_sent):
    split_rows(s[0], logit, logit_own, logit_sent, wide_rows)
    split_rows(s[0], out, out_own, out_sent, wide_rows)
    n = logit_sent.shape[1]
    sent[:, :n] = logit_sent[...]
    sent[:, n:] = out_sent[...]


def gate(values, after, name=None):
    count, total = len(values), len(values) + len(after)

    def run(*refs):
        for source, target in zip(refs[:count], refs[total:], strict=True):
            target[...] = source[...]

    near = pl.BlockSpec(memory_space=pltpu.VMEM)
    return pl.pallas_call(
        run,
        in_specs=[near] * total,
        out_specs=[near] * count,
        out_shape=[pltpu.VMEM(v.shape, v.dtype) for v in values],
        compiler_params=pltpu.CompilerParams(vmem_limit_bytes=SPILL),
        cost_estimate=pl.CostEstimate(flops=0, bytes_accessed=0, transcendentals=0),
        name=name,
    )(*[pin(v) for v in values], *[pin(v) for v in after])


def attend_kernel(
    s, own, got, resets, small, q0, q1, q2, q3, qkv,
    first_ref, triple_ref, mixed_ref, qkv_other_ref, other,
):
    other[...] = tiles_of(got, 0, own.shape[0], 2)
    unit, _ = norm_of(whole_rows(s[0], own, other))
    n = first_ref.shape[1]
    first_ref[...] = (unit * vector(small, FIRST_GAIN, n) + vector(small, FIRST_SHIFT, n)).astype(BF)
    for j, piece in enumerate((q0, q1, q2, q3)):
        size = qkv.shape[1] // 4
        rows = pl.ds(pl.multiple_of((s[1] ^ j) * size, 16), size)
        for c in range(3):
            qkv_other_ref[c, rows, :] = tiles_of(piece, c * 2 * size, size, 2)
    for half, weight in enumerate((qkv, qkv_other_ref)):
        for c in range(3):
            value = mm(first_ref[...], weight[c]).astype(BF)
            triple_ref[:, (half * 3 + c) * 256 : (half * 3 + c + 1) * 256] = value
    units = []
    for block, at in enumerate(blocks_in(own)):
        allowed = allowed_pairs(resets[pl.ds(s[0] * len(blocks_in(own)) + block, 1), :PAD])
        units += [(at, allowed, pair, (pair // 2) * 768 + (pair % 2) * 128) for pair in range(4)]
    for group in range(0, len(units), GROUP):
        some = units[group : group + GROUP]
        scores = [
            mm_bt(two_heads(triple_ref[at, start : start + 128] * HEAD_DIM ** (-0.5)), triple_ref[at, start + 256 : start + 384])
            for at, _, _, start in some
        ]
        weights = [softmax_of(score, allowed).astype(BF) for score, (_, allowed, _, _) in zip(scores, some, strict=True)]
        for weight, (at, _, pair, start) in zip(weights, some, strict=True):
            mixed = one_pair(mm(weight, triple_ref[at, start + 512 : start + 640])).astype(BF)
            mixed_ref[at, pair * 128 : pair * 128 + 128] = mixed


def feed_kernel(
    s, own, other, mixed, small, out, up, down, a0, a1, a2, a3, b0, b1, b2, b3,
    block_other_ref, block_own_ref, middle_ref, second_ref, act_ref, slope_ref, ending_ref, prior_in_ref,
    out_other_ref, up_other_ref, down_other_ref, bias_other,
):
    n, half, wide = out.shape[0], up.shape[1], up.shape[0]
    for j, piece in enumerate(zip((a0, a1, a2, a3), (b0, b1, b2, b3))):
        piece = Packed(piece, wide, half // 4, n // 4)
        place = s[1] ^ j
        out_other_ref[pl.ds(pl.multiple_of(place * (n // 4), 16), n // 4), :] = piece.out()
        at = pl.ds(pl.multiple_of(place * 256, 256), 256)
        up_other_ref[:, at] = piece.up()
        down_other_ref[at, :] = piece.down()
        bias = piece.bias()
        bias_other[:, at] = jnp.concatenate([bias[0:1], bias[1:2]], axis=1)
    middle_ref[...] = (
        whole_rows(s[0], own, other)
        + vector(small, OUT_BIAS, wide)
        + mm(mixed[:, :n], out[...])
        + mm(mixed[:, n:], out_other_ref[...])
    )
    unit, _ = norm_of(middle_ref[...])
    second_ref[...] = (unit * vector(small, SECOND_GAIN, wide) + vector(small, SECOND_SHIFT, wide)).astype(BF)
    total = middle_ref[...] + vector(small, DOWN_BIAS, wide)
    for h, (w_up, w_down) in enumerate(((up, down), (up_other_ref, down_other_ref))):
        for i in range(half // 256):
            at = slice(i * 256, i * 256 + 256)
            to = slice(h * half + i * 256, h * half + i * 256 + 256)
            bias = bias_other[:, at] if h else small[UP_BIAS : UP_BIAS + 1, at]
            for rows in blocks_in(own):
                hidden = mm(second_ref[rows, :], w_up[:, at]) + bias
                square = hidden * hidden
                bent = jnp.tanh(GELU_C * (hidden + GELU_A * hidden * square))
                act_ref[rows, to] = (0.5 * hidden * (1.0 + bent)).astype(BF)
                slope_ref[rows, to] = 0.5 * (1.0 + bent) + (0.5 * GELU_C) * hidden * (1.0 - bent * bent) * (
                    1.0 + (3.0 * GELU_A) * square
                )
        total = total + mm(act_ref[:, h * half : h * half + half], w_down[...])
    ending_ref[...] = total
    unit, _ = norm_of(total)
    prior_in_ref[...] = (unit * vector(small, PRIOR_GAIN, wide) + vector(small, PRIOR_SHIFT, wide)).astype(BF)
    low, high = total[:, :256].astype(BF), total[:, 256:].astype(BF)
    block_own_ref[...] = jnp.where(s[0] == 0, low, high)
    block_other_ref[...] = jnp.where(s[0] == 0, high, low)


def prior_kernel(
    s, ending, small, logit_own, out_own, a0, a1, a2, a3, b0, b1, b2, b3, cotangents, prior,
    grad_ending_ref, ending_grad_ref, vec_ref, bias_ref, weight, bias,
):
    half, n = prior.shape[1], prior.shape[0]
    for j, piece in enumerate(zip((a0, a1, a2, a3), (b0, b1, b2, b3))):
        at = pl.ds(pl.multiple_of((s[1] ^ j) * 128, 128), 128)
        piece = Packed(piece, n, n // 2, n // 8)
        weight[:, at] = piece.prior()
        bias[:, at] = piece.bias()[2:3]
    logit_other = cotangents.at[:, :half]
    back = mm_bt(logit_own[...], prior[...]) + mm_bt(logit_other[...], weight[...])
    unit, factor = norm_of(ending[...])
    gain = vector(small, PRIOR_GAIN, unit.shape[1])
    grad = whole_rows(s[0], out_own, cotangents.at[:, half:]) + norm_back(back, unit, factor, gain)
    grad_ending_ref[...] = grad
    ending_grad_ref[...] = grad.astype(BF)
    vec_ref[...] = jnp.concatenate([col_sum(back * unit), col_sum(back), col_sum(grad)], axis=0)
    bias_ref[:, :half] = col_sum(logit_own[...].astype(F32))
    bias_ref[:, half:] = col_sum(logit_other[...].astype(F32))


def logits_kernel(s, prior_in, small, prior, weight, bias, block_other, frames_other, sent_ref, logits_ref):
    half, n = prior.shape[1], block_other.shape[1]
    sent_ref[:, :half] = (mm(prior_in[...], weight[...]) + bias[...]).astype(BF)
    sent_ref[:, half : half + n] = block_other[...]
    sent_ref[:, half + n :] = frames_other[...]
    logits_ref[...] = mm(prior_in[...], prior[...]) + vector(small, PRIOR_BIAS, half)


def store_piece(keep, send, h, j, start, value):
    at = slice(start, start + value.shape[0])
    if j < 2:
        keep[h * 2 + j, at, :] = value
    else:
        send[h * 2 + j - 2, at, :] = value.astype(BF)


def late_grads_kernel(s, prior_in, logit_own, cotangents, act, ending_grad, keep, send, wide):
    half = act.shape[1] // 2
    logit_other = cotangents.at[:, : logit_own.shape[1]]
    n = prior_in.shape[1]
    for h in range(2):
        wide[...] = mm_at(prior_in[...], (logit_own, logit_other)[h][...])
        for j in (2, 3, 0, 1):
            place = s[1] ^ j
            store_piece(keep, send, h, j, 0, wide[:, pl.ds(pl.multiple_of(place * 128, 128), 128)])
            part = act[:, pl.ds(pl.multiple_of(h * half + place * 256, 256), 256)]
            value = mm_at(part, ending_grad[...])
            for t in range(n // 128):
                store_piece(keep, send, h, j, n + t * 256, value[:, t * 128 : t * 128 + 128])


def up_grads_kernel(s, second, hidden_grad, mixed, middle_grad, keep, send, turned, wide):
    turned[...] = second[...].T
    half = hidden_grad.shape[1] // 2
    n, m = second.shape[1], mixed.shape[1] // 2
    for h in range(2):
        wide[...] = mm_at(mixed[:, h * m : h * m + m], middle_grad[...])
        for j in (2, 3, 0, 1):
            place = s[1] ^ j
            value = mm(turned[...], hidden_grad[:, pl.ds(pl.multiple_of(h * half + place * 256, 256), 256)])
            for t in range(2):
                store_piece(keep, send, h, j, t * n, value[:, t * 128 : t * 128 + 128])
            store_piece(keep, send, h, j, 2 * n, wide[:, pl.ds(pl.multiple_of(place * 128, 128), 128)])


def early_grads_kernel(s, first, grad_own, grad_other, keep, send):
    for h in range(2):
        for j in (2, 3, 0, 1):
            place = pl.multiple_of((s[1] ^ j) * 128, 128)
            value = mm_at(first[:, pl.ds(place, 128)], (grad_own, grad_other)[h][...])
            for c in range(3):
                for t in range(2):
                    at = slice(c * 256 + t * 128, c * 256 + t * 128 + 128)
                    store_piece(keep, send, h, j, (t * 3 + c) * 128, value[:, at])


def feed_back_kernel(
    s, ending_grad, slope, middle, grad_ending, small, down, down_other, up, up_other,
    hidden_grad_ref, grad_middle_ref, middle_grad_ref, vec_ref, bias_ref,
):
    half = up.shape[1]
    back = None
    for h, (w_up, w_down) in enumerate(((up, down), (up_other, down_other))):
        for i in range(half // 256):
            at = slice(i * 256, i * 256 + 256)
            to = slice(h * half + i * 256, h * half + i * 256 + 256)
            sums = [None]
            for rows in blocks_in(ending_grad):
                low = (mm_bt(ending_grad[rows, :], w_down[at, :]) * slope[rows, to]).astype(BF)
                hidden_grad_ref[rows, to] = low
                sums = add_up(sums, [col_sum(low.astype(F32))])
            bias_ref[:, to] = sums[0]
        value = mm_bt(hidden_grad_ref[:, h * half : h * half + half], w_up[...])
        back = value if back is None else back + value
    unit, factor = norm_of(middle[...])
    gain = vector(small, SECOND_GAIN, unit.shape[1])
    total = grad_ending[...] + norm_back(back, unit, factor, gain)
    grad_middle_ref[...] = total
    middle_grad_ref[...] = total.astype(BF)
    vec_ref[...] = jnp.concatenate([col_sum(back * unit), col_sum(back), col_sum(total)], axis=0)


def attend_back_kernel(
    half, s, middle_grad, triple, out, resets,
    triple_grad_ref, mixed_grad,
):
    mixed_grad[...] = mm_bt(middle_grad[...], out[...]).astype(BF)
    factor = HEAD_DIM ** (-0.5)
    units = []
    for block, at in enumerate(blocks_in(triple)):
        allowed = allowed_pairs(resets[pl.ds(s[0] * len(blocks_in(triple)) + block, 1), :PAD])
        units += [(at, allowed, pair) for pair in range(2)]
    for group in range(0, len(units), GROUP_BACK):
        some = units[group : group + GROUP_BACK]
        loaded = []
        for at, _, pair in some:
            start = half * 768 + pair * 128
            query, key, value = (triple[at, start + c * 256 : start + c * 256 + 128] for c in range(3))
            mixed2 = two_heads(mixed_grad[at, pair * 128 : pair * 128 + 128])
            loaded.append((two_heads(query * factor), key, value, mixed2))
        scores = [mm_bt(query2, key) for query2, key, _, _ in loaded]
        weight_grads = [mm_bt(mixed2, value) for _, _, value, mixed2 in loaded]
        inner = []
        for score, weight_grad, (_, allowed, _) in zip(scores, weight_grads, some, strict=True):
            again = softmax_of(score, allowed)
            both = again * weight_grad
            total = jnp.sum(both, axis=-1, keepdims=True)
            inner.append((again.astype(BF), (both - again * total).astype(BF)))
        for (again, score_grad), (query2, key, _, mixed2), (at, _, pair) in zip(inner, loaded, some, strict=True):
            thirds = (
                (one_pair(mm(score_grad, key)) * factor).astype(BF),
                mm_at(score_grad, query2).astype(BF),
                mm_at(again, mixed2).astype(BF),
            )
            for c in range(3):
                triple_grad_ref[at, c * 256 + pair * 128 : c * 256 + pair * 128 + 128] = thirds[c]


def frames_back_kernel(
    s, grad_own, grad_other, grad_middle, own, other, qkv_other, small, qkv,
    sent_ref, frames_own_ref, vec_ref,
):
    back = None
    for part, weight in ((grad_own, qkv), (grad_other, qkv_other)):
        for c in range(3):
            value = mm_bt(part[:, c * 256 : c * 256 + 256], weight[c])
            back = value if back is None else back + value
    unit, scale = norm_of(whole_rows(s[0], own, other))
    total = grad_middle[...] + norm_back(back, unit, scale, vector(small, FIRST_GAIN, unit.shape[1]))
    low, high = total[:, :256], total[:, 256:]
    frames_own_ref[...] = jnp.where(s[0] == 0, low, high)
    sent_ref[...] = jnp.where(s[0] == 0, high, low).astype(BF)
    vec_ref[...] = jnp.concatenate([col_sum(back * unit), col_sum(back)], axis=0)


def late_place_kernel(s, mine, near, far, farther, down_ref, prior_ref):
    n, q = prior_ref.shape[0], down_ref.shape[0] // 4
    for j, piece in enumerate((mine, near, far, farther)):
        place = s[1] ^ j
        rows = pl.ds(pl.multiple_of(place * q, 8), q)
        for t in range(down_ref.shape[1] // 128):
            down_ref[rows, t * 128 : t * 128 + 128] = piece[n + t * q : n + t * q + q, :].astype(F32)
        prior_ref[:, pl.ds(pl.multiple_of(place * 128, 128), 128)] = piece[:n, :].astype(F32)


def up_place_kernel(s, mine, near, far, farther, up_ref, out_ref):
    n, m = up_ref.shape[0], out_ref.shape[0]
    for j, piece in enumerate((mine, near, far, farther)):
        place = s[1] ^ j
        for t in range(2):
            columns = pl.ds(pl.multiple_of(place * 256 + t * 128, 128), 128)
            up_ref[:, columns] = piece[t * n : t * n + n, :].astype(F32)
        out_ref[:, pl.ds(pl.multiple_of(place * 128, 128), 128)] = piece[2 * n : 2 * n + m, :].astype(F32)


def early_place_kernel(s, mine, near, far, farther, qkv_ref, *vecs):
    vecs, sums = vecs[:-1], vecs[-1]
    sums[...] = mine[6 * 128 :, :].astype(F32) + far[6 * 128 :, :].astype(F32)
    for j, piece in enumerate((mine, near, far, farther)):
        at = pl.ds(pl.multiple_of((s[1] ^ j) * 128, 128), 128)
        for c in range(3):
            for t in range(2):
                start = (t * 3 + c) * 128
                qkv_ref[c, at, t * 128 : t * 128 + 128] = piece[start : start + 128, :].astype(F32)
    qkv_ref.send()
    row = 0
    for ref in vecs[:8]:
        for t in range(ref.shape[1] // 128):
            ref[:, t * 128 : t * 128 + 128] = sums[row : row + 1, :]
            row += 1
    for ref in vecs[8:]:
        tiles = ref.shape[1] // 128
        for t in range(tiles):
            ref[:, t * 128 : t * 128 + 128] = sums[pl.ds(row + s[0] * tiles + t, 1), :]
        row += 2 * tiles


def core_kernel(s, keep, got, low, rest):
    n = keep.shape[1]
    for out, places, dtype in ((low, (2, 3), BF), (rest, (0, 1), F32)):
        for k, i in enumerate(places):
            out[k * n : k * n + n, :] = (keep[i] + got[i].astype(F32)).astype(dtype)


def core_all_kernel(s, keep, got, *refs):
    vectors, lows, rest = refs[:-4], refs[-4:-1], refs[-1]
    n = keep.shape[1]
    for i in (1, 2, 3):
        lows[i - 1][:n, :] = (keep[i] + got[i].astype(F32)).astype(BF)
    rest[:n, :] = keep[0] + got[0].astype(F32)
    if vectors:
        put_vectors(s, vectors, rest, n)
        for low in lows:
            low[n:, :] = rest[n:, :].astype(BF)


def put_vectors(s, vectors, rest, row):
    for ref in vectors[:3]:
        for i in range(ref.shape[0]):
            for t in range(ref.shape[1] // 128):
                rest[row : row + 1, :] = ref[i : i + 1, t * 128 : t * 128 + 128]
                row += 1
    for ref in vectors[3:]:
        tiles = ref.shape[1] // 128
        for t in range(tiles):
            place = row + lax.rem(t + s[0] * (tiles // 2), tiles)
            rest[pl.ds(place, 1), :] = ref[:, t * 128 : t * 128 + 128]
        row += tiles
    rest[row:, :] = jnp.zeros((rest.shape[0] - row, 128), F32)


def over_kernel(s, rest, got, low, mine):
    n = low.shape[0]
    low[...] = (rest[n:, :] + got[n:, :].astype(F32)).astype(BF)
    mine[...] = rest[:n, :] + got[:n, :].astype(F32)


def halves_kernel(s, *refs):
    total, (keep, send) = refs[-1], refs[-3:-1]
    total[...] = functools.reduce(lambda x, y: x + y, [r[...].astype(F32) for r in refs[:-3]])
    n = keep.shape[0]
    send[...] = total[pl.ds(pl.multiple_of((1 - s[2]) * n, 16), n), :].astype(BF)
    keep[...] = total[pl.ds(pl.multiple_of(s[2] * n, 16), n), :].astype(BF)


def join_kernel(s, mine, got, out):
    n = mine.shape[0]
    out[pl.ds(pl.multiple_of(s[2] * n, 16), n), :] = mine[...]
    out[pl.ds(pl.multiple_of((1 - s[2]) * n, 16), n), :] = got[...]


def total_kernel(s, *refs):
    refs[-1][...] = functools.reduce(lambda x, y: x + y, [r[...].astype(F32) for r in refs[:-1]]).astype(BF)


def rows_kernel(entries, s, *refs):
    count = len(entries)
    given, outs, rooms = refs[: 2 * count], refs[2 * count : 3 * count], refs[3 * count :]
    for i, columns in enumerate(entries):
        own, got, out, room = given[2 * i], given[2 * i + 1], outs[i], rooms[i]
        rows = out.shape[0] // 2
        for block, at in enumerate(blocks_in(own)):
            for which, ref, cut in ((s[0], own, slice(None)), (1 - s[0], got, columns)):
                start = pl.multiple_of(which * rows + block * BLOCK, 8)
                room[pl.ds(start, BLOCK), :] = ref[at, cut].astype(F32)[:BLOCK]
        out[...] = room[...].astype(out.ref.dtype)
        out.send()


class Loaded:
    def __init__(self, ref, copy):
        self.ref, self.copy, self.shape = ref, copy, ref.shape

    def get(self):
        if self.copy is not None:
            self.copy.wait()
            self.copy = None
        return self.ref

    def __getitem__(self, index):
        return self.get()[index]


class Leaving:
    def __init__(self, ref, copy):
        self.ref, self.copy, self.shape, self.sent = ref, copy, ref.shape, False

    def __getitem__(self, index):
        return self.ref[index]

    def __setitem__(self, index, value):
        self.ref[index] = value

    def send(self):
        if not self.sent:
            self.copy.start()
            self.sent = True


class Far:
    def __init__(self, value, shape=None, cut=None):
        self.value, self.shape, self.cut = value, shape or value.shape, cut or (lambda s, ref: ref)


def call(kernel, scalars, ins, outs, scratch=(), name=None, after=(), cost=1.0, loads=()):
    n_own, n_loads = len(ins), len(loads)
    ins, outs = [*ins, *[Far(v) for v in loads]], [*outs, *[(v.shape, v.dtype, True) for v in loads]]
    n_in, n_out, n_after = len(ins), len(outs), len(after)
    far_in = [i for i, v in enumerate(ins[:n_own]) if isinstance(v, Far)]
    far_out = [i for i, o in enumerate(outs) if not o[2]]
    room = [pltpu.VMEM(ins[i].shape, ins[i].value.dtype) for i in far_in]
    room += [pltpu.VMEM(outs[i][0], outs[i][1]) for i in far_out]
    need = sum(math.prod(r.shape) * jnp.dtype(r.dtype).itemsize for r in room + list(scratch))

    def run(s, *refs):
        given, refs = list(refs[:n_in]), refs[n_in + n_after :]
        made, refs = list(refs[:n_out]), refs[n_out:]
        own, refs = refs[: len(scratch)], refs[len(scratch) :]
        rooms, sems = refs[:-1], refs[-1]
        for k, i in enumerate(far_in):
            copy = pltpu.make_async_copy(ins[i].cut(s, given[i]), rooms[k], sems.at[k])
            copy.start()
            given[i] = Loaded(rooms[k], copy)
        bringing = []
        for k in range(n_loads):
            copy = pltpu.make_async_copy(given[n_own + k], made[n_out - n_loads + k], sems.at[len(rooms) + k])
            copy.start()
            bringing.append(copy)
        leaving = []
        for k, i in enumerate(far_out, len(far_in)):
            made[i] = Leaving(rooms[k], pltpu.make_async_copy(rooms[k], made[i], sems.at[k]))
            leaving.append(made[i])
        kernel(s, *given[:n_own], *made[: n_out - n_loads], *own)
        for copy in bringing:
            copy.wait()
        for value in given:
            if isinstance(value, Loaded):
                value.get()
        for value in leaving:
            value.send()
        for value in leaving:
            value.copy.wait()

    near, far = pl.BlockSpec(memory_space=pltpu.VMEM), pl.BlockSpec(memory_space=pltpu.HBM)
    return pl.pallas_call(
        run,
        in_specs=[pl.BlockSpec(memory_space=pltpu.SMEM)]
        + [far if isinstance(v, Far) else near for v in ins]
        + [far if isinstance(v, Far) else near for v in after],
        out_specs=[near if stays else far for _, _, stays in outs],
        out_shape=[(pltpu.VMEM if stays else pltpu.HBM)(shape, dtype) for shape, dtype, stays in outs],
        scratch_shapes=list(scratch) + room + [pltpu.SemaphoreType.DMA((max(1, len(room) + n_loads),))],
        compiler_params=pltpu.CompilerParams(vmem_limit_bytes=need + SPILL),
        cost_estimate=pl.CostEstimate(flops=int(cost * COST), bytes_accessed=0, transcendentals=0),
        name=name,
    )(scalars, *[pin(v) for v in ins], *[pin(v) for v in after])


def pin(value):
    if isinstance(value, Far):
        return pltpu.with_memory_space_constraint(value.value, pltpu.HBM)
    return pltpu.with_memory_space_constraint(value, pltpu.VMEM)


def swap(value, axes, sizes, mask):
    count = 1
    for size in sizes:
        count *= size
    return lax.ppermute(value, axes, [(i, i ^ mask) for i in range(count)])


class Moves:
    def __init__(self, n_dp, n_tensor):
        self.n_dp, self.n_tensor = n_dp, n_tensor
        self.dp = lax.axis_index("dp")
        self.here = lax.axis_index("tensor")

    def along(self, value, mask):
        return swap(value, "dp", (self.n_dp,), mask)

    def core(self, value):
        return self.along(value, 1)

    def side(self, value):
        return self.along(value, 2)

    def over(self, value):
        return swap(value, "tensor", (self.n_tensor,), 1)

    def cross(self, value):
        return swap(value, ("dp", "tensor"), (self.n_dp, self.n_tensor), 5)


    def reduce_core(self, scalars, keep, sent, name, after=()):
        n = 2 * sent.shape[1]
        outs = [((n, 128), BF, True), ((n, 128), F32, True)]
        return call(core_kernel, scalars, [keep, self.core(sent)], outs, name=name, after=after, cost=FOLD)

    def reduce_over(self, scalars, low, rest, name, after=()):
        n = low.shape[0] // 2
        outs = [((n, 128), BF, True), ((n, 128), F32, True)]
        return call(over_kernel, scalars, [rest, self.over(low)], outs, name=name, after=after, cost=FOLD)

    def reduce_core_all(self, scalars, keep, sent, name, vectors=(), spare=0, after=()):
        n = sent.shape[1] + spare
        outs = [((n, 128), BF, True)] * 3 + [((n, 128), F32, True)]
        ins = [keep, self.core(sent), *vectors]
        return call(core_all_kernel, scalars, ins, outs, name=name, after=after, cost=FOLD)

    def sides(self, lows):
        return [self.side(lows[0]), self.over(lows[1]), self.cross(lows[2])]

    def total(self, scalars, values, name, after=()):
        shape = values[0].shape
        return call(total_kernel, scalars, values, [(shape, BF, True)], name=name, after=after, cost=FOLD)[0]

    def halves(self, scalars, values, name, after=()):
        n = values[0].shape[0]
        return call(
            halves_kernel,
            scalars,
            values,
            [((n // 2, 128), BF, True)] * 2,
            [pltpu.VMEM((n, 128), F32)],
            name=name,
            after=after,
            cost=FOLD,
        )

    def join(self, scalars, mine, got, name, after=()):
        shape = (mine.shape[0] * 2, 128)
        return call(join_kernel, scalars, [mine, got], [(shape, BF, True)], name=name, after=after, cost=FOLD)[0]

    def bits(self):
        return [1 << i for i in range(2, self.n_dp.bit_length() - 1)]

    def gather(self, total):
        near = self.side(total)
        return total, near, self.core(total), self.core(near)


def local(
    n_dp, n_tensor, frames, resets, first_gain, first_shift, qkv_weight, out_weight, out_bias, second_gain,
    second_shift, up_weight, up_bias, down_weight, down_bias, prior_gain, prior_shift, prior_weight,
    prior_bias, out_cotangent, logit_cotangent,
):
    move = Moves(n_dp, n_tensor)
    rows, half = frames.shape
    width = 2 * half
    mine = rows // 2
    blocks = mine // BLOCK
    hidden_width, n_logits = up_bias.shape[0], prior_bias.shape[0]
    row = lambda v: v.reshape(1, -1)
    core, side = move.dp & 1, (move.dp >> 1) & 1
    reset_rows = jnp.pad(resets.reshape(-1, BLOCK), ((0, -(2 * blocks) % 8), (0, -BLOCK % 128)))
    scalars = jnp.stack([move.here, core * 2 + side, (move.dp >> 2) & 1]).astype(jnp.int32)
    total_rows = blocks * PAD
    quarter = hidden_width // 4

    def near_rows(*entries):
        return [((total_rows, n), dtype, True) for n, dtype in entries]

    def pieces(n):
        return [((4, n, 128), F32, True), ((4, n, 128), BF, True)]

    def columns(value, size, which):
        cut = lambda s, ref: ref.at[..., pl.ds(pl.multiple_of(s[which] * size, 128), size)]
        return Far(value, (*value.shape[:-1], size), cut)

    def some_rows(value, size, which):
        cut = lambda s, ref: ref.at[pl.ds(pl.multiple_of(s[which] * size, 16), size), :]
        return Far(value, (size, value.shape[1]), cut)

    vectors = [first_gain, first_shift, out_bias, second_gain, second_shift, down_bias, prior_gain, prior_shift]
    vectors = [row(v) for v in vectors + [up_bias, prior_bias]]
    qkv_rows = 3 * (width // 4) * (half // 128)
    sent_first, sent_one, sent_two, frames_own, small, resets_near = call(
        first_kernel,
        scalars,
        [
            Far(frames),
            Far(
                qkv_weight,
                (3, width // 4, half),
                lambda s, ref: ref.at[:, pl.ds(pl.multiple_of(s[1] * (width // 4), 16), width // 4), :],
            ),
            columns(up_weight, quarter, 1),
            some_rows(out_weight, half // 4, 1),
            some_rows(down_weight, quarter, 1),
            columns(prior_weight, n_logits // 4, 1),
            Far(reset_rows),
            *[Far(v) for v in vectors],
        ],
        [((total_rows * (half // 128) + qkv_rows, 128), BF, True)]
        + [((width * 2 + half + 48, 128), BF, True), ((quarter * 4 + width, 128), BF, True)]
        + near_rows((half, BF))
        + [((16, hidden_width), F32, True), (reset_rows.shape, jnp.int32, True)],
        [pltpu.VMEM((rows + 16, half), F32), pltpu.VMEM((16, 128), F32), pltpu.VMEM((total_rows, half), BF)],
        "first_parts",
        cost=2.0,
    )

    def all_quarters(got):
        beside = move.side(got)
        return [got, beside, move.core(got), move.core(beside)]

    got_first = move.over(sent_first)
    (qkv_got,) = call(cut_kernel, scalars, [got_first], [((qkv_rows, 128), BF, True)], name="cut", cost=100.0)
    (sent_one,) = gate([sent_one], [got_first], "after_first")
    got_one = move.over(sent_one)
    cot_sent, logit_own, out_own, qkv_near, out_near, up_near, down_near, prior_near = call(
        cotangents_kernel,
        scalars,
        [Far(logit_cotangent), Far(out_cotangent)],
        near_rows((n_logits + half, BF), (n_logits, BF), (half, BF)),
        [pltpu.VMEM((rows + 16, n_logits), F32)]
        + [pltpu.VMEM((total_rows, n), BF) for n in (n_logits, half)],
        name="cotangents",
        after=(sent_first,),
        cost=2.3,
        loads=(qkv_weight, out_weight, up_weight, down_weight, prior_weight),
    )
    (sent_two,) = gate([sent_two], [qkv_got, sent_one, cot_sent], "after_cut")
    got_two = move.over(sent_two)
    first, triple, mixed, qkv_other, frames_other = call(
        attend_kernel,
        scalars,
        [frames_own, got_first, resets_near, small, *all_quarters(qkv_got), qkv_near],
        near_rows((width, BF), (3 * width, BF), (width, BF)) + [(qkv_weight.shape, BF, True)] + near_rows((half, BF)),
        name="attend",
        cost=5.5,
    )
    beside_one = move.side(got_one)
    got_two, cot_sent = gate([got_two, cot_sent], [mixed, beside_one], "after_attend")
    beside_two = move.side(got_two)
    packed = [got_one, beside_one, move.core(got_one), move.core(beside_one)]
    packed += [got_two, beside_two, move.core(got_two), move.core(beside_two)]
    cotangents = move.over(cot_sent)
    block_send, block_own, middle, second, act, slope, ending, prior_in, out_other, up_other, down_other = call(
        feed_kernel,
        scalars,
        [frames_own, frames_other, mixed, small, out_near, up_near, down_near, *packed],
        near_rows((half, BF), (half, BF))
        + near_rows((width, F32), (width, BF), (2 * hidden_width, BF), (2 * hidden_width, F32))
        + near_rows((width, F32), (width, BF))
        + [(v.shape, BF, True) for v in (out_weight, up_weight, down_weight)],
        [pltpu.VMEM((1, hidden_width), F32)],
        name="feed",
        cost=7.2,
    )
    grad_ending, ending_grad, vec_three, prior_bias_sum, prior_other, prior_bias_other = call(
        prior_kernel,
        scalars,
        [ending, small, logit_own, out_own, *packed, cotangents, prior_near],
        near_rows((width, F32), (width, BF))
        + [((3, width), F32, True), ((1, 2 * n_logits), F32, True)]
        + [(prior_weight.shape, BF, True), ((1, n_logits), F32, True)],
        name="prior",
        cost=2.5,
    )
    late_keep, late_send = call(
        late_grads_kernel,
        scalars,
        [prior_in, logit_own, cotangents, act, ending_grad],
        pieces(width + hidden_width),
        [pltpu.VMEM((width, n_logits), F32)],
        name="late_grads",
        cost=3.5,
    )
    hidden_grad, grad_middle, middle_grad, vec_two, up_bias_sum = call(
        feed_back_kernel,
        scalars,
        [ending_grad, slope, middle, grad_ending, small, down_near, down_other, up_near, up_other],
        near_rows((2 * hidden_width, BF), (width, F32), (width, BF))
        + [((3, width), F32, True), ((1, 2 * hidden_width), F32, True)],
        name="feed_back",
        cost=6.5,
        after=(late_send,),
    )
    *late_low, late_rest = move.reduce_core_all(scalars, late_keep, late_send, "late_core", after=(hidden_grad,))
    up_keep, up_send = call(
        up_grads_kernel,
        scalars,
        [second, hidden_grad, mixed, middle_grad],
        pieces(width * hidden_width // 512 + half),
        [pltpu.VMEM((width, total_rows), BF), pltpu.VMEM((half, width), F32)],
        name="up_grads",
        after=(late_low[0],),
        cost=3.0,
    )
    def attend_back(half, out, after):
        return call(
            functools.partial(attend_back_kernel, half),
            scalars,
            [middle_grad, triple, out, resets_near],
            near_rows((3 * width // 2, BF)),
            [pltpu.VMEM((total_rows, width // 2), BF)],
            name=f"attend_back_{half}",
            after=after,
            cost=4.5,
        )[0]

    grad_own = attend_back(0, out_near, (up_send,))
    up_low, up_rest = move.reduce_core(scalars, up_keep, up_send, "up_core", (grad_own,))
    grad_other = attend_back(1, out_other, (up_low,))
    keep, send = call(
        early_grads_kernel,
        scalars,
        [first, grad_own, grad_other],
        pieces(768),
        name="early_grads",
        after=(),
        cost=2.0,
    )
    late, late_half = move.halves(scalars, [late_rest, *move.sides(late_low)], "late_1", (send,))
    frames_send, frames_grad, vec_one = call(
        frames_back_kernel,
        scalars,
        [grad_own, grad_other, grad_middle, frames_own, frames_other, qkv_other, small, qkv_near],
        near_rows((half, BF), (half, F32)) + [((2, width), F32, True)],
        name="frames_back",
        after=(late,),
        cost=2.5,
    )
    bits = move.bits()
    spare = 64
    vectors = [vec_one, vec_two, vec_three, up_bias_sum, prior_bias_sum]
    *early_low, early_rest = move.reduce_core_all(scalars, keep, send, "early_core", vectors, spare)
    late = move.total(scalars, [late, move.along(late_half, bits[0])], "late_2", (early_low[0],))
    up_low, up_rest = move.reduce_over(scalars, up_low, up_rest, "up_over", (late,))
    done = up_low
    for bit in bits[1:]:
        done = late = move.total(scalars, [late, move.along(late, bit)], "late_3", (done,))
    done = early = move.total(scalars, [early_rest, *move.sides(early_low)], "early_1", (done,))
    up, up_half = move.halves(scalars, [up_rest, move.side(up_low)], "up_1", (done,))
    back_send, logits_own = call(
        logits_kernel,
        scalars,
        [prior_in, small, prior_near, prior_other, prior_bias_other, block_send, frames_send],
        near_rows((n_logits + 2 * half, BF), (n_logits, F32)),
        name="logits",
        after=(up,),
        cost=2.0,
    )
    done = late = move.join(scalars, late, move.along(late, bits[0]), "late_4", (back_send,))
    for bit in bits[:-1]:
        done = early = move.total(scalars, [early, move.along(early, bit)], "early_2", (done,))
    done = up = move.total(scalars, [up, move.along(up_half, bits[0])], "up_2", (done,))
    down_grad, prior_grad = call(
        late_place_kernel,
        scalars,
        list(move.gather(late)),
        [((hidden_width, width), F32, False), ((width, n_logits), F32, False)],
        name="late_place",
        after=(done,),
        cost=FOLD,
    )
    early = move.total(scalars, [early, move.along(early, bits[-1])], "early_3", (Far(down_grad),))
    done = early
    for bit in bits[1:]:
        done = up = move.total(scalars, [up, move.along(up, bit)], "up_3", (done,))
    up = move.join(scalars, up, move.along(up, bits[0]), "up_4", (done,))
    back_got = move.over(back_send)
    up, early_pieces = move.gather(up), move.gather(early)
    block_out, logits, grad_frames = call(
        functools.partial(
            rows_kernel,
            [slice(n_logits, n_logits + half), slice(0, n_logits), slice(n_logits + half, n_logits + 2 * half)],
        ),
        scalars,
        [v for own in (block_own, logits_own, frames_grad) for v in (own, back_got)],
        [((rows, half), BF, False), ((rows, n_logits), F32, False), ((rows, half), F32, False)],
        [pltpu.VMEM((rows, n), F32) for n in (half, n_logits, half)],
        name="rows_back",
        after=(up[0],),
        cost=FOLD,
    )
    qkv_grad, *named = call(
        early_place_kernel,
        scalars,
        list(early_pieces),
        [((3, width, half), F32, False)]
        + [((1, n), F32, False) for n in [width] * 8 + [hidden_width, n_logits]],
        [pltpu.VMEM((spare, 128), F32)],
        name="early_place",
        after=(Far(block_out),),
        cost=FOLD,
    )
    up_grad, out_grad = call(
        up_place_kernel,
        scalars,
        list(up),
        [((width, hidden_width), F32, False), ((half, width), F32, False)],
        name="up_place",
        after=(Far(qkv_grad),),
        cost=FOLD,
    )
    named = [v.reshape(-1) for v in named]
    return (
        block_out,
        logits,
        grad_frames,
        named[0],
        named[1],
        qkv_grad,
        out_grad,
        named[4],
        named[2],
        named[3],
        up_grad,
        named[8],
        down_grad,
        named[7],
        named[5],
        named[6],
        prior_grad,
        named[9],
    )


def solution(mesh):
    rows, cols = P("dp", "tensor"), P(None, "tensor")
    placed = (
        rows, P("dp"), P(), P(), P(None, None, "tensor"), P("tensor", None), P(), P(), P(), cols, P("tensor"),
        P("tensor", None), P(), P(), P(), cols, P("tensor"), rows, rows,
    )
    given = (
        rows, rows, rows, P(), P(), P(None, None, "tensor"), P("tensor", None), P(), P(), P(), cols,
        P("tensor"), P("tensor", None), P(), P(), P(), cols, P("tensor"),
    )
    return jax.shard_map(
        functools.partial(local, mesh.shape["dp"], mesh.shape["tensor"]),
        mesh=mesh,
        in_specs=placed,
        out_specs=given,
        check_vma=False,
    )
```

profile of v0, /device:TPU:0, one launch (start us, length us, event | category | flops | bytes accessed | tf_op | source)
XLA Modules:
  0.0 175.5 jit_solution(17865431460457396009)
XLA Ops:
  0.7 0.8 reshape.99
  1.4 0.6 pad.4.refs_6_
  2.1 2.3 %first_parts.1 = (bf16[2016,128]{1,0:T(8,128)(2,1)S(1)}, bf16[1328,128]{1,0:T(8,128)(2,1)S(1)}, bf16[1536,128]{1,0:T(8,128)(2,1)S(1)}, bf16[624,256]{1,0:T(8,128...) custom-call(s32[3]{0:T(128)S(1)} %pad_add_fusion.s, bf16[1200,256]{1,0:T(8,128)(2,1)} %refs_0_.2, ...), custom_call_target="tpu_custom_call" | custom-call | flops 200000000 | tf_op jit(solution)/shard_map/first_parts/pallas_call | solution.py:630
  4.4 3.0 %collective-permute-start = (bf16[2016,128]{1,0:T(8,128)(2,1)S(1)}, bf16[2016,128]{1,0:T(8,128)(2,1)S(1)}, u32[]{:S(2)}, u32[]{:S(2)}) collective-permute-start(bf16[2016,128]{1,0:T(8,128)(2,1)S(1)} %get-tuple-element.107.refs_7_), channel_id=1, source_target_pairs={{0,1},{1,0},{2,3},{3,2},{4,5},{5,4},{6,7},{7,6},{8,9},{9,8},{10,11... | collective-permute-start | bytes 1548296 | tf_op jit(solution)/shard_map/ppermute | solution.py:654
  7.5 11.7 %collective-permute-done.refs_0_.refs_1_ = bf16[2016,128]{1,0:T(8,128)(2,1)S(1)} collective-permute-done((bf16[2016,128]{1,0:T(8,128)(2,1)S(1)}, bf16[2016,128]{1,0:T(8,128)(2,1)S(1)}, u32[]{:S(2)}, u32[]{:S(2)}) %collective-permute-start) | collective-permute-done | bytes 516128 | tf_op jit(solution)/shard_map/ppermute | solution.py:654
  19.2 1.8 %collective-permute-start.4 = (bf16[1328,128]{1,0:T(8,128)(2,1)S(1)}, bf16[1328,128]{1,0:T(8,128)(2,1)S(1)}, u32[]{:S(2)}, u32[]{:S(2)}) collective-permute-start(bf16[1328,128]{1,0:T(8,128)(2,1)S(1)} %after_first.1.refs_2_), channel_id=1, source_target_pairs={{0,1},{1,0},{2,3},{3,2},{4,5},{5,4},{6,7},{7,6},{8,9},{9,8},{10,11... | collective-permute-start | bytes 1019912 | tf_op jit(solution)/shard_map/ppermute | solution.py:654
  21.6 1.6 collective-permute-start.1
  23.1 3.1 %cotangents.1 = (bf16[624,768]{1,0:T(8,128)(2,1)S(1)}, bf16[624,512]{1,0:T(8,128)(2,1)S(1)}, bf16[624,256]{1,0:T(8,128)(2,1)S(1)}, bf16[3,512,256]{2,1,0:T(8,128...) custom-call(s32[3]{0:T(128)S(1)} %pad_add_fusion.s, ...), custom_call_target="tpu_custom_call" | custom-call | flops 230000000 | tf_op jit(solution)/shard_map/cotangents/pallas_call | solution.py:630
  26.9 2.4 %collective-permute-done.4.refs_7_.refs_4_ = bf16[1328,128]{1,0:T(8,128)(2,1)S(1)} collective-permute-done((bf16[1328,128]{1,0:T(8,128)(2,1)S(1)}, bf16[1328,128]{1,0:T(8,128)(2,1)S(1)}, u32[]{:S(2)}, u32[]{:S(2)}) %collective-permute-start.4) | collective-permute-done | bytes 340000 | tf_op jit(solution)/shard_map/ppermute | solution.py:654
  29.3 2.3 %collective-permute-start.5 = (bf16[1328,128]{1,0:T(8,128)(2,1)S(1)}, bf16[1328,128]{1,0:T(8,128)(2,1)S(1)}, u32[]{:S(2)}, u32[]{:S(2)}) collective-permute-start(bf16[1328,128]{1,0:T(8,128)(2,1)S(1)} %collective-permute-done.4.refs_7_.refs_4_), channel_id=1, source_target_pairs={{0,4},{2,6},{4,0},{6,2},{8,12},{10,14},{12,8},{14,10},{16,20},{18,... | collective-permute-start | bytes 1019912 | tf_op jit(solution)/shard_map/ppermute | solution.py:654
  32.1 0.9 collective-permute-done.2.refs_6_
  33.3 4.3 %attend.1 = (bf16[624,512]{1,0:T(8,128)(2,1)S(1)}, bf16[624,1536]{1,0:T(8,128)(2,1)S(1)}, bf16[624,512]{1,0:T(8,128)(2,1)S(1)}, bf16[3,512,256]{2,1,0:T(8,128)(2,1)S(1)}, bf16[624,256]{1,0:T(8,128)(2,1)S(1)}) custom-call(s32[3]{0:T(128)S(1)} %pad_add_fusion.s, bf16[624,256]{1,0:T(8,128)(2,1)S(1)} %get-tuple-element.106.refs_0_.refs_3_, ...), custom_call_target="tpu_custom_call" | custom-call | flops 550000000 | tf_op jit(solution)/shard_map/attend/pallas_call | solution.py:630
  37.8 1.9 %collective-permute-start.12 = (bf16[624,768]{1,0:T(8,128)(2,1)S(1)}, bf16[624,768]{1,0:T(8,128)(2,1)S(1)}, u32[]{:S(2)}, u32[]{:S(2)}) collective-permute-start(bf16[624,768]{1,0:T(8,128)(2,1)S(1)} %get-tuple-element.126), channel_id=1, source_target_pairs={{0,1},{1,0},{2,3},{3,2},{4,5},{5,4},{6,7},{7,6},{8,9},{9,8},{10,11... | collective-permute-start | bytes 2875400 | tf_op jit(solution)/shard_map/ppermute | solution.py:654
  39.7 1.1 collective-permute-start.9
  40.8 9.9 %collective-permute-done.9.refs_12_.refs_9_ = bf16[1536,128]{1,0:T(8,128)(2,1)S(1)} collective-permute-done((bf16[1536,128]{1,0:T(8,128)(2,1)S(1)}, bf16[1536,128]{1,0:T(8,128)(2,1)S(1)}, u32[]{:S(2)}, u32[]{:S(2)}) %collective-permute-start.9) | collective-permute-done | bytes 393248 | tf_op jit(solution)/shard_map/ppermute | solution.py:654
  51.2 1.7 collective-permute-done.6.refs_9_.refs_6_
  53.3 6.9 %feed.1 = (bf16[624,256]{1,0:T(8,128)(2,1)S(1)}, bf16[624,256]{1,0:T(8,128)(2,1)S(1)}, f32[624,512]{1,0:T(8,128)S(1)}, bf16[624,512]{1,0:T(8,128)(2,1)S(1)}, bf1...) custom-call(s32[3]{0:T(128)S(1)} %pad_add_fusion.s, ...), custom_call_target="tpu_custom_call" | custom-call | flops 720000000 | tf_op jit(solution)/shard_map/feed/pallas_call | solution.py:630
  60.2 1.1 collective-permute-done.12.refs_12_.refs_2_
  61.3 2.3 %prior.1 = (f32[624,512]{1,0:T(8,128)S(1)}, bf16[624,512]{1,0:T(8,128)(2,1)S(1)}, f32[3,512]{1,0:T(4,128)S(1)}, f32[1,1024]{1,0:T(1,128)S(1)}, bf16[512,512]{1,0:T(8,128)(2,1)S(1)}, /*index=5*/f32[1,512]{1,0:T(1,128)S(1)}) custom-call(s32[3]{0:T(128)S(1)} %pad_add_fusion.s, f32[624,512]{1,0:T(8,128)S(1)} %get-tuple-element.123.refs_0_, ...), custom_call_target="tpu_custom_call" | custom-call | flops 250000000 | tf_op jit(solution)/shard_map/prior/pallas_call | solution.py:630
  63.6 3.5 %late_grads.1 = (f32[4,1536,128]{2,1,0:T(8,128)S(1)}, bf16[4,1536,128]{2,1,0:T(8,128)(2,1)S(1)}) custom-call(s32[3]{0:T(128)S(1)} %pad_add_fusion.s, bf16[624,512]{1,0:T(8,128)(2,1)S(1)} %get-tuple-element.121.refs_0_, bf16[624,512]{1,0:T(8,128)(2,1)S(1)} %get-tuple-element.124.refs_2_.refs_1_, ...), custom_call_target="tpu_custom_call" | custom-call | flops 350000000 | tf_op jit(solution)/shard_map/late_grads/pallas_call | solution.py:630
  67.2 4.9 %feed_back.1 = (bf16[624,2048]{1,0:T(8,128)(2,1)S(1)}, f32[624,512]{1,0:T(8,128)S(1)}, bf16[624,512]{1,0:T(8,128)(2,1)S(1)}, f32[3,512]{1,0:T(4,128)S(1)}, f32[1,2048]{1,0:T(1,128)S(1)}) custom-call(s32[3]{0:T(128)S(1)} %pad_add_fusion.s, bf16[624,512]{1,0:T(8,128)(2,1)S(1)} %get-tuple-element.130.refs_4_.refs_0_, ...), custom_call_target="tpu_custom_call" | custom-call | flops 650000000 | tf_op jit(solution)/shard_map/feed_back/pallas_call | solution.py:630
  72.1 0.8 late_core.1
  72.9 2.9 %up_grads.1 = (f32[4,1280,128]{2,1,0:T(8,128)S(1)}, bf16[4,1280,128]{2,1,0:T(8,128)(2,1)S(1)}) custom-call(s32[3]{0:T(128)S(1)} %pad_add_fusion.s, bf16[624,512]{1,0:T(8,128)(2,1)S(1)} %get-tuple-element.140.refs_0_, bf16[624,2048]{1,0:T(8,128)(2,1)S(1)} %get-tuple-element.141.refs_2_.refs_1_, bf16[624,512]{1,0:T(8,128)(2,1)S(1)} %get-tuple-element.112.refs_2_, ...), custom_call_target="tpu_custom_call" | custom-call | flops 300000000 | tf_op jit(solution)/shard_map/up_grads/pallas_call | solution.py:630
  76.6 1.7 collective-permute-start.16
  78.4 1.6 collective-permute-start.17
  79.9 3.7 %attend_back_0.1.refs_2_.refs_1_.refs_0_ = bf16[624,768]{1,0:T(8,128)(2,1)S(1)} custom-call(s32[3]{0:T(128)S(1)} %pad_add_fusion.s, bf16[624,512]{1,0:T(8,128)(2,1)S(1)} %get-tuple-element.138.refs_3_.refs_0_, bf16[624,1536]{1,0:T(8,128)(2,1)S(1)} %get-tuple-element.139.refs_1_, bf16[256,512]{1,0:T(8,128)(2,1)S(1)} %get-tuple-element.113.refs_4_.refs_2_, ...), custom_call_target="tpu_custom_call" | custom-call | flops 450000000 | tf_op jit(solution)/shard_map/attend_back_0/pallas_call | solution.py:630
  83.9 0.8 up_core.1
  84.7 1.8 %collective-permute-start.18 = (bf16[2560,128]{1,0:T(8,128)(2,1)S(1)}, bf16[2560,128]{1,0:T(8,128)(2,1)S(1)}, u32[]{:S(2)}, u32[]{:S(2)}) collective-permute-start(bf16[2560,128]{1,0:T(8,128)(2,1)S(1)} %get-tuple-element.147.refs_4_), channel_id=1, source_target_pairs={{0,1},{1,0},{2,3},{3,2},{4,5},{5,4},{6,7},{7,6},{8,9},{9,8},{10,11... | collective-permute-start | bytes 1966088 | tf_op jit(solution)/shard_map/ppermute | solution.py:654
  86.5 3.8 %attend_back_1.1.refs_2_.refs_1_ = bf16[624,768]{1,0:T(8,128)(2,1)S(1)} custom-call(s32[3]{0:T(128)S(1)} %pad_add_fusion.s, bf16[624,512]{1,0:T(8,128)(2,1)S(1)} %get-tuple-element.138.refs_3_.refs_0_, bf16[624,1536]{1,0:T(8,128)(2,1)S(1)} %get-tuple-element.139.refs_1_, bf16[256,512]{1,0:T(8,128)(2,1)S(1)} %get-tuple-element.145.refs_2_, ...), custom_call_target="tpu_custom_call" | custom-call | flops 450000000 | tf_op jit(solution)/shard_map/attend_back_1/pallas_call | solution.py:630
  90.2 2.0 %early_grads.1 = (f32[4,768,128]{2,1,0:T(8,128)S(1)}, bf16[4,768,128]{2,1,0:T(8,128)(2,1)S(1)}) custom-call(s32[3]{0:T(128)S(1)} %pad_add_fusion.s, bf16[624,512]{1,0:T(8,128)(2,1)S(1)} %get-tuple-element.153.refs_0_, bf16[624,768]{1,0:T(8,128)(2,1)S(1)} %attend_back_0.1.refs_2_.refs_1_.refs_0_, bf16[624,768]{1,0:T(8,128)(2,1)S(1)} %attend_back_1.1.refs_2_.refs_1_), custom_call_target="tpu_custom_call" | custom-call | flops 200000000 | tf_op jit(solution)/shard_map/early_grads/pallas_call | solution.py:630
  92.3 4.0 %collective-permute-done.16.refs_2_ = bf16[1536,128]{1,0:T(8,128)(2,1)S(1)} collective-permute-done((bf16[1536,128]{1,0:T(8,128)(2,1)S(1)}, bf16[1536,128]{1,0:T(8,128)(2,1)S(1)}, u32[]{:S(2)}, u32[]{:S(2)}) %collective-permute-start.16) | collective-permute-done | bytes 393248 | tf_op jit(solution)/shard_map/ppermute | solution.py:654
  96.3 0.9 collective-permute-done.17.refs_3_
  97.2 0.9 late_1.1
  98.1 1.6 collective-permute-start.19
  99.7 2.3 %frames_back.1 = (bf16[624,256]{1,0:T(8,128)(2,1)S(1)}, f32[624,256]{1,0:T(8,128)S(1)}, f32[2,512]{1,0:T(2,128)S(1)}) custom-call(s32[3]{0:T(128)S(1)} %pad_add_fusion.s, bf16[624,768]{1,0:T(8,128)(2,1)S(1)} %attend_back_0.1.refs_2_.refs_1_.refs_0_, bf16[624,768]{1,0:T(8,128)(2,1)S(1)} %attend_back_1.1.refs_2_.refs_1_, ...), custom_call_target="tpu_custom_call" | custom-call | flops 250000000 | tf_op jit(solution)/shard_map/frames_back/pallas_call | solution.py:630
  102.1 0.8 early_core.1
  102.9 1.7 collective-permute-start.22
  105.2 2.6 %collective-permute-start.25 = (bf16[768,128]{1,0:T(8,128)(2,1)S(1)}, bf16[768,128]{1,0:T(8,128)(2,1)S(1)}, u32[]{:S(2)}, u32[]{:S(2)}) collective-permute-start(bf16[768,128]{1,0:T(8,128)(2,1)S(1)} %late_2.1.refs_2_.refs_0_), channel_id=1, source_target_pairs={{0,16},{2,18},{4,20},{6,22},{8,24},{10,26},{12,28},{14,30},{16,0},... | collective-permute-start | bytes 589832 | tf_op jit(solution)/shard_map/ppermute | solution.py:654
  107.9 1.7 collective-permute-start.23
  109.6 0.6 collective-permute-start.24
  110.2 3.1 %collective-permute-done.18.refs_1_ = bf16[2560,128]{1,0:T(8,128)(2,1)S(1)} collective-permute-done((bf16[2560,128]{1,0:T(8,128)(2,1)S(1)}, bf16[2560,128]{1,0:T(8,128)(2,1)S(1)}, u32[]{:S(2)}, u32[]{:S(2)}) %collective-permute-start.18) | collective-permute-done | bytes 655392 | tf_op jit(solution)/shard_map/ppermute | solution.py:654
  113.4 0.7 up_over.1
  114.1 4.2 %collective-permute-start.21 = (bf16[1280,128]{1,0:T(8,128)(2,1)S(1)}, bf16[1280,128]{1,0:T(8,128)(2,1)S(1)}, u32[]{:S(2)}, u32[]{:S(2)}) collective-permute-start(bf16[1280,128]{1,0:T(8,128)(2,1)S(1)} %get-tuple-element.167.refs_2_), channel_id=1, source_target_pairs={{0,4},{2,6},{4,0},{6,2},{8,12},{10,14},{12,8},{14,10},{16,20},{18,... | collective-permute-start | bytes 983048 | tf_op jit(solution)/shard_map/ppermute | solution.py:654
  118.9 1.6 collective-permute-start.29
  120.5 0.6 early_1.1.refs_2_.refs_0_
  121.7 1.6 collective-permute-done.21.refs_1_
  123.3 0.7 up_1.1
  124.0 1.8 %collective-permute-start.27 = (bf16[640,128]{1,0:T(8,128)(2,1)S(1)}, bf16[640,128]{1,0:T(8,128)(2,1)S(1)}, u32[]{:S(2)}, u32[]{:S(2)}) collective-permute-start(bf16[640,128]{1,0:T(8,128)(2,1)S(1)} %get-tuple-element.175), channel_id=1, source_target_pairs={{0,8},{2,10},{4,12},{6,14},{8,0},{10,2},{12,4},{14,6},{16,24},{18,... | collective-permute-start | bytes 491528 | tf_op jit(solution)/shard_map/ppermute | solution.py:654
  125.8 1.4 logits.1
  127.2 1.8 %collective-permute-start.26 = (bf16[624,1024]{1,0:T(8,128)(2,1)S(1)}, bf16[624,1024]{1,0:T(8,128)(2,1)S(1)}, u32[]{:S(2)}, u32[]{:S(2)}) collective-permute-start(bf16[624,1024]{1,0:T(8,128)(2,1)S(1)} %get-tuple-element.172.refs_2_), channel_id=1, source_target_pairs={{0,1},{1,0},{2,3},{3,2},{4,5},{5,4},{6,7},{7,6},{8,9},{9,8},{10,11... | collective-permute-start | bytes 3833864 | tf_op jit(solution)/shard_map/ppermute | solution.py:654
  129.7 1.9 %collective-permute-start.32 = (bf16[1536,128]{1,0:T(8,128)(2,1)S(1)}, bf16[1536,128]{1,0:T(8,128)(2,1)S(1)}, u32[]{:S(2)}, u32[]{:S(2)}) collective-permute-start(bf16[1536,128]{1,0:T(8,128)(2,1)S(1)} %late_4.1.refs_2_.refs_0_), channel_id=1, source_target_pairs={{0,4},{2,6},{4,0},{6,2},{8,12},{10,14},{12,8},{14,10},{16,20},{18,... | collective-permute-start | bytes 1179656 | tf_op jit(solution)/shard_map/ppermute | solution.py:654
  132.2 2.9 %collective-permute-start.31 = (bf16[832,128]{1,0:T(8,128)(2,1)S(1)}, bf16[832,128]{1,0:T(8,128)(2,1)S(1)}, u32[]{:S(2)}, u32[]{:S(2)}) collective-permute-start(bf16[832,128]{1,0:T(8,128)(2,1)S(1)} %early_2.1.refs_2_.refs_0_), channel_id=1, source_target_pairs={{0,16},{2,18},{4,20},{6,22},{8,24},{10,26},{12,28},{14,30},{16,0},... | collective-permute-start | bytes 638984 | tf_op jit(solution)/shard_map/ppermute | solution.py:654
  135.1 6.2 %collective-permute-done.32.refs_1_ = bf16[1536,128]{1,0:T(8,128)(2,1)S(1)} collective-permute-done((bf16[1536,128]{1,0:T(8,128)(2,1)S(1)}, bf16[1536,128]{1,0:T(8,128)(2,1)S(1)}, u32[]{:S(2)}, u32[]{:S(2)}) %collective-permute-start.32) | collective-permute-done | bytes 393248 | tf_op jit(solution)/shard_map/ppermute | solution.py:654
  141.9 3.2 %collective-permute-start.30 = (bf16[640,128]{1,0:T(8,128)(2,1)S(1)}, bf16[640,128]{1,0:T(8,128)(2,1)S(1)}, u32[]{:S(2)}, u32[]{:S(2)}) collective-permute-start(bf16[640,128]{1,0:T(8,128)(2,1)S(1)} %up_2.1.refs_4_.refs_0_), channel_id=1, source_target_pairs={{0,16},{2,18},{4,20},{6,22},{8,24},{10,26},{12,28},{14,30},{16,0},... | collective-permute-start | bytes 491528 | tf_op jit(solution)/shard_map/ppermute | solution.py:654
  145.1 2.6 %late_place.1 = (f32[1024,512]{1,0:T(8,128)}, f32[512,512]{1,0:T(8,128)}) custom-call(s32[3]{0:T(128)S(1)} %pad_add_fusion.s, bf16[1536,128]{1,0:T(8,128)(2,1)S(1)} %late_4.1.refs_2_.refs_0_, bf16[1536,128]{1,0:T(8,128)(2,1)S(1)} %collective-permute-done.32.refs_1_, bf16[1536,128]{1,0:T(8,128)(2,1)S(1)} %collective-permute-done.33.refs_2_, ...), custom_call_target="tpu_custom_call" | custom-call | flops 10000000000 | tf_op jit(solution)/shard_map/late_place/pallas_call | solution.py:630
  147.7 0.6 early_3.1.refs_2_.refs_0_
  148.3 5.1 %collective-permute-done.30.refs_1_ = bf16[640,128]{1,0:T(8,128)(2,1)S(1)} collective-permute-done((bf16[640,128]{1,0:T(8,128)(2,1)S(1)}, bf16[640,128]{1,0:T(8,128)(2,1)S(1)}, u32[]{:S(2)}, u32[]{:S(2)}) %collective-permute-start.30) | collective-permute-done | bytes 163872 | tf_op jit(solution)/shard_map/ppermute | solution.py:654
  154.2 1.5 collective-permute-start.36
  155.7 4.5 %collective-permute-done.35.refs_1_ = bf16[640,128]{1,0:T(8,128)(2,1)S(1)} collective-permute-done((bf16[640,128]{1,0:T(8,128)(2,1)S(1)}, bf16[640,128]{1,0:T(8,128)(2,1)S(1)}, u32[]{:S(2)}, u32[]{:S(2)}) %collective-permute-start.35) | collective-permute-done | bytes 163872 | tf_op jit(solution)/shard_map/ppermute | solution.py:654
  160.9 1.6 collective-permute-start.39
  162.6 2.9 %rows_back.1 = (bf16[1200,256]{1,0:T(8,128)(2,1)}, f32[1200,512]{1,0:T(8,128)}, f32[1200,256]{1,0:T(8,128)}) custom-call(s32[3]{0:T(128)S(1)} %pad_add_fusion.s, bf16[624,256]{1,0:T(8,128)(2,1)S(1)} %get-tuple-element.120.refs_0_, bf16[624,1024]{1,0:T(8,128)(2,1)S(1)} %collective-permute-done.26.refs_1_.refs_3_.refs_5_, ...), custom_call_target="tpu_custom_call" | custom-call | flops 10000000000 | tf_op jit(solution)/shard_map/rows_back/pallas_call | solution.py:630
  165.5 5.5 %collective-permute-done.39.refs_1_ = bf16[1280,128]{1,0:T(8,128)(2,1)S(1)} collective-permute-done((bf16[1280,128]{1,0:T(8,128)(2,1)S(1)}, bf16[1280,128]{1,0:T(8,128)(2,1)S(1)}, u32[]{:S(2)}, u32[]{:S(2)}) %collective-permute-start.39) | collective-permute-done | bytes 327712 | tf_op jit(solution)/shard_map/ppermute | solution.py:654
  171.0 1.9 %early_place.1 = (f32[3,512,256]{2,1,0:T(8,128)}, f32[1,512]{1,0:T(1,128)}, f32[1,512]{1,0:T(1,128)}, f32[1,512]{1,0:T(1,128)}, f32[1,512]{1,0:T(1,128)}, /*inde...) custom-call(s32[3]{0:T(128)S(1)} %pad_add_fusion.s, ...), custom_call_target="tpu_custom_call" | custom-call | flops 10000000000 | tf_op jit(solution)/shard_map/early_place/pallas_call | solution.py:630
  173.0 2.4 %up_place.1 = (f32[512,1024]{1,0:T(8,128)}, f32[256,512]{1,0:T(8,128)}) custom-call(s32[3]{0:T(128)S(1)} %pad_add_fusion.s, bf16[1280,128]{1,0:T(8,128)(2,1)S(1)} %up_4.1.refs_6_.refs_0_, bf16[1280,128]{1,0:T(8,128)(2,1)S(1)} %collective-permute-done.39.refs_1_, bf16[1280,128]{1,0:T(8,128)(2,1)S(1)} %collective-permute-done.40.refs_2_, ...), custom_call_target="tpu_custom_call" | custom-call | flops 10000000000 | tf_op jit(solution)/shard_map/up_place/pallas_call | solution.py:630
  (59 shorter events, 9.5 us)
Async XLA Ops:
  4.4 14.7 %collective-permute-start = (bf16[2016,128]{1,0:T(8,128)(2,1)S(1)}, bf16[2016,128]{1,0:T(8,128)(2,1)S(1)}, u32[]{:S(2)}, u32[]{:S(2)}) collective-permute-start(bf16[2016,128]{1,0:T(8,128)(2,1)S(1)} %get-tuple-element.107.refs_7_), channel_id=1, source_target_pairs={{0,1},{1,0},{2,3},{3,2},{4,5},{5,4},{6,7},{7,6},{8,9},{9,8},{10,11... | collective-permute-start | bytes 1548296 | tf_op jit(solution)/shard_map/ppermute | solution.py:654
  19.2 10.1 %collective-permute-start.4 = (bf16[1328,128]{1,0:T(8,128)(2,1)S(1)}, bf16[1328,128]{1,0:T(8,128)(2,1)S(1)}, u32[]{:S(2)}, u32[]{:S(2)}) collective-permute-start(bf16[1328,128]{1,0:T(8,128)(2,1)S(1)} %after_first.1.refs_2_), channel_id=1, source_target_pairs={{0,1},{1,0},{2,3},{3,2},{4,5},{5,4},{6,7},{7,6},{8,9},{9,8},{10,11... | collective-permute-start | bytes 1019912 | tf_op jit(solution)/shard_map/ppermute | solution.py:654
  21.6 10.0 %collective-permute-start.1 = (bf16[768,128]{1,0:T(8,128)(2,1)S(1)}, bf16[768,128]{1,0:T(8,128)(2,1)S(1)}, u32[]{:S(2)}, u32[]{:S(2)}) collective-permute-start(bf16[768,128]{1,0:T(8,128)(2,1)S(1)} %cut.1.refs_4_.refs_1_), channel_id=1, source_target_pairs={{0,4},{2,6},{4,0},{6,2},{8,12},{10,14},{12,8},{14,10},{16,20},{18,... | collective-permute-start | bytes 589832 | tf_op jit(solution)/shard_map/ppermute | solution.py:654
  26.3 11.4 %collective-permute-start.8 = (bf16[1536,128]{1,0:T(8,128)(2,1)S(1)}, bf16[1536,128]{1,0:T(8,128)(2,1)S(1)}, u32[]{:S(2)}, u32[]{:S(2)}) collective-permute-start(bf16[1536,128]{1,0:T(8,128)(2,1)S(1)} %after_cut.1), channel_id=1, source_target_pairs={{0,1},{1,0},{2,3},{3,2},{4,5},{5,4},{6,7},{7,6},{8,9},{9,8},{10,11... | collective-permute-start | bytes 1179656 | tf_op jit(solution)/shard_map/ppermute | solution.py:654
  29.3 8.4 %collective-permute-start.5 = (bf16[1328,128]{1,0:T(8,128)(2,1)S(1)}, bf16[1328,128]{1,0:T(8,128)(2,1)S(1)}, u32[]{:S(2)}, u32[]{:S(2)}) collective-permute-start(bf16[1328,128]{1,0:T(8,128)(2,1)S(1)} %collective-permute-done.4.refs_7_.refs_4_), channel_id=1, source_target_pairs={{0,4},{2,6},{4,0},{6,2},{8,12},{10,14},{12,8},{14,10},{16,20},{18,... | collective-permute-start | bytes 1019912 | tf_op jit(solution)/shard_map/ppermute | solution.py:654
  31.6 1.4 collective-permute-start.2
  31.6 1.7 collective-permute-start.3
  37.8 23.5 %collective-permute-start.12 = (bf16[624,768]{1,0:T(8,128)(2,1)S(1)}, bf16[624,768]{1,0:T(8,128)(2,1)S(1)}, u32[]{:S(2)}, u32[]{:S(2)}) collective-permute-start(bf16[624,768]{1,0:T(8,128)(2,1)S(1)} %get-tuple-element.126), channel_id=1, source_target_pairs={{0,1},{1,0},{2,3},{3,2},{4,5},{5,4},{6,7},{7,6},{8,9},{9,8},{10,11... | collective-permute-start | bytes 2875400 | tf_op jit(solution)/shard_map/ppermute | solution.py:654
  39.7 11.0 %collective-permute-start.9 = (bf16[1536,128]{1,0:T(8,128)(2,1)S(1)}, bf16[1536,128]{1,0:T(8,128)(2,1)S(1)}, u32[]{:S(2)}, u32[]{:S(2)}) collective-permute-start(bf16[1536,128]{1,0:T(8,128)(2,1)S(1)} %get-tuple-element.119.refs_11_.refs_8_), channel_id=1, source_target_pairs={{0,4},{2,6},{4,0},{6,2},{8,12},{10,14},{12,8},{14,10},{16,20},{18,... | collective-permute-start | bytes 1179656 | tf_op jit(solution)/shard_map/ppermute | solution.py:654
  40.8 12.6 %collective-permute-start.10 = (bf16[1536,128]{1,0:T(8,128)(2,1)S(1)}, bf16[1536,128]{1,0:T(8,128)(2,1)S(1)}, u32[]{:S(2)}, u32[]{:S(2)}) collective-permute-start(bf16[1536,128]{1,0:T(8,128)(2,1)S(1)} %get-tuple-element.119.refs_11_.refs_8_), channel_id=1, source_target_pairs={{0,2},{2,0},{4,6},{6,4},{8,10},{10,8},{12,14},{14,12},{16,18},{18,... | collective-permute-start | bytes 1179656 | tf_op jit(solution)/shard_map/ppermute | solution.py:654
  50.6 2.7 %collective-permute-start.11 = (bf16[1536,128]{1,0:T(8,128)(2,1)S(1)}, bf16[1536,128]{1,0:T(8,128)(2,1)S(1)}, u32[]{:S(2)}, u32[]{:S(2)}) collective-permute-start(bf16[1536,128]{1,0:T(8,128)(2,1)S(1)} %collective-permute-done.9.refs_12_.refs_9_), channel_id=1, source_target_pairs={{0,2},{2,0},{4,6},{6,4},{8,10},{10,8},{12,14},{14,12},{16,18},{18,... | collective-permute-start | bytes 1179656 | tf_op jit(solution)/shard_map/ppermute | solution.py:654
  50.6 2.2 %collective-permute-start.6 = (bf16[1328,128]{1,0:T(8,128)(2,1)S(1)}, bf16[1328,128]{1,0:T(8,128)(2,1)S(1)}, u32[]{:S(2)}, u32[]{:S(2)}) collective-permute-start(bf16[1328,128]{1,0:T(8,128)(2,1)S(1)} %collective-permute-done.4.refs_7_.refs_4_), channel_id=1, source_target_pairs={{0,2},{2,0},{4,6},{6,4},{8,10},{10,8},{12,14},{14,12},{16,18},{18,... | collective-permute-start | bytes 1019912 | tf_op jit(solution)/shard_map/ppermute | solution.py:654
  51.2 2.2 %collective-permute-start.7 = (bf16[1328,128]{1,0:T(8,128)(2,1)S(1)}, bf16[1328,128]{1,0:T(8,128)(2,1)S(1)}, u32[]{:S(2)}, u32[]{:S(2)}) collective-permute-start(bf16[1328,128]{1,0:T(8,128)(2,1)S(1)} %collective-permute-done.5.refs_3_.refs_8_.refs_5_), channel_id=1, source_target_pairs={{0,2},{2,0},{4,6},{6,4},{8,10},{10,8},{12,14},{14,12},{16,18},{18,... | collective-permute-start | bytes 1019912 | tf_op jit(solution)/shard_map/ppermute | solution.py:654
  67.1 5.0 %collective-permute-start.13 = (bf16[4,1536,128]{2,1,0:T(8,128)(2,1)S(1)}, bf16[4,1536,128]{2,1,0:T(8,128)(2,1)S(1)}, u32[]{:S(2)}, u32[]{:S(2)}) collective-permute-start(bf16[4,1536,128]{2,1,0:T(8,128)(2,1)S(1)} %get-tuple-element.137.refs_9_), channel_id=1, source_target_pairs={{0,2},{2,0},{4,6},{6,4},{8,10},{10,8},{12,14},{14,12},{16,18},{18,... | collective-permute-start | bytes 4718600 | tf_op jit(solution)/shard_map/ppermute | solution.py:654
  75.8 8.0 %collective-permute-start.14 = (bf16[4,1280,128]{2,1,0:T(8,128)(2,1)S(1)}, bf16[4,1280,128]{2,1,0:T(8,128)(2,1)S(1)}, u32[]{:S(2)}, u32[]{:S(2)}) collective-permute-start(bf16[4,1280,128]{2,1,0:T(8,128)(2,1)S(1)} %get-tuple-element.144.refs_4_), channel_id=1, source_target_pairs={{0,2},{2,0},{4,6},{6,4},{8,10},{10,8},{12,14},{14,12},{16,18},{18,... | collective-permute-start | bytes 3932168 | tf_op jit(solution)/shard_map/ppermute | solution.py:654
  76.4 20.8 %collective-permute-start.15 = (bf16[1536,128]{1,0:T(8,128)(2,1)S(1)}, bf16[1536,128]{1,0:T(8,128)(2,1)S(1)}, u32[]{:S(2)}, u32[]{:S(2)}) collective-permute-start(bf16[1536,128]{1,0:T(8,128)(2,1)S(1)} %get-tuple-element.143.refs_4_), channel_id=1, source_target_pairs={{0,4},{2,6},{4,0},{6,2},{8,12},{10,14},{12,8},{14,10},{16,20},{18,... | collective-permute-start | bytes 1179656 | tf_op jit(solution)/shard_map/ppermute | solution.py:654
  76.6 19.7 %collective-permute-start.16 = (bf16[1536,128]{1,0:T(8,128)(2,1)S(1)}, bf16[1536,128]{1,0:T(8,128)(2,1)S(1)}, u32[]{:S(2)}, u32[]{:S(2)}) collective-permute-start(bf16[1536,128]{1,0:T(8,128)(2,1)S(1)} %get-tuple-element.151), channel_id=1, source_target_pairs={{0,1},{1,0},{2,3},{3,2},{4,5},{5,4},{6,7},{7,6},{8,9},{9,8},{10,11... | collective-permute-start | bytes 1179656 | tf_op jit(solution)/shard_map/ppermute | solution.py:654
  78.4 18.9 %collective-permute-start.17 = (bf16[1536,128]{1,0:T(8,128)(2,1)S(1)}, bf16[1536,128]{1,0:T(8,128)(2,1)S(1)}, u32[]{:S(2)}, u32[]{:S(2)}) collective-permute-start(bf16[1536,128]{1,0:T(8,128)(2,1)S(1)} %get-tuple-element.152), channel_id=1, source_target_pairs={{0,5},{1,4},{2,7},{3,6},{4,1},{5,0},{6,3},{7,2},{8,13},{9,12},{10,... | collective-permute-start | bytes 1179656 | tf_op jit(solution)/shard_map/ppermute | solution.py:654
  84.7 28.7 %collective-permute-start.18 = (bf16[2560,128]{1,0:T(8,128)(2,1)S(1)}, bf16[2560,128]{1,0:T(8,128)(2,1)S(1)}, u32[]{:S(2)}, u32[]{:S(2)}) collective-permute-start(bf16[2560,128]{1,0:T(8,128)(2,1)S(1)} %get-tuple-element.147.refs_4_), channel_id=1, source_target_pairs={{0,1},{1,0},{2,3},{3,2},{4,5},{5,4},{6,7},{7,6},{8,9},{9,8},{10,11... | collective-permute-start | bytes 1966088 | tf_op jit(solution)/shard_map/ppermute | solution.py:654
  92.2 9.9 %collective-permute-start.20 = (bf16[4,768,128]{2,1,0:T(8,128)(2,1)S(1)}, bf16[4,768,128]{2,1,0:T(8,128)(2,1)S(1)}, u32[]{:S(2)}, u32[]{:S(2)}) collective-permute-start(bf16[4,768,128]{2,1,0:T(8,128)(2,1)S(1)} %get-tuple-element.154.refs_4_), channel_id=1, source_target_pairs={{0,2},{2,0},{4,6},{6,4},{8,10},{10,8},{12,14},{14,12},{16,18},{18,... | collective-permute-start | bytes 2359304 | tf_op jit(solution)/shard_map/ppermute | solution.py:654
  98.1 6.5 %collective-permute-start.19 = (bf16[768,128]{1,0:T(8,128)(2,1)S(1)}, bf16[768,128]{1,0:T(8,128)(2,1)S(1)}, u32[]{:S(2)}, u32[]{:S(2)}) collective-permute-start(bf16[768,128]{1,0:T(8,128)(2,1)S(1)} %get-tuple-element.158), channel_id=1, source_target_pairs={{0,8},{2,10},{4,12},{6,14},{8,0},{10,2},{12,4},{14,6},{16,24},{18,... | collective-permute-start | bytes 589832 | tf_op jit(solution)/shard_map/ppermute | solution.py:654
  102.9 17.7 %collective-permute-start.22 = (bf16[832,128]{1,0:T(8,128)(2,1)S(1)}, bf16[832,128]{1,0:T(8,128)(2,1)S(1)}, u32[]{:S(2)}, u32[]{:S(2)}) collective-permute-start(bf16[832,128]{1,0:T(8,128)(2,1)S(1)} %get-tuple-element.165.refs_2_), channel_id=1, source_target_pairs={{0,4},{2,6},{4,0},{6,2},{8,12},{10,14},{12,8},{14,10},{16,20},{18,... | collective-permute-start | bytes 638984 | tf_op jit(solution)/shard_map/ppermute | solution.py:654
  105.2 13.0 %collective-permute-start.25 = (bf16[768,128]{1,0:T(8,128)(2,1)S(1)}, bf16[768,128]{1,0:T(8,128)(2,1)S(1)}, u32[]{:S(2)}, u32[]{:S(2)}) collective-permute-start(bf16[768,128]{1,0:T(8,128)(2,1)S(1)} %late_2.1.refs_2_.refs_0_), channel_id=1, source_target_pairs={{0,16},{2,18},{4,20},{6,22},{8,24},{10,26},{12,28},{14,30},{16,0},... | collective-permute-start | bytes 589832 | tf_op jit(solution)/shard_map/ppermute | solution.py:654
  107.9 12.7 %collective-permute-start.23 = (bf16[832,128]{1,0:T(8,128)(2,1)S(1)}, bf16[832,128]{1,0:T(8,128)(2,1)S(1)}, u32[]{:S(2)}, u32[]{:S(2)}) collective-permute-start(bf16[832,128]{1,0:T(8,128)(2,1)S(1)} %get-tuple-element.169), channel_id=1, source_target_pairs={{0,1},{1,0},{2,3},{3,2},{4,5},{5,4},{6,7},{7,6},{8,9},{9,8},{10,11... | collective-permute-start | bytes 638984 | tf_op jit(solution)/shard_map/ppermute | solution.py:654
  109.6 10.9 %collective-permute-start.24 = (bf16[832,128]{1,0:T(8,128)(2,1)S(1)}, bf16[832,128]{1,0:T(8,128)(2,1)S(1)}, u32[]{:S(2)}, u32[]{:S(2)}) collective-permute-start(bf16[832,128]{1,0:T(8,128)(2,1)S(1)} %get-tuple-element.170), channel_id=1, source_target_pairs={{0,5},{1,4},{2,7},{3,6},{4,1},{5,0},{6,3},{7,2},{8,13},{9,12},{10,... | collective-permute-start | bytes 638984 | tf_op jit(solution)/shard_map/ppermute | solution.py:654
  114.1 9.3 %collective-permute-start.21 = (bf16[1280,128]{1,0:T(8,128)(2,1)S(1)}, bf16[1280,128]{1,0:T(8,128)(2,1)S(1)}, u32[]{:S(2)}, u32[]{:S(2)}) collective-permute-start(bf16[1280,128]{1,0:T(8,128)(2,1)S(1)} %get-tuple-element.167.refs_2_), channel_id=1, source_target_pairs={{0,4},{2,6},{4,0},{6,2},{8,12},{10,14},{12,8},{14,10},{16,20},{18,... | collective-permute-start | bytes 983048 | tf_op jit(solution)/shard_map/ppermute | solution.py:654
  118.9 10.1 %collective-permute-start.29 = (bf16[768,128]{1,0:T(8,128)(2,1)S(1)}, bf16[768,128]{1,0:T(8,128)(2,1)S(1)}, u32[]{:S(2)}, u32[]{:S(2)}) collective-permute-start(bf16[768,128]{1,0:T(8,128)(2,1)S(1)} %late_3.1.refs_4_.refs_0_), channel_id=1, source_target_pairs={{0,8},{2,10},{4,12},{6,14},{8,0},{10,2},{12,4},{14,6},{16,24},{18,... | collective-permute-start | bytes 589832 | tf_op jit(solution)/shard_map/ppermute | solution.py:654
  121.2 10.4 %collective-permute-start.28 = (bf16[832,128]{1,0:T(8,128)(2,1)S(1)}, bf16[832,128]{1,0:T(8,128)(2,1)S(1)}, u32[]{:S(2)}, u32[]{:S(2)}) collective-permute-start(bf16[832,128]{1,0:T(8,128)(2,1)S(1)} %early_1.1.refs_2_.refs_0_), channel_id=1, source_target_pairs={{0,8},{2,10},{4,12},{6,14},{8,0},{10,2},{12,4},{14,6},{16,24},{18,... | collective-permute-start | bytes 638984 | tf_op jit(solution)/shard_map/ppermute | solution.py:654
  124.0 17.3 %collective-permute-start.27 = (bf16[640,128]{1,0:T(8,128)(2,1)S(1)}, bf16[640,128]{1,0:T(8,128)(2,1)S(1)}, u32[]{:S(2)}, u32[]{:S(2)}) collective-permute-start(bf16[640,128]{1,0:T(8,128)(2,1)S(1)} %get-tuple-element.175), channel_id=1, source_target_pairs={{0,8},{2,10},{4,12},{6,14},{8,0},{10,2},{12,4},{14,6},{16,24},{18,... | collective-permute-start | bytes 491528 | tf_op jit(solution)/shard_map/ppermute | solution.py:654
  127.2 35.4 %collective-permute-start.26 = (bf16[624,1024]{1,0:T(8,128)(2,1)S(1)}, bf16[624,1024]{1,0:T(8,128)(2,1)S(1)}, u32[]{:S(2)}, u32[]{:S(2)}) collective-permute-start(bf16[624,1024]{1,0:T(8,128)(2,1)S(1)} %get-tuple-element.172.refs_2_), channel_id=1, source_target_pairs={{0,1},{1,0},{2,3},{3,2},{4,5},{5,4},{6,7},{7,6},{8,9},{9,8},{10,11... | collective-permute-start | bytes 3833864 | tf_op jit(solution)/shard_map/ppermute | solution.py:654
  129.6 15.5 %collective-permute-start.33 = (bf16[1536,128]{1,0:T(8,128)(2,1)S(1)}, bf16[1536,128]{1,0:T(8,128)(2,1)S(1)}, u32[]{:S(2)}, u32[]{:S(2)}) collective-permute-start(bf16[1536,128]{1,0:T(8,128)(2,1)S(1)} %late_4.1.refs_2_.refs_0_), channel_id=1, source_target_pairs={{0,2},{2,0},{4,6},{6,4},{8,10},{10,8},{12,14},{14,12},{16,18},{18,... | collective-permute-start | bytes 1179656 | tf_op jit(solution)/shard_map/ppermute | solution.py:654
  129.7 11.6 %collective-permute-start.32 = (bf16[1536,128]{1,0:T(8,128)(2,1)S(1)}, bf16[1536,128]{1,0:T(8,128)(2,1)S(1)}, u32[]{:S(2)}, u32[]{:S(2)}) collective-permute-start(bf16[1536,128]{1,0:T(8,128)(2,1)S(1)} %late_4.1.refs_2_.refs_0_), channel_id=1, source_target_pairs={{0,4},{2,6},{4,0},{6,2},{8,12},{10,14},{12,8},{14,10},{16,20},{18,... | collective-permute-start | bytes 1179656 | tf_op jit(solution)/shard_map/ppermute | solution.py:654
  132.2 15.5 %collective-permute-start.31 = (bf16[832,128]{1,0:T(8,128)(2,1)S(1)}, bf16[832,128]{1,0:T(8,128)(2,1)S(1)}, u32[]{:S(2)}, u32[]{:S(2)}) collective-permute-start(bf16[832,128]{1,0:T(8,128)(2,1)S(1)} %early_2.1.refs_2_.refs_0_), channel_id=1, source_target_pairs={{0,16},{2,18},{4,20},{6,22},{8,24},{10,26},{12,28},{14,30},{16,0},... | collective-permute-start | bytes 638984 | tf_op jit(solution)/shard_map/ppermute | solution.py:654
  141.3 3.8 %collective-permute-start.34 = (bf16[1536,128]{1,0:T(8,128)(2,1)S(1)}, bf16[1536,128]{1,0:T(8,128)(2,1)S(1)}, u32[]{:S(2)}, u32[]{:S(2)}) collective-permute-start(bf16[1536,128]{1,0:T(8,128)(2,1)S(1)} %collective-permute-done.32.refs_1_), channel_id=1, source_target_pairs={{0,2},{2,0},{4,6},{6,4},{8,10},{10,8},{12,14},{14,12},{16,18},{18,... | collective-permute-start | bytes 1179656 | tf_op jit(solution)/shard_map/ppermute | solution.py:654
  141.9 11.5 %collective-permute-start.30 = (bf16[640,128]{1,0:T(8,128)(2,1)S(1)}, bf16[640,128]{1,0:T(8,128)(2,1)S(1)}, u32[]{:S(2)}, u32[]{:S(2)}) collective-permute-start(bf16[640,128]{1,0:T(8,128)(2,1)S(1)} %up_2.1.refs_4_.refs_0_), channel_id=1, source_target_pairs={{0,16},{2,18},{4,20},{6,22},{8,24},{10,26},{12,28},{14,30},{16,0},... | collective-permute-start | bytes 491528 | tf_op jit(solution)/shard_map/ppermute | solution.py:654
  153.9 6.3 %collective-permute-start.35 = (bf16[640,128]{1,0:T(8,128)(2,1)S(1)}, bf16[640,128]{1,0:T(8,128)(2,1)S(1)}, u32[]{:S(2)}, u32[]{:S(2)}) collective-permute-start(bf16[640,128]{1,0:T(8,128)(2,1)S(1)} %up_3.1.refs_0_.refs_2_), channel_id=1, source_target_pairs={{0,8},{2,10},{4,12},{6,14},{8,0},{10,2},{12,4},{14,6},{16,24},{18,... | collective-permute-start | bytes 491528 | tf_op jit(solution)/shard_map/ppermute | solution.py:654
  154.0 17.0 %collective-permute-start.37 = (bf16[832,128]{1,0:T(8,128)(2,1)S(1)}, bf16[832,128]{1,0:T(8,128)(2,1)S(1)}, u32[]{:S(2)}, u32[]{:S(2)}) collective-permute-start(bf16[832,128]{1,0:T(8,128)(2,1)S(1)} %early_3.1.refs_2_.refs_0_), channel_id=1, source_target_pairs={{0,2},{2,0},{4,6},{6,4},{8,10},{10,8},{12,14},{14,12},{16,18},{18,... | collective-permute-start | bytes 638984 | tf_op jit(solution)/shard_map/ppermute | solution.py:654
  154.2 8.2 %collective-permute-start.36 = (bf16[832,128]{1,0:T(8,128)(2,1)S(1)}, bf16[832,128]{1,0:T(8,128)(2,1)S(1)}, u32[]{:S(2)}, u32[]{:S(2)}) collective-permute-start(bf16[832,128]{1,0:T(8,128)(2,1)S(1)} %early_3.1.refs_2_.refs_0_), channel_id=1, source_target_pairs={{0,4},{2,6},{4,0},{6,2},{8,12},{10,14},{12,8},{14,10},{16,20},{18,... | collective-permute-start | bytes 638984 | tf_op jit(solution)/shard_map/ppermute | solution.py:654
  160.8 12.1 %collective-permute-start.40 = (bf16[1280,128]{1,0:T(8,128)(2,1)S(1)}, bf16[1280,128]{1,0:T(8,128)(2,1)S(1)}, u32[]{:S(2)}, u32[]{:S(2)}) collective-permute-start(bf16[1280,128]{1,0:T(8,128)(2,1)S(1)} %up_4.1.refs_6_.refs_0_), channel_id=1, source_target_pairs={{0,2},{2,0},{4,6},{6,4},{8,10},{10,8},{12,14},{14,12},{16,18},{18,... | collective-permute-start | bytes 983048 | tf_op jit(solution)/shard_map/ppermute | solution.py:654
  160.9 10.1 %collective-permute-start.39 = (bf16[1280,128]{1,0:T(8,128)(2,1)S(1)}, bf16[1280,128]{1,0:T(8,128)(2,1)S(1)}, u32[]{:S(2)}, u32[]{:S(2)}) collective-permute-start(bf16[1280,128]{1,0:T(8,128)(2,1)S(1)} %up_4.1.refs_6_.refs_0_), channel_id=1, source_target_pairs={{0,4},{2,6},{4,0},{6,2},{8,12},{10,14},{12,8},{14,10},{16,20},{18,... | collective-permute-start | bytes 983048 | tf_op jit(solution)/shard_map/ppermute | solution.py:654
  162.4 8.6 %collective-permute-start.38 = (bf16[832,128]{1,0:T(8,128)(2,1)S(1)}, bf16[832,128]{1,0:T(8,128)(2,1)S(1)}, u32[]{:S(2)}, u32[]{:S(2)}) collective-permute-start(bf16[832,128]{1,0:T(8,128)(2,1)S(1)} %collective-permute-done.36.refs_1_), channel_id=1, source_target_pairs={{0,2},{2,0},{4,6},{6,4},{8,10},{10,8},{12,14},{14,12},{16,18},{18,... | collective-permute-start | bytes 638984 | tf_op jit(solution)/shard_map/ppermute | solution.py:654
  171.0 1.9 %collective-permute-start.41 = (bf16[1280,128]{1,0:T(8,128)(2,1)S(1)}, bf16[1280,128]{1,0:T(8,128)(2,1)S(1)}, u32[]{:S(2)}, u32[]{:S(2)}) collective-permute-start(bf16[1280,128]{1,0:T(8,128)(2,1)S(1)} %collective-permute-done.39.refs_1_), channel_id=1, source_target_pairs={{0,2},{2,0},{4,6},{6,4},{8,10},{10,8},{12,14},{14,12},{16,18},{18,... | collective-permute-start | bytes 983048 | tf_op jit(solution)/shard_map/ppermute | solution.py:654
where the time goes:
time: 176 us
  Pallas kernels  63.9 us (36%)
  waiting for transfers between devices  59.7 us (34%)
  starting transfers between devices  49.2 us (28%)
    pallas_call x33, Pallas kernels, call(): pl.pallas_call(run, in_specs=[pl.BlockSpec(memory_space=pltpu.SMEM)] + [f...  63.8 us
    ppermute x42, waiting for transfers between devices, swap(): return lax.ppermute(value, axes, [(i, i ^ mask) for i in range(count)])  59.7 us
    ppermute x42, starting transfers between devices, swap(): return lax.ppermute(value, axes, [(i, i ^ mask) for i in range(count)])  49.2 us
  transfers between devices with their start and end apart: 42, of which 17 were waited for; matrix products, arithmetic and copies ran while one was open for 0% of the time, Pallas kernels for 28%

commit v1 on v0

--- a/solution.py
+++ b/solution.py
@@ -319,33 +319,34 @@
         send[h * 2 + j - 2, at, :] = value.astype(BF)
 
 
-def late_grads_kernel(s, prior_in, logit_own, cotangents, act, ending_grad, keep, send, wide):
+def late_grads_kernel(s, act, ending_grad, keep, send):
     half = act.shape[1] // 2
-    logit_other = cotangents.at[:, : logit_own.shape[1]]
-    n = prior_in.shape[1]
     for h in range(2):
-        wide[...] = mm_at(prior_in[...], (logit_own, logit_other)[h][...])
         for j in (2, 3, 0, 1):
-            place = s[1] ^ j
-            store_piece(keep, send, h, j, 0, wide[:, pl.ds(pl.multiple_of(place * 128, 128), 128)])
-            part = act[:, pl.ds(pl.multiple_of(h * half + place * 256, 256), 256)]
+            part = act[:, pl.ds(pl.multiple_of(h * half + (s[1] ^ j) * 256, 256), 256)]
             value = mm_at(part, ending_grad[...])
-            for t in range(n // 128):
-                store_piece(keep, send, h, j, n + t * 256, value[:, t * 128 : t * 128 + 128])
-
-
-def up_grads_kernel(s, second, hidden_grad, mixed, middle_grad, keep, send, turned, wide):
+            for t in range(value.shape[1] // 128):
+                store_piece(keep, send, h, j, t * 256, value[:, t * 128 : t * 128 + 128])
+
+
+def up_grads_kernel(
+    s, second, hidden_grad, mixed, middle_grad, prior_in, logit_own, cotangents, keep, send, turned, wide, tall,
+):
     turned[...] = second[...].T
     half = hidden_grad.shape[1] // 2
     n, m = second.shape[1], mixed.shape[1] // 2
+    logit_other = cotangents.at[:, : logit_own.shape[1]]
     for h in range(2):
         wide[...] = mm_at(mixed[:, h * m : h * m + m], middle_grad[...])
+        tall[...] = mm_at(prior_in[...], (logit_own, logit_other)[h][...])
         for j in (2, 3, 0, 1):
             place = s[1] ^ j
+            at = pl.ds(pl.multiple_of(place * 128, 128), 128)
             value = mm(turned[...], hidden_grad[:, pl.ds(pl.multiple_of(h * half + place * 256, 256), 256)])
             for t in range(2):
                 store_piece(keep, send, h, j, t * n, value[:, t * 128 : t * 128 + 128])
-            store_piece(keep, send, h, j, 2 * n, wide[:, pl.ds(pl.multiple_of(place * 128, 128), 128)])
+            store_piece(keep, send, h, j, 2 * n, wide[:, at])
+            store_piece(keep, send, h, j, 2 * n + m, tall[:, at])
 
 
 def early_grads_kernel(s, first, grad_own, grad_other, keep, send):
@@ -438,24 +439,25 @@
     vec_ref[...] = jnp.concatenate([col_sum(back * unit), col_sum(back)], axis=0)
 
 
-def late_place_kernel(s, mine, near, far, farther, down_ref, prior_ref):
-    n, q = prior_ref.shape[0], down_ref.shape[0] // 4
+def late_place_kernel(s, mine, near, far, farther, down_ref):
+    q = down_ref.shape[0] // 4
     for j, piece in enumerate((mine, near, far, farther)):
-        place = s[1] ^ j
-        rows = pl.ds(pl.multiple_of(place * q, 8), q)
+        rows = pl.ds(pl.multiple_of((s[1] ^ j) * q, 8), q)
         for t in range(down_ref.shape[1] // 128):
-            down_ref[rows, t * 128 : t * 128 + 128] = piece[n + t * q : n + t * q + q, :].astype(F32)
-        prior_ref[:, pl.ds(pl.multiple_of(place * 128, 128), 128)] = piece[:n, :].astype(F32)
-
-
-def up_place_kernel(s, mine, near, far, farther, up_ref, out_ref):
+            down_ref[rows, t * 128 : t * 128 + 128] = piece[t * q : t * q + q, :].astype(F32)
+
+
+def up_place_kernel(s, mine, near, far, farther, up_ref, out_ref, prior_ref, token):
+    token[...] = jnp.zeros_like(token)
     n, m = up_ref.shape[0], out_ref.shape[0]
     for j, piece in enumerate((mine, near, far, farther)):
         place = s[1] ^ j
         for t in range(2):
             columns = pl.ds(pl.multiple_of(place * 256 + t * 128, 128), 128)
             up_ref[:, columns] = piece[t * n : t * n + n, :].astype(F32)
-        out_ref[:, pl.ds(pl.multiple_of(place * 128, 128), 128)] = piece[2 * n : 2 * n + m, :].astype(F32)
+        at = pl.ds(pl.multiple_of(place * 128, 128), 128)
+        out_ref[:, at] = piece[2 * n : 2 * n + m, :].astype(F32)
+        prior_ref[:, at] = piece[2 * n + m :, :].astype(F32)
 
 
 def early_place_kernel(s, mine, near, far, farther, qkv_ref, *vecs):
@@ -540,7 +542,8 @@
 
 def rows_kernel(entries, s, *refs):
     count = len(entries)
-    given, outs, rooms = refs[: 2 * count], refs[2 * count : 3 * count], refs[3 * count :]
+    given, outs, token, rooms = refs[: 2 * count], refs[2 * count : 3 * count], refs[3 * count], refs[3 * count + 1 :]
+    token[...] = jnp.zeros_like(token)
     for i, columns in enumerate(entries):
         own, got, out, room = given[2 * i], given[2 * i + 1], outs[i], rooms[i]
         rows = out.shape[0] // 2
@@ -843,15 +846,6 @@
         name="prior",
         cost=2.5,
     )
-    late_keep, late_send = call(
-        late_grads_kernel,
-        scalars,
-        [prior_in, logit_own, cotangents, act, ending_grad],
-        pieces(width + hidden_width),
-        [pltpu.VMEM((width, n_logits), F32)],
-        name="late_grads",
-        cost=3.5,
-    )
     hidden_grad, grad_middle, middle_grad, vec_two, up_bias_sum = call(
         feed_back_kernel,
         scalars,
@@ -860,19 +854,26 @@
         + [((3, width), F32, True), ((1, 2 * hidden_width), F32, True)],
         name="feed_back",
         cost=6.5,
-        after=(late_send,),
-    )
-    *late_low, late_rest = move.reduce_core_all(scalars, late_keep, late_send, "late_core", after=(hidden_grad,))
+    )
     up_keep, up_send = call(
         up_grads_kernel,
         scalars,
-        [second, hidden_grad, mixed, middle_grad],
-        pieces(width * hidden_width // 512 + half),
-        [pltpu.VMEM((width, total_rows), BF), pltpu.VMEM((half, width), F32)],
+        [second, hidden_grad, mixed, middle_grad, prior_in, logit_own, cotangents],
+        pieces(width * hidden_width // 512 + half + width),
+        [pltpu.VMEM((width, total_rows), BF), pltpu.VMEM((half, width), F32), pltpu.VMEM((width, n_logits), F32)],
         name="up_grads",
-        after=(late_low[0],),
         cost=3.0,
     )
+    late_keep, late_send = call(
+        late_grads_kernel,
+        scalars,
+        [act, ending_grad],
+        pieces(hidden_width),
+        name="late_grads",
+        after=(up_send,),
+        cost=3.5,
+    )
+    *up_low, up_rest = move.reduce_core_all(scalars, up_keep, up_send, "up_core", after=(late_send,))
     def attend_back(half, out, after):
         return call(
             functools.partial(attend_back_kernel, half),
@@ -885,98 +886,100 @@
             cost=4.5,
         )[0]
 
-    grad_own = attend_back(0, out_near, (up_send,))
-    up_low, up_rest = move.reduce_core(scalars, up_keep, up_send, "up_core", (grad_own,))
-    grad_other = attend_back(1, out_other, (up_low,))
+    grad_own = attend_back(0, out_near, (up_low[0],))
+    *late_low, late_rest = move.reduce_core_all(scalars, late_keep, late_send, "late_core", after=(grad_own,))
+    grad_other = attend_back(1, out_other, (late_low[0],))
     keep, send = call(
         early_grads_kernel,
         scalars,
         [first, grad_own, grad_other],
         pieces(768),
         name="early_grads",
-        after=(),
         cost=2.0,
     )
-    late, late_half = move.halves(scalars, [late_rest, *move.sides(late_low)], "late_1", (send,))
     frames_send, frames_grad, vec_one = call(
         frames_back_kernel,
         scalars,
         [grad_own, grad_other, grad_middle, frames_own, frames_other, qkv_other, small, qkv_near],
         near_rows((half, BF), (half, F32)) + [((2, width), F32, True)],
         name="frames_back",
-        after=(late,),
+        after=(send,),
         cost=2.5,
     )
+    up, up_half = move.halves(scalars, [up_rest, *move.sides(up_low)], "up_1", (vec_one,))
     bits = move.bits()
     spare = 64
     vectors = [vec_one, vec_two, vec_three, up_bias_sum, prior_bias_sum]
-    *early_low, early_rest = move.reduce_core_all(scalars, keep, send, "early_core", vectors, spare)
-    late = move.total(scalars, [late, move.along(late_half, bits[0])], "late_2", (early_low[0],))
-    up_low, up_rest = move.reduce_over(scalars, up_low, up_rest, "up_over", (late,))
-    done = up_low
+    *early_low, early_rest = move.reduce_core_all(scalars, keep, send, "early_core", vectors, spare, (up,))
+    done = up = move.total(scalars, [up, move.along(up_half, bits[0])], "up_2", (early_low[0],))
+    done = late, late_half = move.halves(scalars, [late_rest, *move.sides(late_low)], "late_1", (done,))
+    done = late
     for bit in bits[1:]:
-        done = late = move.total(scalars, [late, move.along(late, bit)], "late_3", (done,))
+        done = up = move.total(scalars, [up, move.along(up, bit)], "up_3", (done,))
     done = early = move.total(scalars, [early_rest, *move.sides(early_low)], "early_1", (done,))
-    up, up_half = move.halves(scalars, [up_rest, move.side(up_low)], "up_1", (done,))
+    done = late = move.total(scalars, [late, move.along(late_half, bits[0])], "late_2", (done,))
     back_send, logits_own = call(
         logits_kernel,
         scalars,
         [prior_in, small, prior_near, prior_other, prior_bias_other, block_send, frames_send],
         near_rows((n_logits + 2 * half, BF), (n_logits, F32)),
         name="logits",
-        after=(up,),
+        after=(done,),
         cost=2.0,
     )
-    done = late = move.join(scalars, late, move.along(late, bits[0]), "late_4", (back_send,))
+    done = up = move.join(scalars, up, move.along(up, bits[0]), "up_4", (back_send,))
     for bit in bits[:-1]:
         done = early = move.total(scalars, [early, move.along(early, bit)], "early_2", (done,))
-    done = up = move.total(scalars, [up, move.along(up_half, bits[0])], "up_2", (done,))
-    down_grad, prior_grad = call(
-        late_place_kernel,
-        scalars,
-        list(move.gather(late)),
-        [((hidden_width, width), F32, False), ((width, n_logits), F32, False)],
-        name="late_place",
-        after=(done,),
+    for bit in bits[1:]:
+        done = late = move.total(scalars, [late, move.along(late, bit)], "late_3", (done,))
+    done = early = move.total(scalars, [early, move.along(early, bits[-1])], "early_3", (done,))
+    late = move.join(scalars, late, move.along(late, bits[0]), "late_4", (done,))
+    up_grad, out_grad, prior_grad, up_done = call(
+        up_place_kernel,
+        scalars,
+        list(move.gather(up)),
+        [((width, hidden_width), F32, False), ((half, width), F32, False), ((width, n_logits), F32, False)]
+        + [((8, 128), F32, True)],
+        name="up_place",
+        after=(late,),
         cost=FOLD,
     )
-    early = move.total(scalars, [early, move.along(early, bits[-1])], "early_3", (Far(down_grad),))
-    done = early
-    for bit in bits[1:]:
-        done = up = move.total(scalars, [up, move.along(up, bit)], "up_3", (done,))
-    up = move.join(scalars, up, move.along(up, bits[0]), "up_4", (done,))
     back_got = move.over(back_send)
-    up, early_pieces = move.gather(up), move.gather(early)
-    block_out, logits, grad_frames = call(
+    (early_near,) = gate([move.side(early)], [up_done], "after_up")
+    block_out, logits, grad_frames, rows_done = call(
         functools.partial(
             rows_kernel,
             [slice(n_logits, n_logits + half), slice(0, n_logits), slice(n_logits + half, n_logits + 2 * half)],
         ),
         scalars,
-        [v for own in (block_own, logits_own, frames_grad) for v in (own, back_got)],
-        [((rows, half), BF, False), ((rows, n_logits), F32, False), ((rows, half), F32, False)],
+        [block_own, back_got, logits_own, back_got, frames_grad, back_got],
+        [((rows, half), BF, False), ((rows, n_logits), F32, False), ((rows, half), F32, False)]
+        + [((8, 128), F32, True)],
         [pltpu.VMEM((rows, n), F32) for n in (half, n_logits, half)],
         name="rows_back",
-        after=(up[0],),
+        after=(early_near,),
         cost=FOLD,
     )
+    (late_near,) = gate([move.side(late)], [rows_done], "after_rows")
+    early_pieces = [early, early_near, move.core(early), move.core(early_near)]
+    late_pieces = [late, late_near, move.core(late), move.core(late_near)]
     qkv_grad, *named = call(
         early_place_kernel,
         scalars,
-        list(early_pieces),
+        early_pieces,
         [((3, width, half), F32, False)]
         + [((1, n), F32, False) for n in [width] * 8 + [hidden_width, n_logits]],
         [pltpu.VMEM((spare, 128), F32)],
         name="early_place",
-        after=(Far(block_out),),
+        after=(rows_done,),
         cost=FOLD,
     )
-    up_grad, out_grad = call(
-        up_place_kernel,
-        scalars,
-        list(up),
-        [((width, hidden_width), F32, False), ((half, width), F32, False)],
-        name="up_place",
+    (down_grad,) = call(
+        late_place_kernel,
+        scalars,
+        late_pieces,
+        [((hidden_width, width), F32, False)],
+        name="late_place",
         after=(Far(qkv_grad),),
         cost=FOLD,
     )

time: 176 us -> 168 us (0.955)
  starting transfers between devices: 49.2 us -> 39.1 us
  waiting for transfers between devices: 59.7 us -> 62 us
    ppermute x42 -> x43, starting transfers between devices: 49.2 us -> 39.1 us  [swap(): return lax.ppermute(value, axes, [(i, i ^ mask) for i in range(count)])]
    ppermute x42 -> x43, waiting for transfers between devices: 59.7 us -> 62 us  [swap(): return lax.ppermute(value, axes, [(i, i ^ mask) for i in range(count)])]
    pallas_call x33 -> x32, Pallas kernels: 63.8 us -> 63.5 us  [call(): pl.pallas_call(run, in_specs=[pl.BlockSpec(memory_space=pltpu.SMEM)] + [f...]
  transfers between devices with their start and end apart: 42 -> 43, of which waited for: 17 -> 20; matrix products, arithmetic and copies ran while one was open for 0% -> 0% of each run, Pallas kernels for 28% -> 29%
where the time goes in v1:
time: 168 us
  Pallas kernels  63.6 us (38%)
  waiting for transfers between devices  62 us (37%)
  starting transfers between devices  39.1 us (23%)
    pallas_call x32, Pallas kernels, call(): pl.pallas_call(run, in_specs=[pl.BlockSpec(memory_space=pltpu.SMEM)] + [f...  63.5 us
    ppermute x43, waiting for transfers between devices, swap(): return lax.ppermute(value, axes, [(i, i ^ mask) for i in range(count)])  62 us
    ppermute x43, starting transfers between devices, swap(): return lax.ppermute(value, axes, [(i, i ^ mask) for i in range(count)])  39.1 us
  transfers between devices with their start and end apart: 43, of which 20 were waited for; matrix products, arithmetic and copies ran while one was open for 0% of the time, Pallas kernels for 29%

profile of v1, /device:TPU:0, one launch (start us, length us, event | category | flops | bytes accessed | tf_op | source)
XLA Modules:
  0.0 167.5 jit_solution(11872875548305653856)
XLA Ops:
  0.7 0.8 reshape.99
  1.4 0.6 pad.4.refs_6_
  2.1 2.3 %first_parts.1 = (bf16[2016,128]{1,0:T(8,128)(2,1)S(1)}, bf16[1328,128]{1,0:T(8,128)(2,1)S(1)}, bf16[1536,128]{1,0:T(8,128)(2,1)S(1)}, bf16[624,256]{1,0:T(8,128...) custom-call(s32[3]{0:T(128)S(1)} %pad_add_fusion.s, bf16[1200,256]{1,0:T(8,128)(2,1)} %refs_0_.2, ...), custom_call_target="tpu_custom_call" | custom-call | flops 200000000 | tf_op jit(solution)/shard_map/first_parts/pallas_call | solution.py:633
  4.4 3.0 %collective-permute-start = (bf16[2016,128]{1,0:T(8,128)(2,1)S(1)}, bf16[2016,128]{1,0:T(8,128)(2,1)S(1)}, u32[]{:S(2)}, u32[]{:S(2)}) collective-permute-start(bf16[2016,128]{1,0:T(8,128)(2,1)S(1)} %get-tuple-element.108.refs_7_), channel_id=1, source_target_pairs={{0,1},{1,0},{2,3},{3,2},{4,5},{5,4},{6,7},{7,6},{8,9},{9,8},{10,11... | collective-permute-start | bytes 1548296 | tf_op jit(solution)/shard_map/ppermute | solution.py:657
  7.5 11.7 %collective-permute-done.refs_0_.refs_1_ = bf16[2016,128]{1,0:T(8,128)(2,1)S(1)} collective-permute-done((bf16[2016,128]{1,0:T(8,128)(2,1)S(1)}, bf16[2016,128]{1,0:T(8,128)(2,1)S(1)}, u32[]{:S(2)}, u32[]{:S(2)}) %collective-permute-start) | collective-permute-done | bytes 516128 | tf_op jit(solution)/shard_map/ppermute | solution.py:657
  19.2 1.8 %collective-permute-start.4 = (bf16[1328,128]{1,0:T(8,128)(2,1)S(1)}, bf16[1328,128]{1,0:T(8,128)(2,1)S(1)}, u32[]{:S(2)}, u32[]{:S(2)}) collective-permute-start(bf16[1328,128]{1,0:T(8,128)(2,1)S(1)} %after_first.1.refs_2_), channel_id=1, source_target_pairs={{0,1},{1,0},{2,3},{3,2},{4,5},{5,4},{6,7},{7,6},{8,9},{9,8},{10,11... | collective-permute-start | bytes 1019912 | tf_op jit(solution)/shard_map/ppermute | solution.py:657
  21.6 1.6 collective-permute-start.1
  23.1 3.1 %cotangents.1 = (bf16[624,768]{1,0:T(8,128)(2,1)S(1)}, bf16[624,512]{1,0:T(8,128)(2,1)S(1)}, bf16[624,256]{1,0:T(8,128)(2,1)S(1)}, bf16[3,512,256]{2,1,0:T(8,128...) custom-call(s32[3]{0:T(128)S(1)} %pad_add_fusion.s, ...), custom_call_target="tpu_custom_call" | custom-call | flops 230000000 | tf_op jit(solution)/shard_map/cotangents/pallas_call | solution.py:633
  26.9 2.4 %collective-permute-done.4.refs_7_.refs_4_ = bf16[1328,128]{1,0:T(8,128)(2,1)S(1)} collective-permute-done((bf16[1328,128]{1,0:T(8,128)(2,1)S(1)}, bf16[1328,128]{1,0:T(8,128)(2,1)S(1)}, u32[]{:S(2)}, u32[]{:S(2)}) %collective-permute-start.4) | collective-permute-done | bytes 340000 | tf_op jit(solution)/shard_map/ppermute | solution.py:657
  29.3 2.3 %collective-permute-start.5 = (bf16[1328,128]{1,0:T(8,128)(2,1)S(1)}, bf16[1328,128]{1,0:T(8,128)(2,1)S(1)}, u32[]{:S(2)}, u32[]{:S(2)}) collective-permute-start(bf16[1328,128]{1,0:T(8,128)(2,1)S(1)} %collective-permute-done.4.refs_7_.refs_4_), channel_id=1, source_target_pairs={{0,4},{2,6},{4,0},{6,2},{8,12},{10,14},{12,8},{14,10},{16,20},{18,... | collective-permute-start | bytes 1019912 | tf_op jit(solution)/shard_map/ppermute | solution.py:657
  32.1 0.9 collective-permute-done.2.refs_6_
  33.3 4.3 %attend.1 = (bf16[624,512]{1,0:T(8,128)(2,1)S(1)}, bf16[624,1536]{1,0:T(8,128)(2,1)S(1)}, bf16[624,512]{1,0:T(8,128)(2,1)S(1)}, bf16[3,512,256]{2,1,0:T(8,128)(2,1)S(1)}, bf16[624,256]{1,0:T(8,128)(2,1)S(1)}) custom-call(s32[3]{0:T(128)S(1)} %pad_add_fusion.s, bf16[624,256]{1,0:T(8,128)(2,1)S(1)} %get-tuple-element.107.refs_0_.refs_3_, ...), custom_call_target="tpu_custom_call" | custom-call | flops 550000000 | tf_op jit(solution)/shard_map/attend/pallas_call | solution.py:633
  37.8 1.9 %collective-permute-start.12 = (bf16[624,768]{1,0:T(8,128)(2,1)S(1)}, bf16[624,768]{1,0:T(8,128)(2,1)S(1)}, u32[]{:S(2)}, u32[]{:S(2)}) collective-permute-start(bf16[624,768]{1,0:T(8,128)(2,1)S(1)} %get-tuple-element.127), channel_id=1, source_target_pairs={{0,1},{1,0},{2,3},{3,2},{4,5},{5,4},{6,7},{7,6},{8,9},{9,8},{10,11... | collective-permute-start | bytes 2875400 | tf_op jit(solution)/shard_map/ppermute | solution.py:657
  39.7 1.1 collective-permute-start.9
  40.8 9.9 %collective-permute-done.9.refs_12_.refs_9_ = bf16[1536,128]{1,0:T(8,128)(2,1)S(1)} collective-permute-done((bf16[1536,128]{1,0:T(8,128)(2,1)S(1)}, bf16[1536,128]{1,0:T(8,128)(2,1)S(1)}, u32[]{:S(2)}, u32[]{:S(2)}) %collective-permute-start.9) | collective-permute-done | bytes 393248 | tf_op jit(solution)/shard_map/ppermute | solution.py:657
  51.1 1.7 %collective-permute-done.6.refs_9_.refs_6_ = bf16[1328,128]{1,0:T(8,128)(2,1)S(1)} collective-permute-done((bf16[1328,128]{1,0:T(8,128)(2,1)S(1)}, bf16[1328,128]{1,0:T(8,128)(2,1)S(1)}, u32[]{:S(2)}, u32[]{:S(2)}) %collective-permute-start.6) | collective-permute-done | bytes 340000 | tf_op jit(solution)/shard_map/ppermute | solution.py:657
  53.3 6.9 %feed.1 = (bf16[624,256]{1,0:T(8,128)(2,1)S(1)}, bf16[624,256]{1,0:T(8,128)(2,1)S(1)}, f32[624,512]{1,0:T(8,128)S(1)}, bf16[624,512]{1,0:T(8,128)(2,1)S(1)}, bf1...) custom-call(s32[3]{0:T(128)S(1)} %pad_add_fusion.s, ...), custom_call_target="tpu_custom_call" | custom-call | flops 720000000 | tf_op jit(solution)/shard_map/feed/pallas_call | solution.py:633
  60.2 1.1 collective-permute-done.12.refs_12_.refs_6_
  61.3 2.3 %prior.1 = (f32[624,512]{1,0:T(8,128)S(1)}, bf16[624,512]{1,0:T(8,128)(2,1)S(1)}, f32[3,512]{1,0:T(4,128)S(1)}, f32[1,1024]{1,0:T(1,128)S(1)}, bf16[512,512]{1,0:T(8,128)(2,1)S(1)}, /*index=5*/f32[1,512]{1,0:T(1,128)S(1)}) custom-call(s32[3]{0:T(128)S(1)} %pad_add_fusion.s, f32[624,512]{1,0:T(8,128)S(1)} %get-tuple-element.124.refs_0_, ...), custom_call_target="tpu_custom_call" | custom-call | flops 250000000 | tf_op jit(solution)/shard_map/prior/pallas_call | solution.py:633
  63.6 4.9 %feed_back.1 = (bf16[624,2048]{1,0:T(8,128)(2,1)S(1)}, f32[624,512]{1,0:T(8,128)S(1)}, bf16[624,512]{1,0:T(8,128)(2,1)S(1)}, f32[3,512]{1,0:T(4,128)S(1)}, f32[1,2048]{1,0:T(1,128)S(1)}) custom-call(s32[3]{0:T(128)S(1)} %pad_add_fusion.s, bf16[624,512]{1,0:T(8,128)(2,1)S(1)} %get-tuple-element.131.refs_0_.refs_1_, ...), custom_call_target="tpu_custom_call" | custom-call | flops 650000000 | tf_op jit(solution)/shard_map/feed_back/pallas_call | solution.py:633
  68.5 3.9 %up_grads.1 = (f32[4,1792,128]{2,1,0:T(8,128)S(1)}, bf16[4,1792,128]{2,1,0:T(8,128)(2,1)S(1)}) custom-call(s32[3]{0:T(128)S(1)} %pad_add_fusion.s, bf16[624,512]{1,0:T(8,128)(2,1)S(1)} %get-tuple-element.139.refs_0_, bf16[624,2048]{1,0:T(8,128)(2,1)S(1)} %get-tuple-element.140.refs_1_, bf16[624,512]{1,0:T(8,128)(2,1)S(1)} %get-tuple-element.113.refs_2_, ...), custom_call_target="tpu_custom_call" | custom-call | flops 300000000 | tf_op jit(solution)/shard_map/up_grads/pallas_call | solution.py:633
  72.6 2.4 %late_grads.1 = (f32[4,1024,128]{2,1,0:T(8,128)S(1)}, bf16[4,1024,128]{2,1,0:T(8,128)(2,1)S(1)}) custom-call(s32[3]{0:T(128)S(1)} %pad_add_fusion.s, bf16[624,2048]{1,0:T(8,128)(2,1)S(1)} %get-tuple-element.143.refs_0_, bf16[624,512]{1,0:T(8,128)(2,1)S(1)} %get-tuple-element.131.refs_0_.refs_1_, bf16[4,1792,128]{2,1,0:T(8,128)(2,1)S(1)} %get-tuple-element.142.refs_2_), custom_call_target="tpu_custom_call" | custom-call | flops 350000000 | tf_op jit(solution)/shard_map/late_grads/pallas_call | solution.py:633
  75.5 0.8 collective-permute-done.13.refs_1_
  76.3 0.9 up_core.1
  77.3 1.8 %collective-permute-start.19 = (bf16[1792,128]{1,0:T(8,128)(2,1)S(1)}, bf16[1792,128]{1,0:T(8,128)(2,1)S(1)}, u32[]{:S(2)}, u32[]{:S(2)}) collective-permute-start(bf16[1792,128]{1,0:T(8,128)(2,1)S(1)} %get-tuple-element.158), channel_id=1, source_target_pairs={{0,1},{1,0},{2,3},{3,2},{4,5},{5,4},{6,7},{7,6},{8,9},{9,8},{10,11... | collective-permute-start | bytes 1376264 | tf_op jit(solution)/shard_map/ppermute | solution.py:657
  79.1 1.7 %collective-permute-start.18 = (bf16[1792,128]{1,0:T(8,128)(2,1)S(1)}, bf16[1792,128]{1,0:T(8,128)(2,1)S(1)}, u32[]{:S(2)}, u32[]{:S(2)}) collective-permute-start(bf16[1792,128]{1,0:T(8,128)(2,1)S(1)} %get-tuple-element.145.refs_4_), channel_id=1, source_target_pairs={{0,4},{2,6},{4,0},{6,2},{8,12},{10,14},{12,8},{14,10},{16,20},{18,... | collective-permute-start | bytes 1376264 | tf_op jit(solution)/shard_map/ppermute | solution.py:657
  80.8 4.0 %attend_back_0.1.refs_2_.refs_1_.refs_0_ = bf16[624,768]{1,0:T(8,128)(2,1)S(1)} custom-call(s32[3]{0:T(128)S(1)} %pad_add_fusion.s, bf16[624,512]{1,0:T(8,128)(2,1)S(1)} %get-tuple-element.137.refs_3_.refs_0_, bf16[624,1536]{1,0:T(8,128)(2,1)S(1)} %get-tuple-element.138.refs_1_, bf16[256,512]{1,0:T(8,128)(2,1)S(1)} %get-tuple-element.114.refs_4_.refs_2_, ...), custom_call_target="tpu_custom_call" | custom-call | flops 450000000 | tf_op jit(solution)/shard_map/attend_back_0/pallas_call | solution.py:633
  84.8 0.8 late_core.1
  85.9 3.7 %attend_back_1.1.refs_2_.refs_1_ = bf16[624,768]{1,0:T(8,128)(2,1)S(1)} custom-call(s32[3]{0:T(128)S(1)} %pad_add_fusion.s, bf16[624,512]{1,0:T(8,128)(2,1)S(1)} %get-tuple-element.137.refs_3_.refs_0_, bf16[624,1536]{1,0:T(8,128)(2,1)S(1)} %get-tuple-element.138.refs_1_, bf16[256,512]{1,0:T(8,128)(2,1)S(1)} %get-tuple-element.146.refs_2_, ...), custom_call_target="tpu_custom_call" | custom-call | flops 450000000 | tf_op jit(solution)/shard_map/attend_back_1/pallas_call | solution.py:633
  89.6 2.0 %early_grads.1 = (f32[4,768,128]{2,1,0:T(8,128)S(1)}, bf16[4,768,128]{2,1,0:T(8,128)(2,1)S(1)}) custom-call(s32[3]{0:T(128)S(1)} %pad_add_fusion.s, bf16[624,512]{1,0:T(8,128)(2,1)S(1)} %get-tuple-element.151.refs_0_, bf16[624,768]{1,0:T(8,128)(2,1)S(1)} %attend_back_0.1.refs_2_.refs_1_.refs_0_, bf16[624,768]{1,0:T(8,128)(2,1)S(1)} %attend_back_1.1.refs_2_.refs_1_), custom_call_target="tpu_custom_call" | custom-call | flops 200000000 | tf_op jit(solution)/shard_map/early_grads/pallas_call | solution.py:633
  91.7 2.3 %frames_back.1 = (bf16[624,256]{1,0:T(8,128)(2,1)S(1)}, f32[624,256]{1,0:T(8,128)S(1)}, f32[2,512]{1,0:T(2,128)S(1)}) custom-call(s32[3]{0:T(128)S(1)} %pad_add_fusion.s, bf16[624,768]{1,0:T(8,128)(2,1)S(1)} %attend_back_0.1.refs_2_.refs_1_.refs_0_, bf16[624,768]{1,0:T(8,128)(2,1)S(1)} %attend_back_1.1.refs_2_.refs_1_, ...), custom_call_target="tpu_custom_call" | custom-call | flops 250000000 | tf_op jit(solution)/shard_map/frames_back/pallas_call | solution.py:633
  94.1 5.6 %collective-permute-done.19.refs_2_ = bf16[1792,128]{1,0:T(8,128)(2,1)S(1)} collective-permute-done((bf16[1792,128]{1,0:T(8,128)(2,1)S(1)}, bf16[1792,128]{1,0:T(8,128)(2,1)S(1)}, u32[]{:S(2)}, u32[]{:S(2)}) %collective-permute-start.19) | collective-permute-done | bytes 458784 | tf_op jit(solution)/shard_map/ppermute | solution.py:657
  99.7 1.7 %collective-permute-start.16 = (bf16[1024,128]{1,0:T(8,128)(2,1)S(1)}, bf16[1024,128]{1,0:T(8,128)(2,1)S(1)}, u32[]{:S(2)}, u32[]{:S(2)}) collective-permute-start(bf16[1024,128]{1,0:T(8,128)(2,1)S(1)} %get-tuple-element.155), channel_id=1, source_target_pairs={{0,1},{1,0},{2,3},{3,2},{4,5},{5,4},{6,7},{7,6},{8,9},{9,8},{10,11... | collective-permute-start | bytes 786440 | tf_op jit(solution)/shard_map/ppermute | solution.py:657
  102.0 0.9 up_1.1
  102.9 1.6 collective-permute-start.21
  104.6 0.8 early_core.1
  105.4 1.3 collective-permute-start.24
  106.7 2.4 %collective-permute-done.21.refs_1_ = bf16[896,128]{1,0:T(8,128)(2,1)S(1)} collective-permute-done((bf16[896,128]{1,0:T(8,128)(2,1)S(1)}, bf16[896,128]{1,0:T(8,128)(2,1)S(1)}, u32[]{:S(2)}, u32[]{:S(2)}) %collective-permute-start.21) | collective-permute-done | bytes 229408 | tf_op jit(solution)/shard_map/ppermute | solution.py:657
  109.0 0.6 up_2.1.refs_4_.refs_0_
  109.6 2.7 %collective-permute-start.27 = (bf16[896,128]{1,0:T(8,128)(2,1)S(1)}, bf16[896,128]{1,0:T(8,128)(2,1)S(1)}, u32[]{:S(2)}, u32[]{:S(2)}) collective-permute-start(bf16[896,128]{1,0:T(8,128)(2,1)S(1)} %up_2.1.refs_4_.refs_0_), channel_id=1, source_target_pairs={{0,16},{2,18},{4,20},{6,22},{8,24},{10,26},{12,28},{14,30},{16,0},... | collective-permute-start | bytes 688136 | tf_op jit(solution)/shard_map/ppermute | solution.py:657
  112.3 2.1 %collective-permute-done.17.refs_3_ = bf16[1024,128]{1,0:T(8,128)(2,1)S(1)} collective-permute-done((bf16[1024,128]{1,0:T(8,128)(2,1)S(1)}, bf16[1024,128]{1,0:T(8,128)(2,1)S(1)}, u32[]{:S(2)}, u32[]{:S(2)}) %collective-permute-start.17) | collective-permute-done | bytes 262176 | tf_op jit(solution)/shard_map/ppermute | solution.py:657
  114.4 0.8 late_1.1
  115.2 1.6 collective-permute-start.23
  117.2 1.4 collective-permute-start.26
  118.6 2.2 %collective-permute-done.27.refs_1_ = bf16[896,128]{1,0:T(8,128)(2,1)S(1)} collective-permute-done((bf16[896,128]{1,0:T(8,128)(2,1)S(1)}, bf16[896,128]{1,0:T(8,128)(2,1)S(1)}, u32[]{:S(2)}, u32[]{:S(2)}) %collective-permute-start.27) | collective-permute-done | bytes 229408 | tf_op jit(solution)/shard_map/ppermute | solution.py:657
  120.8 0.6 up_3.1.refs_4_.refs_0_
  121.4 0.7 collective-permute-start.30
  122.1 4.2 %collective-permute-done.25.refs_2_ = bf16[832,128]{1,0:T(8,128)(2,1)S(1)} collective-permute-done((bf16[832,128]{1,0:T(8,128)(2,1)S(1)}, bf16[832,128]{1,0:T(8,128)(2,1)S(1)}, u32[]{:S(2)}, u32[]{:S(2)}) %collective-permute-start.25) | collective-permute-done | bytes 213024 | tf_op jit(solution)/shard_map/ppermute | solution.py:657
  126.3 0.6 early_1.1.refs_2_.refs_0_
  128.0 2.6 %collective-permute-start.32 = (bf16[512,128]{1,0:T(8,128)(2,1)S(1)}, bf16[512,128]{1,0:T(8,128)(2,1)S(1)}, u32[]{:S(2)}, u32[]{:S(2)}) collective-permute-start(bf16[512,128]{1,0:T(8,128)(2,1)S(1)} %late_2.1.refs_7_.refs_0_), channel_id=1, source_target_pairs={{0,16},{2,18},{4,20},{6,22},{8,24},{10,26},{12,28},{14,30},{16,0},... | collective-permute-start | bytes 393224 | tf_op jit(solution)/shard_map/ppermute | solution.py:657
  130.7 1.4 logits.1
  133.3 0.7 collective-permute-start.34
  134.0 1.7 %collective-permute-done.29.refs_1_ = bf16[832,128]{1,0:T(8,128)(2,1)S(1)} collective-permute-done((bf16[832,128]{1,0:T(8,128)(2,1)S(1)}, bf16[832,128]{1,0:T(8,128)(2,1)S(1)}, u32[]{:S(2)}, u32[]{:S(2)}) %collective-permute-start.29) | collective-permute-done | bytes 213024 | tf_op jit(solution)/shard_map/ppermute | solution.py:657
  136.4 1.2 collective-permute-start.31
  138.2 1.3 collective-permute-start.37
  139.5 8.0 %collective-permute-done.31.refs_1_ = bf16[832,128]{1,0:T(8,128)(2,1)S(1)} collective-permute-done((bf16[832,128]{1,0:T(8,128)(2,1)S(1)}, bf16[832,128]{1,0:T(8,128)(2,1)S(1)}, u32[]{:S(2)}, u32[]{:S(2)}) %collective-permute-start.31) | collective-permute-done | bytes 213024 | tf_op jit(solution)/shard_map/ppermute | solution.py:657
  148.2 1.6 collective-permute-start.33
  151.0 0.7 collective-permute-done.36.refs_3_
  152.1 2.8 %up_place.1 = (f32[512,1024]{1,0:T(8,128)}, f32[256,512]{1,0:T(8,128)}, f32[512,512]{1,0:T(8,128)}, f32[8,128]{1,0:T(8,128)S(1)}) custom-call(s32[3]{0:T(128)S(1)} %pad_add_fusion.s, bf16[1792,128]{1,0:T(8,128)(2,1)S(1)} %up_4.1.refs_2_.refs_0_, bf16[1792,128]{1,0:T(8,128)(2,1)S(1)} %collective-permute-done.34.refs_1_, ...), custom_call_target="tpu_custom_call" | custom-call | flops 10000000000 | tf_op jit(solution)/shard_map/up_place/pallas_call | solution.py:633
  154.9 1.4 collective-permute-done.33.refs_0_
  156.4 3.8 %collective-permute-done.28.refs_1_.refs_3_.refs_5_ = bf16[624,1024]{1,0:T(8,128)(2,1)S(1)} collective-permute-done((bf16[624,1024]{1,0:T(8,128)(2,1)S(1)}, bf16[624,1024]{1,0:T(8,128)(2,1)S(1)}, u32[]{:S(2)}, u32[]{:S(2)}) %collective-permute-start.28) | collective-permute-done | bytes 1277984 | tf_op jit(solution)/shard_map/ppermute | solution.py:657
  160.3 2.9 %rows_back.1 = (bf16[1200,256]{1,0:T(8,128)(2,1)}, f32[1200,512]{1,0:T(8,128)}, f32[1200,256]{1,0:T(8,128)}, f32[8,128]{1,0:T(8,128)S(1)}) custom-call(s32[3]{0:T(128)S(1)} %pad_add_fusion.s, bf16[624,256]{1,0:T(8,128)(2,1)S(1)} %get-tuple-element.121.refs_0_, bf16[624,1024]{1,0:T(8,128)(2,1)S(1)} %collective-permute-done.28.refs_1_.refs_3_.refs_5_, ...), custom_call_target="tpu_custom_call" | custom-call | flops 10000000000 | tf_op jit(solution)/shard_map/rows_back/pallas_call | solution.py:633
  163.3 1.9 %early_place.1 = (f32[3,512,256]{2,1,0:T(8,128)}, f32[1,512]{1,0:T(1,128)}, f32[1,512]{1,0:T(1,128)}, f32[1,512]{1,0:T(1,128)}, f32[1,512]{1,0:T(1,128)}, /*inde...) custom-call(s32[3]{0:T(128)S(1)} %pad_add_fusion.s, ...), custom_call_target="tpu_custom_call" | custom-call | flops 10000000000 | tf_op jit(solution)/shard_map/early_place/pallas_call | solution.py:633
  165.2 2.1 %late_place.1 = f32[1024,512]{1,0:T(8,128)} custom-call(s32[3]{0:T(128)S(1)} %pad_add_fusion.s, bf16[1024,128]{1,0:T(8,128)(2,1)S(1)} %late_4.1.refs_4_.refs_0_, bf16[1024,128]{1,0:T(8,128)(2,1)S(1)} %after_rows.1.refs_1_, bf16[1024,128]{1,0:T(8,128)(2,1)S(1)} %collective-permute-done.41.refs_2_, bf16[1024,128]{1,0:T(8,128)(2,1)S(1)} %collective-permute-done.42.refs_3_, ...), custom_call_target="tpu_custom_call" | custom-call | flops 10000000000 | tf_op jit(solution)/shard_map/late_place/pallas_call | solution.py:633
  (62 shorter events, 11.1 us)
Async XLA Ops:
  4.4 14.7 %collective-permute-start = (bf16[2016,128]{1,0:T(8,128)(2,1)S(1)}, bf16[2016,128]{1,0:T(8,128)(2,1)S(1)}, u32[]{:S(2)}, u32[]{:S(2)}) collective-permute-start(bf16[2016,128]{1,0:T(8,128)(2,1)S(1)} %get-tuple-element.108.refs_7_), channel_id=1, source_target_pairs={{0,1},{1,0},{2,3},{3,2},{4,5},{5,4},{6,7},{7,6},{8,9},{9,8},{10,11... | collective-permute-start | bytes 1548296 | tf_op jit(solution)/shard_map/ppermute | solution.py:657
  19.2 10.1 %collective-permute-start.4 = (bf16[1328,128]{1,0:T(8,128)(2,1)S(1)}, bf16[1328,128]{1,0:T(8,128)(2,1)S(1)}, u32[]{:S(2)}, u32[]{:S(2)}) collective-permute-start(bf16[1328,128]{1,0:T(8,128)(2,1)S(1)} %after_first.1.refs_2_), channel_id=1, source_target_pairs={{0,1},{1,0},{2,3},{3,2},{4,5},{5,4},{6,7},{7,6},{8,9},{9,8},{10,11... | collective-permute-start | bytes 1019912 | tf_op jit(solution)/shard_map/ppermute | solution.py:657
  21.6 10.0 %collective-permute-start.1 = (bf16[768,128]{1,0:T(8,128)(2,1)S(1)}, bf16[768,128]{1,0:T(8,128)(2,1)S(1)}, u32[]{:S(2)}, u32[]{:S(2)}) collective-permute-start(bf16[768,128]{1,0:T(8,128)(2,1)S(1)} %cut.1.refs_4_.refs_1_), channel_id=1, source_target_pairs={{0,4},{2,6},{4,0},{6,2},{8,12},{10,14},{12,8},{14,10},{16,20},{18,... | collective-permute-start | bytes 589832 | tf_op jit(solution)/shard_map/ppermute | solution.py:657
  26.3 11.4 %collective-permute-start.8 = (bf16[1536,128]{1,0:T(8,128)(2,1)S(1)}, bf16[1536,128]{1,0:T(8,128)(2,1)S(1)}, u32[]{:S(2)}, u32[]{:S(2)}) collective-permute-start(bf16[1536,128]{1,0:T(8,128)(2,1)S(1)} %after_cut.1), channel_id=1, source_target_pairs={{0,1},{1,0},{2,3},{3,2},{4,5},{5,4},{6,7},{7,6},{8,9},{9,8},{10,11... | collective-permute-start | bytes 1179656 | tf_op jit(solution)/shard_map/ppermute | solution.py:657
  29.3 8.4 %collective-permute-start.5 = (bf16[1328,128]{1,0:T(8,128)(2,1)S(1)}, bf16[1328,128]{1,0:T(8,128)(2,1)S(1)}, u32[]{:S(2)}, u32[]{:S(2)}) collective-permute-start(bf16[1328,128]{1,0:T(8,128)(2,1)S(1)} %collective-permute-done.4.refs_7_.refs_4_), channel_id=1, source_target_pairs={{0,4},{2,6},{4,0},{6,2},{8,12},{10,14},{12,8},{14,10},{16,20},{18,... | collective-permute-start | bytes 1019912 | tf_op jit(solution)/shard_map/ppermute | solution.py:657
  31.6 1.4 collective-permute-start.2
  31.6 1.7 %collective-permute-start.3 = (bf16[768,128]{1,0:T(8,128)(2,1)S(1)}, bf16[768,128]{1,0:T(8,128)(2,1)S(1)}, u32[]{:S(2)}, u32[]{:S(2)}) collective-permute-start(bf16[768,128]{1,0:T(8,128)(2,1)S(1)} %collective-permute-done.1.refs_5_), channel_id=1, source_target_pairs={{0,2},{2,0},{4,6},{6,4},{8,10},{10,8},{12,14},{14,12},{16,18},{18,... | collective-permute-start | bytes 589832 | tf_op jit(solution)/shard_map/ppermute | solution.py:657
  37.8 23.5 %collective-permute-start.12 = (bf16[624,768]{1,0:T(8,128)(2,1)S(1)}, bf16[624,768]{1,0:T(8,128)(2,1)S(1)}, u32[]{:S(2)}, u32[]{:S(2)}) collective-permute-start(bf16[624,768]{1,0:T(8,128)(2,1)S(1)} %get-tuple-element.127), channel_id=1, source_target_pairs={{0,1},{1,0},{2,3},{3,2},{4,5},{5,4},{6,7},{7,6},{8,9},{9,8},{10,11... | collective-permute-start | bytes 2875400 | tf_op jit(solution)/shard_map/ppermute | solution.py:657
  39.7 11.0 %collective-permute-start.9 = (bf16[1536,128]{1,0:T(8,128)(2,1)S(1)}, bf16[1536,128]{1,0:T(8,128)(2,1)S(1)}, u32[]{:S(2)}, u32[]{:S(2)}) collective-permute-start(bf16[1536,128]{1,0:T(8,128)(2,1)S(1)} %get-tuple-element.120.refs_11_.refs_8_), channel_id=1, source_target_pairs={{0,4},{2,6},{4,0},{6,2},{8,12},{10,14},{12,8},{14,10},{16,20},{18,... | collective-permute-start | bytes 1179656 | tf_op jit(solution)/shard_map/ppermute | solution.py:657
  40.8 12.6 %collective-permute-start.10 = (bf16[1536,128]{1,0:T(8,128)(2,1)S(1)}, bf16[1536,128]{1,0:T(8,128)(2,1)S(1)}, u32[]{:S(2)}, u32[]{:S(2)}) collective-permute-start(bf16[1536,128]{1,0:T(8,128)(2,1)S(1)} %get-tuple-element.120.refs_11_.refs_8_), channel_id=1, source_target_pairs={{0,2},{2,0},{4,6},{6,4},{8,10},{10,8},{12,14},{14,12},{16,18},{18,... | collective-permute-start | bytes 1179656 | tf_op jit(solution)/shard_map/ppermute | solution.py:657
  50.6 2.7 %collective-permute-start.11 = (bf16[1536,128]{1,0:T(8,128)(2,1)S(1)}, bf16[1536,128]{1,0:T(8,128)(2,1)S(1)}, u32[]{:S(2)}, u32[]{:S(2)}) collective-permute-start(bf16[1536,128]{1,0:T(8,128)(2,1)S(1)} %collective-permute-done.9.refs_12_.refs_9_), channel_id=1, source_target_pairs={{0,2},{2,0},{4,6},{6,4},{8,10},{10,8},{12,14},{14,12},{16,18},{18,... | collective-permute-start | bytes 1179656 | tf_op jit(solution)/shard_map/ppermute | solution.py:657
  50.6 2.2 %collective-permute-start.6 = (bf16[1328,128]{1,0:T(8,128)(2,1)S(1)}, bf16[1328,128]{1,0:T(8,128)(2,1)S(1)}, u32[]{:S(2)}, u32[]{:S(2)}) collective-permute-start(bf16[1328,128]{1,0:T(8,128)(2,1)S(1)} %collective-permute-done.4.refs_7_.refs_4_), channel_id=1, source_target_pairs={{0,2},{2,0},{4,6},{6,4},{8,10},{10,8},{12,14},{14,12},{16,18},{18,... | collective-permute-start | bytes 1019912 | tf_op jit(solution)/shard_map/ppermute | solution.py:657
  51.1 2.2 %collective-permute-start.7 = (bf16[1328,128]{1,0:T(8,128)(2,1)S(1)}, bf16[1328,128]{1,0:T(8,128)(2,1)S(1)}, u32[]{:S(2)}, u32[]{:S(2)}) collective-permute-start(bf16[1328,128]{1,0:T(8,128)(2,1)S(1)} %collective-permute-done.5.refs_3_.refs_8_.refs_5_), channel_id=1, source_target_pairs={{0,2},{2,0},{4,6},{6,4},{8,10},{10,8},{12,14},{14,12},{16,18},{18,... | collective-permute-start | bytes 1019912 | tf_op jit(solution)/shard_map/ppermute | solution.py:657
  72.5 3.9 %collective-permute-start.13 = (bf16[4,1792,128]{2,1,0:T(8,128)(2,1)S(1)}, bf16[4,1792,128]{2,1,0:T(8,128)(2,1)S(1)}, u32[]{:S(2)}, u32[]{:S(2)}) collective-permute-start(bf16[4,1792,128]{2,1,0:T(8,128)(2,1)S(1)} %get-tuple-element.142.refs_2_), channel_id=1, source_target_pairs={{0,2},{2,0},{4,6},{6,4},{8,10},{10,8},{12,14},{14,12},{16,18},{18,... | collective-permute-start | bytes 5505032 | tf_op jit(solution)/shard_map/ppermute | solution.py:657
  75.0 9.8 %collective-permute-start.14 = (bf16[4,1024,128]{2,1,0:T(8,128)(2,1)S(1)}, bf16[4,1024,128]{2,1,0:T(8,128)(2,1)S(1)}, u32[]{:S(2)}, u32[]{:S(2)}) collective-permute-start(bf16[4,1024,128]{2,1,0:T(8,128)(2,1)S(1)} %get-tuple-element.144.refs_2_), channel_id=1, source_target_pairs={{0,2},{2,0},{4,6},{6,4},{8,10},{10,8},{12,14},{14,12},{16,18},{18,... | collective-permute-start | bytes 3145736 | tf_op jit(solution)/shard_map/ppermute | solution.py:657
  77.3 22.5 %collective-permute-start.19 = (bf16[1792,128]{1,0:T(8,128)(2,1)S(1)}, bf16[1792,128]{1,0:T(8,128)(2,1)S(1)}, u32[]{:S(2)}, u32[]{:S(2)}) collective-permute-start(bf16[1792,128]{1,0:T(8,128)(2,1)S(1)} %get-tuple-element.158), channel_id=1, source_target_pairs={{0,1},{1,0},{2,3},{3,2},{4,5},{5,4},{6,7},{7,6},{8,9},{9,8},{10,11... | collective-permute-start | bytes 1376264 | tf_op jit(solution)/shard_map/ppermute | solution.py:657
  79.1 22.4 %collective-permute-start.20 = (bf16[1792,128]{1,0:T(8,128)(2,1)S(1)}, bf16[1792,128]{1,0:T(8,128)(2,1)S(1)}, u32[]{:S(2)}, u32[]{:S(2)}) collective-permute-start(bf16[1792,128]{1,0:T(8,128)(2,1)S(1)} %get-tuple-element.159), channel_id=1, source_target_pairs={{0,5},{1,4},{2,7},{3,6},{4,1},{5,0},{6,3},{7,2},{8,13},{9,12},{10,... | collective-permute-start | bytes 1376264 | tf_op jit(solution)/shard_map/ppermute | solution.py:657
  79.1 22.9 %collective-permute-start.18 = (bf16[1792,128]{1,0:T(8,128)(2,1)S(1)}, bf16[1792,128]{1,0:T(8,128)(2,1)S(1)}, u32[]{:S(2)}, u32[]{:S(2)}) collective-permute-start(bf16[1792,128]{1,0:T(8,128)(2,1)S(1)} %get-tuple-element.145.refs_4_), channel_id=1, source_target_pairs={{0,4},{2,6},{4,0},{6,2},{8,12},{10,14},{12,8},{14,10},{16,20},{18,... | collective-permute-start | bytes 1376264 | tf_op jit(solution)/shard_map/ppermute | solution.py:657
  85.5 28.9 %collective-permute-start.15 = (bf16[1024,128]{1,0:T(8,128)(2,1)S(1)}, bf16[1024,128]{1,0:T(8,128)(2,1)S(1)}, u32[]{:S(2)}, u32[]{:S(2)}) collective-permute-start(bf16[1024,128]{1,0:T(8,128)(2,1)S(1)} %get-tuple-element.148.refs_4_), channel_id=1, source_target_pairs={{0,4},{2,6},{4,0},{6,2},{8,12},{10,14},{12,8},{14,10},{16,20},{18,... | collective-permute-start | bytes 786440 | tf_op jit(solution)/shard_map/ppermute | solution.py:657
  91.7 12.9 %collective-permute-start.22 = (bf16[4,768,128]{2,1,0:T(8,128)(2,1)S(1)}, bf16[4,768,128]{2,1,0:T(8,128)(2,1)S(1)}, u32[]{:S(2)}, u32[]{:S(2)}) collective-permute-start(bf16[4,768,128]{2,1,0:T(8,128)(2,1)S(1)} %get-tuple-element.152.refs_8_), channel_id=1, source_target_pairs={{0,2},{2,0},{4,6},{6,4},{8,10},{10,8},{12,14},{14,12},{16,18},{18,... | collective-permute-start | bytes 2359304 | tf_op jit(solution)/shard_map/ppermute | solution.py:657
  99.7 12.6 %collective-permute-start.16 = (bf16[1024,128]{1,0:T(8,128)(2,1)S(1)}, bf16[1024,128]{1,0:T(8,128)(2,1)S(1)}, u32[]{:S(2)}, u32[]{:S(2)}) collective-permute-start(bf16[1024,128]{1,0:T(8,128)(2,1)S(1)} %get-tuple-element.155), channel_id=1, source_target_pairs={{0,1},{1,0},{2,3},{3,2},{4,5},{5,4},{6,7},{7,6},{8,9},{9,8},{10,11... | collective-permute-start | bytes 786440 | tf_op jit(solution)/shard_map/ppermute | solution.py:657
  101.5 13.0 %collective-permute-start.17 = (bf16[1024,128]{1,0:T(8,128)(2,1)S(1)}, bf16[1024,128]{1,0:T(8,128)(2,1)S(1)}, u32[]{:S(2)}, u32[]{:S(2)}) collective-permute-start(bf16[1024,128]{1,0:T(8,128)(2,1)S(1)} %get-tuple-element.156), channel_id=1, source_target_pairs={{0,5},{1,4},{2,7},{3,6},{4,1},{5,0},{6,3},{7,2},{8,13},{9,12},{10,... | collective-permute-start | bytes 786440 | tf_op jit(solution)/shard_map/ppermute | solution.py:657
  102.9 6.1 %collective-permute-start.21 = (bf16[896,128]{1,0:T(8,128)(2,1)S(1)}, bf16[896,128]{1,0:T(8,128)(2,1)S(1)}, u32[]{:S(2)}, u32[]{:S(2)}) collective-permute-start(bf16[896,128]{1,0:T(8,128)(2,1)S(1)} %get-tuple-element.162), channel_id=1, source_target_pairs={{0,8},{2,10},{4,12},{6,14},{8,0},{10,2},{12,4},{14,6},{16,24},{18,... | collective-permute-start | bytes 688136 | tf_op jit(solution)/shard_map/ppermute | solution.py:657
  105.4 20.9 %collective-permute-start.24 = (bf16[832,128]{1,0:T(8,128)(2,1)S(1)}, bf16[832,128]{1,0:T(8,128)(2,1)S(1)}, u32[]{:S(2)}, u32[]{:S(2)}) collective-permute-start(bf16[832,128]{1,0:T(8,128)(2,1)S(1)} %get-tuple-element.168.refs_2_), channel_id=1, source_target_pairs={{0,4},{2,6},{4,0},{6,2},{8,12},{10,14},{12,8},{14,10},{16,20},{18,... | collective-permute-start | bytes 638984 | tf_op jit(solution)/shard_map/ppermute | solution.py:657
  109.6 11.1 %collective-permute-start.27 = (bf16[896,128]{1,0:T(8,128)(2,1)S(1)}, bf16[896,128]{1,0:T(8,128)(2,1)S(1)}, u32[]{:S(2)}, u32[]{:S(2)}) collective-permute-start(bf16[896,128]{1,0:T(8,128)(2,1)S(1)} %up_2.1.refs_4_.refs_0_), channel_id=1, source_target_pairs={{0,16},{2,18},{4,20},{6,22},{8,24},{10,26},{12,28},{14,30},{16,0},... | collective-permute-start | bytes 688136 | tf_op jit(solution)/shard_map/ppermute | solution.py:657
  115.2 12.2 %collective-permute-start.23 = (bf16[512,128]{1,0:T(8,128)(2,1)S(1)}, bf16[512,128]{1,0:T(8,128)(2,1)S(1)}, u32[]{:S(2)}, u32[]{:S(2)}) collective-permute-start(bf16[512,128]{1,0:T(8,128)(2,1)S(1)} %get-tuple-element.170), channel_id=1, source_target_pairs={{0,8},{2,10},{4,12},{6,14},{8,0},{10,2},{12,4},{14,6},{16,24},{18,... | collective-permute-start | bytes 393224 | tf_op jit(solution)/shard_map/ppermute | solution.py:657
  116.9 9.4 %collective-permute-start.25 = (bf16[832,128]{1,0:T(8,128)(2,1)S(1)}, bf16[832,128]{1,0:T(8,128)(2,1)S(1)}, u32[]{:S(2)}, u32[]{:S(2)}) collective-permute-start(bf16[832,128]{1,0:T(8,128)(2,1)S(1)} %get-tuple-element.172), channel_id=1, source_target_pairs={{0,1},{1,0},{2,3},{3,2},{4,5},{5,4},{6,7},{7,6},{8,9},{9,8},{10,11... | collective-permute-start | bytes 638984 | tf_op jit(solution)/shard_map/ppermute | solution.py:657
  117.2 9.1 %collective-permute-start.26 = (bf16[832,128]{1,0:T(8,128)(2,1)S(1)}, bf16[832,128]{1,0:T(8,128)(2,1)S(1)}, u32[]{:S(2)}, u32[]{:S(2)}) collective-permute-start(bf16[832,128]{1,0:T(8,128)(2,1)S(1)} %get-tuple-element.173), channel_id=1, source_target_pairs={{0,5},{1,4},{2,7},{3,6},{4,1},{5,0},{6,3},{7,2},{8,13},{9,12},{10,... | collective-permute-start | bytes 638984 | tf_op jit(solution)/shard_map/ppermute | solution.py:657
  121.4 11.2 %collective-permute-start.30 = (bf16[896,128]{1,0:T(8,128)(2,1)S(1)}, bf16[896,128]{1,0:T(8,128)(2,1)S(1)}, u32[]{:S(2)}, u32[]{:S(2)}) collective-permute-start(bf16[896,128]{1,0:T(8,128)(2,1)S(1)} %up_3.1.refs_4_.refs_0_), channel_id=1, source_target_pairs={{0,8},{2,10},{4,12},{6,14},{8,0},{10,2},{12,4},{14,6},{16,24},{18,... | collective-permute-start | bytes 688136 | tf_op jit(solution)/shard_map/ppermute | solution.py:657
  126.9 8.9 %collective-permute-start.29 = (bf16[832,128]{1,0:T(8,128)(2,1)S(1)}, bf16[832,128]{1,0:T(8,128)(2,1)S(1)}, u32[]{:S(2)}, u32[]{:S(2)}) collective-permute-start(bf16[832,128]{1,0:T(8,128)(2,1)S(1)} %early_1.1.refs_2_.refs_0_), channel_id=1, source_target_pairs={{0,8},{2,10},{4,12},{6,14},{8,0},{10,2},{12,4},{14,6},{16,24},{18,... | collective-permute-start | bytes 638984 | tf_op jit(solution)/shard_map/ppermute | solution.py:657
  128.0 9.6 %collective-permute-start.32 = (bf16[512,128]{1,0:T(8,128)(2,1)S(1)}, bf16[512,128]{1,0:T(8,128)(2,1)S(1)}, u32[]{:S(2)}, u32[]{:S(2)}) collective-permute-start(bf16[512,128]{1,0:T(8,128)(2,1)S(1)} %late_2.1.refs_7_.refs_0_), channel_id=1, source_target_pairs={{0,16},{2,18},{4,20},{6,22},{8,24},{10,26},{12,28},{14,30},{16,0},... | collective-permute-start | bytes 393224 | tf_op jit(solution)/shard_map/ppermute | solution.py:657
  132.1 28.2 %collective-permute-start.28 = (bf16[624,1024]{1,0:T(8,128)(2,1)S(1)}, bf16[624,1024]{1,0:T(8,128)(2,1)S(1)}, u32[]{:S(2)}, u32[]{:S(2)}) collective-permute-start(bf16[624,1024]{1,0:T(8,128)(2,1)S(1)} %get-tuple-element.174.refs_2_), channel_id=1, source_target_pairs={{0,1},{1,0},{2,3},{3,2},{4,5},{5,4},{6,7},{7,6},{8,9},{9,8},{10,11... | collective-permute-start | bytes 3833864 | tf_op jit(solution)/shard_map/ppermute | solution.py:657
  133.2 17.4 %collective-permute-start.35 = (bf16[1792,128]{1,0:T(8,128)(2,1)S(1)}, bf16[1792,128]{1,0:T(8,128)(2,1)S(1)}, u32[]{:S(2)}, u32[]{:S(2)}) collective-permute-start(bf16[1792,128]{1,0:T(8,128)(2,1)S(1)} %up_4.1.refs_2_.refs_0_), channel_id=1, source_target_pairs={{0,2},{2,0},{4,6},{6,4},{8,10},{10,8},{12,14},{14,12},{16,18},{18,... | collective-permute-start | bytes 1376264 | tf_op jit(solution)/shard_map/ppermute | solution.py:657
  133.3 16.5 %collective-permute-start.34 = (bf16[1792,128]{1,0:T(8,128)(2,1)S(1)}, bf16[1792,128]{1,0:T(8,128)(2,1)S(1)}, u32[]{:S(2)}, u32[]{:S(2)}) collective-permute-start(bf16[1792,128]{1,0:T(8,128)(2,1)S(1)} %up_4.1.refs_2_.refs_0_), channel_id=1, source_target_pairs={{0,4},{2,6},{4,0},{6,2},{8,12},{10,14},{12,8},{14,10},{16,20},{18,... | collective-permute-start | bytes 1376264 | tf_op jit(solution)/shard_map/ppermute | solution.py:657
  136.4 11.1 %collective-permute-start.31 = (bf16[832,128]{1,0:T(8,128)(2,1)S(1)}, bf16[832,128]{1,0:T(8,128)(2,1)S(1)}, u32[]{:S(2)}, u32[]{:S(2)}) collective-permute-start(bf16[832,128]{1,0:T(8,128)(2,1)S(1)} %early_2.1.refs_2_.refs_0_), channel_id=1, source_target_pairs={{0,16},{2,18},{4,20},{6,22},{8,24},{10,26},{12,28},{14,30},{16,0},... | collective-permute-start | bytes 638984 | tf_op jit(solution)/shard_map/ppermute | solution.py:657
  138.2 10.0 %collective-permute-start.37 = (bf16[512,128]{1,0:T(8,128)(2,1)S(1)}, bf16[512,128]{1,0:T(8,128)(2,1)S(1)}, u32[]{:S(2)}, u32[]{:S(2)}) collective-permute-start(bf16[512,128]{1,0:T(8,128)(2,1)S(1)} %late_3.1.refs_2_.refs_0_), channel_id=1, source_target_pairs={{0,8},{2,10},{4,12},{6,14},{8,0},{10,2},{12,4},{14,6},{16,24},{18,... | collective-permute-start | bytes 393224 | tf_op jit(solution)/shard_map/ppermute | solution.py:657
  148.1 15.1 %collective-permute-start.38 = (bf16[832,128]{1,0:T(8,128)(2,1)S(1)}, bf16[832,128]{1,0:T(8,128)(2,1)S(1)}, u32[]{:S(2)}, u32[]{:S(2)}) collective-permute-start(bf16[832,128]{1,0:T(8,128)(2,1)S(1)} %early_3.1.refs_2_.refs_0_), channel_id=1, source_target_pairs={{0,2},{2,0},{4,6},{6,4},{8,10},{10,8},{12,14},{14,12},{16,18},{18,... | collective-permute-start | bytes 638984 | tf_op jit(solution)/shard_map/ppermute | solution.py:657
  148.2 8.1 %collective-permute-start.33 = (bf16[832,128]{1,0:T(8,128)(2,1)S(1)}, bf16[832,128]{1,0:T(8,128)(2,1)S(1)}, u32[]{:S(2)}, u32[]{:S(2)}) collective-permute-start(bf16[832,128]{1,0:T(8,128)(2,1)S(1)} %early_3.1.refs_2_.refs_0_), channel_id=1, source_target_pairs={{0,4},{2,6},{4,0},{6,2},{8,12},{10,14},{12,8},{14,10},{16,20},{18,... | collective-permute-start | bytes 638984 | tf_op jit(solution)/shard_map/ppermute | solution.py:657
  149.8 1.8 %collective-permute-start.36 = (bf16[1792,128]{1,0:T(8,128)(2,1)S(1)}, bf16[1792,128]{1,0:T(8,128)(2,1)S(1)}, u32[]{:S(2)}, u32[]{:S(2)}) collective-permute-start(bf16[1792,128]{1,0:T(8,128)(2,1)S(1)} %collective-permute-done.34.refs_1_), channel_id=1, source_target_pairs={{0,2},{2,0},{4,6},{6,4},{8,10},{10,8},{12,14},{14,12},{16,18},{18,... | collective-permute-start | bytes 1376264 | tf_op jit(solution)/shard_map/ppermute | solution.py:657
  150.6 14.6 %collective-permute-start.41 = (bf16[1024,128]{1,0:T(8,128)(2,1)S(1)}, bf16[1024,128]{1,0:T(8,128)(2,1)S(1)}, u32[]{:S(2)}, u32[]{:S(2)}) collective-permute-start(bf16[1024,128]{1,0:T(8,128)(2,1)S(1)} %late_4.1.refs_4_.refs_0_), channel_id=1, source_target_pairs={{0,2},{2,0},{4,6},{6,4},{8,10},{10,8},{12,14},{14,12},{16,18},{18,... | collective-permute-start | bytes 786440 | tf_op jit(solution)/shard_map/ppermute | solution.py:657
  151.7 11.5 %collective-permute-start.40 = (bf16[1024,128]{1,0:T(8,128)(2,1)S(1)}, bf16[1024,128]{1,0:T(8,128)(2,1)S(1)}, u32[]{:S(2)}, u32[]{:S(2)}) collective-permute-start(bf16[1024,128]{1,0:T(8,128)(2,1)S(1)} %late_4.1.refs_4_.refs_0_), channel_id=1, source_target_pairs={{0,4},{2,6},{4,0},{6,2},{8,12},{10,14},{12,8},{14,10},{16,20},{18,... | collective-permute-start | bytes 786440 | tf_op jit(solution)/shard_map/ppermute | solution.py:657
  156.3 6.9 %collective-permute-start.39 = (bf16[832,128]{1,0:T(8,128)(2,1)S(1)}, bf16[832,128]{1,0:T(8,128)(2,1)S(1)}, u32[]{:S(2)}, u32[]{:S(2)}) collective-permute-start(bf16[832,128]{1,0:T(8,128)(2,1)S(1)} %after_up.1.refs_6_.refs_1_), channel_id=1, source_target_pairs={{0,2},{2,0},{4,6},{6,4},{8,10},{10,8},{12,14},{14,12},{16,18},{18,... | collective-permute-start | bytes 638984 | tf_op jit(solution)/shard_map/ppermute | solution.py:657
  163.2 2.0 %collective-permute-start.42 = (bf16[1024,128]{1,0:T(8,128)(2,1)S(1)}, bf16[1024,128]{1,0:T(8,128)(2,1)S(1)}, u32[]{:S(2)}, u32[]{:S(2)}) collective-permute-start(bf16[1024,128]{1,0:T(8,128)(2,1)S(1)} %after_rows.1.refs_1_), channel_id=1, source_target_pairs={{0,2},{2,0},{4,6},{6,4},{8,10},{10,8},{12,14},{14,12},{16,18},{18,... | collective-permute-start | bytes 786440 | tf_op jit(solution)/shard_map/ppermute | solution.py:657

commit v2 on v1

--- a/solution.py
+++ b/solution.py
@@ -149,12 +149,15 @@
 
 def first_kernel(s, frames, qkv, up, out, down, prior, resets, *refs):
     smalls, refs = refs[:-9], refs[-9:]
-    sent_ref, one_ref, two_ref, own_ref, small_ref, resets_ref, wide_rows, rows, other = refs
-    resets_ref[...] = resets[...]
-    split_rows(s[0], frames, own_ref, other, wide_rows)
-    start = put_tiles(sent_ref, 0, other)
+    qkv_ref, sent_ref, one_ref, two_ref, own_ref, small_ref, resets_ref, wide_rows, rows = refs
+    start = 0
     for c in range(3):
-        start = put_tiles(sent_ref, start, qkv.get().at[c])
+        start = put_tiles(qkv_ref, start, qkv.get().at[c])
+    split_rows(s[0], frames, own_ref, sent_ref, wide_rows)
+    resets_ref[...] = jnp.zeros_like(resets_ref)
+    line = resets[...].reshape(1, -1)
+    for block in range(line.shape[1] // BLOCK):
+        resets_ref[block : block + 1, :BLOCK] = line[:, block * BLOCK : block * BLOCK + BLOCK]
     start = put_tiles(one_ref, put_tiles(one_ref, 0, up), out)
     for i, ref in enumerate(smalls):
         small_ref[i : i + 1, : ref.shape[1]] = ref[...]
@@ -171,10 +174,6 @@
     put_tiles(two_ref, put_tiles(two_ref, 0, down), prior)
 
 
-def cut_kernel(s, got, qkv_ref):
-    qkv_ref[...] = got[got.shape[0] - qkv_ref.shape[0] :, :]
-
-
 def cotangents_kernel(s, logit, out, sent, logit_own, out_own, wide_rows, logit_sent, out_sent):
     split_rows(s[0], logit, logit_own, logit_sent, wide_rows)
     split_rows(s[0], out, out_own, out_sent, wide_rows)
@@ -203,10 +202,9 @@
 
 
 def attend_kernel(
-    s, own, got, resets, small, q0, q1, q2, q3, qkv,
-    first_ref, triple_ref, mixed_ref, qkv_other_ref, other,
+    s, own, other, resets, small, q0, q1, q2, q3, qkv,
+    first_ref, triple_ref, mixed_ref, qkv_other_ref,
 ):
-    other[...] = tiles_of(got, 0, own.shape[0], 2)
     unit, _ = norm_of(whole_rows(s[0], own, other))
     n = first_ref.shape[1]
     first_ref[...] = (unit * vector(small, FIRST_GAIN, n) + vector(small, FIRST_SHIFT, n)).astype(BF)
@@ -740,7 +738,6 @@
     hidden_width, n_logits = up_bias.shape[0], prior_bias.shape[0]
     row = lambda v: v.reshape(1, -1)
     core, side = move.dp & 1, (move.dp >> 1) & 1
-    reset_rows = jnp.pad(resets.reshape(-1, BLOCK), ((0, -(2 * blocks) % 8), (0, -BLOCK % 128)))
     scalars = jnp.stack([move.here, core * 2 + side, (move.dp >> 2) & 1]).astype(jnp.int32)
     total_rows = blocks * PAD
     quarter = hidden_width // 4
@@ -762,7 +759,7 @@
     vectors = [first_gain, first_shift, out_bias, second_gain, second_shift, down_bias, prior_gain, prior_shift]
     vectors = [row(v) for v in vectors + [up_bias, prior_bias]]
     qkv_rows = 3 * (width // 4) * (half // 128)
-    sent_first, sent_one, sent_two, frames_own, small, resets_near = call(
+    sent_qkv, sent_frames, sent_one, sent_two, frames_own, small, resets_near = call(
         first_kernel,
         scalars,
         [
@@ -776,14 +773,15 @@
             some_rows(out_weight, half // 4, 1),
             some_rows(down_weight, quarter, 1),
             columns(prior_weight, n_logits // 4, 1),
-            Far(reset_rows),
+            Far(resets),
             *[Far(v) for v in vectors],
         ],
-        [((total_rows * (half // 128) + qkv_rows, 128), BF, True)]
+        [((qkv_rows, 128), BF, True)]
+        + near_rows((half, BF))
         + [((width * 2 + half + 48, 128), BF, True), ((quarter * 4 + width, 128), BF, True)]
         + near_rows((half, BF))
-        + [((16, hidden_width), F32, True), (reset_rows.shape, jnp.int32, True)],
-        [pltpu.VMEM((rows + 16, half), F32), pltpu.VMEM((16, 128), F32), pltpu.VMEM((total_rows, half), BF)],
+        + [((16, hidden_width), F32, True), ((-(-2 * blocks // 8) * 8, -(-BLOCK // 128) * 128), jnp.int32, True)],
+        [pltpu.VMEM((rows + 16, half), F32), pltpu.VMEM((16, 128), F32)],
         "first_parts",
         cost=2.0,
     )
@@ -792,10 +790,9 @@
         beside = move.side(got)
         return [got, beside, move.core(got), move.core(beside)]
 
-    got_first = move.over(sent_first)
-    (qkv_got,) = call(cut_kernel, scalars, [got_first], [((qkv_rows, 128), BF, True)], name="cut", cost=100.0)
-    (sent_one,) = gate([sent_one], [got_first], "after_first")
-    got_one = move.over(sent_one)
+    qkv_got = move.over(sent_qkv)
+    frames_other = move.over(sent_frames)
+    qkv_pieces = all_quarters(qkv_got)
     cot_sent, logit_own, out_own, qkv_near, out_near, up_near, down_near, prior_near = call(
         cotangents_kernel,
         scalars,
@@ -804,23 +801,25 @@
         [pltpu.VMEM((rows + 16, n_logits), F32)]
         + [pltpu.VMEM((total_rows, n), BF) for n in (n_logits, half)],
         name="cotangents",
-        after=(sent_first,),
+        after=(sent_frames,),
         cost=2.3,
         loads=(qkv_weight, out_weight, up_weight, down_weight, prior_weight),
     )
-    (sent_two,) = gate([sent_two], [qkv_got, sent_one, cot_sent], "after_cut")
+    (sent_one,) = gate([sent_one], [frames_other, cot_sent], "after_frames")
+    got_one = move.over(sent_one)
+    (sent_two,) = gate([sent_two], [sent_one, qkv_pieces[1]], "after_one")
     got_two = move.over(sent_two)
-    first, triple, mixed, qkv_other, frames_other = call(
+    first, triple, mixed, qkv_other = call(
         attend_kernel,
         scalars,
-        [frames_own, got_first, resets_near, small, *all_quarters(qkv_got), qkv_near],
-        near_rows((width, BF), (3 * width, BF), (width, BF)) + [(qkv_weight.shape, BF, True)] + near_rows((half, BF)),
+        [frames_own, frames_other, resets_near, small, *qkv_pieces, qkv_near],
+        near_rows((width, BF), (3 * width, BF), (width, BF)) + [(qkv_weight.shape, BF, True)],
         name="attend",
         cost=5.5,
     )
     beside_one = move.side(got_one)
-    got_two, cot_sent = gate([got_two, cot_sent], [mixed, beside_one], "after_attend")
-    beside_two = move.side(got_two)
+    (cot_sent,) = gate([cot_sent], [got_two, beside_one], "after_two")
+    (beside_two,) = gate([move.side(got_two)], [mixed], "after_attend")
     packed = [got_one, beside_one, move.core(got_one), move.core(beside_one)]
     packed += [got_two, beside_two, move.core(got_two), move.core(beside_two)]
     cotangents = move.over(cot_sent)
@@ -916,8 +915,6 @@
     done = late
     for bit in bits[1:]:
         done = up = move.total(scalars, [up, move.along(up, bit)], "up_3", (done,))
-    done = early = move.total(scalars, [early_rest, *move.sides(early_low)], "early_1", (done,))
-    done = late = move.total(scalars, [late, move.along(late_half, bits[0])], "late_2", (done,))
     back_send, logits_own = call(
         logits_kernel,
         scalars,
@@ -927,7 +924,10 @@
         after=(done,),
         cost=2.0,
     )
-    done = up = move.join(scalars, up, move.along(up, bits[0]), "up_4", (back_send,))
+    done = back_send
+    done = early = move.total(scalars, [early_rest, *move.sides(early_low)], "early_1", (done,))
+    done = late = move.total(scalars, [late, move.along(late_half, bits[0])], "late_2", (done,))
+    done = up = move.join(scalars, up, move.along(up, bits[0]), "up_4", (done,))
     for bit in bits[:-1]:
         done = early = move.total(scalars, [early, move.along(early, bit)], "early_2", (done,))
     for bit in bits[1:]:

time: 168 us -> 159 us (0.946)
  waiting for transfers between devices: 62 us -> 47.5 us
  starting transfers between devices: 39.1 us -> 47.4 us
    ppermute x43 -> x44, waiting for transfers between devices: 62 us -> 47.5 us  [swap(): return lax.ppermute(value, axes, [(i, i ^ mask) for i in range(count)])]
    ppermute x43 -> x44, starting transfers between devices: 39.1 us -> 47.4 us  [swap(): return lax.ppermute(value, axes, [(i, i ^ mask) for i in range(count)])]
    pallas_call x32 -> x31, Pallas kernels: 63.5 us -> 62.8 us  [call(): pl.pallas_call(run, in_specs=[pl.BlockSpec(memory_space=pltpu.SMEM)] + [f...]
  transfers between devices with their start and end apart: 43 -> 44, of which waited for: 20 -> 22; matrix products, arithmetic and copies ran while one was open for 0% -> 0% of each run, Pallas kernels for 29% -> 30%
where the time goes in v2:
time: 159 us
  Pallas kernels  63 us (40%)
  waiting for transfers between devices  47.5 us (30%)
  starting transfers between devices  47.4 us (30%)
    pallas_call x31, Pallas kernels, call(): pl.pallas_call(run, in_specs=[pl.BlockSpec(memory_space=pltpu.SMEM)] + [f...  62.8 us
    ppermute x44, waiting for transfers between devices, swap(): return lax.ppermute(value, axes, [(i, i ^ mask) for i in range(count)])  47.5 us
    ppermute x44, starting transfers between devices, swap(): return lax.ppermute(value, axes, [(i, i ^ mask) for i in range(count)])  47.4 us
  transfers between devices with their start and end apart: 44, of which 22 were waited for; matrix products, arithmetic and copies ran while one was open for 0% of the time, Pallas kernels for 30%

profile of v2, /device:TPU:0, one launch (start us, length us, event | category | flops | bytes accessed | tf_op | source)
XLA Modules:
  0.0 159.3 jit_solution(8687821574039459454)
XLA Ops:
  0.7 2.2 %first_parts.1 = (bf16[768,128]{1,0:T(8,128)(2,1)S(1)}, bf16[624,256]{1,0:T(8,128)(2,1)S(1)}, bf16[1328,128]{1,0:T(8,128)(2,1)S(1)}, bf16[1536,128]{1,0:T(8,128)...) custom-call(s32[3]{0:T(128)S(1)} %pad_add_fusion.s, ...), custom_call_target="tpu_custom_call" | custom-call | flops 200000000 | tf_op jit(solution)/shard_map/first_parts/pallas_call | solution.py:631
  3.0 3.0 %collective-permute-start = (bf16[624,256]{1,0:T(8,128)(2,1)S(1)}, bf16[624,256]{1,0:T(8,128)(2,1)S(1)}, u32[]{:S(2)}, u32[]{:S(2)}) collective-permute-start(bf16[624,256]{1,0:T(8,128)(2,1)S(1)} %get-tuple-element.106.refs_7_), channel_id=1, source_target_pairs={{0,1},{1,0},{2,3},{3,2},{4,5},{5,4},{6,7},{7,6},{8,9},{9,8},{10,11... | collective-permute-start | bytes 958472 | tf_op jit(solution)/shard_map/ppermute | solution.py:655
  6.1 3.1 %cotangents.1 = (bf16[624,768]{1,0:T(8,128)(2,1)S(1)}, bf16[624,512]{1,0:T(8,128)(2,1)S(1)}, bf16[624,256]{1,0:T(8,128)(2,1)S(1)}, bf16[3,512,256]{2,1,0:T(8,128...) custom-call(s32[3]{0:T(128)S(1)} %pad_add_fusion.s, ...), custom_call_target="tpu_custom_call" | custom-call | flops 230000000 | tf_op jit(solution)/shard_map/cotangents/pallas_call | solution.py:631
  9.2 5.1 %collective-permute-done.refs_1_.refs_4_ = bf16[624,256]{1,0:T(8,128)(2,1)S(1)} collective-permute-done((bf16[624,256]{1,0:T(8,128)(2,1)S(1)}, bf16[624,256]{1,0:T(8,128)(2,1)S(1)}, u32[]{:S(2)}, u32[]{:S(2)}) %collective-permute-start) | collective-permute-done | bytes 319520 | tf_op jit(solution)/shard_map/ppermute | solution.py:655
  14.4 2.1 %collective-permute-start.5 = (bf16[1328,128]{1,0:T(8,128)(2,1)S(1)}, bf16[1328,128]{1,0:T(8,128)(2,1)S(1)}, u32[]{:S(2)}, u32[]{:S(2)}) collective-permute-start(bf16[1328,128]{1,0:T(8,128)(2,1)S(1)} %after_frames.1.refs_1_), channel_id=1, source_target_pairs={{0,1},{1,0},{2,3},{3,2},{4,5},{5,4},{6,7},{7,6},{8,9},{9,8},{10,11... | collective-permute-start | bytes 1019912 | tf_op jit(solution)/shard_map/ppermute | solution.py:655
  16.5 2.1 %collective-permute-done.1.refs_4_ = bf16[768,128]{1,0:T(8,128)(2,1)S(1)} collective-permute-done((bf16[768,128]{1,0:T(8,128)(2,1)S(1)}, bf16[768,128]{1,0:T(8,128)(2,1)S(1)}, u32[]{:S(2)}, u32[]{:S(2)}) %collective-permute-start.1) | collective-permute-done | bytes 196640 | tf_op jit(solution)/shard_map/ppermute | solution.py:655
  18.6 2.0 %collective-permute-start.2 = (bf16[768,128]{1,0:T(8,128)(2,1)S(1)}, bf16[768,128]{1,0:T(8,128)(2,1)S(1)}, u32[]{:S(2)}, u32[]{:S(2)}) collective-permute-start(bf16[768,128]{1,0:T(8,128)(2,1)S(1)} %collective-permute-done.1.refs_4_), channel_id=1, source_target_pairs={{0,4},{2,6},{4,0},{6,2},{8,12},{10,14},{12,8},{14,10},{16,20},{18,... | collective-permute-start | bytes 589832 | tf_op jit(solution)/shard_map/ppermute | solution.py:655
  20.6 3.6 %collective-permute-done.2.refs_5_.refs_2_ = bf16[768,128]{1,0:T(8,128)(2,1)S(1)} collective-permute-done((bf16[768,128]{1,0:T(8,128)(2,1)S(1)}, bf16[768,128]{1,0:T(8,128)(2,1)S(1)}, u32[]{:S(2)}, u32[]{:S(2)}) %collective-permute-start.2) | collective-permute-done | bytes 196640 | tf_op jit(solution)/shard_map/ppermute | solution.py:655
  24.3 2.1 %collective-permute-start.9 = (bf16[1536,128]{1,0:T(8,128)(2,1)S(1)}, bf16[1536,128]{1,0:T(8,128)(2,1)S(1)}, u32[]{:S(2)}, u32[]{:S(2)}) collective-permute-start(bf16[1536,128]{1,0:T(8,128)(2,1)S(1)} %after_one.1), channel_id=1, source_target_pairs={{0,1},{1,0},{2,3},{3,2},{4,5},{5,4},{6,7},{7,6},{8,9},{9,8},{10,11... | collective-permute-start | bytes 1179656 | tf_op jit(solution)/shard_map/ppermute | solution.py:655
  26.4 1.5 collective-permute-start.6
  27.9 5.6 %collective-permute-done.9.refs_11_.refs_1_.refs_8_ = bf16[1536,128]{1,0:T(8,128)(2,1)S(1)} collective-permute-done((bf16[1536,128]{1,0:T(8,128)(2,1)S(1)}, bf16[1536,128]{1,0:T(8,128)(2,1)S(1)}, u32[]{:S(2)}, u32[]{:S(2)}) %collective-permute-start.9) | collective-permute-done | bytes 393248 | tf_op jit(solution)/shard_map/ppermute | solution.py:655
  33.5 0.7 collective-permute-done.6.refs_8_.refs_2_.refs_5_
  34.3 1.5 collective-permute-start.13
  35.7 1.5 collective-permute-start.10
  37.7 0.9 collective-permute-done.3.refs_6_
  39.0 4.3 %attend.1 = (bf16[624,512]{1,0:T(8,128)(2,1)S(1)}, bf16[624,1536]{1,0:T(8,128)(2,1)S(1)}, bf16[624,512]{1,0:T(8,128)(2,1)S(1)}, bf16[3,512,256]{2,1,0:T(8,128)(2,1)S(1)}) custom-call(s32[3]{0:T(128)S(1)} %pad_add_fusion.s, bf16[624,256]{1,0:T(8,128)(2,1)S(1)} %get-tuple-element.105.refs_0_.refs_3_, ...), custom_call_target="tpu_custom_call" | custom-call | flops 550000000 | tf_op jit(solution)/shard_map/attend/pallas_call | solution.py:631
  44.5 1.7 %collective-permute-done.7.refs_9_.refs_6_ = bf16[1328,128]{1,0:T(8,128)(2,1)S(1)} collective-permute-done((bf16[1328,128]{1,0:T(8,128)(2,1)S(1)}, bf16[1328,128]{1,0:T(8,128)(2,1)S(1)}, u32[]{:S(2)}, u32[]{:S(2)}) %collective-permute-start.7) | collective-permute-done | bytes 340000 | tf_op jit(solution)/shard_map/ppermute | solution.py:655
  46.6 6.9 %feed.1 = (bf16[624,256]{1,0:T(8,128)(2,1)S(1)}, bf16[624,256]{1,0:T(8,128)(2,1)S(1)}, f32[624,512]{1,0:T(8,128)S(1)}, bf16[624,512]{1,0:T(8,128)(2,1)S(1)}, bf1...) custom-call(s32[3]{0:T(128)S(1)} %pad_add_fusion.s, ...), custom_call_target="tpu_custom_call" | custom-call | flops 720000000 | tf_op jit(solution)/shard_map/feed/pallas_call | solution.py:631
  53.5 0.9 collective-permute-done.13.refs_12_.refs_6_
  54.4 2.3 %prior.1 = (f32[624,512]{1,0:T(8,128)S(1)}, bf16[624,512]{1,0:T(8,128)(2,1)S(1)}, f32[3,512]{1,0:T(4,128)S(1)}, f32[1,1024]{1,0:T(1,128)S(1)}, bf16[512,512]{1,0:T(8,128)(2,1)S(1)}, /*index=5*/f32[1,512]{1,0:T(1,128)S(1)}) custom-call(s32[3]{0:T(128)S(1)} %pad_add_fusion.s, f32[624,512]{1,0:T(8,128)S(1)} %get-tuple-element.121.refs_0_, ...), custom_call_target="tpu_custom_call" | custom-call | flops 250000000 | tf_op jit(solution)/shard_map/prior/pallas_call | solution.py:631
  56.8 4.9 %feed_back.1 = (bf16[624,2048]{1,0:T(8,128)(2,1)S(1)}, f32[624,512]{1,0:T(8,128)S(1)}, bf16[624,512]{1,0:T(8,128)(2,1)S(1)}, f32[3,512]{1,0:T(4,128)S(1)}, f32[1,2048]{1,0:T(1,128)S(1)}) custom-call(s32[3]{0:T(128)S(1)} %pad_add_fusion.s, bf16[624,512]{1,0:T(8,128)(2,1)S(1)} %get-tuple-element.127.refs_0_.refs_1_, ...), custom_call_target="tpu_custom_call" | custom-call | flops 650000000 | tf_op jit(solution)/shard_map/feed_back/pallas_call | solution.py:631
  61.7 3.9 %up_grads.1 = (f32[4,1792,128]{2,1,0:T(8,128)S(1)}, bf16[4,1792,128]{2,1,0:T(8,128)(2,1)S(1)}) custom-call(s32[3]{0:T(128)S(1)} %pad_add_fusion.s, bf16[624,512]{1,0:T(8,128)(2,1)S(1)} %get-tuple-element.135.refs_0_, bf16[624,2048]{1,0:T(8,128)(2,1)S(1)} %get-tuple-element.136.refs_1_, bf16[624,512]{1,0:T(8,128)(2,1)S(1)} %get-tuple-element.111.refs_1_.refs_2_, ...), custom_call_target="tpu_custom_call" | custom-call | flops 300000000 | tf_op jit(solution)/shard_map/up_grads/pallas_call | solution.py:631
  65.7 2.4 %late_grads.1 = (f32[4,1024,128]{2,1,0:T(8,128)S(1)}, bf16[4,1024,128]{2,1,0:T(8,128)(2,1)S(1)}) custom-call(s32[3]{0:T(128)S(1)} %pad_add_fusion.s, bf16[624,2048]{1,0:T(8,128)(2,1)S(1)} %get-tuple-element.139.refs_0_, bf16[624,512]{1,0:T(8,128)(2,1)S(1)} %get-tuple-element.127.refs_0_.refs_1_, bf16[4,1792,128]{2,1,0:T(8,128)(2,1)S(1)} %get-tuple-element.138.refs_2_), custom_call_target="tpu_custom_call" | custom-call | flops 350000000 | tf_op jit(solution)/shard_map/late_grads/pallas_call | solution.py:631
  68.7 0.8 collective-permute-done.14.refs_1_
  69.5 0.9 up_core.1
  70.4 1.8 %collective-permute-start.17 = (bf16[1792,128]{1,0:T(8,128)(2,1)S(1)}, bf16[1792,128]{1,0:T(8,128)(2,1)S(1)}, u32[]{:S(2)}, u32[]{:S(2)}) collective-permute-start(bf16[1792,128]{1,0:T(8,128)(2,1)S(1)} %get-tuple-element.151), channel_id=1, source_target_pairs={{0,1},{1,0},{2,3},{3,2},{4,5},{5,4},{6,7},{7,6},{8,9},{9,8},{10,11... | collective-permute-start | bytes 1376264 | tf_op jit(solution)/shard_map/ppermute | solution.py:655
  72.2 1.2 collective-permute-start.18
  74.0 3.9 %attend_back_0.1.refs_2_.refs_1_.refs_0_ = bf16[624,768]{1,0:T(8,128)(2,1)S(1)} custom-call(s32[3]{0:T(128)S(1)} %pad_add_fusion.s, bf16[624,512]{1,0:T(8,128)(2,1)S(1)} %get-tuple-element.133.refs_3_.refs_0_, bf16[624,1536]{1,0:T(8,128)(2,1)S(1)} %get-tuple-element.134.refs_1_, bf16[256,512]{1,0:T(8,128)(2,1)S(1)} %get-tuple-element.112.refs_4_.refs_2_, ...), custom_call_target="tpu_custom_call" | custom-call | flops 450000000 | tf_op jit(solution)/shard_map/attend_back_0/pallas_call | solution.py:631
  77.9 0.8 late_core.1
  78.7 1.6 collective-permute-start.22
  80.3 3.7 %attend_back_1.1.refs_2_.refs_1_ = bf16[624,768]{1,0:T(8,128)(2,1)S(1)} custom-call(s32[3]{0:T(128)S(1)} %pad_add_fusion.s, bf16[624,512]{1,0:T(8,128)(2,1)S(1)} %get-tuple-element.133.refs_3_.refs_0_, bf16[624,1536]{1,0:T(8,128)(2,1)S(1)} %get-tuple-element.134.refs_1_, bf16[256,512]{1,0:T(8,128)(2,1)S(1)} %get-tuple-element.142.refs_2_, ...), custom_call_target="tpu_custom_call" | custom-call | flops 450000000 | tf_op jit(solution)/shard_map/attend_back_1/pallas_call | solution.py:631
  84.0 2.0 %early_grads.1 = (f32[4,768,128]{2,1,0:T(8,128)S(1)}, bf16[4,768,128]{2,1,0:T(8,128)(2,1)S(1)}) custom-call(s32[3]{0:T(128)S(1)} %pad_add_fusion.s, bf16[624,512]{1,0:T(8,128)(2,1)S(1)} %get-tuple-element.147.refs_0_, bf16[624,768]{1,0:T(8,128)(2,1)S(1)} %attend_back_0.1.refs_2_.refs_1_.refs_0_, bf16[624,768]{1,0:T(8,128)(2,1)S(1)} %attend_back_1.1.refs_2_.refs_1_), custom_call_target="tpu_custom_call" | custom-call | flops 200000000 | tf_op jit(solution)/shard_map/early_grads/pallas_call | solution.py:631
  86.1 2.3 %frames_back.1 = (bf16[624,256]{1,0:T(8,128)(2,1)S(1)}, f32[624,256]{1,0:T(8,128)S(1)}, f32[2,512]{1,0:T(2,128)S(1)}) custom-call(s32[3]{0:T(128)S(1)} %pad_add_fusion.s, bf16[624,768]{1,0:T(8,128)(2,1)S(1)} %attend_back_0.1.refs_2_.refs_1_.refs_0_, bf16[624,768]{1,0:T(8,128)(2,1)S(1)} %attend_back_1.1.refs_2_.refs_1_, ...), custom_call_target="tpu_custom_call" | custom-call | flops 250000000 | tf_op jit(solution)/shard_map/frames_back/pallas_call | solution.py:631
  88.5 4.4 %collective-permute-done.17.refs_2_ = bf16[1792,128]{1,0:T(8,128)(2,1)S(1)} collective-permute-done((bf16[1792,128]{1,0:T(8,128)(2,1)S(1)}, bf16[1792,128]{1,0:T(8,128)(2,1)S(1)}, u32[]{:S(2)}, u32[]{:S(2)}) %collective-permute-start.17) | collective-permute-done | bytes 458784 | tf_op jit(solution)/shard_map/ppermute | solution.py:655
  92.9 1.7 %collective-permute-start.23 = (bf16[1024,128]{1,0:T(8,128)(2,1)S(1)}, bf16[1024,128]{1,0:T(8,128)(2,1)S(1)}, u32[]{:S(2)}, u32[]{:S(2)}) collective-permute-start(bf16[1024,128]{1,0:T(8,128)(2,1)S(1)} %get-tuple-element.163), channel_id=1, source_target_pairs={{0,1},{1,0},{2,3},{3,2},{4,5},{5,4},{6,7},{7,6},{8,9},{9,8},{10,11... | collective-permute-start | bytes 786440 | tf_op jit(solution)/shard_map/ppermute | solution.py:655
  94.6 1.2 collective-permute-start.24
  95.9 0.9 up_1.1
  96.8 1.7 %collective-permute-start.19 = (bf16[896,128]{1,0:T(8,128)(2,1)S(1)}, bf16[896,128]{1,0:T(8,128)(2,1)S(1)}, u32[]{:S(2)}, u32[]{:S(2)}) collective-permute-start(bf16[896,128]{1,0:T(8,128)(2,1)S(1)} %get-tuple-element.155), channel_id=1, source_target_pairs={{0,8},{2,10},{4,12},{6,14},{8,0},{10,2},{12,4},{14,6},{16,24},{18,... | collective-permute-start | bytes 688136 | tf_op jit(solution)/shard_map/ppermute | solution.py:655
  98.4 0.8 early_core.1
  99.2 0.9 collective-permute-start.26
  100.1 3.0 %collective-permute-done.19.refs_1_ = bf16[896,128]{1,0:T(8,128)(2,1)S(1)} collective-permute-done((bf16[896,128]{1,0:T(8,128)(2,1)S(1)}, bf16[896,128]{1,0:T(8,128)(2,1)S(1)}, u32[]{:S(2)}, u32[]{:S(2)}) %collective-permute-start.19) | collective-permute-done | bytes 229408 | tf_op jit(solution)/shard_map/ppermute | solution.py:655
  103.7 2.7 %collective-permute-start.21 = (bf16[896,128]{1,0:T(8,128)(2,1)S(1)}, bf16[896,128]{1,0:T(8,128)(2,1)S(1)}, u32[]{:S(2)}, u32[]{:S(2)}) collective-permute-start(bf16[896,128]{1,0:T(8,128)(2,1)S(1)} %up_2.1.refs_4_.refs_0_), channel_id=1, source_target_pairs={{0,16},{2,18},{4,20},{6,22},{8,24},{10,26},{12,28},{14,30},{16,0},... | collective-permute-start | bytes 688136 | tf_op jit(solution)/shard_map/ppermute | solution.py:655
  106.4 1.2 collective-permute-done.24.refs_3_
  107.6 0.8 late_1.1
  108.4 1.6 %collective-permute-start.31 = (bf16[512,128]{1,0:T(8,128)(2,1)S(1)}, bf16[512,128]{1,0:T(8,128)(2,1)S(1)}, u32[]{:S(2)}, u32[]{:S(2)}) collective-permute-start(bf16[512,128]{1,0:T(8,128)(2,1)S(1)} %get-tuple-element.172), channel_id=1, source_target_pairs={{0,8},{2,10},{4,12},{6,14},{8,0},{10,2},{12,4},{14,6},{16,24},{18,... | collective-permute-start | bytes 393224 | tf_op jit(solution)/shard_map/ppermute | solution.py:655
  110.5 2.4 %collective-permute-start.28 = (bf16[832,128]{1,0:T(8,128)(2,1)S(1)}, bf16[832,128]{1,0:T(8,128)(2,1)S(1)}, u32[]{:S(2)}, u32[]{:S(2)}) collective-permute-start(bf16[832,128]{1,0:T(8,128)(2,1)S(1)} %get-tuple-element.171), channel_id=1, source_target_pairs={{0,5},{1,4},{2,7},{3,6},{4,1},{5,0},{6,3},{7,2},{8,13},{9,12},{10,... | collective-permute-start | bytes 638984 | tf_op jit(solution)/shard_map/ppermute | solution.py:655
  113.0 2.1 %collective-permute-done.21.refs_1_ = bf16[896,128]{1,0:T(8,128)(2,1)S(1)} collective-permute-done((bf16[896,128]{1,0:T(8,128)(2,1)S(1)}, bf16[896,128]{1,0:T(8,128)(2,1)S(1)}, u32[]{:S(2)}, u32[]{:S(2)}) %collective-permute-start.21) | collective-permute-done | bytes 229408 | tf_op jit(solution)/shard_map/ppermute | solution.py:655
  116.4 1.4 logits.1
  117.8 1.7 %collective-permute-done.27.refs_2_ = bf16[832,128]{1,0:T(8,128)(2,1)S(1)} collective-permute-done((bf16[832,128]{1,0:T(8,128)(2,1)S(1)}, bf16[832,128]{1,0:T(8,128)(2,1)S(1)}, u32[]{:S(2)}, u32[]{:S(2)}) %collective-permute-start.27) | collective-permute-done | bytes 213024 | tf_op jit(solution)/shard_map/ppermute | solution.py:655
  120.6 1.0 collective-permute-start.29
  122.2 2.2 %collective-permute-start.33 = (bf16[512,128]{1,0:T(8,128)(2,1)S(1)}, bf16[512,128]{1,0:T(8,128)(2,1)S(1)}, u32[]{:S(2)}, u32[]{:S(2)}) collective-permute-start(bf16[512,128]{1,0:T(8,128)(2,1)S(1)} %late_2.1.refs_2_.refs_0_), channel_id=1, source_target_pairs={{0,16},{2,18},{4,20},{6,22},{8,24},{10,26},{12,28},{14,30},{16,0},... | collective-permute-start | bytes 393224 | tf_op jit(solution)/shard_map/ppermute | solution.py:655
  125.1 1.5 collective-permute-start.35
  126.6 2.8 %collective-permute-done.29.refs_1_ = bf16[832,128]{1,0:T(8,128)(2,1)S(1)} collective-permute-done((bf16[832,128]{1,0:T(8,128)(2,1)S(1)}, bf16[832,128]{1,0:T(8,128)(2,1)S(1)}, u32[]{:S(2)}, u32[]{:S(2)}) %collective-permute-start.29) | collective-permute-done | bytes 213024 | tf_op jit(solution)/shard_map/ppermute | solution.py:655
  130.0 1.6 %collective-permute-start.32 = (bf16[832,128]{1,0:T(8,128)(2,1)S(1)}, bf16[832,128]{1,0:T(8,128)(2,1)S(1)}, u32[]{:S(2)}, u32[]{:S(2)}) collective-permute-start(bf16[832,128]{1,0:T(8,128)(2,1)S(1)} %early_2.1.refs_2_.refs_0_), channel_id=1, source_target_pairs={{0,16},{2,18},{4,20},{6,22},{8,24},{10,26},{12,28},{14,30},{16,0},... | collective-permute-start | bytes 638984 | tf_op jit(solution)/shard_map/ppermute | solution.py:655
  132.2 3.0 %collective-permute-start.38 = (bf16[512,128]{1,0:T(8,128)(2,1)S(1)}, bf16[512,128]{1,0:T(8,128)(2,1)S(1)}, u32[]{:S(2)}, u32[]{:S(2)}) collective-permute-start(bf16[512,128]{1,0:T(8,128)(2,1)S(1)} %late_3.1.refs_2_.refs_0_), channel_id=1, source_target_pairs={{0,8},{2,10},{4,12},{6,14},{8,0},{10,2},{12,4},{14,6},{16,24},{18,... | collective-permute-start | bytes 393224 | tf_op jit(solution)/shard_map/ppermute | solution.py:655
  135.2 5.7 %collective-permute-done.32.refs_1_ = bf16[832,128]{1,0:T(8,128)(2,1)S(1)} collective-permute-done((bf16[832,128]{1,0:T(8,128)(2,1)S(1)}, bf16[832,128]{1,0:T(8,128)(2,1)S(1)}, u32[]{:S(2)}, u32[]{:S(2)}) %collective-permute-start.32) | collective-permute-done | bytes 213024 | tf_op jit(solution)/shard_map/ppermute | solution.py:655
  141.6 0.7 collective-permute-start.34
  144.2 1.3 collective-permute-start.41
  145.5 2.8 %up_place.1 = (f32[512,1024]{1,0:T(8,128)}, f32[256,512]{1,0:T(8,128)}, f32[512,512]{1,0:T(8,128)}, f32[8,128]{1,0:T(8,128)S(1)}) custom-call(s32[3]{0:T(128)S(1)} %pad_add_fusion.s, bf16[1792,128]{1,0:T(8,128)(2,1)S(1)} %up_4.1.refs_2_.refs_0_, bf16[1792,128]{1,0:T(8,128)(2,1)S(1)} %collective-permute-done.35.refs_1_, ...), custom_call_target="tpu_custom_call" | custom-call | flops 10000000000 | tf_op jit(solution)/shard_map/up_place/pallas_call | solution.py:631
  148.3 1.4 collective-permute-done.34.refs_0_
  149.9 2.9 %rows_back.1 = (bf16[1200,256]{1,0:T(8,128)(2,1)}, f32[1200,512]{1,0:T(8,128)}, f32[1200,256]{1,0:T(8,128)}, f32[8,128]{1,0:T(8,128)S(1)}) custom-call(s32[3]{0:T(128)S(1)} %pad_add_fusion.s, bf16[624,256]{1,0:T(8,128)(2,1)S(1)} %get-tuple-element.118.refs_0_, bf16[624,1024]{1,0:T(8,128)(2,1)S(1)} %collective-permute-done.25.refs_1_.refs_3_.refs_5_, ...), custom_call_target="tpu_custom_call" | custom-call | flops 10000000000 | tf_op jit(solution)/shard_map/rows_back/pallas_call | solution.py:631
  152.7 2.2 %collective-permute-done.41.refs_0_ = bf16[1024,128]{1,0:T(8,128)(2,1)S(1)} collective-permute-done((bf16[1024,128]{1,0:T(8,128)(2,1)S(1)}, bf16[1024,128]{1,0:T(8,128)(2,1)S(1)}, u32[]{:S(2)}, u32[]{:S(2)}) %collective-permute-start.41) | collective-permute-done | bytes 262176 | tf_op jit(solution)/shard_map/ppermute | solution.py:655
  155.0 1.9 %early_place.1 = (f32[3,512,256]{2,1,0:T(8,128)}, f32[1,512]{1,0:T(1,128)}, f32[1,512]{1,0:T(1,128)}, f32[1,512]{1,0:T(1,128)}, f32[1,512]{1,0:T(1,128)}, /*inde...) custom-call(s32[3]{0:T(128)S(1)} %pad_add_fusion.s, ...), custom_call_target="tpu_custom_call" | custom-call | flops 10000000000 | tf_op jit(solution)/shard_map/early_place/pallas_call | solution.py:631
  157.0 2.1 %late_place.1 = f32[1024,512]{1,0:T(8,128)} custom-call(s32[3]{0:T(128)S(1)} %pad_add_fusion.s, bf16[1024,128]{1,0:T(8,128)(2,1)S(1)} %late_4.1.refs_4_.refs_0_, bf16[1024,128]{1,0:T(8,128)(2,1)S(1)} %after_rows.1.refs_1_, bf16[1024,128]{1,0:T(8,128)(2,1)S(1)} %collective-permute-done.42.refs_2_, bf16[1024,128]{1,0:T(8,128)(2,1)S(1)} %collective-permute-done.43.refs_3_, ...), custom_call_target="tpu_custom_call" | custom-call | flops 10000000000 | tf_op jit(solution)/shard_map/late_place/pallas_call | solution.py:631
  (62 shorter events, 12.6 us)
Async XLA Ops:
  3.0 11.4 %collective-permute-start = (bf16[624,256]{1,0:T(8,128)(2,1)S(1)}, bf16[624,256]{1,0:T(8,128)(2,1)S(1)}, u32[]{:S(2)}, u32[]{:S(2)}) collective-permute-start(bf16[624,256]{1,0:T(8,128)(2,1)S(1)} %get-tuple-element.106.refs_7_), channel_id=1, source_target_pairs={{0,1},{1,0},{2,3},{3,2},{4,5},{5,4},{6,7},{7,6},{8,9},{9,8},{10,11... | collective-permute-start | bytes 958472 | tf_op jit(solution)/shard_map/ppermute | solution.py:655
  6.0 12.6 %collective-permute-start.1 = (bf16[768,128]{1,0:T(8,128)(2,1)S(1)}, bf16[768,128]{1,0:T(8,128)(2,1)S(1)}, u32[]{:S(2)}, u32[]{:S(2)}) collective-permute-start(bf16[768,128]{1,0:T(8,128)(2,1)S(1)} %get-tuple-element.109), channel_id=1, source_target_pairs={{0,1},{1,0},{2,3},{3,2},{4,5},{5,4},{6,7},{7,6},{8,9},{9,8},{10,11... | collective-permute-start | bytes 589832 | tf_op jit(solution)/shard_map/ppermute | solution.py:655
  14.4 12.0 %collective-permute-start.5 = (bf16[1328,128]{1,0:T(8,128)(2,1)S(1)}, bf16[1328,128]{1,0:T(8,128)(2,1)S(1)}, u32[]{:S(2)}, u32[]{:S(2)}) collective-permute-start(bf16[1328,128]{1,0:T(8,128)(2,1)S(1)} %after_frames.1.refs_1_), channel_id=1, source_target_pairs={{0,1},{1,0},{2,3},{3,2},{4,5},{5,4},{6,7},{7,6},{8,9},{9,8},{10,11... | collective-permute-start | bytes 1019912 | tf_op jit(solution)/shard_map/ppermute | solution.py:655
  18.6 5.7 %collective-permute-start.2 = (bf16[768,128]{1,0:T(8,128)(2,1)S(1)}, bf16[768,128]{1,0:T(8,128)(2,1)S(1)}, u32[]{:S(2)}, u32[]{:S(2)}) collective-permute-start(bf16[768,128]{1,0:T(8,128)(2,1)S(1)} %collective-permute-done.1.refs_4_), channel_id=1, source_target_pairs={{0,4},{2,6},{4,0},{6,2},{8,12},{10,14},{12,8},{14,10},{16,20},{18,... | collective-permute-start | bytes 589832 | tf_op jit(solution)/shard_map/ppermute | solution.py:655
  24.3 9.2 %collective-permute-start.9 = (bf16[1536,128]{1,0:T(8,128)(2,1)S(1)}, bf16[1536,128]{1,0:T(8,128)(2,1)S(1)}, u32[]{:S(2)}, u32[]{:S(2)}) collective-permute-start(bf16[1536,128]{1,0:T(8,128)(2,1)S(1)} %after_one.1), channel_id=1, source_target_pairs={{0,1},{1,0},{2,3},{3,2},{4,5},{5,4},{6,7},{7,6},{8,9},{9,8},{10,11... | collective-permute-start | bytes 1179656 | tf_op jit(solution)/shard_map/ppermute | solution.py:655
  26.4 7.8 %collective-permute-start.6 = (bf16[1328,128]{1,0:T(8,128)(2,1)S(1)}, bf16[1328,128]{1,0:T(8,128)(2,1)S(1)}, u32[]{:S(2)}, u32[]{:S(2)}) collective-permute-start(bf16[1328,128]{1,0:T(8,128)(2,1)S(1)} %collective-permute-done.5.refs_7_.refs_4_), channel_id=1, source_target_pairs={{0,4},{2,6},{4,0},{6,2},{8,12},{10,14},{12,8},{14,10},{16,20},{18,... | collective-permute-start | bytes 1019912 | tf_op jit(solution)/shard_map/ppermute | solution.py:655
  34.3 20.2 %collective-permute-start.13 = (bf16[624,768]{1,0:T(8,128)(2,1)S(1)}, bf16[624,768]{1,0:T(8,128)(2,1)S(1)}, u32[]{:S(2)}, u32[]{:S(2)}) collective-permute-start(bf16[624,768]{1,0:T(8,128)(2,1)S(1)} %after_two.1), channel_id=1, source_target_pairs={{0,1},{1,0},{2,3},{3,2},{4,5},{5,4},{6,7},{7,6},{8,9},{9,8},{10,11... | collective-permute-start | bytes 2875400 | tf_op jit(solution)/shard_map/ppermute | solution.py:655
  35.7 8.0 %collective-permute-start.10 = (bf16[1536,128]{1,0:T(8,128)(2,1)S(1)}, bf16[1536,128]{1,0:T(8,128)(2,1)S(1)}, u32[]{:S(2)}, u32[]{:S(2)}) collective-permute-start(bf16[1536,128]{1,0:T(8,128)(2,1)S(1)} %collective-permute-done.9.refs_11_.refs_1_.refs_8_), channel_id=1, source_target_pairs={{0,4},{2,6},{4,0},{6,2},{8,12},{10,14},{12,8},{14,10},{16,20},{18,... | collective-permute-start | bytes 1179656 | tf_op jit(solution)/shard_map/ppermute | solution.py:655
  37.2 1.4 collective-permute-start.3
  37.2 1.7 %collective-permute-start.4 = (bf16[768,128]{1,0:T(8,128)(2,1)S(1)}, bf16[768,128]{1,0:T(8,128)(2,1)S(1)}, u32[]{:S(2)}, u32[]{:S(2)}) collective-permute-start(bf16[768,128]{1,0:T(8,128)(2,1)S(1)} %collective-permute-done.2.refs_5_.refs_2_), channel_id=1, source_target_pairs={{0,2},{2,0},{4,6},{6,4},{8,10},{10,8},{12,14},{14,12},{16,18},{18,... | collective-permute-start | bytes 589832 | tf_op jit(solution)/shard_map/ppermute | solution.py:655
  43.3 2.8 %collective-permute-start.11 = (bf16[1536,128]{1,0:T(8,128)(2,1)S(1)}, bf16[1536,128]{1,0:T(8,128)(2,1)S(1)}, u32[]{:S(2)}, u32[]{:S(2)}) collective-permute-start(bf16[1536,128]{1,0:T(8,128)(2,1)S(1)} %collective-permute-done.9.refs_11_.refs_1_.refs_8_), channel_id=1, source_target_pairs={{0,2},{2,0},{4,6},{6,4},{8,10},{10,8},{12,14},{14,12},{16,18},{18,... | collective-permute-start | bytes 1179656 | tf_op jit(solution)/shard_map/ppermute | solution.py:655
  43.8 2.8 %collective-permute-start.12 = (bf16[1536,128]{1,0:T(8,128)(2,1)S(1)}, bf16[1536,128]{1,0:T(8,128)(2,1)S(1)}, u32[]{:S(2)}, u32[]{:S(2)}) collective-permute-start(bf16[1536,128]{1,0:T(8,128)(2,1)S(1)} %after_attend.1.refs_12_.refs_9_), channel_id=1, source_target_pairs={{0,2},{2,0},{4,6},{6,4},{8,10},{10,8},{12,14},{14,12},{16,18},{18,... | collective-permute-start | bytes 1179656 | tf_op jit(solution)/shard_map/ppermute | solution.py:655
  44.0 2.2 %collective-permute-start.7 = (bf16[1328,128]{1,0:T(8,128)(2,1)S(1)}, bf16[1328,128]{1,0:T(8,128)(2,1)S(1)}, u32[]{:S(2)}, u32[]{:S(2)}) collective-permute-start(bf16[1328,128]{1,0:T(8,128)(2,1)S(1)} %collective-permute-done.5.refs_7_.refs_4_), channel_id=1, source_target_pairs={{0,2},{2,0},{4,6},{6,4},{8,10},{10,8},{12,14},{14,12},{16,18},{18,... | collective-permute-start | bytes 1019912 | tf_op jit(solution)/shard_map/ppermute | solution.py:655
  44.4 2.2 %collective-permute-start.8 = (bf16[1328,128]{1,0:T(8,128)(2,1)S(1)}, bf16[1328,128]{1,0:T(8,128)(2,1)S(1)}, u32[]{:S(2)}, u32[]{:S(2)}) collective-permute-start(bf16[1328,128]{1,0:T(8,128)(2,1)S(1)} %collective-permute-done.6.refs_8_.refs_2_.refs_5_), channel_id=1, source_target_pairs={{0,2},{2,0},{4,6},{6,4},{8,10},{10,8},{12,14},{14,12},{16,18},{18,... | collective-permute-start | bytes 1019912 | tf_op jit(solution)/shard_map/ppermute | solution.py:655
  65.7 3.9 %collective-permute-start.14 = (bf16[4,1792,128]{2,1,0:T(8,128)(2,1)S(1)}, bf16[4,1792,128]{2,1,0:T(8,128)(2,1)S(1)}, u32[]{:S(2)}, u32[]{:S(2)}) collective-permute-start(bf16[4,1792,128]{2,1,0:T(8,128)(2,1)S(1)} %get-tuple-element.138.refs_2_), channel_id=1, source_target_pairs={{0,2},{2,0},{4,6},{6,4},{8,10},{10,8},{12,14},{14,12},{16,18},{18,... | collective-permute-start | bytes 5505032 | tf_op jit(solution)/shard_map/ppermute | solution.py:655
  68.1 9.8 %collective-permute-start.15 = (bf16[4,1024,128]{2,1,0:T(8,128)(2,1)S(1)}, bf16[4,1024,128]{2,1,0:T(8,128)(2,1)S(1)}, u32[]{:S(2)}, u32[]{:S(2)}) collective-permute-start(bf16[4,1024,128]{2,1,0:T(8,128)(2,1)S(1)} %get-tuple-element.140.refs_2_), channel_id=1, source_target_pairs={{0,2},{2,0},{4,6},{6,4},{8,10},{10,8},{12,14},{14,12},{16,18},{18,... | collective-permute-start | bytes 3145736 | tf_op jit(solution)/shard_map/ppermute | solution.py:655
  70.4 22.5 %collective-permute-start.17 = (bf16[1792,128]{1,0:T(8,128)(2,1)S(1)}, bf16[1792,128]{1,0:T(8,128)(2,1)S(1)}, u32[]{:S(2)}, u32[]{:S(2)}) collective-permute-start(bf16[1792,128]{1,0:T(8,128)(2,1)S(1)} %get-tuple-element.151), channel_id=1, source_target_pairs={{0,1},{1,0},{2,3},{3,2},{4,5},{5,4},{6,7},{7,6},{8,9},{9,8},{10,11... | collective-permute-start | bytes 1376264 | tf_op jit(solution)/shard_map/ppermute | solution.py:655
  72.2 22.4 %collective-permute-start.18 = (bf16[1792,128]{1,0:T(8,128)(2,1)S(1)}, bf16[1792,128]{1,0:T(8,128)(2,1)S(1)}, u32[]{:S(2)}, u32[]{:S(2)}) collective-permute-start(bf16[1792,128]{1,0:T(8,128)(2,1)S(1)} %get-tuple-element.152), channel_id=1, source_target_pairs={{0,5},{1,4},{2,7},{3,6},{4,1},{5,0},{6,3},{7,2},{8,13},{9,12},{10,... | collective-permute-start | bytes 1376264 | tf_op jit(solution)/shard_map/ppermute | solution.py:655
  73.4 22.4 %collective-permute-start.16 = (bf16[1792,128]{1,0:T(8,128)(2,1)S(1)}, bf16[1792,128]{1,0:T(8,128)(2,1)S(1)}, u32[]{:S(2)}, u32[]{:S(2)}) collective-permute-start(bf16[1792,128]{1,0:T(8,128)(2,1)S(1)} %get-tuple-element.141.refs_4_), channel_id=1, source_target_pairs={{0,4},{2,6},{4,0},{6,2},{8,12},{10,14},{12,8},{14,10},{16,20},{18,... | collective-permute-start | bytes 1376264 | tf_op jit(solution)/shard_map/ppermute | solution.py:655
  78.7 28.9 %collective-permute-start.22 = (bf16[1024,128]{1,0:T(8,128)(2,1)S(1)}, bf16[1024,128]{1,0:T(8,128)(2,1)S(1)}, u32[]{:S(2)}, u32[]{:S(2)}) collective-permute-start(bf16[1024,128]{1,0:T(8,128)(2,1)S(1)} %get-tuple-element.144.refs_4_), channel_id=1, source_target_pairs={{0,4},{2,6},{4,0},{6,2},{8,12},{10,14},{12,8},{14,10},{16,20},{18,... | collective-permute-start | bytes 786440 | tf_op jit(solution)/shard_map/ppermute | solution.py:655
  86.0 12.4 %collective-permute-start.20 = (bf16[4,768,128]{2,1,0:T(8,128)(2,1)S(1)}, bf16[4,768,128]{2,1,0:T(8,128)(2,1)S(1)}, u32[]{:S(2)}, u32[]{:S(2)}) collective-permute-start(bf16[4,768,128]{2,1,0:T(8,128)(2,1)S(1)} %get-tuple-element.148.refs_8_), channel_id=1, source_target_pairs={{0,2},{2,0},{4,6},{6,4},{8,10},{10,8},{12,14},{14,12},{16,18},{18,... | collective-permute-start | bytes 2359304 | tf_op jit(solution)/shard_map/ppermute | solution.py:655
  92.9 13.5 %collective-permute-start.23 = (bf16[1024,128]{1,0:T(8,128)(2,1)S(1)}, bf16[1024,128]{1,0:T(8,128)(2,1)S(1)}, u32[]{:S(2)}, u32[]{:S(2)}) collective-permute-start(bf16[1024,128]{1,0:T(8,128)(2,1)S(1)} %get-tuple-element.163), channel_id=1, source_target_pairs={{0,1},{1,0},{2,3},{3,2},{4,5},{5,4},{6,7},{7,6},{8,9},{9,8},{10,11... | collective-permute-start | bytes 786440 | tf_op jit(solution)/shard_map/ppermute | solution.py:655
  94.6 13.0 %collective-permute-start.24 = (bf16[1024,128]{1,0:T(8,128)(2,1)S(1)}, bf16[1024,128]{1,0:T(8,128)(2,1)S(1)}, u32[]{:S(2)}, u32[]{:S(2)}) collective-permute-start(bf16[1024,128]{1,0:T(8,128)(2,1)S(1)} %get-tuple-element.164), channel_id=1, source_target_pairs={{0,5},{1,4},{2,7},{3,6},{4,1},{5,0},{6,3},{7,2},{8,13},{9,12},{10,... | collective-permute-start | bytes 786440 | tf_op jit(solution)/shard_map/ppermute | solution.py:655
  96.8 6.3 %collective-permute-start.19 = (bf16[896,128]{1,0:T(8,128)(2,1)S(1)}, bf16[896,128]{1,0:T(8,128)(2,1)S(1)}, u32[]{:S(2)}, u32[]{:S(2)}) collective-permute-start(bf16[896,128]{1,0:T(8,128)(2,1)S(1)} %get-tuple-element.155), channel_id=1, source_target_pairs={{0,8},{2,10},{4,12},{6,14},{8,0},{10,2},{12,4},{14,6},{16,24},{18,... | collective-permute-start | bytes 688136 | tf_op jit(solution)/shard_map/ppermute | solution.py:655
  99.2 20.7 %collective-permute-start.26 = (bf16[832,128]{1,0:T(8,128)(2,1)S(1)}, bf16[832,128]{1,0:T(8,128)(2,1)S(1)}, u32[]{:S(2)}, u32[]{:S(2)}) collective-permute-start(bf16[832,128]{1,0:T(8,128)(2,1)S(1)} %get-tuple-element.161.refs_2_), channel_id=1, source_target_pairs={{0,4},{2,6},{4,0},{6,2},{8,12},{10,14},{12,8},{14,10},{16,20},{18,... | collective-permute-start | bytes 638984 | tf_op jit(solution)/shard_map/ppermute | solution.py:655
  103.7 11.3 %collective-permute-start.21 = (bf16[896,128]{1,0:T(8,128)(2,1)S(1)}, bf16[896,128]{1,0:T(8,128)(2,1)S(1)}, u32[]{:S(2)}, u32[]{:S(2)}) collective-permute-start(bf16[896,128]{1,0:T(8,128)(2,1)S(1)} %up_2.1.refs_4_.refs_0_), channel_id=1, source_target_pairs={{0,16},{2,18},{4,20},{6,22},{8,24},{10,26},{12,28},{14,30},{16,0},... | collective-permute-start | bytes 688136 | tf_op jit(solution)/shard_map/ppermute | solution.py:655
  108.4 13.2 %collective-permute-start.31 = (bf16[512,128]{1,0:T(8,128)(2,1)S(1)}, bf16[512,128]{1,0:T(8,128)(2,1)S(1)}, u32[]{:S(2)}, u32[]{:S(2)}) collective-permute-start(bf16[512,128]{1,0:T(8,128)(2,1)S(1)} %get-tuple-element.172), channel_id=1, source_target_pairs={{0,8},{2,10},{4,12},{6,14},{8,0},{10,2},{12,4},{14,6},{16,24},{18,... | collective-permute-start | bytes 393224 | tf_op jit(solution)/shard_map/ppermute | solution.py:655
  110.0 9.4 %collective-permute-start.27 = (bf16[832,128]{1,0:T(8,128)(2,1)S(1)}, bf16[832,128]{1,0:T(8,128)(2,1)S(1)}, u32[]{:S(2)}, u32[]{:S(2)}) collective-permute-start(bf16[832,128]{1,0:T(8,128)(2,1)S(1)} %get-tuple-element.170), channel_id=1, source_target_pairs={{0,1},{1,0},{2,3},{3,2},{4,5},{5,4},{6,7},{7,6},{8,9},{9,8},{10,11... | collective-permute-start | bytes 638984 | tf_op jit(solution)/shard_map/ppermute | solution.py:655
  110.5 9.4 %collective-permute-start.28 = (bf16[832,128]{1,0:T(8,128)(2,1)S(1)}, bf16[832,128]{1,0:T(8,128)(2,1)S(1)}, u32[]{:S(2)}, u32[]{:S(2)}) collective-permute-start(bf16[832,128]{1,0:T(8,128)(2,1)S(1)} %get-tuple-element.171), channel_id=1, source_target_pairs={{0,5},{1,4},{2,7},{3,6},{4,1},{5,0},{6,3},{7,2},{8,13},{9,12},{10,... | collective-permute-start | bytes 638984 | tf_op jit(solution)/shard_map/ppermute | solution.py:655
  115.7 8.7 %collective-permute-start.30 = (bf16[896,128]{1,0:T(8,128)(2,1)S(1)}, bf16[896,128]{1,0:T(8,128)(2,1)S(1)}, u32[]{:S(2)}, u32[]{:S(2)}) collective-permute-start(bf16[896,128]{1,0:T(8,128)(2,1)S(1)} %up_3.1.refs_7_.refs_0_), channel_id=1, source_target_pairs={{0,8},{2,10},{4,12},{6,14},{8,0},{10,2},{12,4},{14,6},{16,24},{18,... | collective-permute-start | bytes 688136 | tf_op jit(solution)/shard_map/ppermute | solution.py:655
  119.4 30.4 %collective-permute-start.25 = (bf16[624,1024]{1,0:T(8,128)(2,1)S(1)}, bf16[624,1024]{1,0:T(8,128)(2,1)S(1)}, u32[]{:S(2)}, u32[]{:S(2)}) collective-permute-start(bf16[624,1024]{1,0:T(8,128)(2,1)S(1)} %get-tuple-element.166.refs_4_), channel_id=1, source_target_pairs={{0,1},{1,0},{2,3},{3,2},{4,5},{5,4},{6,7},{7,6},{8,9},{9,8},{10,11... | collective-permute-start | bytes 3833864 | tf_op jit(solution)/shard_map/ppermute | solution.py:655
  120.6 8.8 %collective-permute-start.29 = (bf16[832,128]{1,0:T(8,128)(2,1)S(1)}, bf16[832,128]{1,0:T(8,128)(2,1)S(1)}, u32[]{:S(2)}, u32[]{:S(2)}) collective-permute-start(bf16[832,128]{1,0:T(8,128)(2,1)S(1)} %early_1.1.refs_2_.refs_0_), channel_id=1, source_target_pairs={{0,8},{2,10},{4,12},{6,14},{8,0},{10,2},{12,4},{14,6},{16,24},{18,... | collective-permute-start | bytes 638984 | tf_op jit(solution)/shard_map/ppermute | solution.py:655
  122.2 9.5 %collective-permute-start.33 = (bf16[512,128]{1,0:T(8,128)(2,1)S(1)}, bf16[512,128]{1,0:T(8,128)(2,1)S(1)}, u32[]{:S(2)}, u32[]{:S(2)}) collective-permute-start(bf16[512,128]{1,0:T(8,128)(2,1)S(1)} %late_2.1.refs_2_.refs_0_), channel_id=1, source_target_pairs={{0,16},{2,18},{4,20},{6,22},{8,24},{10,26},{12,28},{14,30},{16,0},... | collective-permute-start | bytes 393224 | tf_op jit(solution)/shard_map/ppermute | solution.py:655
  125.0 18.1 %collective-permute-start.36 = (bf16[1792,128]{1,0:T(8,128)(2,1)S(1)}, bf16[1792,128]{1,0:T(8,128)(2,1)S(1)}, u32[]{:S(2)}, u32[]{:S(2)}) collective-permute-start(bf16[1792,128]{1,0:T(8,128)(2,1)S(1)} %up_4.1.refs_2_.refs_0_), channel_id=1, source_target_pairs={{0,2},{2,0},{4,6},{6,4},{8,10},{10,8},{12,14},{14,12},{16,18},{18,... | collective-permute-start | bytes 1376264 | tf_op jit(solution)/shard_map/ppermute | solution.py:655
  125.1 17.3 %collective-permute-start.35 = (bf16[1792,128]{1,0:T(8,128)(2,1)S(1)}, bf16[1792,128]{1,0:T(8,128)(2,1)S(1)}, u32[]{:S(2)}, u32[]{:S(2)}) collective-permute-start(bf16[1792,128]{1,0:T(8,128)(2,1)S(1)} %up_4.1.refs_2_.refs_0_), channel_id=1, source_target_pairs={{0,4},{2,6},{4,0},{6,2},{8,12},{10,14},{12,8},{14,10},{16,20},{18,... | collective-permute-start | bytes 1376264 | tf_op jit(solution)/shard_map/ppermute | solution.py:655
  130.0 10.9 %collective-permute-start.32 = (bf16[832,128]{1,0:T(8,128)(2,1)S(1)}, bf16[832,128]{1,0:T(8,128)(2,1)S(1)}, u32[]{:S(2)}, u32[]{:S(2)}) collective-permute-start(bf16[832,128]{1,0:T(8,128)(2,1)S(1)} %early_2.1.refs_2_.refs_0_), channel_id=1, source_target_pairs={{0,16},{2,18},{4,20},{6,22},{8,24},{10,26},{12,28},{14,30},{16,0},... | collective-permute-start | bytes 638984 | tf_op jit(solution)/shard_map/ppermute | solution.py:655
  132.2 9.4 %collective-permute-start.38 = (bf16[512,128]{1,0:T(8,128)(2,1)S(1)}, bf16[512,128]{1,0:T(8,128)(2,1)S(1)}, u32[]{:S(2)}, u32[]{:S(2)}) collective-permute-start(bf16[512,128]{1,0:T(8,128)(2,1)S(1)} %late_3.1.refs_2_.refs_0_), channel_id=1, source_target_pairs={{0,8},{2,10},{4,12},{6,14},{8,0},{10,2},{12,4},{14,6},{16,24},{18,... | collective-permute-start | bytes 393224 | tf_op jit(solution)/shard_map/ppermute | solution.py:655
  141.5 13.5 %collective-permute-start.39 = (bf16[832,128]{1,0:T(8,128)(2,1)S(1)}, bf16[832,128]{1,0:T(8,128)(2,1)S(1)}, u32[]{:S(2)}, u32[]{:S(2)}) collective-permute-start(bf16[832,128]{1,0:T(8,128)(2,1)S(1)} %early_3.1.refs_2_.refs_0_), channel_id=1, source_target_pairs={{0,2},{2,0},{4,6},{6,4},{8,10},{10,8},{12,14},{14,12},{16,18},{18,... | collective-permute-start | bytes 638984 | tf_op jit(solution)/shard_map/ppermute | solution.py:655
  141.6 8.1 %collective-permute-start.34 = (bf16[832,128]{1,0:T(8,128)(2,1)S(1)}, bf16[832,128]{1,0:T(8,128)(2,1)S(1)}, u32[]{:S(2)}, u32[]{:S(2)}) collective-permute-start(bf16[832,128]{1,0:T(8,128)(2,1)S(1)} %early_3.1.refs_2_.refs_0_), channel_id=1, source_target_pairs={{0,4},{2,6},{4,0},{6,2},{8,12},{10,14},{12,8},{14,10},{16,20},{18,... | collective-permute-start | bytes 638984 | tf_op jit(solution)/shard_map/ppermute | solution.py:655
  142.4 1.8 %collective-permute-start.37 = (bf16[1792,128]{1,0:T(8,128)(2,1)S(1)}, bf16[1792,128]{1,0:T(8,128)(2,1)S(1)}, u32[]{:S(2)}, u32[]{:S(2)}) collective-permute-start(bf16[1792,128]{1,0:T(8,128)(2,1)S(1)} %collective-permute-done.35.refs_1_), channel_id=1, source_target_pairs={{0,2},{2,0},{4,6},{6,4},{8,10},{10,8},{12,14},{14,12},{16,18},{18,... | collective-permute-start | bytes 1376264 | tf_op jit(solution)/shard_map/ppermute | solution.py:655
  143.1 13.8 %collective-permute-start.42 = (bf16[1024,128]{1,0:T(8,128)(2,1)S(1)}, bf16[1024,128]{1,0:T(8,128)(2,1)S(1)}, u32[]{:S(2)}, u32[]{:S(2)}) collective-permute-start(bf16[1024,128]{1,0:T(8,128)(2,1)S(1)} %late_4.1.refs_4_.refs_0_), channel_id=1, source_target_pairs={{0,2},{2,0},{4,6},{6,4},{8,10},{10,8},{12,14},{14,12},{16,18},{18,... | collective-permute-start | bytes 786440 | tf_op jit(solution)/shard_map/ppermute | solution.py:655
  144.2 10.7 %collective-permute-start.41 = (bf16[1024,128]{1,0:T(8,128)(2,1)S(1)}, bf16[1024,128]{1,0:T(8,128)(2,1)S(1)}, u32[]{:S(2)}, u32[]{:S(2)}) collective-permute-start(bf16[1024,128]{1,0:T(8,128)(2,1)S(1)} %late_4.1.refs_4_.refs_0_), channel_id=1, source_target_pairs={{0,4},{2,6},{4,0},{6,2},{8,12},{10,14},{12,8},{14,10},{16,20},{18,... | collective-permute-start | bytes 786440 | tf_op jit(solution)/shard_map/ppermute | solution.py:655
  149.8 5.3 %collective-permute-start.40 = (bf16[832,128]{1,0:T(8,128)(2,1)S(1)}, bf16[832,128]{1,0:T(8,128)(2,1)S(1)}, u32[]{:S(2)}, u32[]{:S(2)}) collective-permute-start(bf16[832,128]{1,0:T(8,128)(2,1)S(1)} %after_up.1.refs_6_.refs_1_), channel_id=1, source_target_pairs={{0,2},{2,0},{4,6},{6,4},{8,10},{10,8},{12,14},{14,12},{16,18},{18,... | collective-permute-start | bytes 638984 | tf_op jit(solution)/shard_map/ppermute | solution.py:655
  154.9 2.0 %collective-permute-start.43 = (bf16[1024,128]{1,0:T(8,128)(2,1)S(1)}, bf16[1024,128]{1,0:T(8,128)(2,1)S(1)}, u32[]{:S(2)}, u32[]{:S(2)}) collective-permute-start(bf16[1024,128]{1,0:T(8,128)(2,1)S(1)} %after_rows.1.refs_1_), channel_id=1, source_target_pairs={{0,2},{2,0},{4,6},{6,4},{8,10},{10,8},{12,14},{14,12},{16,18},{18,... | collective-permute-start | bytes 786440 | tf_op jit(solution)/shard_map/ppermute | solution.py:655

commit v3 on v2

--- a/solution.py
+++ b/solution.py
@@ -363,19 +363,22 @@
     hidden_grad_ref, grad_middle_ref, middle_grad_ref, vec_ref, bias_ref,
 ):
     half = up.shape[1]
-    back = None
-    for h, (w_up, w_down) in enumerate(((up, down), (up_other, down_other))):
-        for i in range(half // 256):
-            at = slice(i * 256, i * 256 + 256)
-            to = slice(h * half + i * 256, h * half + i * 256 + 256)
-            sums = [None]
-            for rows in blocks_in(ending_grad):
-                low = (mm_bt(ending_grad[rows, :], w_down[at, :]) * slope[rows, to]).astype(BF)
-                hidden_grad_ref[rows, to] = low
-                sums = add_up(sums, [col_sum(low.astype(F32))])
-            bias_ref[:, to] = sums[0]
-        value = mm_bt(hidden_grad_ref[:, h * half : h * half + half], w_up[...])
-        back = value if back is None else back + value
+    back, steps = None, half // 256
+    tasks = [(h, i) for h in range(2) for i in range(steps)]
+
+    def product(h, i):
+        return mm_bt(ending_grad[...], (down, down_other)[h][i * 256 : i * 256 + 256, :])
+
+    ahead = product(*tasks[0])
+    for k, (h, i) in enumerate(tasks):
+        value, ahead = ahead, product(*tasks[k + 1]) if k + 1 < len(tasks) else None
+        to = slice(h * half + i * 256, h * half + i * 256 + 256)
+        low = (value * slope[:, to]).astype(BF)
+        hidden_grad_ref[:, to] = low
+        bias_ref[:, to] = col_sum(low.astype(F32))
+        if i + 1 == steps:
+            part = mm_bt(hidden_grad_ref[:, h * half : h * half + half], (up, up_other)[h][...])
+            back = part if back is None else back + part
     unit, factor = norm_of(middle[...])
     gain = vector(small, SECOND_GAIN, unit.shape[1])
     total = grad_ending[...] + norm_back(back, unit, factor, gain)
@@ -458,8 +461,10 @@
         prior_ref[:, at] = piece[2 * n + m :, :].astype(F32)
 
 
-def early_place_kernel(s, mine, near, far, farther, qkv_ref, *vecs):
+def last_place_kernel(s, mine, near, far, farther, l0, l1, l2, l3, qkv_ref, down_ref, *vecs):
     vecs, sums = vecs[:-1], vecs[-1]
+    late_place_kernel(s, l0, l1, l2, l3, down_ref)
+    down_ref.send()
     sums[...] = mine[6 * 128 :, :].astype(F32) + far[6 * 128 :, :].astype(F32)
     for j, piece in enumerate((mine, near, far, farther)):
         at = pl.ds(pl.multiple_of((s[1] ^ j) * 128, 128), 128)
@@ -925,27 +930,29 @@
         cost=2.0,
     )
     done = back_send
-    done = early = move.total(scalars, [early_rest, *move.sides(early_low)], "early_1", (done,))
+    early, early_half = move.halves(scalars, [early_rest, *move.sides(early_low)], "early_1", (done,))
+    done = early
     done = late = move.total(scalars, [late, move.along(late_half, bits[0])], "late_2", (done,))
     done = up = move.join(scalars, up, move.along(up, bits[0]), "up_4", (done,))
-    for bit in bits[:-1]:
-        done = early = move.total(scalars, [early, move.along(early, bit)], "early_2", (done,))
+    done = early = move.total(scalars, [early, move.along(early_half, bits[0])], "early_2", (done,))
     for bit in bits[1:]:
         done = late = move.total(scalars, [late, move.along(late, bit)], "late_3", (done,))
-    done = early = move.total(scalars, [early, move.along(early, bits[-1])], "early_3", (done,))
-    late = move.join(scalars, late, move.along(late, bits[0]), "late_4", (done,))
+    for bit in bits[1:]:
+        done = early = move.total(scalars, [early, move.along(early, bit)], "early_3", (done,))
+    up_pieces = list(move.gather(up))
+    late = move.join(scalars, late, move.along(late, bits[0]), "late_4", (done, up_pieces[2]))
+    early = move.join(scalars, early, move.along(early, bits[0]), "early_4", (late,))
     up_grad, out_grad, prior_grad, up_done = call(
         up_place_kernel,
         scalars,
-        list(move.gather(up)),
+        up_pieces,
         [((width, hidden_width), F32, False), ((half, width), F32, False), ((width, n_logits), F32, False)]
         + [((8, 128), F32, True)],
         name="up_place",
-        after=(late,),
+        after=(early,),
         cost=FOLD,
     )
     back_got = move.over(back_send)
-    (early_near,) = gate([move.side(early)], [up_done], "after_up")
     block_out, logits, grad_frames, rows_done = call(
         functools.partial(
             rows_kernel,
@@ -957,30 +964,22 @@
         + [((8, 128), F32, True)],
         [pltpu.VMEM((rows, n), F32) for n in (half, n_logits, half)],
         name="rows_back",
-        after=(early_near,),
+        after=(up_done,),
         cost=FOLD,
     )
+    (early_near,) = gate([move.side(early)], [up_done], "after_up")
     (late_near,) = gate([move.side(late)], [rows_done], "after_rows")
     early_pieces = [early, early_near, move.core(early), move.core(early_near)]
     late_pieces = [late, late_near, move.core(late), move.core(late_near)]
-    qkv_grad, *named = call(
-        early_place_kernel,
-        scalars,
-        early_pieces,
-        [((3, width, half), F32, False)]
+    qkv_grad, down_grad, *named = call(
+        last_place_kernel,
+        scalars,
+        early_pieces + late_pieces,
+        [((3, width, half), F32, False), ((hidden_width, width), F32, False)]
         + [((1, n), F32, False) for n in [width] * 8 + [hidden_width, n_logits]],
         [pltpu.VMEM((spare, 128), F32)],
-        name="early_place",
+        name="last_place",
         after=(rows_done,),
-        cost=FOLD,
-    )
-    (down_grad,) = call(
-        late_place_kernel,
-        scalars,
-        late_pieces,
-        [((hidden_width, width), F32, False)],
-        name="late_place",
-        after=(Far(qkv_grad),),
         cost=FOLD,
     )
     named = [v.reshape(-1) for v in named]

time: 159 us -> 156 us (0.981)
  Pallas kernels: 63 us -> 61.3 us
  waiting for transfers between devices: 47.5 us -> 45.9 us
    pallas_call x31, Pallas kernels: 62.8 us -> 61.1 us  [call(): pl.pallas_call(run, in_specs=[pl.BlockSpec(memory_space=pltpu.SMEM)] + [f...]
    ppermute x44 -> x45, waiting for transfers between devices: 47.5 us -> 45.9 us  [swap(): return lax.ppermute(value, axes, [(i, i ^ mask) for i in range(count)])]
    ppermute x44 -> x45, starting transfers between devices: 47.4 us -> 47.1 us  [swap(): return lax.ppermute(value, axes, [(i, i ^ mask) for i in range(count)])]
  transfers between devices with their start and end apart: 44 -> 45, of which waited for: 22 -> 24; matrix products, arithmetic and copies ran while one was open for 0% -> 0% of each run, Pallas kernels for 30% -> 29%
where the time goes in v3:
time: 156 us; the launch traced here: 155 us
  Pallas kernels  61.3 us (39%)
  starting transfers between devices  47.1 us (30%)
  waiting for transfers between devices  45.9 us (29%)
    pallas_call x31, Pallas kernels, call(): pl.pallas_call(run, in_specs=[pl.BlockSpec(memory_space=pltpu.SMEM)] + [f...  61.1 us
    ppermute x45, starting transfers between devices, swap(): return lax.ppermute(value, axes, [(i, i ^ mask) for i in range(count)])  47.1 us
    ppermute x45, waiting for transfers between devices, swap(): return lax.ppermute(value, axes, [(i, i ^ mask) for i in range(count)])  45.9 us
  transfers between devices with their start and end apart: 45, of which 24 were waited for; matrix products, arithmetic and copies ran while one was open for 0% of the time, Pallas kernels for 29%

profile of v3, /device:TPU:0, one launch (start us, length us, event | category | flops | bytes accessed | tf_op | source)
XLA Modules:
  0.0 155.5 jit_solution(16694619190666898109)
XLA Ops:
  0.7 2.2 %first_parts.1 = (bf16[768,128]{1,0:T(8,128)(2,1)S(1)}, bf16[624,256]{1,0:T(8,128)(2,1)S(1)}, bf16[1328,128]{1,0:T(8,128)(2,1)S(1)}, bf16[1536,128]{1,0:T(8,128)...) custom-call(s32[3]{0:T(128)S(1)} %pad_add_fusion.s, ...), custom_call_target="tpu_custom_call" | custom-call | flops 200000000 | tf_op jit(solution)/shard_map/first_parts/pallas_call | solution.py:636
  3.0 3.0 %collective-permute-start = (bf16[624,256]{1,0:T(8,128)(2,1)S(1)}, bf16[624,256]{1,0:T(8,128)(2,1)S(1)}, u32[]{:S(2)}, u32[]{:S(2)}) collective-permute-start(bf16[624,256]{1,0:T(8,128)(2,1)S(1)} %get-tuple-element.109.refs_7_), channel_id=1, source_target_pairs={{0,1},{1,0},{2,3},{3,2},{4,5},{5,4},{6,7},{7,6},{8,9},{9,8},{10,11... | collective-permute-start | bytes 958472 | tf_op jit(solution)/shard_map/ppermute | solution.py:660
  6.1 3.1 %cotangents.1 = (bf16[624,768]{1,0:T(8,128)(2,1)S(1)}, bf16[624,512]{1,0:T(8,128)(2,1)S(1)}, bf16[624,256]{1,0:T(8,128)(2,1)S(1)}, bf16[3,512,256]{2,1,0:T(8,128...) custom-call(s32[3]{0:T(128)S(1)} %pad_add_fusion.s, ...), custom_call_target="tpu_custom_call" | custom-call | flops 230000000 | tf_op jit(solution)/shard_map/cotangents/pallas_call | solution.py:636
  9.2 5.1 %collective-permute-done.refs_1_.refs_4_ = bf16[624,256]{1,0:T(8,128)(2,1)S(1)} collective-permute-done((bf16[624,256]{1,0:T(8,128)(2,1)S(1)}, bf16[624,256]{1,0:T(8,128)(2,1)S(1)}, u32[]{:S(2)}, u32[]{:S(2)}) %collective-permute-start) | collective-permute-done | bytes 319520 | tf_op jit(solution)/shard_map/ppermute | solution.py:660
  14.4 2.1 %collective-permute-start.5 = (bf16[1328,128]{1,0:T(8,128)(2,1)S(1)}, bf16[1328,128]{1,0:T(8,128)(2,1)S(1)}, u32[]{:S(2)}, u32[]{:S(2)}) collective-permute-start(bf16[1328,128]{1,0:T(8,128)(2,1)S(1)} %after_frames.1.refs_1_), channel_id=1, source_target_pairs={{0,1},{1,0},{2,3},{3,2},{4,5},{5,4},{6,7},{7,6},{8,9},{9,8},{10,11... | collective-permute-start | bytes 1019912 | tf_op jit(solution)/shard_map/ppermute | solution.py:660
  16.5 2.1 %collective-permute-done.1.refs_4_ = bf16[768,128]{1,0:T(8,128)(2,1)S(1)} collective-permute-done((bf16[768,128]{1,0:T(8,128)(2,1)S(1)}, bf16[768,128]{1,0:T(8,128)(2,1)S(1)}, u32[]{:S(2)}, u32[]{:S(2)}) %collective-permute-start.1) | collective-permute-done | bytes 196640 | tf_op jit(solution)/shard_map/ppermute | solution.py:660
  18.6 2.0 %collective-permute-start.2 = (bf16[768,128]{1,0:T(8,128)(2,1)S(1)}, bf16[768,128]{1,0:T(8,128)(2,1)S(1)}, u32[]{:S(2)}, u32[]{:S(2)}) collective-permute-start(bf16[768,128]{1,0:T(8,128)(2,1)S(1)} %collective-permute-done.1.refs_4_), channel_id=1, source_target_pairs={{0,4},{2,6},{4,0},{6,2},{8,12},{10,14},{12,8},{14,10},{16,20},{18,... | collective-permute-start | bytes 589832 | tf_op jit(solution)/shard_map/ppermute | solution.py:660
  20.6 3.6 %collective-permute-done.2.refs_5_.refs_2_ = bf16[768,128]{1,0:T(8,128)(2,1)S(1)} collective-permute-done((bf16[768,128]{1,0:T(8,128)(2,1)S(1)}, bf16[768,128]{1,0:T(8,128)(2,1)S(1)}, u32[]{:S(2)}, u32[]{:S(2)}) %collective-permute-start.2) | collective-permute-done | bytes 196640 | tf_op jit(solution)/shard_map/ppermute | solution.py:660
  24.3 2.1 %collective-permute-start.9 = (bf16[1536,128]{1,0:T(8,128)(2,1)S(1)}, bf16[1536,128]{1,0:T(8,128)(2,1)S(1)}, u32[]{:S(2)}, u32[]{:S(2)}) collective-permute-start(bf16[1536,128]{1,0:T(8,128)(2,1)S(1)} %after_one.1), channel_id=1, source_target_pairs={{0,1},{1,0},{2,3},{3,2},{4,5},{5,4},{6,7},{7,6},{8,9},{9,8},{10,11... | collective-permute-start | bytes 1179656 | tf_op jit(solution)/shard_map/ppermute | solution.py:660
  26.4 1.5 collective-permute-start.6
  27.9 5.6 %collective-permute-done.9.refs_11_.refs_1_.refs_8_ = bf16[1536,128]{1,0:T(8,128)(2,1)S(1)} collective-permute-done((bf16[1536,128]{1,0:T(8,128)(2,1)S(1)}, bf16[1536,128]{1,0:T(8,128)(2,1)S(1)}, u32[]{:S(2)}, u32[]{:S(2)}) %collective-permute-start.9) | collective-permute-done | bytes 393248 | tf_op jit(solution)/shard_map/ppermute | solution.py:660
  33.5 0.7 collective-permute-done.6.refs_8_.refs_2_.refs_5_
  34.3 1.5 collective-permute-start.13
  35.7 1.5 collective-permute-start.10
  37.7 0.9 collective-permute-done.3.refs_6_
  39.0 4.3 %attend.1 = (bf16[624,512]{1,0:T(8,128)(2,1)S(1)}, bf16[624,1536]{1,0:T(8,128)(2,1)S(1)}, bf16[624,512]{1,0:T(8,128)(2,1)S(1)}, bf16[3,512,256]{2,1,0:T(8,128)(2,1)S(1)}) custom-call(s32[3]{0:T(128)S(1)} %pad_add_fusion.s, bf16[624,256]{1,0:T(8,128)(2,1)S(1)} %get-tuple-element.108.refs_0_.refs_3_, ...), custom_call_target="tpu_custom_call" | custom-call | flops 550000000 | tf_op jit(solution)/shard_map/attend/pallas_call | solution.py:636
  44.5 1.7 %collective-permute-done.7.refs_9_.refs_6_ = bf16[1328,128]{1,0:T(8,128)(2,1)S(1)} collective-permute-done((bf16[1328,128]{1,0:T(8,128)(2,1)S(1)}, bf16[1328,128]{1,0:T(8,128)(2,1)S(1)}, u32[]{:S(2)}, u32[]{:S(2)}) %collective-permute-start.7) | collective-permute-done | bytes 340000 | tf_op jit(solution)/shard_map/ppermute | solution.py:660
  46.6 6.9 %feed.1 = (bf16[624,256]{1,0:T(8,128)(2,1)S(1)}, bf16[624,256]{1,0:T(8,128)(2,1)S(1)}, f32[624,512]{1,0:T(8,128)S(1)}, bf16[624,512]{1,0:T(8,128)(2,1)S(1)}, bf1...) custom-call(s32[3]{0:T(128)S(1)} %pad_add_fusion.s, ...), custom_call_target="tpu_custom_call" | custom-call | flops 720000000 | tf_op jit(solution)/shard_map/feed/pallas_call | solution.py:636
  53.5 0.9 collective-permute-done.13.refs_12_.refs_6_
  54.4 2.3 %prior.1 = (f32[624,512]{1,0:T(8,128)S(1)}, bf16[624,512]{1,0:T(8,128)(2,1)S(1)}, f32[3,512]{1,0:T(4,128)S(1)}, f32[1,1024]{1,0:T(1,128)S(1)}, bf16[512,512]{1,0:T(8,128)(2,1)S(1)}, /*index=5*/f32[1,512]{1,0:T(1,128)S(1)}) custom-call(s32[3]{0:T(128)S(1)} %pad_add_fusion.s, f32[624,512]{1,0:T(8,128)S(1)} %get-tuple-element.124.refs_0_, ...), custom_call_target="tpu_custom_call" | custom-call | flops 250000000 | tf_op jit(solution)/shard_map/prior/pallas_call | solution.py:636
  56.8 4.1 %feed_back.1 = (bf16[624,2048]{1,0:T(8,128)(2,1)S(1)}, f32[624,512]{1,0:T(8,128)S(1)}, bf16[624,512]{1,0:T(8,128)(2,1)S(1)}, f32[3,512]{1,0:T(4,128)S(1)}, f32[1,2048]{1,0:T(1,128)S(1)}) custom-call(s32[3]{0:T(128)S(1)} %pad_add_fusion.s, bf16[624,512]{1,0:T(8,128)(2,1)S(1)} %get-tuple-element.130.refs_0_.refs_1_, ...), custom_call_target="tpu_custom_call" | custom-call | flops 650000000 | tf_op jit(solution)/shard_map/feed_back/pallas_call | solution.py:636
  60.9 3.9 %up_grads.1 = (f32[4,1792,128]{2,1,0:T(8,128)S(1)}, bf16[4,1792,128]{2,1,0:T(8,128)(2,1)S(1)}) custom-call(s32[3]{0:T(128)S(1)} %pad_add_fusion.s, bf16[624,512]{1,0:T(8,128)(2,1)S(1)} %get-tuple-element.138.refs_0_, bf16[624,2048]{1,0:T(8,128)(2,1)S(1)} %get-tuple-element.139.refs_1_, bf16[624,512]{1,0:T(8,128)(2,1)S(1)} %get-tuple-element.114.refs_1_.refs_2_, ...), custom_call_target="tpu_custom_call" | custom-call | flops 300000000 | tf_op jit(solution)/shard_map/up_grads/pallas_call | solution.py:636
  64.9 2.4 %late_grads.1 = (f32[4,1024,128]{2,1,0:T(8,128)S(1)}, bf16[4,1024,128]{2,1,0:T(8,128)(2,1)S(1)}) custom-call(s32[3]{0:T(128)S(1)} %pad_add_fusion.s, bf16[624,2048]{1,0:T(8,128)(2,1)S(1)} %get-tuple-element.142.refs_0_, bf16[624,512]{1,0:T(8,128)(2,1)S(1)} %get-tuple-element.130.refs_0_.refs_1_, bf16[4,1792,128]{2,1,0:T(8,128)(2,1)S(1)} %get-tuple-element.141.refs_2_), custom_call_target="tpu_custom_call" | custom-call | flops 350000000 | tf_op jit(solution)/shard_map/late_grads/pallas_call | solution.py:636
  67.9 0.8 collective-permute-done.14.refs_1_
  68.7 0.9 up_core.1
  69.6 1.8 %collective-permute-start.17 = (bf16[1792,128]{1,0:T(8,128)(2,1)S(1)}, bf16[1792,128]{1,0:T(8,128)(2,1)S(1)}, u32[]{:S(2)}, u32[]{:S(2)}) collective-permute-start(bf16[1792,128]{1,0:T(8,128)(2,1)S(1)} %get-tuple-element.154), channel_id=1, source_target_pairs={{0,1},{1,0},{2,3},{3,2},{4,5},{5,4},{6,7},{7,6},{8,9},{9,8},{10,11... | collective-permute-start | bytes 1376264 | tf_op jit(solution)/shard_map/ppermute | solution.py:660
  71.4 1.2 collective-permute-start.18
  73.2 3.7 %attend_back_0.1.refs_2_.refs_1_.refs_0_ = bf16[624,768]{1,0:T(8,128)(2,1)S(1)} custom-call(s32[3]{0:T(128)S(1)} %pad_add_fusion.s, bf16[624,512]{1,0:T(8,128)(2,1)S(1)} %get-tuple-element.136.refs_3_.refs_0_, bf16[624,1536]{1,0:T(8,128)(2,1)S(1)} %get-tuple-element.137.refs_1_, bf16[256,512]{1,0:T(8,128)(2,1)S(1)} %get-tuple-element.115.refs_4_.refs_2_, ...), custom_call_target="tpu_custom_call" | custom-call | flops 450000000 | tf_op jit(solution)/shard_map/attend_back_0/pallas_call | solution.py:636
  76.9 0.8 late_core.1
  77.7 1.8 %collective-permute-start.22 = (bf16[1024,128]{1,0:T(8,128)(2,1)S(1)}, bf16[1024,128]{1,0:T(8,128)(2,1)S(1)}, u32[]{:S(2)}, u32[]{:S(2)}) collective-permute-start(bf16[1024,128]{1,0:T(8,128)(2,1)S(1)} %get-tuple-element.147.refs_4_), channel_id=1, source_target_pairs={{0,4},{2,6},{4,0},{6,2},{8,12},{10,14},{12,8},{14,10},{16,20},{18,... | collective-permute-start | bytes 786440 | tf_op jit(solution)/shard_map/ppermute | solution.py:660
  79.5 3.8 %attend_back_1.1.refs_2_.refs_1_ = bf16[624,768]{1,0:T(8,128)(2,1)S(1)} custom-call(s32[3]{0:T(128)S(1)} %pad_add_fusion.s, bf16[624,512]{1,0:T(8,128)(2,1)S(1)} %get-tuple-element.136.refs_3_.refs_0_, bf16[624,1536]{1,0:T(8,128)(2,1)S(1)} %get-tuple-element.137.refs_1_, bf16[256,512]{1,0:T(8,128)(2,1)S(1)} %get-tuple-element.145.refs_2_, ...), custom_call_target="tpu_custom_call" | custom-call | flops 450000000 | tf_op jit(solution)/shard_map/attend_back_1/pallas_call | solution.py:636
  83.2 2.0 %early_grads.1 = (f32[4,768,128]{2,1,0:T(8,128)S(1)}, bf16[4,768,128]{2,1,0:T(8,128)(2,1)S(1)}) custom-call(s32[3]{0:T(128)S(1)} %pad_add_fusion.s, bf16[624,512]{1,0:T(8,128)(2,1)S(1)} %get-tuple-element.150.refs_0_, bf16[624,768]{1,0:T(8,128)(2,1)S(1)} %attend_back_0.1.refs_2_.refs_1_.refs_0_, bf16[624,768]{1,0:T(8,128)(2,1)S(1)} %attend_back_1.1.refs_2_.refs_1_), custom_call_target="tpu_custom_call" | custom-call | flops 200000000 | tf_op jit(solution)/shard_map/early_grads/pallas_call | solution.py:636
  85.3 2.3 %frames_back.1 = (bf16[624,256]{1,0:T(8,128)(2,1)S(1)}, f32[624,256]{1,0:T(8,128)S(1)}, f32[2,512]{1,0:T(2,128)S(1)}) custom-call(s32[3]{0:T(128)S(1)} %pad_add_fusion.s, bf16[624,768]{1,0:T(8,128)(2,1)S(1)} %attend_back_0.1.refs_2_.refs_1_.refs_0_, bf16[624,768]{1,0:T(8,128)(2,1)S(1)} %attend_back_1.1.refs_2_.refs_1_, ...), custom_call_target="tpu_custom_call" | custom-call | flops 250000000 | tf_op jit(solution)/shard_map/frames_back/pallas_call | solution.py:636
  87.7 4.4 %collective-permute-done.17.refs_2_ = bf16[1792,128]{1,0:T(8,128)(2,1)S(1)} collective-permute-done((bf16[1792,128]{1,0:T(8,128)(2,1)S(1)}, bf16[1792,128]{1,0:T(8,128)(2,1)S(1)}, u32[]{:S(2)}, u32[]{:S(2)}) %collective-permute-start.17) | collective-permute-done | bytes 458784 | tf_op jit(solution)/shard_map/ppermute | solution.py:660
  92.1 1.7 %collective-permute-start.23 = (bf16[1024,128]{1,0:T(8,128)(2,1)S(1)}, bf16[1024,128]{1,0:T(8,128)(2,1)S(1)}, u32[]{:S(2)}, u32[]{:S(2)}) collective-permute-start(bf16[1024,128]{1,0:T(8,128)(2,1)S(1)} %get-tuple-element.166), channel_id=1, source_target_pairs={{0,1},{1,0},{2,3},{3,2},{4,5},{5,4},{6,7},{7,6},{8,9},{9,8},{10,11... | collective-permute-start | bytes 786440 | tf_op jit(solution)/shard_map/ppermute | solution.py:660
  93.8 1.2 collective-permute-start.24
  95.0 0.9 up_1.1
  96.0 1.6 %collective-permute-start.19 = (bf16[896,128]{1,0:T(8,128)(2,1)S(1)}, bf16[896,128]{1,0:T(8,128)(2,1)S(1)}, u32[]{:S(2)}, u32[]{:S(2)}) collective-permute-start(bf16[896,128]{1,0:T(8,128)(2,1)S(1)} %get-tuple-element.158), channel_id=1, source_target_pairs={{0,8},{2,10},{4,12},{6,14},{8,0},{10,2},{12,4},{14,6},{16,24},{18,... | collective-permute-start | bytes 688136 | tf_op jit(solution)/shard_map/ppermute | solution.py:660
  97.6 0.8 early_core.1
  98.4 0.9 collective-permute-start.28
  99.3 3.0 %collective-permute-done.19.refs_1_ = bf16[896,128]{1,0:T(8,128)(2,1)S(1)} collective-permute-done((bf16[896,128]{1,0:T(8,128)(2,1)S(1)}, bf16[896,128]{1,0:T(8,128)(2,1)S(1)}, u32[]{:S(2)}, u32[]{:S(2)}) %collective-permute-start.19) | collective-permute-done | bytes 229408 | tf_op jit(solution)/shard_map/ppermute | solution.py:660
  102.9 2.7 %collective-permute-start.21 = (bf16[896,128]{1,0:T(8,128)(2,1)S(1)}, bf16[896,128]{1,0:T(8,128)(2,1)S(1)}, u32[]{:S(2)}, u32[]{:S(2)}) collective-permute-start(bf16[896,128]{1,0:T(8,128)(2,1)S(1)} %up_2.1.refs_4_.refs_0_), channel_id=1, source_target_pairs={{0,16},{2,18},{4,20},{6,22},{8,24},{10,26},{12,28},{14,30},{16,0},... | collective-permute-start | bytes 688136 | tf_op jit(solution)/shard_map/ppermute | solution.py:660
  105.6 1.2 collective-permute-done.24.refs_3_
  106.8 0.8 late_1.1
  107.6 1.6 %collective-permute-start.27 = (bf16[512,128]{1,0:T(8,128)(2,1)S(1)}, bf16[512,128]{1,0:T(8,128)(2,1)S(1)}, u32[]{:S(2)}, u32[]{:S(2)}) collective-permute-start(bf16[512,128]{1,0:T(8,128)(2,1)S(1)} %get-tuple-element.172), channel_id=1, source_target_pairs={{0,8},{2,10},{4,12},{6,14},{8,0},{10,2},{12,4},{14,6},{16,24},{18,... | collective-permute-start | bytes 393224 | tf_op jit(solution)/shard_map/ppermute | solution.py:660
  109.7 2.4 %collective-permute-start.30 = (bf16[832,128]{1,0:T(8,128)(2,1)S(1)}, bf16[832,128]{1,0:T(8,128)(2,1)S(1)}, u32[]{:S(2)}, u32[]{:S(2)}) collective-permute-start(bf16[832,128]{1,0:T(8,128)(2,1)S(1)} %get-tuple-element.175), channel_id=1, source_target_pairs={{0,5},{1,4},{2,7},{3,6},{4,1},{5,0},{6,3},{7,2},{8,13},{9,12},{10,... | collective-permute-start | bytes 638984 | tf_op jit(solution)/shard_map/ppermute | solution.py:660
  112.2 2.1 %collective-permute-done.21.refs_1_ = bf16[896,128]{1,0:T(8,128)(2,1)S(1)} collective-permute-done((bf16[896,128]{1,0:T(8,128)(2,1)S(1)}, bf16[896,128]{1,0:T(8,128)(2,1)S(1)}, u32[]{:S(2)}, u32[]{:S(2)}) %collective-permute-start.21) | collective-permute-done | bytes 229408 | tf_op jit(solution)/shard_map/ppermute | solution.py:660
  114.9 0.7 collective-permute-start.26
  115.5 1.4 logits.1
  116.9 1.7 %collective-permute-done.29.refs_2_ = bf16[832,128]{1,0:T(8,128)(2,1)S(1)} collective-permute-done((bf16[832,128]{1,0:T(8,128)(2,1)S(1)}, bf16[832,128]{1,0:T(8,128)(2,1)S(1)}, u32[]{:S(2)}, u32[]{:S(2)}) %collective-permute-start.29) | collective-permute-done | bytes 213024 | tf_op jit(solution)/shard_map/ppermute | solution.py:660
  119.1 0.7 early_1.1
  119.8 1.0 collective-permute-start.34
  121.4 2.2 %collective-permute-start.36 = (bf16[512,128]{1,0:T(8,128)(2,1)S(1)}, bf16[512,128]{1,0:T(8,128)(2,1)S(1)}, u32[]{:S(2)}, u32[]{:S(2)}) collective-permute-start(bf16[512,128]{1,0:T(8,128)(2,1)S(1)} %late_2.1.refs_2_.refs_0_), channel_id=1, source_target_pairs={{0,16},{2,18},{4,20},{6,22},{8,24},{10,26},{12,28},{14,30},{16,0},... | collective-permute-start | bytes 393224 | tf_op jit(solution)/shard_map/ppermute | solution.py:660
  124.4 1.5 collective-permute-start.31
  126.4 2.1 %collective-permute-start.35 = (bf16[416,128]{1,0:T(8,128)(2,1)S(1)}, bf16[416,128]{1,0:T(8,128)(2,1)S(1)}, u32[]{:S(2)}, u32[]{:S(2)}) collective-permute-start(bf16[416,128]{1,0:T(8,128)(2,1)S(1)} %early_2.1.refs_2_.refs_0_), channel_id=1, source_target_pairs={{0,16},{2,18},{4,20},{6,22},{8,24},{10,26},{12,28},{14,30},{16,0},... | collective-permute-start | bytes 319496 | tf_op jit(solution)/shard_map/ppermute | solution.py:660
  129.6 2.7 %collective-permute-start.38 = (bf16[512,128]{1,0:T(8,128)(2,1)S(1)}, bf16[512,128]{1,0:T(8,128)(2,1)S(1)}, u32[]{:S(2)}, u32[]{:S(2)}) collective-permute-start(bf16[512,128]{1,0:T(8,128)(2,1)S(1)} %late_3.1.refs_2_.refs_0_), channel_id=1, source_target_pairs={{0,8},{2,10},{4,12},{6,14},{8,0},{10,2},{12,4},{14,6},{16,24},{18,... | collective-permute-start | bytes 393224 | tf_op jit(solution)/shard_map/ppermute | solution.py:660
  132.3 2.5 %collective-permute-done.35.refs_1_ = bf16[416,128]{1,0:T(8,128)(2,1)S(1)} collective-permute-done((bf16[416,128]{1,0:T(8,128)(2,1)S(1)}, bf16[416,128]{1,0:T(8,128)(2,1)S(1)}, u32[]{:S(2)}, u32[]{:S(2)}) %collective-permute-start.35) | collective-permute-done | bytes 106528 | tf_op jit(solution)/shard_map/ppermute | solution.py:660
  137.4 2.8 %collective-permute-done.37.refs_1_ = bf16[416,128]{1,0:T(8,128)(2,1)S(1)} collective-permute-done((bf16[416,128]{1,0:T(8,128)(2,1)S(1)}, bf16[416,128]{1,0:T(8,128)(2,1)S(1)}, u32[]{:S(2)}, u32[]{:S(2)}) %collective-permute-start.37) | collective-permute-done | bytes 106528 | tf_op jit(solution)/shard_map/ppermute | solution.py:660
  140.7 0.7 collective-permute-start.39
  141.4 2.8 %up_place.1 = (f32[512,1024]{1,0:T(8,128)}, f32[256,512]{1,0:T(8,128)}, f32[512,512]{1,0:T(8,128)}, f32[8,128]{1,0:T(8,128)S(1)}) custom-call(s32[3]{0:T(128)S(1)} %pad_add_fusion.s, bf16[1792,128]{1,0:T(8,128)(2,1)S(1)} %up_4.1.refs_2_.refs_0_, bf16[1792,128]{1,0:T(8,128)(2,1)S(1)} %collective-permute-done.31.refs_1_, ...), custom_call_target="tpu_custom_call" | custom-call | flops 10000000000 | tf_op jit(solution)/shard_map/up_place/pallas_call | solution.py:636
  144.2 3.2 %collective-permute-done.25.refs_1_.refs_3_.refs_5_ = bf16[624,1024]{1,0:T(8,128)(2,1)S(1)} collective-permute-done((bf16[624,1024]{1,0:T(8,128)(2,1)S(1)}, bf16[624,1024]{1,0:T(8,128)(2,1)S(1)}, u32[]{:S(2)}, u32[]{:S(2)}) %collective-permute-start.25) | collective-permute-done | bytes 1277984 | tf_op jit(solution)/shard_map/ppermute | solution.py:660
  147.4 2.9 %rows_back.1 = (bf16[1200,256]{1,0:T(8,128)(2,1)}, f32[1200,512]{1,0:T(8,128)}, f32[1200,256]{1,0:T(8,128)}, f32[8,128]{1,0:T(8,128)S(1)}) custom-call(s32[3]{0:T(128)S(1)} %pad_add_fusion.s, bf16[624,256]{1,0:T(8,128)(2,1)S(1)} %get-tuple-element.121.refs_0_, bf16[624,1024]{1,0:T(8,128)(2,1)S(1)} %collective-permute-done.25.refs_1_.refs_3_.refs_5_, ...), custom_call_target="tpu_custom_call" | custom-call | flops 10000000000 | tf_op jit(solution)/shard_map/rows_back/pallas_call | solution.py:636
  151.1 1.2 collective-permute-done.40.refs_2_
  152.6 2.7 %last_place.1 = (f32[3,512,256]{2,1,0:T(8,128)}, f32[1024,512]{1,0:T(8,128)}, f32[1,512]{1,0:T(1,128)}, f32[1,512]{1,0:T(1,128)}, f32[1,512]{1,0:T(1,128)}, /*in...) custom-call(s32[3]{0:T(128)S(1)} %pad_add_fusion.s, ...), custom_call_target="tpu_custom_call" | custom-call | flops 10000000000 | tf_op jit(solution)/shard_map/last_place/pallas_call | solution.py:636
  (64 shorter events, 13.3 us)
Async XLA Ops:
  3.0 11.4 %collective-permute-start = (bf16[624,256]{1,0:T(8,128)(2,1)S(1)}, bf16[624,256]{1,0:T(8,128)(2,1)S(1)}, u32[]{:S(2)}, u32[]{:S(2)}) collective-permute-start(bf16[624,256]{1,0:T(8,128)(2,1)S(1)} %get-tuple-element.109.refs_7_), channel_id=1, source_target_pairs={{0,1},{1,0},{2,3},{3,2},{4,5},{5,4},{6,7},{7,6},{8,9},{9,8},{10,11... | collective-permute-start | bytes 958472 | tf_op jit(solution)/shard_map/ppermute | solution.py:660
  6.0 12.6 %collective-permute-start.1 = (bf16[768,128]{1,0:T(8,128)(2,1)S(1)}, bf16[768,128]{1,0:T(8,128)(2,1)S(1)}, u32[]{:S(2)}, u32[]{:S(2)}) collective-permute-start(bf16[768,128]{1,0:T(8,128)(2,1)S(1)} %get-tuple-element.112), channel_id=1, source_target_pairs={{0,1},{1,0},{2,3},{3,2},{4,5},{5,4},{6,7},{7,6},{8,9},{9,8},{10,11... | collective-permute-start | bytes 589832 | tf_op jit(solution)/shard_map/ppermute | solution.py:660
  14.4 12.0 %collective-permute-start.5 = (bf16[1328,128]{1,0:T(8,128)(2,1)S(1)}, bf16[1328,128]{1,0:T(8,128)(2,1)S(1)}, u32[]{:S(2)}, u32[]{:S(2)}) collective-permute-start(bf16[1328,128]{1,0:T(8,128)(2,1)S(1)} %after_frames.1.refs_1_), channel_id=1, source_target_pairs={{0,1},{1,0},{2,3},{3,2},{4,5},{5,4},{6,7},{7,6},{8,9},{9,8},{10,11... | collective-permute-start | bytes 1019912 | tf_op jit(solution)/shard_map/ppermute | solution.py:660
  18.6 5.7 %collective-permute-start.2 = (bf16[768,128]{1,0:T(8,128)(2,1)S(1)}, bf16[768,128]{1,0:T(8,128)(2,1)S(1)}, u32[]{:S(2)}, u32[]{:S(2)}) collective-permute-start(bf16[768,128]{1,0:T(8,128)(2,1)S(1)} %collective-permute-done.1.refs_4_), channel_id=1, source_target_pairs={{0,4},{2,6},{4,0},{6,2},{8,12},{10,14},{12,8},{14,10},{16,20},{18,... | collective-permute-start | bytes 589832 | tf_op jit(solution)/shard_map/ppermute | solution.py:660
  24.3 9.2 %collective-permute-start.9 = (bf16[1536,128]{1,0:T(8,128)(2,1)S(1)}, bf16[1536,128]{1,0:T(8,128)(2,1)S(1)}, u32[]{:S(2)}, u32[]{:S(2)}) collective-permute-start(bf16[1536,128]{1,0:T(8,128)(2,1)S(1)} %after_one.1), channel_id=1, source_target_pairs={{0,1},{1,0},{2,3},{3,2},{4,5},{5,4},{6,7},{7,6},{8,9},{9,8},{10,11... | collective-permute-start | bytes 1179656 | tf_op jit(solution)/shard_map/ppermute | solution.py:660
  26.4 7.8 %collective-permute-start.6 = (bf16[1328,128]{1,0:T(8,128)(2,1)S(1)}, bf16[1328,128]{1,0:T(8,128)(2,1)S(1)}, u32[]{:S(2)}, u32[]{:S(2)}) collective-permute-start(bf16[1328,128]{1,0:T(8,128)(2,1)S(1)} %collective-permute-done.5.refs_7_.refs_4_), channel_id=1, source_target_pairs={{0,4},{2,6},{4,0},{6,2},{8,12},{10,14},{12,8},{14,10},{16,20},{18,... | collective-permute-start | bytes 1019912 | tf_op jit(solution)/shard_map/ppermute | solution.py:660
  34.3 20.2 %collective-permute-start.13 = (bf16[624,768]{1,0:T(8,128)(2,1)S(1)}, bf16[624,768]{1,0:T(8,128)(2,1)S(1)}, u32[]{:S(2)}, u32[]{:S(2)}) collective-permute-start(bf16[624,768]{1,0:T(8,128)(2,1)S(1)} %after_two.1), channel_id=1, source_target_pairs={{0,1},{1,0},{2,3},{3,2},{4,5},{5,4},{6,7},{7,6},{8,9},{9,8},{10,11... | collective-permute-start | bytes 2875400 | tf_op jit(solution)/shard_map/ppermute | solution.py:660
  35.7 8.0 %collective-permute-start.10 = (bf16[1536,128]{1,0:T(8,128)(2,1)S(1)}, bf16[1536,128]{1,0:T(8,128)(2,1)S(1)}, u32[]{:S(2)}, u32[]{:S(2)}) collective-permute-start(bf16[1536,128]{1,0:T(8,128)(2,1)S(1)} %collective-permute-done.9.refs_11_.refs_1_.refs_8_), channel_id=1, source_target_pairs={{0,4},{2,6},{4,0},{6,2},{8,12},{10,14},{12,8},{14,10},{16,20},{18,... | collective-permute-start | bytes 1179656 | tf_op jit(solution)/shard_map/ppermute | solution.py:660
  37.2 1.4 collective-permute-start.3
  37.2 1.7 %collective-permute-start.4 = (bf16[768,128]{1,0:T(8,128)(2,1)S(1)}, bf16[768,128]{1,0:T(8,128)(2,1)S(1)}, u32[]{:S(2)}, u32[]{:S(2)}) collective-permute-start(bf16[768,128]{1,0:T(8,128)(2,1)S(1)} %collective-permute-done.2.refs_5_.refs_2_), channel_id=1, source_target_pairs={{0,2},{2,0},{4,6},{6,4},{8,10},{10,8},{12,14},{14,12},{16,18},{18,... | collective-permute-start | bytes 589832 | tf_op jit(solution)/shard_map/ppermute | solution.py:660
  43.3 2.8 %collective-permute-start.11 = (bf16[1536,128]{1,0:T(8,128)(2,1)S(1)}, bf16[1536,128]{1,0:T(8,128)(2,1)S(1)}, u32[]{:S(2)}, u32[]{:S(2)}) collective-permute-start(bf16[1536,128]{1,0:T(8,128)(2,1)S(1)} %collective-permute-done.9.refs_11_.refs_1_.refs_8_), channel_id=1, source_target_pairs={{0,2},{2,0},{4,6},{6,4},{8,10},{10,8},{12,14},{14,12},{16,18},{18,... | collective-permute-start | bytes 1179656 | tf_op jit(solution)/shard_map/ppermute | solution.py:660
  43.8 2.8 %collective-permute-start.12 = (bf16[1536,128]{1,0:T(8,128)(2,1)S(1)}, bf16[1536,128]{1,0:T(8,128)(2,1)S(1)}, u32[]{:S(2)}, u32[]{:S(2)}) collective-permute-start(bf16[1536,128]{1,0:T(8,128)(2,1)S(1)} %after_attend.1.refs_12_.refs_9_), channel_id=1, source_target_pairs={{0,2},{2,0},{4,6},{6,4},{8,10},{10,8},{12,14},{14,12},{16,18},{18,... | collective-permute-start | bytes 1179656 | tf_op jit(solution)/shard_map/ppermute | solution.py:660
  44.0 2.2 %collective-permute-start.7 = (bf16[1328,128]{1,0:T(8,128)(2,1)S(1)}, bf16[1328,128]{1,0:T(8,128)(2,1)S(1)}, u32[]{:S(2)}, u32[]{:S(2)}) collective-permute-start(bf16[1328,128]{1,0:T(8,128)(2,1)S(1)} %collective-permute-done.5.refs_7_.refs_4_), channel_id=1, source_target_pairs={{0,2},{2,0},{4,6},{6,4},{8,10},{10,8},{12,14},{14,12},{16,18},{18,... | collective-permute-start | bytes 1019912 | tf_op jit(solution)/shard_map/ppermute | solution.py:660
  44.4 2.2 %collective-permute-start.8 = (bf16[1328,128]{1,0:T(8,128)(2,1)S(1)}, bf16[1328,128]{1,0:T(8,128)(2,1)S(1)}, u32[]{:S(2)}, u32[]{:S(2)}) collective-permute-start(bf16[1328,128]{1,0:T(8,128)(2,1)S(1)} %collective-permute-done.6.refs_8_.refs_2_.refs_5_), channel_id=1, source_target_pairs={{0,2},{2,0},{4,6},{6,4},{8,10},{10,8},{12,14},{14,12},{16,18},{18,... | collective-permute-start | bytes 1019912 | tf_op jit(solution)/shard_map/ppermute | solution.py:660
  64.9 3.9 %collective-permute-start.14 = (bf16[4,1792,128]{2,1,0:T(8,128)(2,1)S(1)}, bf16[4,1792,128]{2,1,0:T(8,128)(2,1)S(1)}, u32[]{:S(2)}, u32[]{:S(2)}) collective-permute-start(bf16[4,1792,128]{2,1,0:T(8,128)(2,1)S(1)} %get-tuple-element.141.refs_2_), channel_id=1, source_target_pairs={{0,2},{2,0},{4,6},{6,4},{8,10},{10,8},{12,14},{14,12},{16,18},{18,... | collective-permute-start | bytes 5505032 | tf_op jit(solution)/shard_map/ppermute | solution.py:660
  67.4 9.6 %collective-permute-start.15 = (bf16[4,1024,128]{2,1,0:T(8,128)(2,1)S(1)}, bf16[4,1024,128]{2,1,0:T(8,128)(2,1)S(1)}, u32[]{:S(2)}, u32[]{:S(2)}) collective-permute-start(bf16[4,1024,128]{2,1,0:T(8,128)(2,1)S(1)} %get-tuple-element.143.refs_2_), channel_id=1, source_target_pairs={{0,2},{2,0},{4,6},{6,4},{8,10},{10,8},{12,14},{14,12},{16,18},{18,... | collective-permute-start | bytes 3145736 | tf_op jit(solution)/shard_map/ppermute | solution.py:660
  69.6 22.5 %collective-permute-start.17 = (bf16[1792,128]{1,0:T(8,128)(2,1)S(1)}, bf16[1792,128]{1,0:T(8,128)(2,1)S(1)}, u32[]{:S(2)}, u32[]{:S(2)}) collective-permute-start(bf16[1792,128]{1,0:T(8,128)(2,1)S(1)} %get-tuple-element.154), channel_id=1, source_target_pairs={{0,1},{1,0},{2,3},{3,2},{4,5},{5,4},{6,7},{7,6},{8,9},{9,8},{10,11... | collective-permute-start | bytes 1376264 | tf_op jit(solution)/shard_map/ppermute | solution.py:660
  71.4 22.4 %collective-permute-start.18 = (bf16[1792,128]{1,0:T(8,128)(2,1)S(1)}, bf16[1792,128]{1,0:T(8,128)(2,1)S(1)}, u32[]{:S(2)}, u32[]{:S(2)}) collective-permute-start(bf16[1792,128]{1,0:T(8,128)(2,1)S(1)} %get-tuple-element.155), channel_id=1, source_target_pairs={{0,5},{1,4},{2,7},{3,6},{4,1},{5,0},{6,3},{7,2},{8,13},{9,12},{10,... | collective-permute-start | bytes 1376264 | tf_op jit(solution)/shard_map/ppermute | solution.py:660
  72.6 22.4 %collective-permute-start.16 = (bf16[1792,128]{1,0:T(8,128)(2,1)S(1)}, bf16[1792,128]{1,0:T(8,128)(2,1)S(1)}, u32[]{:S(2)}, u32[]{:S(2)}) collective-permute-start(bf16[1792,128]{1,0:T(8,128)(2,1)S(1)} %get-tuple-element.144.refs_4_), channel_id=1, source_target_pairs={{0,4},{2,6},{4,0},{6,2},{8,12},{10,14},{12,8},{14,10},{16,20},{18,... | collective-permute-start | bytes 1376264 | tf_op jit(solution)/shard_map/ppermute | solution.py:660
  77.7 29.1 %collective-permute-start.22 = (bf16[1024,128]{1,0:T(8,128)(2,1)S(1)}, bf16[1024,128]{1,0:T(8,128)(2,1)S(1)}, u32[]{:S(2)}, u32[]{:S(2)}) collective-permute-start(bf16[1024,128]{1,0:T(8,128)(2,1)S(1)} %get-tuple-element.147.refs_4_), channel_id=1, source_target_pairs={{0,4},{2,6},{4,0},{6,2},{8,12},{10,14},{12,8},{14,10},{16,20},{18,... | collective-permute-start | bytes 786440 | tf_op jit(solution)/shard_map/ppermute | solution.py:660
  85.3 12.4 %collective-permute-start.20 = (bf16[4,768,128]{2,1,0:T(8,128)(2,1)S(1)}, bf16[4,768,128]{2,1,0:T(8,128)(2,1)S(1)}, u32[]{:S(2)}, u32[]{:S(2)}) collective-permute-start(bf16[4,768,128]{2,1,0:T(8,128)(2,1)S(1)} %get-tuple-element.151.refs_8_), channel_id=1, source_target_pairs={{0,2},{2,0},{4,6},{6,4},{8,10},{10,8},{12,14},{14,12},{16,18},{18,... | collective-permute-start | bytes 2359304 | tf_op jit(solution)/shard_map/ppermute | solution.py:660
  92.1 13.5 %collective-permute-start.23 = (bf16[1024,128]{1,0:T(8,128)(2,1)S(1)}, bf16[1024,128]{1,0:T(8,128)(2,1)S(1)}, u32[]{:S(2)}, u32[]{:S(2)}) collective-permute-start(bf16[1024,128]{1,0:T(8,128)(2,1)S(1)} %get-tuple-element.166), channel_id=1, source_target_pairs={{0,1},{1,0},{2,3},{3,2},{4,5},{5,4},{6,7},{7,6},{8,9},{9,8},{10,11... | collective-permute-start | bytes 786440 | tf_op jit(solution)/shard_map/ppermute | solution.py:660
  93.8 13.0 %collective-permute-start.24 = (bf16[1024,128]{1,0:T(8,128)(2,1)S(1)}, bf16[1024,128]{1,0:T(8,128)(2,1)S(1)}, u32[]{:S(2)}, u32[]{:S(2)}) collective-permute-start(bf16[1024,128]{1,0:T(8,128)(2,1)S(1)} %get-tuple-element.167), channel_id=1, source_target_pairs={{0,5},{1,4},{2,7},{3,6},{4,1},{5,0},{6,3},{7,2},{8,13},{9,12},{10,... | collective-permute-start | bytes 786440 | tf_op jit(solution)/shard_map/ppermute | solution.py:660
  96.0 6.3 %collective-permute-start.19 = (bf16[896,128]{1,0:T(8,128)(2,1)S(1)}, bf16[896,128]{1,0:T(8,128)(2,1)S(1)}, u32[]{:S(2)}, u32[]{:S(2)}) collective-permute-start(bf16[896,128]{1,0:T(8,128)(2,1)S(1)} %get-tuple-element.158), channel_id=1, source_target_pairs={{0,8},{2,10},{4,12},{6,14},{8,0},{10,2},{12,4},{14,6},{16,24},{18,... | collective-permute-start | bytes 688136 | tf_op jit(solution)/shard_map/ppermute | solution.py:660
  98.4 20.7 %collective-permute-start.28 = (bf16[832,128]{1,0:T(8,128)(2,1)S(1)}, bf16[832,128]{1,0:T(8,128)(2,1)S(1)}, u32[]{:S(2)}, u32[]{:S(2)}) collective-permute-start(bf16[832,128]{1,0:T(8,128)(2,1)S(1)} %get-tuple-element.164.refs_2_), channel_id=1, source_target_pairs={{0,4},{2,6},{4,0},{6,2},{8,12},{10,14},{12,8},{14,10},{16,20},{18,... | collective-permute-start | bytes 638984 | tf_op jit(solution)/shard_map/ppermute | solution.py:660
  102.9 11.3 %collective-permute-start.21 = (bf16[896,128]{1,0:T(8,128)(2,1)S(1)}, bf16[896,128]{1,0:T(8,128)(2,1)S(1)}, u32[]{:S(2)}, u32[]{:S(2)}) collective-permute-start(bf16[896,128]{1,0:T(8,128)(2,1)S(1)} %up_2.1.refs_4_.refs_0_), channel_id=1, source_target_pairs={{0,16},{2,18},{4,20},{6,22},{8,24},{10,26},{12,28},{14,30},{16,0},... | collective-permute-start | bytes 688136 | tf_op jit(solution)/shard_map/ppermute | solution.py:660
  107.6 13.3 %collective-permute-start.27 = (bf16[512,128]{1,0:T(8,128)(2,1)S(1)}, bf16[512,128]{1,0:T(8,128)(2,1)S(1)}, u32[]{:S(2)}, u32[]{:S(2)}) collective-permute-start(bf16[512,128]{1,0:T(8,128)(2,1)S(1)} %get-tuple-element.172), channel_id=1, source_target_pairs={{0,8},{2,10},{4,12},{6,14},{8,0},{10,2},{12,4},{14,6},{16,24},{18,... | collective-permute-start | bytes 393224 | tf_op jit(solution)/shard_map/ppermute | solution.py:660
  109.2 9.4 %collective-permute-start.29 = (bf16[832,128]{1,0:T(8,128)(2,1)S(1)}, bf16[832,128]{1,0:T(8,128)(2,1)S(1)}, u32[]{:S(2)}, u32[]{:S(2)}) collective-permute-start(bf16[832,128]{1,0:T(8,128)(2,1)S(1)} %get-tuple-element.174), channel_id=1, source_target_pairs={{0,1},{1,0},{2,3},{3,2},{4,5},{5,4},{6,7},{7,6},{8,9},{9,8},{10,11... | collective-permute-start | bytes 638984 | tf_op jit(solution)/shard_map/ppermute | solution.py:660
  109.7 9.4 %collective-permute-start.30 = (bf16[832,128]{1,0:T(8,128)(2,1)S(1)}, bf16[832,128]{1,0:T(8,128)(2,1)S(1)}, u32[]{:S(2)}, u32[]{:S(2)}) collective-permute-start(bf16[832,128]{1,0:T(8,128)(2,1)S(1)} %get-tuple-element.175), channel_id=1, source_target_pairs={{0,5},{1,4},{2,7},{3,6},{4,1},{5,0},{6,3},{7,2},{8,13},{9,12},{10,... | collective-permute-start | bytes 638984 | tf_op jit(solution)/shard_map/ppermute | solution.py:660
  114.9 8.8 %collective-permute-start.26 = (bf16[896,128]{1,0:T(8,128)(2,1)S(1)}, bf16[896,128]{1,0:T(8,128)(2,1)S(1)}, u32[]{:S(2)}, u32[]{:S(2)}) collective-permute-start(bf16[896,128]{1,0:T(8,128)(2,1)S(1)} %up_3.1.refs_7_.refs_0_), channel_id=1, source_target_pairs={{0,8},{2,10},{4,12},{6,14},{8,0},{10,2},{12,4},{14,6},{16,24},{18,... | collective-permute-start | bytes 688136 | tf_op jit(solution)/shard_map/ppermute | solution.py:660
  118.6 28.8 %collective-permute-start.25 = (bf16[624,1024]{1,0:T(8,128)(2,1)S(1)}, bf16[624,1024]{1,0:T(8,128)(2,1)S(1)}, u32[]{:S(2)}, u32[]{:S(2)}) collective-permute-start(bf16[624,1024]{1,0:T(8,128)(2,1)S(1)} %get-tuple-element.169.refs_4_), channel_id=1, source_target_pairs={{0,1},{1,0},{2,3},{3,2},{4,5},{5,4},{6,7},{7,6},{8,9},{9,8},{10,11... | collective-permute-start | bytes 3833864 | tf_op jit(solution)/shard_map/ppermute | solution.py:660
  119.8 6.0 %collective-permute-start.34 = (bf16[416,128]{1,0:T(8,128)(2,1)S(1)}, bf16[416,128]{1,0:T(8,128)(2,1)S(1)}, u32[]{:S(2)}, u32[]{:S(2)}) collective-permute-start(bf16[416,128]{1,0:T(8,128)(2,1)S(1)} %get-tuple-element.177), channel_id=1, source_target_pairs={{0,8},{2,10},{4,12},{6,14},{8,0},{10,2},{12,4},{14,6},{16,24},{18,... | collective-permute-start | bytes 319496 | tf_op jit(solution)/shard_map/ppermute | solution.py:660
  121.4 7.6 %collective-permute-start.36 = (bf16[512,128]{1,0:T(8,128)(2,1)S(1)}, bf16[512,128]{1,0:T(8,128)(2,1)S(1)}, u32[]{:S(2)}, u32[]{:S(2)}) collective-permute-start(bf16[512,128]{1,0:T(8,128)(2,1)S(1)} %late_2.1.refs_2_.refs_0_), channel_id=1, source_target_pairs={{0,16},{2,18},{4,20},{6,22},{8,24},{10,26},{12,28},{14,30},{16,0},... | collective-permute-start | bytes 393224 | tf_op jit(solution)/shard_map/ppermute | solution.py:660
  124.3 11.9 %collective-permute-start.32 = (bf16[1792,128]{1,0:T(8,128)(2,1)S(1)}, bf16[1792,128]{1,0:T(8,128)(2,1)S(1)}, u32[]{:S(2)}, u32[]{:S(2)}) collective-permute-start(bf16[1792,128]{1,0:T(8,128)(2,1)S(1)} %up_4.1.refs_2_.refs_0_), channel_id=1, source_target_pairs={{0,2},{2,0},{4,6},{6,4},{8,10},{10,8},{12,14},{14,12},{16,18},{18,... | collective-permute-start | bytes 1376264 | tf_op jit(solution)/shard_map/ppermute | solution.py:660
  124.4 12.9 %collective-permute-start.31 = (bf16[1792,128]{1,0:T(8,128)(2,1)S(1)}, bf16[1792,128]{1,0:T(8,128)(2,1)S(1)}, u32[]{:S(2)}, u32[]{:S(2)}) collective-permute-start(bf16[1792,128]{1,0:T(8,128)(2,1)S(1)} %up_4.1.refs_2_.refs_0_), channel_id=1, source_target_pairs={{0,4},{2,6},{4,0},{6,2},{8,12},{10,14},{12,8},{14,10},{16,20},{18,... | collective-permute-start | bytes 1376264 | tf_op jit(solution)/shard_map/ppermute | solution.py:660
  126.4 8.4 %collective-permute-start.35 = (bf16[416,128]{1,0:T(8,128)(2,1)S(1)}, bf16[416,128]{1,0:T(8,128)(2,1)S(1)}, u32[]{:S(2)}, u32[]{:S(2)}) collective-permute-start(bf16[416,128]{1,0:T(8,128)(2,1)S(1)} %early_2.1.refs_2_.refs_0_), channel_id=1, source_target_pairs={{0,16},{2,18},{4,20},{6,22},{8,24},{10,26},{12,28},{14,30},{16,0},... | collective-permute-start | bytes 319496 | tf_op jit(solution)/shard_map/ppermute | solution.py:660
  129.6 6.5 %collective-permute-start.38 = (bf16[512,128]{1,0:T(8,128)(2,1)S(1)}, bf16[512,128]{1,0:T(8,128)(2,1)S(1)}, u32[]{:S(2)}, u32[]{:S(2)}) collective-permute-start(bf16[512,128]{1,0:T(8,128)(2,1)S(1)} %late_3.1.refs_2_.refs_0_), channel_id=1, source_target_pairs={{0,8},{2,10},{4,12},{6,14},{8,0},{10,2},{12,4},{14,6},{16,24},{18,... | collective-permute-start | bytes 393224 | tf_op jit(solution)/shard_map/ppermute | solution.py:660
  135.4 4.8 %collective-permute-start.37 = (bf16[416,128]{1,0:T(8,128)(2,1)S(1)}, bf16[416,128]{1,0:T(8,128)(2,1)S(1)}, u32[]{:S(2)}, u32[]{:S(2)}) collective-permute-start(bf16[416,128]{1,0:T(8,128)(2,1)S(1)} %early_3.1.refs_2_.refs_0_), channel_id=1, source_target_pairs={{0,8},{2,10},{4,12},{6,14},{8,0},{10,2},{12,4},{14,6},{16,24},{18,... | collective-permute-start | bytes 319496 | tf_op jit(solution)/shard_map/ppermute | solution.py:660
  136.7 15.5 %collective-permute-start.43 = (bf16[1024,128]{1,0:T(8,128)(2,1)S(1)}, bf16[1024,128]{1,0:T(8,128)(2,1)S(1)}, u32[]{:S(2)}, u32[]{:S(2)}) collective-permute-start(bf16[1024,128]{1,0:T(8,128)(2,1)S(1)} %late_4.1.refs_2_.refs_4_), channel_id=1, source_target_pairs={{0,2},{2,0},{4,6},{6,4},{8,10},{10,8},{12,14},{14,12},{16,18},{18,... | collective-permute-start | bytes 786440 | tf_op jit(solution)/shard_map/ppermute | solution.py:660
  136.8 13.5 %collective-permute-start.42 = (bf16[1024,128]{1,0:T(8,128)(2,1)S(1)}, bf16[1024,128]{1,0:T(8,128)(2,1)S(1)}, u32[]{:S(2)}, u32[]{:S(2)}) collective-permute-start(bf16[1024,128]{1,0:T(8,128)(2,1)S(1)} %late_4.1.refs_2_.refs_4_), channel_id=1, source_target_pairs={{0,4},{2,6},{4,0},{6,2},{8,12},{10,14},{12,8},{14,10},{16,20},{18,... | collective-permute-start | bytes 786440 | tf_op jit(solution)/shard_map/ppermute | solution.py:660
  137.3 4.1 %collective-permute-start.33 = (bf16[1792,128]{1,0:T(8,128)(2,1)S(1)}, bf16[1792,128]{1,0:T(8,128)(2,1)S(1)}, u32[]{:S(2)}, u32[]{:S(2)}) collective-permute-start(bf16[1792,128]{1,0:T(8,128)(2,1)S(1)} %collective-permute-done.31.refs_1_), channel_id=1, source_target_pairs={{0,2},{2,0},{4,6},{6,4},{8,10},{10,8},{12,14},{14,12},{16,18},{18,... | collective-permute-start | bytes 1376264 | tf_op jit(solution)/shard_map/ppermute | solution.py:660
  140.7 10.2 %collective-permute-start.39 = (bf16[832,128]{1,0:T(8,128)(2,1)S(1)}, bf16[832,128]{1,0:T(8,128)(2,1)S(1)}, u32[]{:S(2)}, u32[]{:S(2)}) collective-permute-start(bf16[832,128]{1,0:T(8,128)(2,1)S(1)} %early_4.1.refs_4_.refs_0_), channel_id=1, source_target_pairs={{0,4},{2,6},{4,0},{6,2},{8,12},{10,14},{12,8},{14,10},{16,20},{18,... | collective-permute-start | bytes 638984 | tf_op jit(solution)/shard_map/ppermute | solution.py:660
  150.3 2.2 %collective-permute-start.44 = (bf16[1024,128]{1,0:T(8,128)(2,1)S(1)}, bf16[1024,128]{1,0:T(8,128)(2,1)S(1)}, u32[]{:S(2)}, u32[]{:S(2)}) collective-permute-start(bf16[1024,128]{1,0:T(8,128)(2,1)S(1)} %after_rows.1.refs_5_), channel_id=1, source_target_pairs={{0,2},{2,0},{4,6},{6,4},{8,10},{10,8},{12,14},{14,12},{16,18},{18,... | collective-permute-start | bytes 786440 | tf_op jit(solution)/shard_map/ppermute | solution.py:660
  150.4 1.8 %collective-permute-start.40 = (bf16[832,128]{1,0:T(8,128)(2,1)S(1)}, bf16[832,128]{1,0:T(8,128)(2,1)S(1)}, u32[]{:S(2)}, u32[]{:S(2)}) collective-permute-start(bf16[832,128]{1,0:T(8,128)(2,1)S(1)} %early_4.1.refs_4_.refs_0_), channel_id=1, source_target_pairs={{0,2},{2,0},{4,6},{6,4},{8,10},{10,8},{12,14},{14,12},{16,18},{18,... | collective-permute-start | bytes 638984 | tf_op jit(solution)/shard_map/ppermute | solution.py:660
  150.9 1.6 %collective-permute-start.41 = (bf16[832,128]{1,0:T(8,128)(2,1)S(1)}, bf16[832,128]{1,0:T(8,128)(2,1)S(1)}, u32[]{:S(2)}, u32[]{:S(2)}) collective-permute-start(bf16[832,128]{1,0:T(8,128)(2,1)S(1)} %after_up.1.refs_1_), channel_id=1, source_target_pairs={{0,2},{2,0},{4,6},{6,4},{8,10},{10,8},{12,14},{14,12},{16,18},{18,... | collective-permute-start | bytes 638984 | tf_op jit(solution)/shard_map/ppermute | solution.py:660

commit v4 on v3

--- a/solution.py
+++ b/solution.py
@@ -147,9 +147,7 @@
     return start
 
 
-def first_kernel(s, frames, qkv, up, out, down, prior, resets, *refs):
-    smalls, refs = refs[:-9], refs[-9:]
-    qkv_ref, sent_ref, one_ref, two_ref, own_ref, small_ref, resets_ref, wide_rows, rows = refs
+def first_kernel(s, frames, qkv, resets, qkv_ref, sent_ref, own_ref, resets_ref, wide_rows):
     start = 0
     for c in range(3):
         start = put_tiles(qkv_ref, start, qkv.get().at[c])
@@ -158,6 +156,10 @@
     line = resets[...].reshape(1, -1)
     for block in range(line.shape[1] // BLOCK):
         resets_ref[block : block + 1, :BLOCK] = line[:, block * BLOCK : block * BLOCK + BLOCK]
+
+
+def packs_kernel(s, up, out, down, prior, *refs):
+    smalls, (one_ref, two_ref, small_ref, rows) = refs[:-4], refs[-4:]
     start = put_tiles(one_ref, put_tiles(one_ref, 0, up), out)
     for i, ref in enumerate(smalls):
         small_ref[i : i + 1, : ref.shape[1]] = ref[...]
@@ -545,16 +547,19 @@
 
 def rows_kernel(entries, s, *refs):
     count = len(entries)
-    given, outs, token, rooms = refs[: 2 * count], refs[2 * count : 3 * count], refs[3 * count], refs[3 * count + 1 :]
+    given, outs, token, room = refs[: 2 * count], refs[2 * count : 3 * count], refs[3 * count], refs[-1]
     token[...] = jnp.zeros_like(token)
     for i, columns in enumerate(entries):
-        own, got, out, room = given[2 * i], given[2 * i + 1], outs[i], rooms[i]
+        own, got, out = given[2 * i], given[2 * i + 1], outs[i]
+        whole = out.ref.dtype == F32
+        target = out.ref if whole else room
         rows = out.shape[0] // 2
         for block, at in enumerate(blocks_in(own)):
             for which, ref, cut in ((s[0], own, slice(None)), (1 - s[0], got, columns)):
                 start = pl.multiple_of(which * rows + block * BLOCK, 8)
-                room[pl.ds(start, BLOCK), :] = ref[at, cut].astype(F32)[:BLOCK]
-        out[...] = room[...].astype(out.ref.dtype)
+                target[pl.ds(start, BLOCK), :] = ref[at, cut].astype(F32)[:BLOCK]
+        if not whole:
+            out[...] = room[...].astype(out.ref.dtype)
         out.send()
 
 
@@ -764,7 +769,7 @@
     vectors = [first_gain, first_shift, out_bias, second_gain, second_shift, down_bias, prior_gain, prior_shift]
     vectors = [row(v) for v in vectors + [up_bias, prior_bias]]
     qkv_rows = 3 * (width // 4) * (half // 128)
-    sent_qkv, sent_frames, sent_one, sent_two, frames_own, small, resets_near = call(
+    sent_qkv, sent_frames, frames_own, resets_near = call(
         first_kernel,
         scalars,
         [
@@ -774,20 +779,30 @@
                 (3, width // 4, half),
                 lambda s, ref: ref.at[:, pl.ds(pl.multiple_of(s[1] * (width // 4), 16), width // 4), :],
             ),
+            Far(resets),
+        ],
+        [((qkv_rows, 128), BF, True)]
+        + near_rows((half, BF), (half, BF))
+        + [((-(-2 * blocks // 8) * 8, -(-BLOCK // 128) * 128), jnp.int32, True)],
+        [pltpu.VMEM((rows + 16, half), F32)],
+        "first_parts",
+        cost=2.0,
+    )
+    sent_one, sent_two, small = call(
+        packs_kernel,
+        scalars,
+        [
             columns(up_weight, quarter, 1),
             some_rows(out_weight, half // 4, 1),
             some_rows(down_weight, quarter, 1),
             columns(prior_weight, n_logits // 4, 1),
-            Far(resets),
             *[Far(v) for v in vectors],
         ],
-        [((qkv_rows, 128), BF, True)]
-        + near_rows((half, BF))
-        + [((width * 2 + half + 48, 128), BF, True), ((quarter * 4 + width, 128), BF, True)]
-        + near_rows((half, BF))
-        + [((16, hidden_width), F32, True), ((-(-2 * blocks // 8) * 8, -(-BLOCK // 128) * 128), jnp.int32, True)],
-        [pltpu.VMEM((rows + 16, half), F32), pltpu.VMEM((16, 128), F32)],
-        "first_parts",
+        [((width * 2 + half + 48, 128), BF, True), ((quarter * 4 + width, 128), BF, True)]
+        + [((16, hidden_width), F32, True)],
+        [pltpu.VMEM((16, 128), F32)],
+        "packs",
+        after=(sent_frames,),
         cost=2.0,
     )
 
@@ -953,16 +968,16 @@
         cost=FOLD,
     )
     back_got = move.over(back_send)
-    block_out, logits, grad_frames, rows_done = call(
+    logits, grad_frames, block_out, rows_done = call(
         functools.partial(
             rows_kernel,
-            [slice(n_logits, n_logits + half), slice(0, n_logits), slice(n_logits + half, n_logits + 2 * half)],
+            [slice(0, n_logits), slice(n_logits + half, n_logits + 2 * half), slice(n_logits, n_logits + half)],
         ),
         scalars,
-        [block_own, back_got, logits_own, back_got, frames_grad, back_got],
-        [((rows, half), BF, False), ((rows, n_logits), F32, False), ((rows, half), F32, False)]
+        [logits_own, back_got, frames_grad, back_got, block_own, back_got],
+        [((rows, n_logits), F32, False), ((rows, half), F32, False), ((rows, half), BF, False)]
         + [((8, 128), F32, True)],
-        [pltpu.VMEM((rows, n), F32) for n in (half, n_logits, half)],
+        [pltpu.VMEM((rows, half), F32)],
         name="rows_back",
         after=(up_done,),
         cost=FOLD,

time: 156 us -> 155 us (level)
  waiting for transfers between devices: 45.9 us -> 43.3 us
    ppermute x45, waiting for transfers between devices: 45.9 us -> 43.3 us  [swap(): return lax.ppermute(value, axes, [(i, i ^ mask) for i in range(count)])]
    pallas_call x31 -> x32, Pallas kernels: 61.1 us -> 62.5 us  [call(): pl.pallas_call(run, in_specs=[pl.BlockSpec(memory_space=pltpu.SMEM)] + [f...]
  transfers between devices with their start and end apart: 45 -> 45, of which waited for: 24 -> 24; matrix products, arithmetic and copies ran while one was open for 0% -> 0% of each run, Pallas kernels for 29% -> 31%
where the time goes in v4:
time: 155 us
  Pallas kernels  62.7 us (40%)
  starting transfers between devices  47.8 us (31%)
  waiting for transfers between devices  43.3 us (28%)
    pallas_call x32, Pallas kernels, call(): pl.pallas_call(run, in_specs=[pl.BlockSpec(memory_space=pltpu.SMEM)] + [f...  62.5 us
    ppermute x45, starting transfers between devices, swap(): return lax.ppermute(value, axes, [(i, i ^ mask) for i in range(count)])  47.8 us
    ppermute x45, waiting for transfers between devices, swap(): return lax.ppermute(value, axes, [(i, i ^ mask) for i in range(count)])  43.3 us
  transfers between devices with their start and end apart: 45, of which 24 were waited for; matrix products, arithmetic and copies ran while one was open for 0% of the time, Pallas kernels for 31%

profile of v4, /device:TPU:0, one launch (start us, length us, event | category | flops | bytes accessed | tf_op | source)
XLA Modules:
  0.0 155.1 jit_solution(11331320584570793320)
XLA Ops:
  0.7 1.9 %first_parts.1 = (bf16[768,128]{1,0:T(8,128)(2,1)S(1)}, bf16[624,256]{1,0:T(8,128)(2,1)S(1)}, bf16[624,256]{1,0:T(8,128)(2,1)S(1)}, s32[8,256]{1,0:T(8,128)S(1)}) custom-call(s32[3]{0:T(128)S(1)} %pad_add_fusion.s, bf16[1200,256]{1,0:T(8,128)(2,1)} %refs_0_.3, bf16[3,512,256]{2,1,0:T(8,128)(2,1)} %refs_2_.5, s32[1200]{0:T(1024)} %refs_2_.3), custom_call_target="tpu_custom_call" | custom-call | flops 200000000 | tf_op jit(solution)/shard_map/first_parts/pallas_call | solution.py:641
  2.7 3.0 %collective-permute-start = (bf16[624,256]{1,0:T(8,128)(2,1)S(1)}, bf16[624,256]{1,0:T(8,128)(2,1)S(1)}, u32[]{:S(2)}, u32[]{:S(2)}) collective-permute-start(bf16[624,256]{1,0:T(8,128)(2,1)S(1)} %get-tuple-element.109.refs_14_.refs_7_), channel_id=1, source_target_pairs={{0,1},{1,0},{2,3},{3,2},{4,5},{5,4},{6,7},{7,6},{8,9},{9,8},{10,11... | collective-permute-start | bytes 958472 | tf_op jit(solution)/shard_map/ppermute | solution.py:665
  5.8 1.8 %packs.1 = (bf16[1328,128]{1,0:T(8,128)(2,1)S(1)}, bf16[1536,128]{1,0:T(8,128)(2,1)S(1)}, f32[16,1024]{1,0:T(8,128)S(1)}) custom-call(s32[3]{0:T(128)S(1)} %pad_add_fusion.s, bf16[512,1024]{1,0:T(8,128)(2,1)} %refs_4_.1, bf16[256,512]{1,0:T(8,128)(2,1)} %refs_3_.3, bf16[1024,512]{1,0:T(8,128)(2,1)} %refs_5_.1, bf16[512,512]{1,0:T(8,128)(2,1)} %refs_6_.1, ...), custom_call_target="tpu_custom_call" | custom-call | flops 200000000 | tf_op jit(solution)/shard_map/packs/pallas_call | solution.py:641
  7.6 3.2 %cotangents.1 = (bf16[624,768]{1,0:T(8,128)(2,1)S(1)}, bf16[624,512]{1,0:T(8,128)(2,1)S(1)}, bf16[624,256]{1,0:T(8,128)(2,1)S(1)}, bf16[3,512,256]{2,1,0:T(8,128...) custom-call(s32[3]{0:T(128)S(1)} %pad_add_fusion.s, ...), custom_call_target="tpu_custom_call" | custom-call | flops 230000000 | tf_op jit(solution)/shard_map/cotangents/pallas_call | solution.py:641
  10.7 3.3 %collective-permute-done.refs_1_.refs_4_ = bf16[624,256]{1,0:T(8,128)(2,1)S(1)} collective-permute-done((bf16[624,256]{1,0:T(8,128)(2,1)S(1)}, bf16[624,256]{1,0:T(8,128)(2,1)S(1)}, u32[]{:S(2)}, u32[]{:S(2)}) %collective-permute-start) | collective-permute-done | bytes 319520 | tf_op jit(solution)/shard_map/ppermute | solution.py:665
  14.1 2.1 %collective-permute-start.5 = (bf16[1328,128]{1,0:T(8,128)(2,1)S(1)}, bf16[1328,128]{1,0:T(8,128)(2,1)S(1)}, u32[]{:S(2)}, u32[]{:S(2)}) collective-permute-start(bf16[1328,128]{1,0:T(8,128)(2,1)S(1)} %after_frames.1.refs_1_), channel_id=1, source_target_pairs={{0,1},{1,0},{2,3},{3,2},{4,5},{5,4},{6,7},{7,6},{8,9},{9,8},{10,11... | collective-permute-start | bytes 1019912 | tf_op jit(solution)/shard_map/ppermute | solution.py:665
  16.2 2.1 %collective-permute-done.1.refs_4_ = bf16[768,128]{1,0:T(8,128)(2,1)S(1)} collective-permute-done((bf16[768,128]{1,0:T(8,128)(2,1)S(1)}, bf16[768,128]{1,0:T(8,128)(2,1)S(1)}, u32[]{:S(2)}, u32[]{:S(2)}) %collective-permute-start.1) | collective-permute-done | bytes 196640 | tf_op jit(solution)/shard_map/ppermute | solution.py:665
  18.3 2.0 %collective-permute-start.2 = (bf16[768,128]{1,0:T(8,128)(2,1)S(1)}, bf16[768,128]{1,0:T(8,128)(2,1)S(1)}, u32[]{:S(2)}, u32[]{:S(2)}) collective-permute-start(bf16[768,128]{1,0:T(8,128)(2,1)S(1)} %collective-permute-done.1.refs_4_), channel_id=1, source_target_pairs={{0,4},{2,6},{4,0},{6,2},{8,12},{10,14},{12,8},{14,10},{16,20},{18,... | collective-permute-start | bytes 589832 | tf_op jit(solution)/shard_map/ppermute | solution.py:665
  20.3 3.6 %collective-permute-done.2.refs_5_.refs_2_ = bf16[768,128]{1,0:T(8,128)(2,1)S(1)} collective-permute-done((bf16[768,128]{1,0:T(8,128)(2,1)S(1)}, bf16[768,128]{1,0:T(8,128)(2,1)S(1)}, u32[]{:S(2)}, u32[]{:S(2)}) %collective-permute-start.2) | collective-permute-done | bytes 196640 | tf_op jit(solution)/shard_map/ppermute | solution.py:665
  24.0 2.1 %collective-permute-start.9 = (bf16[1536,128]{1,0:T(8,128)(2,1)S(1)}, bf16[1536,128]{1,0:T(8,128)(2,1)S(1)}, u32[]{:S(2)}, u32[]{:S(2)}) collective-permute-start(bf16[1536,128]{1,0:T(8,128)(2,1)S(1)} %after_one.1), channel_id=1, source_target_pairs={{0,1},{1,0},{2,3},{3,2},{4,5},{5,4},{6,7},{7,6},{8,9},{9,8},{10,11... | collective-permute-start | bytes 1179656 | tf_op jit(solution)/shard_map/ppermute | solution.py:665
  26.1 1.5 collective-permute-start.6
  27.6 5.6 %collective-permute-done.9.refs_11_.refs_1_.refs_8_ = bf16[1536,128]{1,0:T(8,128)(2,1)S(1)} collective-permute-done((bf16[1536,128]{1,0:T(8,128)(2,1)S(1)}, bf16[1536,128]{1,0:T(8,128)(2,1)S(1)}, u32[]{:S(2)}, u32[]{:S(2)}) %collective-permute-start.9) | collective-permute-done | bytes 393248 | tf_op jit(solution)/shard_map/ppermute | solution.py:665
  33.2 0.7 collective-permute-done.6.refs_8_.refs_2_.refs_5_
  34.0 1.5 collective-permute-start.13
  35.5 1.5 collective-permute-start.10
  37.5 0.9 collective-permute-done.3.refs_6_
  38.7 4.3 %attend.1 = (bf16[624,512]{1,0:T(8,128)(2,1)S(1)}, bf16[624,1536]{1,0:T(8,128)(2,1)S(1)}, bf16[624,512]{1,0:T(8,128)(2,1)S(1)}, bf16[3,512,256]{2,1,0:T(8,128)(2,1)S(1)}) custom-call(s32[3]{0:T(128)S(1)} %pad_add_fusion.s, bf16[624,256]{1,0:T(8,128)(2,1)S(1)} %get-tuple-element.108.refs_0_.refs_3_, ...), custom_call_target="tpu_custom_call" | custom-call | flops 550000000 | tf_op jit(solution)/shard_map/attend/pallas_call | solution.py:641
  44.2 1.7 %collective-permute-done.7.refs_9_.refs_6_ = bf16[1328,128]{1,0:T(8,128)(2,1)S(1)} collective-permute-done((bf16[1328,128]{1,0:T(8,128)(2,1)S(1)}, bf16[1328,128]{1,0:T(8,128)(2,1)S(1)}, u32[]{:S(2)}, u32[]{:S(2)}) %collective-permute-start.7) | collective-permute-done | bytes 340000 | tf_op jit(solution)/shard_map/ppermute | solution.py:665
  46.4 6.9 %feed.1 = (bf16[624,256]{1,0:T(8,128)(2,1)S(1)}, bf16[624,256]{1,0:T(8,128)(2,1)S(1)}, f32[624,512]{1,0:T(8,128)S(1)}, bf16[624,512]{1,0:T(8,128)(2,1)S(1)}, bf1...) custom-call(s32[3]{0:T(128)S(1)} %pad_add_fusion.s, ...), custom_call_target="tpu_custom_call" | custom-call | flops 720000000 | tf_op jit(solution)/shard_map/feed/pallas_call | solution.py:641
  53.2 0.9 collective-permute-done.13.refs_12_.refs_6_
  54.2 2.3 %prior.1 = (f32[624,512]{1,0:T(8,128)S(1)}, bf16[624,512]{1,0:T(8,128)(2,1)S(1)}, f32[3,512]{1,0:T(4,128)S(1)}, f32[1,1024]{1,0:T(1,128)S(1)}, bf16[512,512]{1,0:T(8,128)(2,1)S(1)}, /*index=5*/f32[1,512]{1,0:T(1,128)S(1)}) custom-call(s32[3]{0:T(128)S(1)} %pad_add_fusion.s, f32[624,512]{1,0:T(8,128)S(1)} %get-tuple-element.123.refs_0_, ...), custom_call_target="tpu_custom_call" | custom-call | flops 250000000 | tf_op jit(solution)/shard_map/prior/pallas_call | solution.py:641
  56.5 4.1 %feed_back.1 = (bf16[624,2048]{1,0:T(8,128)(2,1)S(1)}, f32[624,512]{1,0:T(8,128)S(1)}, bf16[624,512]{1,0:T(8,128)(2,1)S(1)}, f32[3,512]{1,0:T(4,128)S(1)}, f32[1,2048]{1,0:T(1,128)S(1)}) custom-call(s32[3]{0:T(128)S(1)} %pad_add_fusion.s, bf16[624,512]{1,0:T(8,128)(2,1)S(1)} %get-tuple-element.129.refs_0_.refs_1_, ...), custom_call_target="tpu_custom_call" | custom-call | flops 650000000 | tf_op jit(solution)/shard_map/feed_back/pallas_call | solution.py:641
  60.6 3.9 %up_grads.1 = (f32[4,1792,128]{2,1,0:T(8,128)S(1)}, bf16[4,1792,128]{2,1,0:T(8,128)(2,1)S(1)}) custom-call(s32[3]{0:T(128)S(1)} %pad_add_fusion.s, bf16[624,512]{1,0:T(8,128)(2,1)S(1)} %get-tuple-element.137.refs_0_, bf16[624,2048]{1,0:T(8,128)(2,1)S(1)} %get-tuple-element.138.refs_1_, bf16[624,512]{1,0:T(8,128)(2,1)S(1)} %get-tuple-element.114.refs_1_.refs_2_, ...), custom_call_target="tpu_custom_call" | custom-call | flops 300000000 | tf_op jit(solution)/shard_map/up_grads/pallas_call | solution.py:641
  64.7 2.4 %late_grads.1 = (f32[4,1024,128]{2,1,0:T(8,128)S(1)}, bf16[4,1024,128]{2,1,0:T(8,128)(2,1)S(1)}) custom-call(s32[3]{0:T(128)S(1)} %pad_add_fusion.s, bf16[624,2048]{1,0:T(8,128)(2,1)S(1)} %get-tuple-element.141.refs_0_, bf16[624,512]{1,0:T(8,128)(2,1)S(1)} %get-tuple-element.129.refs_0_.refs_1_, bf16[4,1792,128]{2,1,0:T(8,128)(2,1)S(1)} %get-tuple-element.140.refs_2_), custom_call_target="tpu_custom_call" | custom-call | flops 350000000 | tf_op jit(solution)/shard_map/late_grads/pallas_call | solution.py:641
  67.6 0.8 collective-permute-done.14.refs_1_
  68.4 0.9 up_core.1
  69.4 1.8 %collective-permute-start.17 = (bf16[1792,128]{1,0:T(8,128)(2,1)S(1)}, bf16[1792,128]{1,0:T(8,128)(2,1)S(1)}, u32[]{:S(2)}, u32[]{:S(2)}) collective-permute-start(bf16[1792,128]{1,0:T(8,128)(2,1)S(1)} %get-tuple-element.153), channel_id=1, source_target_pairs={{0,1},{1,0},{2,3},{3,2},{4,5},{5,4},{6,7},{7,6},{8,9},{9,8},{10,11... | collective-permute-start | bytes 1376264 | tf_op jit(solution)/shard_map/ppermute | solution.py:665
  71.1 1.2 collective-permute-start.18
  72.9 3.7 %attend_back_0.1.refs_2_.refs_1_.refs_0_ = bf16[624,768]{1,0:T(8,128)(2,1)S(1)} custom-call(s32[3]{0:T(128)S(1)} %pad_add_fusion.s, bf16[624,512]{1,0:T(8,128)(2,1)S(1)} %get-tuple-element.135.refs_3_.refs_0_, bf16[624,1536]{1,0:T(8,128)(2,1)S(1)} %get-tuple-element.136.refs_1_, bf16[256,512]{1,0:T(8,128)(2,1)S(1)} %get-tuple-element.115.refs_4_.refs_2_, ...), custom_call_target="tpu_custom_call" | custom-call | flops 450000000 | tf_op jit(solution)/shard_map/attend_back_0/pallas_call | solution.py:641
  76.7 0.8 late_core.1
  77.4 1.8 %collective-permute-start.22 = (bf16[1024,128]{1,0:T(8,128)(2,1)S(1)}, bf16[1024,128]{1,0:T(8,128)(2,1)S(1)}, u32[]{:S(2)}, u32[]{:S(2)}) collective-permute-start(bf16[1024,128]{1,0:T(8,128)(2,1)S(1)} %get-tuple-element.146.refs_4_), channel_id=1, source_target_pairs={{0,4},{2,6},{4,0},{6,2},{8,12},{10,14},{12,8},{14,10},{16,20},{18,... | collective-permute-start | bytes 786440 | tf_op jit(solution)/shard_map/ppermute | solution.py:665
  79.2 3.8 %attend_back_1.1.refs_2_.refs_1_ = bf16[624,768]{1,0:T(8,128)(2,1)S(1)} custom-call(s32[3]{0:T(128)S(1)} %pad_add_fusion.s, bf16[624,512]{1,0:T(8,128)(2,1)S(1)} %get-tuple-element.135.refs_3_.refs_0_, bf16[624,1536]{1,0:T(8,128)(2,1)S(1)} %get-tuple-element.136.refs_1_, bf16[256,512]{1,0:T(8,128)(2,1)S(1)} %get-tuple-element.144.refs_2_, ...), custom_call_target="tpu_custom_call" | custom-call | flops 450000000 | tf_op jit(solution)/shard_map/attend_back_1/pallas_call | solution.py:641
  83.0 2.0 %early_grads.1 = (f32[4,768,128]{2,1,0:T(8,128)S(1)}, bf16[4,768,128]{2,1,0:T(8,128)(2,1)S(1)}) custom-call(s32[3]{0:T(128)S(1)} %pad_add_fusion.s, bf16[624,512]{1,0:T(8,128)(2,1)S(1)} %get-tuple-element.149.refs_0_, bf16[624,768]{1,0:T(8,128)(2,1)S(1)} %attend_back_0.1.refs_2_.refs_1_.refs_0_, bf16[624,768]{1,0:T(8,128)(2,1)S(1)} %attend_back_1.1.refs_2_.refs_1_), custom_call_target="tpu_custom_call" | custom-call | flops 200000000 | tf_op jit(solution)/shard_map/early_grads/pallas_call | solution.py:641
  85.1 2.3 %frames_back.1 = (bf16[624,256]{1,0:T(8,128)(2,1)S(1)}, f32[624,256]{1,0:T(8,128)S(1)}, f32[2,512]{1,0:T(2,128)S(1)}) custom-call(s32[3]{0:T(128)S(1)} %pad_add_fusion.s, bf16[624,768]{1,0:T(8,128)(2,1)S(1)} %attend_back_0.1.refs_2_.refs_1_.refs_0_, bf16[624,768]{1,0:T(8,128)(2,1)S(1)} %attend_back_1.1.refs_2_.refs_1_, ...), custom_call_target="tpu_custom_call" | custom-call | flops 250000000 | tf_op jit(solution)/shard_map/frames_back/pallas_call | solution.py:641
  87.4 4.4 %collective-permute-done.17.refs_2_ = bf16[1792,128]{1,0:T(8,128)(2,1)S(1)} collective-permute-done((bf16[1792,128]{1,0:T(8,128)(2,1)S(1)}, bf16[1792,128]{1,0:T(8,128)(2,1)S(1)}, u32[]{:S(2)}, u32[]{:S(2)}) %collective-permute-start.17) | collective-permute-done | bytes 458784 | tf_op jit(solution)/shard_map/ppermute | solution.py:665
  91.8 1.7 %collective-permute-start.23 = (bf16[1024,128]{1,0:T(8,128)(2,1)S(1)}, bf16[1024,128]{1,0:T(8,128)(2,1)S(1)}, u32[]{:S(2)}, u32[]{:S(2)}) collective-permute-start(bf16[1024,128]{1,0:T(8,128)(2,1)S(1)} %get-tuple-element.165), channel_id=1, source_target_pairs={{0,1},{1,0},{2,3},{3,2},{4,5},{5,4},{6,7},{7,6},{8,9},{9,8},{10,11... | collective-permute-start | bytes 786440 | tf_op jit(solution)/shard_map/ppermute | solution.py:665
  93.5 1.2 collective-permute-start.24
  94.8 0.9 up_1.1
  95.7 1.6 %collective-permute-start.19 = (bf16[896,128]{1,0:T(8,128)(2,1)S(1)}, bf16[896,128]{1,0:T(8,128)(2,1)S(1)}, u32[]{:S(2)}, u32[]{:S(2)}) collective-permute-start(bf16[896,128]{1,0:T(8,128)(2,1)S(1)} %get-tuple-element.157), channel_id=1, source_target_pairs={{0,8},{2,10},{4,12},{6,14},{8,0},{10,2},{12,4},{14,6},{16,24},{18,... | collective-permute-start | bytes 688136 | tf_op jit(solution)/shard_map/ppermute | solution.py:665
  97.4 0.8 early_core.1
  98.1 0.9 collective-permute-start.28
  99.0 3.0 %collective-permute-done.19.refs_1_ = bf16[896,128]{1,0:T(8,128)(2,1)S(1)} collective-permute-done((bf16[896,128]{1,0:T(8,128)(2,1)S(1)}, bf16[896,128]{1,0:T(8,128)(2,1)S(1)}, u32[]{:S(2)}, u32[]{:S(2)}) %collective-permute-start.19) | collective-permute-done | bytes 229408 | tf_op jit(solution)/shard_map/ppermute | solution.py:665
  102.6 2.7 %collective-permute-start.21 = (bf16[896,128]{1,0:T(8,128)(2,1)S(1)}, bf16[896,128]{1,0:T(8,128)(2,1)S(1)}, u32[]{:S(2)}, u32[]{:S(2)}) collective-permute-start(bf16[896,128]{1,0:T(8,128)(2,1)S(1)} %up_2.1.refs_4_.refs_0_), channel_id=1, source_target_pairs={{0,16},{2,18},{4,20},{6,22},{8,24},{10,26},{12,28},{14,30},{16,0},... | collective-permute-start | bytes 688136 | tf_op jit(solution)/shard_map/ppermute | solution.py:665
  105.3 1.2 collective-permute-done.24.refs_3_
  106.5 0.8 late_1.1
  107.3 1.6 %collective-permute-start.27 = (bf16[512,128]{1,0:T(8,128)(2,1)S(1)}, bf16[512,128]{1,0:T(8,128)(2,1)S(1)}, u32[]{:S(2)}, u32[]{:S(2)}) collective-permute-start(bf16[512,128]{1,0:T(8,128)(2,1)S(1)} %get-tuple-element.172), channel_id=1, source_target_pairs={{0,8},{2,10},{4,12},{6,14},{8,0},{10,2},{12,4},{14,6},{16,24},{18,... | collective-permute-start | bytes 393224 | tf_op jit(solution)/shard_map/ppermute | solution.py:665
  109.5 2.4 %collective-permute-start.30 = (bf16[832,128]{1,0:T(8,128)(2,1)S(1)}, bf16[832,128]{1,0:T(8,128)(2,1)S(1)}, u32[]{:S(2)}, u32[]{:S(2)}) collective-permute-start(bf16[832,128]{1,0:T(8,128)(2,1)S(1)} %get-tuple-element.175), channel_id=1, source_target_pairs={{0,5},{1,4},{2,7},{3,6},{4,1},{5,0},{6,3},{7,2},{8,13},{9,12},{10,... | collective-permute-start | bytes 638984 | tf_op jit(solution)/shard_map/ppermute | solution.py:665
  111.9 2.1 %collective-permute-done.21.refs_1_ = bf16[896,128]{1,0:T(8,128)(2,1)S(1)} collective-permute-done((bf16[896,128]{1,0:T(8,128)(2,1)S(1)}, bf16[896,128]{1,0:T(8,128)(2,1)S(1)}, u32[]{:S(2)}, u32[]{:S(2)}) %collective-permute-start.21) | collective-permute-done | bytes 229408 | tf_op jit(solution)/shard_map/ppermute | solution.py:665
  115.3 1.4 logits.1
  116.7 1.7 %collective-permute-done.29.refs_2_ = bf16[832,128]{1,0:T(8,128)(2,1)S(1)} collective-permute-done((bf16[832,128]{1,0:T(8,128)(2,1)S(1)}, bf16[832,128]{1,0:T(8,128)(2,1)S(1)}, u32[]{:S(2)}, u32[]{:S(2)}) %collective-permute-start.29) | collective-permute-done | bytes 213024 | tf_op jit(solution)/shard_map/ppermute | solution.py:665
  118.8 0.7 early_1.1
  119.5 1.0 collective-permute-start.34
  121.2 2.2 %collective-permute-start.36 = (bf16[512,128]{1,0:T(8,128)(2,1)S(1)}, bf16[512,128]{1,0:T(8,128)(2,1)S(1)}, u32[]{:S(2)}, u32[]{:S(2)}) collective-permute-start(bf16[512,128]{1,0:T(8,128)(2,1)S(1)} %late_2.1.refs_2_.refs_0_), channel_id=1, source_target_pairs={{0,16},{2,18},{4,20},{6,22},{8,24},{10,26},{12,28},{14,30},{16,0},... | collective-permute-start | bytes 393224 | tf_op jit(solution)/shard_map/ppermute | solution.py:665
  124.1 1.5 collective-permute-start.31
  126.2 2.1 %collective-permute-start.35 = (bf16[416,128]{1,0:T(8,128)(2,1)S(1)}, bf16[416,128]{1,0:T(8,128)(2,1)S(1)}, u32[]{:S(2)}, u32[]{:S(2)}) collective-permute-start(bf16[416,128]{1,0:T(8,128)(2,1)S(1)} %early_2.1.refs_2_.refs_0_), channel_id=1, source_target_pairs={{0,16},{2,18},{4,20},{6,22},{8,24},{10,26},{12,28},{14,30},{16,0},... | collective-permute-start | bytes 319496 | tf_op jit(solution)/shard_map/ppermute | solution.py:665
  129.3 2.7 %collective-permute-start.38 = (bf16[512,128]{1,0:T(8,128)(2,1)S(1)}, bf16[512,128]{1,0:T(8,128)(2,1)S(1)}, u32[]{:S(2)}, u32[]{:S(2)}) collective-permute-start(bf16[512,128]{1,0:T(8,128)(2,1)S(1)} %late_3.1.refs_2_.refs_0_), channel_id=1, source_target_pairs={{0,8},{2,10},{4,12},{6,14},{8,0},{10,2},{12,4},{14,6},{16,24},{18,... | collective-permute-start | bytes 393224 | tf_op jit(solution)/shard_map/ppermute | solution.py:665
  132.0 2.5 %collective-permute-done.35.refs_1_ = bf16[416,128]{1,0:T(8,128)(2,1)S(1)} collective-permute-done((bf16[416,128]{1,0:T(8,128)(2,1)S(1)}, bf16[416,128]{1,0:T(8,128)(2,1)S(1)}, u32[]{:S(2)}, u32[]{:S(2)}) %collective-permute-start.35) | collective-permute-done | bytes 106528 | tf_op jit(solution)/shard_map/ppermute | solution.py:665
  136.5 1.1 collective-permute-start.42
  137.8 2.1 %collective-permute-done.37.refs_1_ = bf16[416,128]{1,0:T(8,128)(2,1)S(1)} collective-permute-done((bf16[416,128]{1,0:T(8,128)(2,1)S(1)}, bf16[416,128]{1,0:T(8,128)(2,1)S(1)}, u32[]{:S(2)}, u32[]{:S(2)}) %collective-permute-start.37) | collective-permute-done | bytes 106528 | tf_op jit(solution)/shard_map/ppermute | solution.py:665
  141.1 2.8 %up_place.1 = (f32[512,1024]{1,0:T(8,128)}, f32[256,512]{1,0:T(8,128)}, f32[512,512]{1,0:T(8,128)}, f32[8,128]{1,0:T(8,128)S(1)}) custom-call(s32[3]{0:T(128)S(1)} %pad_add_fusion.s, bf16[1792,128]{1,0:T(8,128)(2,1)S(1)} %up_4.1.refs_2_.refs_0_, bf16[1792,128]{1,0:T(8,128)(2,1)S(1)} %collective-permute-done.31.refs_1_, ...), custom_call_target="tpu_custom_call" | custom-call | flops 10000000000 | tf_op jit(solution)/shard_map/up_place/pallas_call | solution.py:641
  143.9 3.2 %collective-permute-done.25.refs_1_.refs_3_.refs_5_ = bf16[624,1024]{1,0:T(8,128)(2,1)S(1)} collective-permute-done((bf16[624,1024]{1,0:T(8,128)(2,1)S(1)}, bf16[624,1024]{1,0:T(8,128)(2,1)S(1)}, u32[]{:S(2)}, u32[]{:S(2)}) %collective-permute-start.25) | collective-permute-done | bytes 1277984 | tf_op jit(solution)/shard_map/ppermute | solution.py:665
  147.1 2.8 %rows_back.1 = (f32[1200,512]{1,0:T(8,128)}, f32[1200,256]{1,0:T(8,128)}, bf16[1200,256]{1,0:T(8,128)(2,1)}, f32[8,128]{1,0:T(8,128)S(1)}) custom-call(s32[3]{0:T(128)S(1)} %pad_add_fusion.s, f32[624,512]{1,0:T(8,128)S(1)} %get-tuple-element.168.refs_0_, bf16[624,1024]{1,0:T(8,128)(2,1)S(1)} %collective-permute-done.25.refs_1_.refs_3_.refs_5_, ...), custom_call_target="tpu_custom_call" | custom-call | flops 10000000000 | tf_op jit(solution)/shard_map/rows_back/pallas_call | solution.py:641
  150.7 1.2 collective-permute-done.40.refs_2_
  152.2 2.7 %last_place.1 = (f32[3,512,256]{2,1,0:T(8,128)}, f32[1024,512]{1,0:T(8,128)}, f32[1,512]{1,0:T(1,128)}, f32[1,512]{1,0:T(1,128)}, f32[1,512]{1,0:T(1,128)}, /*in...) custom-call(s32[3]{0:T(128)S(1)} %pad_add_fusion.s, ...), custom_call_target="tpu_custom_call" | custom-call | flops 10000000000 | tf_op jit(solution)/shard_map/last_place/pallas_call | solution.py:641
  (65 shorter events, 14.2 us)
Async XLA Ops:
  2.7 11.4 %collective-permute-start = (bf16[624,256]{1,0:T(8,128)(2,1)S(1)}, bf16[624,256]{1,0:T(8,128)(2,1)S(1)}, u32[]{:S(2)}, u32[]{:S(2)}) collective-permute-start(bf16[624,256]{1,0:T(8,128)(2,1)S(1)} %get-tuple-element.109.refs_14_.refs_7_), channel_id=1, source_target_pairs={{0,1},{1,0},{2,3},{3,2},{4,5},{5,4},{6,7},{7,6},{8,9},{9,8},{10,11... | collective-permute-start | bytes 958472 | tf_op jit(solution)/shard_map/ppermute | solution.py:665
  5.7 12.6 %collective-permute-start.1 = (bf16[768,128]{1,0:T(8,128)(2,1)S(1)}, bf16[768,128]{1,0:T(8,128)(2,1)S(1)}, u32[]{:S(2)}, u32[]{:S(2)}) collective-permute-start(bf16[768,128]{1,0:T(8,128)(2,1)S(1)} %get-tuple-element.112), channel_id=1, source_target_pairs={{0,1},{1,0},{2,3},{3,2},{4,5},{5,4},{6,7},{7,6},{8,9},{9,8},{10,11... | collective-permute-start | bytes 589832 | tf_op jit(solution)/shard_map/ppermute | solution.py:665
  14.1 12.0 %collective-permute-start.5 = (bf16[1328,128]{1,0:T(8,128)(2,1)S(1)}, bf16[1328,128]{1,0:T(8,128)(2,1)S(1)}, u32[]{:S(2)}, u32[]{:S(2)}) collective-permute-start(bf16[1328,128]{1,0:T(8,128)(2,1)S(1)} %after_frames.1.refs_1_), channel_id=1, source_target_pairs={{0,1},{1,0},{2,3},{3,2},{4,5},{5,4},{6,7},{7,6},{8,9},{9,8},{10,11... | collective-permute-start | bytes 1019912 | tf_op jit(solution)/shard_map/ppermute | solution.py:665
  18.3 5.7 %collective-permute-start.2 = (bf16[768,128]{1,0:T(8,128)(2,1)S(1)}, bf16[768,128]{1,0:T(8,128)(2,1)S(1)}, u32[]{:S(2)}, u32[]{:S(2)}) collective-permute-start(bf16[768,128]{1,0:T(8,128)(2,1)S(1)} %collective-permute-done.1.refs_4_), channel_id=1, source_target_pairs={{0,4},{2,6},{4,0},{6,2},{8,12},{10,14},{12,8},{14,10},{16,20},{18,... | collective-permute-start | bytes 589832 | tf_op jit(solution)/shard_map/ppermute | solution.py:665
  24.0 9.2 %collective-permute-start.9 = (bf16[1536,128]{1,0:T(8,128)(2,1)S(1)}, bf16[1536,128]{1,0:T(8,128)(2,1)S(1)}, u32[]{:S(2)}, u32[]{:S(2)}) collective-permute-start(bf16[1536,128]{1,0:T(8,128)(2,1)S(1)} %after_one.1), channel_id=1, source_target_pairs={{0,1},{1,0},{2,3},{3,2},{4,5},{5,4},{6,7},{7,6},{8,9},{9,8},{10,11... | collective-permute-start | bytes 1179656 | tf_op jit(solution)/shard_map/ppermute | solution.py:665
  26.1 7.8 %collective-permute-start.6 = (bf16[1328,128]{1,0:T(8,128)(2,1)S(1)}, bf16[1328,128]{1,0:T(8,128)(2,1)S(1)}, u32[]{:S(2)}, u32[]{:S(2)}) collective-permute-start(bf16[1328,128]{1,0:T(8,128)(2,1)S(1)} %collective-permute-done.5.refs_7_.refs_4_), channel_id=1, source_target_pairs={{0,4},{2,6},{4,0},{6,2},{8,12},{10,14},{12,8},{14,10},{16,20},{18,... | collective-permute-start | bytes 1019912 | tf_op jit(solution)/shard_map/ppermute | solution.py:665
  34.0 20.2 %collective-permute-start.13 = (bf16[624,768]{1,0:T(8,128)(2,1)S(1)}, bf16[624,768]{1,0:T(8,128)(2,1)S(1)}, u32[]{:S(2)}, u32[]{:S(2)}) collective-permute-start(bf16[624,768]{1,0:T(8,128)(2,1)S(1)} %after_two.1), channel_id=1, source_target_pairs={{0,1},{1,0},{2,3},{3,2},{4,5},{5,4},{6,7},{7,6},{8,9},{9,8},{10,11... | collective-permute-start | bytes 2875400 | tf_op jit(solution)/shard_map/ppermute | solution.py:665
  35.5 8.0 %collective-permute-start.10 = (bf16[1536,128]{1,0:T(8,128)(2,1)S(1)}, bf16[1536,128]{1,0:T(8,128)(2,1)S(1)}, u32[]{:S(2)}, u32[]{:S(2)}) collective-permute-start(bf16[1536,128]{1,0:T(8,128)(2,1)S(1)} %collective-permute-done.9.refs_11_.refs_1_.refs_8_), channel_id=1, source_target_pairs={{0,4},{2,6},{4,0},{6,2},{8,12},{10,14},{12,8},{14,10},{16,20},{18,... | collective-permute-start | bytes 1179656 | tf_op jit(solution)/shard_map/ppermute | solution.py:665
  37.0 1.4 collective-permute-start.3
  37.0 1.7 %collective-permute-start.4 = (bf16[768,128]{1,0:T(8,128)(2,1)S(1)}, bf16[768,128]{1,0:T(8,128)(2,1)S(1)}, u32[]{:S(2)}, u32[]{:S(2)}) collective-permute-start(bf16[768,128]{1,0:T(8,128)(2,1)S(1)} %collective-permute-done.2.refs_5_.refs_2_), channel_id=1, source_target_pairs={{0,2},{2,0},{4,6},{6,4},{8,10},{10,8},{12,14},{14,12},{16,18},{18,... | collective-permute-start | bytes 589832 | tf_op jit(solution)/shard_map/ppermute | solution.py:665
  43.0 2.8 %collective-permute-start.11 = (bf16[1536,128]{1,0:T(8,128)(2,1)S(1)}, bf16[1536,128]{1,0:T(8,128)(2,1)S(1)}, u32[]{:S(2)}, u32[]{:S(2)}) collective-permute-start(bf16[1536,128]{1,0:T(8,128)(2,1)S(1)} %collective-permute-done.9.refs_11_.refs_1_.refs_8_), channel_id=1, source_target_pairs={{0,2},{2,0},{4,6},{6,4},{8,10},{10,8},{12,14},{14,12},{16,18},{18,... | collective-permute-start | bytes 1179656 | tf_op jit(solution)/shard_map/ppermute | solution.py:665
  43.5 2.8 %collective-permute-start.12 = (bf16[1536,128]{1,0:T(8,128)(2,1)S(1)}, bf16[1536,128]{1,0:T(8,128)(2,1)S(1)}, u32[]{:S(2)}, u32[]{:S(2)}) collective-permute-start(bf16[1536,128]{1,0:T(8,128)(2,1)S(1)} %after_attend.1.refs_12_.refs_9_), channel_id=1, source_target_pairs={{0,2},{2,0},{4,6},{6,4},{8,10},{10,8},{12,14},{14,12},{16,18},{18,... | collective-permute-start | bytes 1179656 | tf_op jit(solution)/shard_map/ppermute | solution.py:665
  43.7 2.2 %collective-permute-start.7 = (bf16[1328,128]{1,0:T(8,128)(2,1)S(1)}, bf16[1328,128]{1,0:T(8,128)(2,1)S(1)}, u32[]{:S(2)}, u32[]{:S(2)}) collective-permute-start(bf16[1328,128]{1,0:T(8,128)(2,1)S(1)} %collective-permute-done.5.refs_7_.refs_4_), channel_id=1, source_target_pairs={{0,2},{2,0},{4,6},{6,4},{8,10},{10,8},{12,14},{14,12},{16,18},{18,... | collective-permute-start | bytes 1019912 | tf_op jit(solution)/shard_map/ppermute | solution.py:665
  44.1 2.2 %collective-permute-start.8 = (bf16[1328,128]{1,0:T(8,128)(2,1)S(1)}, bf16[1328,128]{1,0:T(8,128)(2,1)S(1)}, u32[]{:S(2)}, u32[]{:S(2)}) collective-permute-start(bf16[1328,128]{1,0:T(8,128)(2,1)S(1)} %collective-permute-done.6.refs_8_.refs_2_.refs_5_), channel_id=1, source_target_pairs={{0,2},{2,0},{4,6},{6,4},{8,10},{10,8},{12,14},{14,12},{16,18},{18,... | collective-permute-start | bytes 1019912 | tf_op jit(solution)/shard_map/ppermute | solution.py:665
  64.6 3.9 %collective-permute-start.14 = (bf16[4,1792,128]{2,1,0:T(8,128)(2,1)S(1)}, bf16[4,1792,128]{2,1,0:T(8,128)(2,1)S(1)}, u32[]{:S(2)}, u32[]{:S(2)}) collective-permute-start(bf16[4,1792,128]{2,1,0:T(8,128)(2,1)S(1)} %get-tuple-element.140.refs_2_), channel_id=1, source_target_pairs={{0,2},{2,0},{4,6},{6,4},{8,10},{10,8},{12,14},{14,12},{16,18},{18,... | collective-permute-start | bytes 5505032 | tf_op jit(solution)/shard_map/ppermute | solution.py:665
  67.1 9.6 %collective-permute-start.15 = (bf16[4,1024,128]{2,1,0:T(8,128)(2,1)S(1)}, bf16[4,1024,128]{2,1,0:T(8,128)(2,1)S(1)}, u32[]{:S(2)}, u32[]{:S(2)}) collective-permute-start(bf16[4,1024,128]{2,1,0:T(8,128)(2,1)S(1)} %get-tuple-element.142.refs_2_), channel_id=1, source_target_pairs={{0,2},{2,0},{4,6},{6,4},{8,10},{10,8},{12,14},{14,12},{16,18},{18,... | collective-permute-start | bytes 3145736 | tf_op jit(solution)/shard_map/ppermute | solution.py:665
  69.4 22.5 %collective-permute-start.17 = (bf16[1792,128]{1,0:T(8,128)(2,1)S(1)}, bf16[1792,128]{1,0:T(8,128)(2,1)S(1)}, u32[]{:S(2)}, u32[]{:S(2)}) collective-permute-start(bf16[1792,128]{1,0:T(8,128)(2,1)S(1)} %get-tuple-element.153), channel_id=1, source_target_pairs={{0,1},{1,0},{2,3},{3,2},{4,5},{5,4},{6,7},{7,6},{8,9},{9,8},{10,11... | collective-permute-start | bytes 1376264 | tf_op jit(solution)/shard_map/ppermute | solution.py:665
  71.1 22.4 %collective-permute-start.18 = (bf16[1792,128]{1,0:T(8,128)(2,1)S(1)}, bf16[1792,128]{1,0:T(8,128)(2,1)S(1)}, u32[]{:S(2)}, u32[]{:S(2)}) collective-permute-start(bf16[1792,128]{1,0:T(8,128)(2,1)S(1)} %get-tuple-element.154), channel_id=1, source_target_pairs={{0,5},{1,4},{2,7},{3,6},{4,1},{5,0},{6,3},{7,2},{8,13},{9,12},{10,... | collective-permute-start | bytes 1376264 | tf_op jit(solution)/shard_map/ppermute | solution.py:665
  72.4 22.4 %collective-permute-start.16 = (bf16[1792,128]{1,0:T(8,128)(2,1)S(1)}, bf16[1792,128]{1,0:T(8,128)(2,1)S(1)}, u32[]{:S(2)}, u32[]{:S(2)}) collective-permute-start(bf16[1792,128]{1,0:T(8,128)(2,1)S(1)} %get-tuple-element.143.refs_4_), channel_id=1, source_target_pairs={{0,4},{2,6},{4,0},{6,2},{8,12},{10,14},{12,8},{14,10},{16,20},{18,... | collective-permute-start | bytes 1376264 | tf_op jit(solution)/shard_map/ppermute | solution.py:665
  77.4 29.1 %collective-permute-start.22 = (bf16[1024,128]{1,0:T(8,128)(2,1)S(1)}, bf16[1024,128]{1,0:T(8,128)(2,1)S(1)}, u32[]{:S(2)}, u32[]{:S(2)}) collective-permute-start(bf16[1024,128]{1,0:T(8,128)(2,1)S(1)} %get-tuple-element.146.refs_4_), channel_id=1, source_target_pairs={{0,4},{2,6},{4,0},{6,2},{8,12},{10,14},{12,8},{14,10},{16,20},{18,... | collective-permute-start | bytes 786440 | tf_op jit(solution)/shard_map/ppermute | solution.py:665
  85.0 12.4 %collective-permute-start.20 = (bf16[4,768,128]{2,1,0:T(8,128)(2,1)S(1)}, bf16[4,768,128]{2,1,0:T(8,128)(2,1)S(1)}, u32[]{:S(2)}, u32[]{:S(2)}) collective-permute-start(bf16[4,768,128]{2,1,0:T(8,128)(2,1)S(1)} %get-tuple-element.150.refs_8_), channel_id=1, source_target_pairs={{0,2},{2,0},{4,6},{6,4},{8,10},{10,8},{12,14},{14,12},{16,18},{18,... | collective-permute-start | bytes 2359304 | tf_op jit(solution)/shard_map/ppermute | solution.py:665
  91.8 13.5 %collective-permute-start.23 = (bf16[1024,128]{1,0:T(8,128)(2,1)S(1)}, bf16[1024,128]{1,0:T(8,128)(2,1)S(1)}, u32[]{:S(2)}, u32[]{:S(2)}) collective-permute-start(bf16[1024,128]{1,0:T(8,128)(2,1)S(1)} %get-tuple-element.165), channel_id=1, source_target_pairs={{0,1},{1,0},{2,3},{3,2},{4,5},{5,4},{6,7},{7,6},{8,9},{9,8},{10,11... | collective-permute-start | bytes 786440 | tf_op jit(solution)/shard_map/ppermute | solution.py:665
  93.5 13.0 %collective-permute-start.24 = (bf16[1024,128]{1,0:T(8,128)(2,1)S(1)}, bf16[1024,128]{1,0:T(8,128)(2,1)S(1)}, u32[]{:S(2)}, u32[]{:S(2)}) collective-permute-start(bf16[1024,128]{1,0:T(8,128)(2,1)S(1)} %get-tuple-element.166), channel_id=1, source_target_pairs={{0,5},{1,4},{2,7},{3,6},{4,1},{5,0},{6,3},{7,2},{8,13},{9,12},{10,... | collective-permute-start | bytes 786440 | tf_op jit(solution)/shard_map/ppermute | solution.py:665
  95.7 6.3 %collective-permute-start.19 = (bf16[896,128]{1,0:T(8,128)(2,1)S(1)}, bf16[896,128]{1,0:T(8,128)(2,1)S(1)}, u32[]{:S(2)}, u32[]{:S(2)}) collective-permute-start(bf16[896,128]{1,0:T(8,128)(2,1)S(1)} %get-tuple-element.157), channel_id=1, source_target_pairs={{0,8},{2,10},{4,12},{6,14},{8,0},{10,2},{12,4},{14,6},{16,24},{18,... | collective-permute-start | bytes 688136 | tf_op jit(solution)/shard_map/ppermute | solution.py:665
  98.1 20.7 %collective-permute-start.28 = (bf16[832,128]{1,0:T(8,128)(2,1)S(1)}, bf16[832,128]{1,0:T(8,128)(2,1)S(1)}, u32[]{:S(2)}, u32[]{:S(2)}) collective-permute-start(bf16[832,128]{1,0:T(8,128)(2,1)S(1)} %get-tuple-element.163.refs_2_), channel_id=1, source_target_pairs={{0,4},{2,6},{4,0},{6,2},{8,12},{10,14},{12,8},{14,10},{16,20},{18,... | collective-permute-start | bytes 638984 | tf_op jit(solution)/shard_map/ppermute | solution.py:665
  102.6 11.3 %collective-permute-start.21 = (bf16[896,128]{1,0:T(8,128)(2,1)S(1)}, bf16[896,128]{1,0:T(8,128)(2,1)S(1)}, u32[]{:S(2)}, u32[]{:S(2)}) collective-permute-start(bf16[896,128]{1,0:T(8,128)(2,1)S(1)} %up_2.1.refs_4_.refs_0_), channel_id=1, source_target_pairs={{0,16},{2,18},{4,20},{6,22},{8,24},{10,26},{12,28},{14,30},{16,0},... | collective-permute-start | bytes 688136 | tf_op jit(solution)/shard_map/ppermute | solution.py:665
  107.3 13.3 %collective-permute-start.27 = (bf16[512,128]{1,0:T(8,128)(2,1)S(1)}, bf16[512,128]{1,0:T(8,128)(2,1)S(1)}, u32[]{:S(2)}, u32[]{:S(2)}) collective-permute-start(bf16[512,128]{1,0:T(8,128)(2,1)S(1)} %get-tuple-element.172), channel_id=1, source_target_pairs={{0,8},{2,10},{4,12},{6,14},{8,0},{10,2},{12,4},{14,6},{16,24},{18,... | collective-permute-start | bytes 393224 | tf_op jit(solution)/shard_map/ppermute | solution.py:665
  108.9 9.4 %collective-permute-start.29 = (bf16[832,128]{1,0:T(8,128)(2,1)S(1)}, bf16[832,128]{1,0:T(8,128)(2,1)S(1)}, u32[]{:S(2)}, u32[]{:S(2)}) collective-permute-start(bf16[832,128]{1,0:T(8,128)(2,1)S(1)} %get-tuple-element.174), channel_id=1, source_target_pairs={{0,1},{1,0},{2,3},{3,2},{4,5},{5,4},{6,7},{7,6},{8,9},{9,8},{10,11... | collective-permute-start | bytes 638984 | tf_op jit(solution)/shard_map/ppermute | solution.py:665
  109.5 9.3 %collective-permute-start.30 = (bf16[832,128]{1,0:T(8,128)(2,1)S(1)}, bf16[832,128]{1,0:T(8,128)(2,1)S(1)}, u32[]{:S(2)}, u32[]{:S(2)}) collective-permute-start(bf16[832,128]{1,0:T(8,128)(2,1)S(1)} %get-tuple-element.175), channel_id=1, source_target_pairs={{0,5},{1,4},{2,7},{3,6},{4,1},{5,0},{6,3},{7,2},{8,13},{9,12},{10,... | collective-permute-start | bytes 638984 | tf_op jit(solution)/shard_map/ppermute | solution.py:665
  114.6 8.8 %collective-permute-start.26 = (bf16[896,128]{1,0:T(8,128)(2,1)S(1)}, bf16[896,128]{1,0:T(8,128)(2,1)S(1)}, u32[]{:S(2)}, u32[]{:S(2)}) collective-permute-start(bf16[896,128]{1,0:T(8,128)(2,1)S(1)} %up_3.1.refs_7_.refs_0_), channel_id=1, source_target_pairs={{0,8},{2,10},{4,12},{6,14},{8,0},{10,2},{12,4},{14,6},{16,24},{18,... | collective-permute-start | bytes 688136 | tf_op jit(solution)/shard_map/ppermute | solution.py:665
  118.3 28.8 %collective-permute-start.25 = (bf16[624,1024]{1,0:T(8,128)(2,1)S(1)}, bf16[624,1024]{1,0:T(8,128)(2,1)S(1)}, u32[]{:S(2)}, u32[]{:S(2)}) collective-permute-start(bf16[624,1024]{1,0:T(8,128)(2,1)S(1)} %get-tuple-element.169.refs_4_), channel_id=1, source_target_pairs={{0,1},{1,0},{2,3},{3,2},{4,5},{5,4},{6,7},{7,6},{8,9},{9,8},{10,11... | collective-permute-start | bytes 3833864 | tf_op jit(solution)/shard_map/ppermute | solution.py:665
  119.5 6.0 %collective-permute-start.34 = (bf16[416,128]{1,0:T(8,128)(2,1)S(1)}, bf16[416,128]{1,0:T(8,128)(2,1)S(1)}, u32[]{:S(2)}, u32[]{:S(2)}) collective-permute-start(bf16[416,128]{1,0:T(8,128)(2,1)S(1)} %get-tuple-element.177), channel_id=1, source_target_pairs={{0,8},{2,10},{4,12},{6,14},{8,0},{10,2},{12,4},{14,6},{16,24},{18,... | collective-permute-start | bytes 319496 | tf_op jit(solution)/shard_map/ppermute | solution.py:665
  121.2 7.6 %collective-permute-start.36 = (bf16[512,128]{1,0:T(8,128)(2,1)S(1)}, bf16[512,128]{1,0:T(8,128)(2,1)S(1)}, u32[]{:S(2)}, u32[]{:S(2)}) collective-permute-start(bf16[512,128]{1,0:T(8,128)(2,1)S(1)} %late_2.1.refs_2_.refs_0_), channel_id=1, source_target_pairs={{0,16},{2,18},{4,20},{6,22},{8,24},{10,26},{12,28},{14,30},{16,0},... | collective-permute-start | bytes 393224 | tf_op jit(solution)/shard_map/ppermute | solution.py:665
  124.0 11.9 %collective-permute-start.32 = (bf16[1792,128]{1,0:T(8,128)(2,1)S(1)}, bf16[1792,128]{1,0:T(8,128)(2,1)S(1)}, u32[]{:S(2)}, u32[]{:S(2)}) collective-permute-start(bf16[1792,128]{1,0:T(8,128)(2,1)S(1)} %up_4.1.refs_2_.refs_0_), channel_id=1, source_target_pairs={{0,2},{2,0},{4,6},{6,4},{8,10},{10,8},{12,14},{14,12},{16,18},{18,... | collective-permute-start | bytes 1376264 | tf_op jit(solution)/shard_map/ppermute | solution.py:665
  124.1 13.6 %collective-permute-start.31 = (bf16[1792,128]{1,0:T(8,128)(2,1)S(1)}, bf16[1792,128]{1,0:T(8,128)(2,1)S(1)}, u32[]{:S(2)}, u32[]{:S(2)}) collective-permute-start(bf16[1792,128]{1,0:T(8,128)(2,1)S(1)} %up_4.1.refs_2_.refs_0_), channel_id=1, source_target_pairs={{0,4},{2,6},{4,0},{6,2},{8,12},{10,14},{12,8},{14,10},{16,20},{18,... | collective-permute-start | bytes 1376264 | tf_op jit(solution)/shard_map/ppermute | solution.py:665
  126.2 8.4 %collective-permute-start.35 = (bf16[416,128]{1,0:T(8,128)(2,1)S(1)}, bf16[416,128]{1,0:T(8,128)(2,1)S(1)}, u32[]{:S(2)}, u32[]{:S(2)}) collective-permute-start(bf16[416,128]{1,0:T(8,128)(2,1)S(1)} %early_2.1.refs_2_.refs_0_), channel_id=1, source_target_pairs={{0,16},{2,18},{4,20},{6,22},{8,24},{10,26},{12,28},{14,30},{16,0},... | collective-permute-start | bytes 319496 | tf_op jit(solution)/shard_map/ppermute | solution.py:665
  129.3 6.5 %collective-permute-start.38 = (bf16[512,128]{1,0:T(8,128)(2,1)S(1)}, bf16[512,128]{1,0:T(8,128)(2,1)S(1)}, u32[]{:S(2)}, u32[]{:S(2)}) collective-permute-start(bf16[512,128]{1,0:T(8,128)(2,1)S(1)} %late_3.1.refs_2_.refs_0_), channel_id=1, source_target_pairs={{0,8},{2,10},{4,12},{6,14},{8,0},{10,2},{12,4},{14,6},{16,24},{18,... | collective-permute-start | bytes 393224 | tf_op jit(solution)/shard_map/ppermute | solution.py:665
  135.1 4.8 %collective-permute-start.37 = (bf16[416,128]{1,0:T(8,128)(2,1)S(1)}, bf16[416,128]{1,0:T(8,128)(2,1)S(1)}, u32[]{:S(2)}, u32[]{:S(2)}) collective-permute-start(bf16[416,128]{1,0:T(8,128)(2,1)S(1)} %early_3.1.refs_2_.refs_0_), channel_id=1, source_target_pairs={{0,8},{2,10},{4,12},{6,14},{8,0},{10,2},{12,4},{14,6},{16,24},{18,... | collective-permute-start | bytes 319496 | tf_op jit(solution)/shard_map/ppermute | solution.py:665
  136.4 15.4 %collective-permute-start.43 = (bf16[1024,128]{1,0:T(8,128)(2,1)S(1)}, bf16[1024,128]{1,0:T(8,128)(2,1)S(1)}, u32[]{:S(2)}, u32[]{:S(2)}) collective-permute-start(bf16[1024,128]{1,0:T(8,128)(2,1)S(1)} %late_4.1.refs_2_.refs_4_), channel_id=1, source_target_pairs={{0,2},{2,0},{4,6},{6,4},{8,10},{10,8},{12,14},{14,12},{16,18},{18,... | collective-permute-start | bytes 786440 | tf_op jit(solution)/shard_map/ppermute | solution.py:665
  136.5 13.4 %collective-permute-start.42 = (bf16[1024,128]{1,0:T(8,128)(2,1)S(1)}, bf16[1024,128]{1,0:T(8,128)(2,1)S(1)}, u32[]{:S(2)}, u32[]{:S(2)}) collective-permute-start(bf16[1024,128]{1,0:T(8,128)(2,1)S(1)} %late_4.1.refs_2_.refs_4_), channel_id=1, source_target_pairs={{0,4},{2,6},{4,0},{6,2},{8,12},{10,14},{12,8},{14,10},{16,20},{18,... | collective-permute-start | bytes 786440 | tf_op jit(solution)/shard_map/ppermute | solution.py:665
  137.6 3.5 %collective-permute-start.33 = (bf16[1792,128]{1,0:T(8,128)(2,1)S(1)}, bf16[1792,128]{1,0:T(8,128)(2,1)S(1)}, u32[]{:S(2)}, u32[]{:S(2)}) collective-permute-start(bf16[1792,128]{1,0:T(8,128)(2,1)S(1)} %collective-permute-done.31.refs_1_), channel_id=1, source_target_pairs={{0,2},{2,0},{4,6},{6,4},{8,10},{10,8},{12,14},{14,12},{16,18},{18,... | collective-permute-start | bytes 1376264 | tf_op jit(solution)/shard_map/ppermute | solution.py:665
  140.5 10.1 %collective-permute-start.39 = (bf16[832,128]{1,0:T(8,128)(2,1)S(1)}, bf16[832,128]{1,0:T(8,128)(2,1)S(1)}, u32[]{:S(2)}, u32[]{:S(2)}) collective-permute-start(bf16[832,128]{1,0:T(8,128)(2,1)S(1)} %early_4.1.refs_4_.refs_0_), channel_id=1, source_target_pairs={{0,4},{2,6},{4,0},{6,2},{8,12},{10,14},{12,8},{14,10},{16,20},{18,... | collective-permute-start | bytes 638984 | tf_op jit(solution)/shard_map/ppermute | solution.py:665
  150.0 2.2 %collective-permute-start.44 = (bf16[1024,128]{1,0:T(8,128)(2,1)S(1)}, bf16[1024,128]{1,0:T(8,128)(2,1)S(1)}, u32[]{:S(2)}, u32[]{:S(2)}) collective-permute-start(bf16[1024,128]{1,0:T(8,128)(2,1)S(1)} %after_rows.1.refs_5_), channel_id=1, source_target_pairs={{0,2},{2,0},{4,6},{6,4},{8,10},{10,8},{12,14},{14,12},{16,18},{18,... | collective-permute-start | bytes 786440 | tf_op jit(solution)/shard_map/ppermute | solution.py:665
  150.0 1.8 %collective-permute-start.40 = (bf16[832,128]{1,0:T(8,128)(2,1)S(1)}, bf16[832,128]{1,0:T(8,128)(2,1)S(1)}, u32[]{:S(2)}, u32[]{:S(2)}) collective-permute-start(bf16[832,128]{1,0:T(8,128)(2,1)S(1)} %early_4.1.refs_4_.refs_0_), channel_id=1, source_target_pairs={{0,2},{2,0},{4,6},{6,4},{8,10},{10,8},{12,14},{14,12},{16,18},{18,... | collective-permute-start | bytes 638984 | tf_op jit(solution)/shard_map/ppermute | solution.py:665
  150.6 1.6 %collective-permute-start.41 = (bf16[832,128]{1,0:T(8,128)(2,1)S(1)}, bf16[832,128]{1,0:T(8,128)(2,1)S(1)}, u32[]{:S(2)}, u32[]{:S(2)}) collective-permute-start(bf16[832,128]{1,0:T(8,128)(2,1)S(1)} %after_up.1.refs_1_), channel_id=1, source_target_pairs={{0,2},{2,0},{4,6},{6,4},{8,10},{10,8},{12,14},{14,12},{16,18},{18,... | collective-permute-start | bytes 638984 | tf_op jit(solution)/shard_map/ppermute | solution.py:665

commit v5 on v4

--- a/solution.py
+++ b/solution.py
@@ -330,15 +330,16 @@
 
 
 def up_grads_kernel(
-    s, second, hidden_grad, mixed, middle_grad, prior_in, logit_own, cotangents, keep, send, turned, wide, tall,
+    s, second, hidden_grad, mixed, middle_grad, prior_in, logit_own, cotangents, keep, send, turned, wide, tall, turned_in,
 ):
     turned[...] = second[...].T
+    turned_in[...] = prior_in[...].T
     half = hidden_grad.shape[1] // 2
     n, m = second.shape[1], mixed.shape[1] // 2
     logit_other = cotangents.at[:, : logit_own.shape[1]]
     for h in range(2):
         wide[...] = mm_at(mixed[:, h * m : h * m + m], middle_grad[...])
-        tall[...] = mm_at(prior_in[...], (logit_own, logit_other)[h][...])
+        tall[...] = mm(turned_in[...], (logit_own, logit_other)[h][...])
         for j in (2, 3, 0, 1):
             place = s[1] ^ j
             at = pl.ds(pl.multiple_of(place * 128, 128), 128)
@@ -879,7 +880,8 @@
         scalars,
         [second, hidden_grad, mixed, middle_grad, prior_in, logit_own, cotangents],
         pieces(width * hidden_width // 512 + half + width),
-        [pltpu.VMEM((width, total_rows), BF), pltpu.VMEM((half, width), F32), pltpu.VMEM((width, n_logits), F32)],
+        [pltpu.VMEM((width, total_rows), BF), pltpu.VMEM((half, width), F32), pltpu.VMEM((width, n_logits), F32)]
+        + [pltpu.VMEM((width, total_rows), BF)],
         name="up_grads",
         cost=3.0,
     )

time: 155 us -> 155 us (level)
  no operation moved by 1% of the time
where the time goes in v5:
time: 155 us
  Pallas kernels  62.8 us (41%)
  starting transfers between devices  46.7 us (30%)
  waiting for transfers between devices  44.2 us (29%)
    pallas_call x32, Pallas kernels, call(): pl.pallas_call(run, in_specs=[pl.BlockSpec(memory_space=pltpu.SMEM)] + [f...  62.7 us
    ppermute x45, starting transfers between devices, swap(): return lax.ppermute(value, axes, [(i, i ^ mask) for i in range(count)])  46.7 us
    ppermute x45, waiting for transfers between devices, swap(): return lax.ppermute(value, axes, [(i, i ^ mask) for i in range(count)])  44.2 us
  transfers between devices with their start and end apart: 45, of which 24 were waited for; matrix products, arithmetic and copies ran while one was open for 0% of the time, Pallas kernels for 31%

profile of v5, /device:TPU:0, one launch (start us, length us, event | category | flops | bytes accessed | tf_op | source)
XLA Modules:
  0.0 155.1 jit_solution(12033956239010358189)
XLA Ops:
  0.7 1.9 %first_parts.1 = (bf16[768,128]{1,0:T(8,128)(2,1)S(1)}, bf16[624,256]{1,0:T(8,128)(2,1)S(1)}, bf16[624,256]{1,0:T(8,128)(2,1)S(1)}, s32[8,256]{1,0:T(8,128)S(1)}) custom-call(s32[3]{0:T(128)S(1)} %pad_add_fusion.s, bf16[1200,256]{1,0:T(8,128)(2,1)} %refs_0_.3, bf16[3,512,256]{2,1,0:T(8,128)(2,1)} %refs_2_.5, s32[1200]{0:T(1024)} %refs_2_.3), custom_call_target="tpu_custom_call" | custom-call | flops 200000000 | tf_op jit(solution)/shard_map/first_parts/pallas_call | solution.py:642
  2.7 3.0 %collective-permute-start = (bf16[624,256]{1,0:T(8,128)(2,1)S(1)}, bf16[624,256]{1,0:T(8,128)(2,1)S(1)}, u32[]{:S(2)}, u32[]{:S(2)}) collective-permute-start(bf16[624,256]{1,0:T(8,128)(2,1)S(1)} %get-tuple-element.109.refs_14_.refs_7_), channel_id=1, source_target_pairs={{0,1},{1,0},{2,3},{3,2},{4,5},{5,4},{6,7},{7,6},{8,9},{9,8},{10,11... | collective-permute-start | bytes 958472 | tf_op jit(solution)/shard_map/ppermute | solution.py:666
  5.8 1.8 %packs.1 = (bf16[1328,128]{1,0:T(8,128)(2,1)S(1)}, bf16[1536,128]{1,0:T(8,128)(2,1)S(1)}, f32[16,1024]{1,0:T(8,128)S(1)}) custom-call(s32[3]{0:T(128)S(1)} %pad_add_fusion.s, bf16[512,1024]{1,0:T(8,128)(2,1)} %refs_4_.1, bf16[256,512]{1,0:T(8,128)(2,1)} %refs_3_.3, bf16[1024,512]{1,0:T(8,128)(2,1)} %refs_5_.1, bf16[512,512]{1,0:T(8,128)(2,1)} %refs_6_.1, ...), custom_call_target="tpu_custom_call" | custom-call | flops 200000000 | tf_op jit(solution)/shard_map/packs/pallas_call | solution.py:642
  7.6 3.2 %cotangents.1 = (bf16[624,768]{1,0:T(8,128)(2,1)S(1)}, bf16[624,512]{1,0:T(8,128)(2,1)S(1)}, bf16[624,256]{1,0:T(8,128)(2,1)S(1)}, bf16[3,512,256]{2,1,0:T(8,128...) custom-call(s32[3]{0:T(128)S(1)} %pad_add_fusion.s, ...), custom_call_target="tpu_custom_call" | custom-call | flops 230000000 | tf_op jit(solution)/shard_map/cotangents/pallas_call | solution.py:642
  10.7 3.3 %collective-permute-done.refs_1_.refs_4_ = bf16[624,256]{1,0:T(8,128)(2,1)S(1)} collective-permute-done((bf16[624,256]{1,0:T(8,128)(2,1)S(1)}, bf16[624,256]{1,0:T(8,128)(2,1)S(1)}, u32[]{:S(2)}, u32[]{:S(2)}) %collective-permute-start) | collective-permute-done | bytes 319520 | tf_op jit(solution)/shard_map/ppermute | solution.py:666
  14.1 2.1 %collective-permute-start.5 = (bf16[1328,128]{1,0:T(8,128)(2,1)S(1)}, bf16[1328,128]{1,0:T(8,128)(2,1)S(1)}, u32[]{:S(2)}, u32[]{:S(2)}) collective-permute-start(bf16[1328,128]{1,0:T(8,128)(2,1)S(1)} %after_frames.1.refs_1_), channel_id=1, source_target_pairs={{0,1},{1,0},{2,3},{3,2},{4,5},{5,4},{6,7},{7,6},{8,9},{9,8},{10,11... | collective-permute-start | bytes 1019912 | tf_op jit(solution)/shard_map/ppermute | solution.py:666
  16.2 2.1 %collective-permute-done.1.refs_4_ = bf16[768,128]{1,0:T(8,128)(2,1)S(1)} collective-permute-done((bf16[768,128]{1,0:T(8,128)(2,1)S(1)}, bf16[768,128]{1,0:T(8,128)(2,1)S(1)}, u32[]{:S(2)}, u32[]{:S(2)}) %collective-permute-start.1) | collective-permute-done | bytes 196640 | tf_op jit(solution)/shard_map/ppermute | solution.py:666
  18.3 2.0 %collective-permute-start.2 = (bf16[768,128]{1,0:T(8,128)(2,1)S(1)}, bf16[768,128]{1,0:T(8,128)(2,1)S(1)}, u32[]{:S(2)}, u32[]{:S(2)}) collective-permute-start(bf16[768,128]{1,0:T(8,128)(2,1)S(1)} %collective-permute-done.1.refs_4_), channel_id=1, source_target_pairs={{0,4},{2,6},{4,0},{6,2},{8,12},{10,14},{12,8},{14,10},{16,20},{18,... | collective-permute-start | bytes 589832 | tf_op jit(solution)/shard_map/ppermute | solution.py:666
  20.3 3.6 %collective-permute-done.2.refs_5_.refs_2_ = bf16[768,128]{1,0:T(8,128)(2,1)S(1)} collective-permute-done((bf16[768,128]{1,0:T(8,128)(2,1)S(1)}, bf16[768,128]{1,0:T(8,128)(2,1)S(1)}, u32[]{:S(2)}, u32[]{:S(2)}) %collective-permute-start.2) | collective-permute-done | bytes 196640 | tf_op jit(solution)/shard_map/ppermute | solution.py:666
  24.0 2.1 %collective-permute-start.9 = (bf16[1536,128]{1,0:T(8,128)(2,1)S(1)}, bf16[1536,128]{1,0:T(8,128)(2,1)S(1)}, u32[]{:S(2)}, u32[]{:S(2)}) collective-permute-start(bf16[1536,128]{1,0:T(8,128)(2,1)S(1)} %after_one.1), channel_id=1, source_target_pairs={{0,1},{1,0},{2,3},{3,2},{4,5},{5,4},{6,7},{7,6},{8,9},{9,8},{10,11... | collective-permute-start | bytes 1179656 | tf_op jit(solution)/shard_map/ppermute | solution.py:666
  26.1 1.5 collective-permute-start.6
  27.6 5.6 %collective-permute-done.9.refs_11_.refs_1_.refs_8_ = bf16[1536,128]{1,0:T(8,128)(2,1)S(1)} collective-permute-done((bf16[1536,128]{1,0:T(8,128)(2,1)S(1)}, bf16[1536,128]{1,0:T(8,128)(2,1)S(1)}, u32[]{:S(2)}, u32[]{:S(2)}) %collective-permute-start.9) | collective-permute-done | bytes 393248 | tf_op jit(solution)/shard_map/ppermute | solution.py:666
  33.2 0.7 collective-permute-done.6.refs_8_.refs_2_.refs_5_
  34.0 1.5 collective-permute-start.13
  35.5 1.5 collective-permute-start.10
  37.5 0.9 collective-permute-done.3.refs_6_
  38.7 4.3 %attend.1 = (bf16[624,512]{1,0:T(8,128)(2,1)S(1)}, bf16[624,1536]{1,0:T(8,128)(2,1)S(1)}, bf16[624,512]{1,0:T(8,128)(2,1)S(1)}, bf16[3,512,256]{2,1,0:T(8,128)(2,1)S(1)}) custom-call(s32[3]{0:T(128)S(1)} %pad_add_fusion.s, bf16[624,256]{1,0:T(8,128)(2,1)S(1)} %get-tuple-element.108.refs_0_.refs_3_, ...), custom_call_target="tpu_custom_call" | custom-call | flops 550000000 | tf_op jit(solution)/shard_map/attend/pallas_call | solution.py:642
  44.2 1.7 %collective-permute-done.7.refs_9_.refs_6_ = bf16[1328,128]{1,0:T(8,128)(2,1)S(1)} collective-permute-done((bf16[1328,128]{1,0:T(8,128)(2,1)S(1)}, bf16[1328,128]{1,0:T(8,128)(2,1)S(1)}, u32[]{:S(2)}, u32[]{:S(2)}) %collective-permute-start.7) | collective-permute-done | bytes 340000 | tf_op jit(solution)/shard_map/ppermute | solution.py:666
  46.3 6.8 %feed.1 = (bf16[624,256]{1,0:T(8,128)(2,1)S(1)}, bf16[624,256]{1,0:T(8,128)(2,1)S(1)}, f32[624,512]{1,0:T(8,128)S(1)}, bf16[624,512]{1,0:T(8,128)(2,1)S(1)}, bf1...) custom-call(s32[3]{0:T(128)S(1)} %pad_add_fusion.s, ...), custom_call_target="tpu_custom_call" | custom-call | flops 720000000 | tf_op jit(solution)/shard_map/feed/pallas_call | solution.py:642
  53.2 1.0 collective-permute-done.13.refs_12_.refs_6_
  54.2 2.3 %prior.1 = (f32[624,512]{1,0:T(8,128)S(1)}, bf16[624,512]{1,0:T(8,128)(2,1)S(1)}, f32[3,512]{1,0:T(4,128)S(1)}, f32[1,1024]{1,0:T(1,128)S(1)}, bf16[512,512]{1,0:T(8,128)(2,1)S(1)}, /*index=5*/f32[1,512]{1,0:T(1,128)S(1)}) custom-call(s32[3]{0:T(128)S(1)} %pad_add_fusion.s, f32[624,512]{1,0:T(8,128)S(1)} %get-tuple-element.123.refs_0_, ...), custom_call_target="tpu_custom_call" | custom-call | flops 250000000 | tf_op jit(solution)/shard_map/prior/pallas_call | solution.py:642
  56.5 4.1 %feed_back.1 = (bf16[624,2048]{1,0:T(8,128)(2,1)S(1)}, f32[624,512]{1,0:T(8,128)S(1)}, bf16[624,512]{1,0:T(8,128)(2,1)S(1)}, f32[3,512]{1,0:T(4,128)S(1)}, f32[1,2048]{1,0:T(1,128)S(1)}) custom-call(s32[3]{0:T(128)S(1)} %pad_add_fusion.s, bf16[624,512]{1,0:T(8,128)(2,1)S(1)} %get-tuple-element.129.refs_0_.refs_1_, ...), custom_call_target="tpu_custom_call" | custom-call | flops 650000000 | tf_op jit(solution)/shard_map/feed_back/pallas_call | solution.py:642
  60.6 4.0 %up_grads.1 = (f32[4,1792,128]{2,1,0:T(8,128)S(1)}, bf16[4,1792,128]{2,1,0:T(8,128)(2,1)S(1)}) custom-call(s32[3]{0:T(128)S(1)} %pad_add_fusion.s, bf16[624,512]{1,0:T(8,128)(2,1)S(1)} %get-tuple-element.137.refs_0_, bf16[624,2048]{1,0:T(8,128)(2,1)S(1)} %get-tuple-element.138.refs_1_, bf16[624,512]{1,0:T(8,128)(2,1)S(1)} %get-tuple-element.114.refs_1_.refs_2_, ...), custom_call_target="tpu_custom_call" | custom-call | flops 300000000 | tf_op jit(solution)/shard_map/up_grads/pallas_call | solution.py:642
  64.7 2.4 %late_grads.1 = (f32[4,1024,128]{2,1,0:T(8,128)S(1)}, bf16[4,1024,128]{2,1,0:T(8,128)(2,1)S(1)}) custom-call(s32[3]{0:T(128)S(1)} %pad_add_fusion.s, bf16[624,2048]{1,0:T(8,128)(2,1)S(1)} %get-tuple-element.141.refs_0_, bf16[624,512]{1,0:T(8,128)(2,1)S(1)} %get-tuple-element.129.refs_0_.refs_1_, bf16[4,1792,128]{2,1,0:T(8,128)(2,1)S(1)} %get-tuple-element.140.refs_2_), custom_call_target="tpu_custom_call" | custom-call | flops 350000000 | tf_op jit(solution)/shard_map/late_grads/pallas_call | solution.py:642
  67.6 0.8 collective-permute-done.14.refs_1_
  68.4 0.8 up_core.1
  69.3 1.8 %collective-permute-start.17 = (bf16[1792,128]{1,0:T(8,128)(2,1)S(1)}, bf16[1792,128]{1,0:T(8,128)(2,1)S(1)}, u32[]{:S(2)}, u32[]{:S(2)}) collective-permute-start(bf16[1792,128]{1,0:T(8,128)(2,1)S(1)} %get-tuple-element.153), channel_id=1, source_target_pairs={{0,1},{1,0},{2,3},{3,2},{4,5},{5,4},{6,7},{7,6},{8,9},{9,8},{10,11... | collective-permute-start | bytes 1376264 | tf_op jit(solution)/shard_map/ppermute | solution.py:666
  71.1 1.2 collective-permute-start.18
  72.9 3.7 %attend_back_0.1.refs_2_.refs_1_.refs_0_ = bf16[624,768]{1,0:T(8,128)(2,1)S(1)} custom-call(s32[3]{0:T(128)S(1)} %pad_add_fusion.s, bf16[624,512]{1,0:T(8,128)(2,1)S(1)} %get-tuple-element.135.refs_3_.refs_0_, bf16[624,1536]{1,0:T(8,128)(2,1)S(1)} %get-tuple-element.136.refs_1_, bf16[256,512]{1,0:T(8,128)(2,1)S(1)} %get-tuple-element.115.refs_4_.refs_2_, ...), custom_call_target="tpu_custom_call" | custom-call | flops 450000000 | tf_op jit(solution)/shard_map/attend_back_0/pallas_call | solution.py:642
  76.6 0.8 late_core.1
  77.4 1.5 collective-permute-start.22
  78.9 4.0 %attend_back_1.1.refs_2_.refs_1_ = bf16[624,768]{1,0:T(8,128)(2,1)S(1)} custom-call(s32[3]{0:T(128)S(1)} %pad_add_fusion.s, bf16[624,512]{1,0:T(8,128)(2,1)S(1)} %get-tuple-element.135.refs_3_.refs_0_, bf16[624,1536]{1,0:T(8,128)(2,1)S(1)} %get-tuple-element.136.refs_1_, bf16[256,512]{1,0:T(8,128)(2,1)S(1)} %get-tuple-element.144.refs_2_, ...), custom_call_target="tpu_custom_call" | custom-call | flops 450000000 | tf_op jit(solution)/shard_map/attend_back_1/pallas_call | solution.py:642
  82.9 2.0 %early_grads.1 = (f32[4,768,128]{2,1,0:T(8,128)S(1)}, bf16[4,768,128]{2,1,0:T(8,128)(2,1)S(1)}) custom-call(s32[3]{0:T(128)S(1)} %pad_add_fusion.s, bf16[624,512]{1,0:T(8,128)(2,1)S(1)} %get-tuple-element.149.refs_0_, bf16[624,768]{1,0:T(8,128)(2,1)S(1)} %attend_back_0.1.refs_2_.refs_1_.refs_0_, bf16[624,768]{1,0:T(8,128)(2,1)S(1)} %attend_back_1.1.refs_2_.refs_1_), custom_call_target="tpu_custom_call" | custom-call | flops 200000000 | tf_op jit(solution)/shard_map/early_grads/pallas_call | solution.py:642
  85.0 2.3 %frames_back.1 = (bf16[624,256]{1,0:T(8,128)(2,1)S(1)}, f32[624,256]{1,0:T(8,128)S(1)}, f32[2,512]{1,0:T(2,128)S(1)}) custom-call(s32[3]{0:T(128)S(1)} %pad_add_fusion.s, bf16[624,768]{1,0:T(8,128)(2,1)S(1)} %attend_back_0.1.refs_2_.refs_1_.refs_0_, bf16[624,768]{1,0:T(8,128)(2,1)S(1)} %attend_back_1.1.refs_2_.refs_1_, ...), custom_call_target="tpu_custom_call" | custom-call | flops 250000000 | tf_op jit(solution)/shard_map/frames_back/pallas_call | solution.py:642
  87.3 4.4 %collective-permute-done.17.refs_2_ = bf16[1792,128]{1,0:T(8,128)(2,1)S(1)} collective-permute-done((bf16[1792,128]{1,0:T(8,128)(2,1)S(1)}, bf16[1792,128]{1,0:T(8,128)(2,1)S(1)}, u32[]{:S(2)}, u32[]{:S(2)}) %collective-permute-start.17) | collective-permute-done | bytes 458784 | tf_op jit(solution)/shard_map/ppermute | solution.py:666
  91.8 1.7 %collective-permute-start.23 = (bf16[1024,128]{1,0:T(8,128)(2,1)S(1)}, bf16[1024,128]{1,0:T(8,128)(2,1)S(1)}, u32[]{:S(2)}, u32[]{:S(2)}) collective-permute-start(bf16[1024,128]{1,0:T(8,128)(2,1)S(1)} %get-tuple-element.165), channel_id=1, source_target_pairs={{0,1},{1,0},{2,3},{3,2},{4,5},{5,4},{6,7},{7,6},{8,9},{9,8},{10,11... | collective-permute-start | bytes 786440 | tf_op jit(solution)/shard_map/ppermute | solution.py:666
  93.5 1.2 collective-permute-start.24
  94.7 0.9 up_1.1
  95.6 1.6 %collective-permute-start.19 = (bf16[896,128]{1,0:T(8,128)(2,1)S(1)}, bf16[896,128]{1,0:T(8,128)(2,1)S(1)}, u32[]{:S(2)}, u32[]{:S(2)}) collective-permute-start(bf16[896,128]{1,0:T(8,128)(2,1)S(1)} %get-tuple-element.157), channel_id=1, source_target_pairs={{0,8},{2,10},{4,12},{6,14},{8,0},{10,2},{12,4},{14,6},{16,24},{18,... | collective-permute-start | bytes 688136 | tf_op jit(solution)/shard_map/ppermute | solution.py:666
  97.3 0.8 early_core.1
  98.1 0.9 collective-permute-start.28
  99.0 3.0 %collective-permute-done.19.refs_1_ = bf16[896,128]{1,0:T(8,128)(2,1)S(1)} collective-permute-done((bf16[896,128]{1,0:T(8,128)(2,1)S(1)}, bf16[896,128]{1,0:T(8,128)(2,1)S(1)}, u32[]{:S(2)}, u32[]{:S(2)}) %collective-permute-start.19) | collective-permute-done | bytes 229408 | tf_op jit(solution)/shard_map/ppermute | solution.py:666
  102.6 2.7 %collective-permute-start.21 = (bf16[896,128]{1,0:T(8,128)(2,1)S(1)}, bf16[896,128]{1,0:T(8,128)(2,1)S(1)}, u32[]{:S(2)}, u32[]{:S(2)}) collective-permute-start(bf16[896,128]{1,0:T(8,128)(2,1)S(1)} %up_2.1.refs_4_.refs_0_), channel_id=1, source_target_pairs={{0,16},{2,18},{4,20},{6,22},{8,24},{10,26},{12,28},{14,30},{16,0},... | collective-permute-start | bytes 688136 | tf_op jit(solution)/shard_map/ppermute | solution.py:666
  105.2 1.2 collective-permute-done.24.refs_3_
  106.5 0.8 late_1.1
  107.2 1.6 %collective-permute-start.27 = (bf16[512,128]{1,0:T(8,128)(2,1)S(1)}, bf16[512,128]{1,0:T(8,128)(2,1)S(1)}, u32[]{:S(2)}, u32[]{:S(2)}) collective-permute-start(bf16[512,128]{1,0:T(8,128)(2,1)S(1)} %get-tuple-element.172), channel_id=1, source_target_pairs={{0,8},{2,10},{4,12},{6,14},{8,0},{10,2},{12,4},{14,6},{16,24},{18,... | collective-permute-start | bytes 393224 | tf_op jit(solution)/shard_map/ppermute | solution.py:666
  109.4 2.4 %collective-permute-start.30 = (bf16[832,128]{1,0:T(8,128)(2,1)S(1)}, bf16[832,128]{1,0:T(8,128)(2,1)S(1)}, u32[]{:S(2)}, u32[]{:S(2)}) collective-permute-start(bf16[832,128]{1,0:T(8,128)(2,1)S(1)} %get-tuple-element.175), channel_id=1, source_target_pairs={{0,5},{1,4},{2,7},{3,6},{4,1},{5,0},{6,3},{7,2},{8,13},{9,12},{10,... | collective-permute-start | bytes 638984 | tf_op jit(solution)/shard_map/ppermute | solution.py:666
  111.8 2.1 %collective-permute-done.21.refs_1_ = bf16[896,128]{1,0:T(8,128)(2,1)S(1)} collective-permute-done((bf16[896,128]{1,0:T(8,128)(2,1)S(1)}, bf16[896,128]{1,0:T(8,128)(2,1)S(1)}, u32[]{:S(2)}, u32[]{:S(2)}) %collective-permute-start.21) | collective-permute-done | bytes 229408 | tf_op jit(solution)/shard_map/ppermute | solution.py:666
  114.5 0.7 collective-permute-start.26
  115.2 1.4 logits.1
  116.6 1.7 %collective-permute-done.29.refs_2_ = bf16[832,128]{1,0:T(8,128)(2,1)S(1)} collective-permute-done((bf16[832,128]{1,0:T(8,128)(2,1)S(1)}, bf16[832,128]{1,0:T(8,128)(2,1)S(1)}, u32[]{:S(2)}, u32[]{:S(2)}) %collective-permute-start.29) | collective-permute-done | bytes 213024 | tf_op jit(solution)/shard_map/ppermute | solution.py:666
  118.8 0.7 early_1.1
  119.5 1.0 collective-permute-start.34
  121.1 2.2 %collective-permute-start.36 = (bf16[512,128]{1,0:T(8,128)(2,1)S(1)}, bf16[512,128]{1,0:T(8,128)(2,1)S(1)}, u32[]{:S(2)}, u32[]{:S(2)}) collective-permute-start(bf16[512,128]{1,0:T(8,128)(2,1)S(1)} %late_2.1.refs_2_.refs_0_), channel_id=1, source_target_pairs={{0,16},{2,18},{4,20},{6,22},{8,24},{10,26},{12,28},{14,30},{16,0},... | collective-permute-start | bytes 393224 | tf_op jit(solution)/shard_map/ppermute | solution.py:666
  124.0 1.5 collective-permute-start.31
  126.1 2.1 %collective-permute-start.35 = (bf16[416,128]{1,0:T(8,128)(2,1)S(1)}, bf16[416,128]{1,0:T(8,128)(2,1)S(1)}, u32[]{:S(2)}, u32[]{:S(2)}) collective-permute-start(bf16[416,128]{1,0:T(8,128)(2,1)S(1)} %early_2.1.refs_2_.refs_0_), channel_id=1, source_target_pairs={{0,16},{2,18},{4,20},{6,22},{8,24},{10,26},{12,28},{14,30},{16,0},... | collective-permute-start | bytes 319496 | tf_op jit(solution)/shard_map/ppermute | solution.py:666
  129.2 2.7 %collective-permute-start.38 = (bf16[512,128]{1,0:T(8,128)(2,1)S(1)}, bf16[512,128]{1,0:T(8,128)(2,1)S(1)}, u32[]{:S(2)}, u32[]{:S(2)}) collective-permute-start(bf16[512,128]{1,0:T(8,128)(2,1)S(1)} %late_3.1.refs_2_.refs_0_), channel_id=1, source_target_pairs={{0,8},{2,10},{4,12},{6,14},{8,0},{10,2},{12,4},{14,6},{16,24},{18,... | collective-permute-start | bytes 393224 | tf_op jit(solution)/shard_map/ppermute | solution.py:666
  132.0 2.5 %collective-permute-done.35.refs_1_ = bf16[416,128]{1,0:T(8,128)(2,1)S(1)} collective-permute-done((bf16[416,128]{1,0:T(8,128)(2,1)S(1)}, bf16[416,128]{1,0:T(8,128)(2,1)S(1)}, u32[]{:S(2)}, u32[]{:S(2)}) %collective-permute-start.35) | collective-permute-done | bytes 106528 | tf_op jit(solution)/shard_map/ppermute | solution.py:666
  137.0 2.8 %collective-permute-done.37.refs_1_ = bf16[416,128]{1,0:T(8,128)(2,1)S(1)} collective-permute-done((bf16[416,128]{1,0:T(8,128)(2,1)S(1)}, bf16[416,128]{1,0:T(8,128)(2,1)S(1)}, u32[]{:S(2)}, u32[]{:S(2)}) %collective-permute-start.37) | collective-permute-done | bytes 106528 | tf_op jit(solution)/shard_map/ppermute | solution.py:666
  141.0 2.8 %up_place.1 = (f32[512,1024]{1,0:T(8,128)}, f32[256,512]{1,0:T(8,128)}, f32[512,512]{1,0:T(8,128)}, f32[8,128]{1,0:T(8,128)S(1)}) custom-call(s32[3]{0:T(128)S(1)} %pad_add_fusion.s, bf16[1792,128]{1,0:T(8,128)(2,1)S(1)} %up_4.1.refs_2_.refs_0_, bf16[1792,128]{1,0:T(8,128)(2,1)S(1)} %collective-permute-done.31.refs_1_, ...), custom_call_target="tpu_custom_call" | custom-call | flops 10000000000 | tf_op jit(solution)/shard_map/up_place/pallas_call | solution.py:642
  143.8 3.3 %collective-permute-done.25.refs_1_.refs_3_.refs_5_ = bf16[624,1024]{1,0:T(8,128)(2,1)S(1)} collective-permute-done((bf16[624,1024]{1,0:T(8,128)(2,1)S(1)}, bf16[624,1024]{1,0:T(8,128)(2,1)S(1)}, u32[]{:S(2)}, u32[]{:S(2)}) %collective-permute-start.25) | collective-permute-done | bytes 1277984 | tf_op jit(solution)/shard_map/ppermute | solution.py:666
  147.1 2.8 %rows_back.1 = (f32[1200,512]{1,0:T(8,128)}, f32[1200,256]{1,0:T(8,128)}, bf16[1200,256]{1,0:T(8,128)(2,1)}, f32[8,128]{1,0:T(8,128)S(1)}) custom-call(s32[3]{0:T(128)S(1)} %pad_add_fusion.s, f32[624,512]{1,0:T(8,128)S(1)} %get-tuple-element.168.refs_0_, bf16[624,1024]{1,0:T(8,128)(2,1)S(1)} %collective-permute-done.25.refs_1_.refs_3_.refs_5_, ...), custom_call_target="tpu_custom_call" | custom-call | flops 10000000000 | tf_op jit(solution)/shard_map/rows_back/pallas_call | solution.py:642
  150.7 1.2 collective-permute-done.40.refs_2_
  152.1 2.7 %last_place.1 = (f32[3,512,256]{2,1,0:T(8,128)}, f32[1024,512]{1,0:T(8,128)}, f32[1,512]{1,0:T(1,128)}, f32[1,512]{1,0:T(1,128)}, f32[1,512]{1,0:T(1,128)}, /*in...) custom-call(s32[3]{0:T(128)S(1)} %pad_add_fusion.s, ...), custom_call_target="tpu_custom_call" | custom-call | flops 10000000000 | tf_op jit(solution)/shard_map/last_place/pallas_call | solution.py:642
  (65 shorter events, 13.9 us)
Async XLA Ops:
  2.7 11.4 %collective-permute-start = (bf16[624,256]{1,0:T(8,128)(2,1)S(1)}, bf16[624,256]{1,0:T(8,128)(2,1)S(1)}, u32[]{:S(2)}, u32[]{:S(2)}) collective-permute-start(bf16[624,256]{1,0:T(8,128)(2,1)S(1)} %get-tuple-element.109.refs_14_.refs_7_), channel_id=1, source_target_pairs={{0,1},{1,0},{2,3},{3,2},{4,5},{5,4},{6,7},{7,6},{8,9},{9,8},{10,11... | collective-permute-start | bytes 958472 | tf_op jit(solution)/shard_map/ppermute | solution.py:666
  5.7 12.6 %collective-permute-start.1 = (bf16[768,128]{1,0:T(8,128)(2,1)S(1)}, bf16[768,128]{1,0:T(8,128)(2,1)S(1)}, u32[]{:S(2)}, u32[]{:S(2)}) collective-permute-start(bf16[768,128]{1,0:T(8,128)(2,1)S(1)} %get-tuple-element.112), channel_id=1, source_target_pairs={{0,1},{1,0},{2,3},{3,2},{4,5},{5,4},{6,7},{7,6},{8,9},{9,8},{10,11... | collective-permute-start | bytes 589832 | tf_op jit(solution)/shard_map/ppermute | solution.py:666
  14.1 12.0 %collective-permute-start.5 = (bf16[1328,128]{1,0:T(8,128)(2,1)S(1)}, bf16[1328,128]{1,0:T(8,128)(2,1)S(1)}, u32[]{:S(2)}, u32[]{:S(2)}) collective-permute-start(bf16[1328,128]{1,0:T(8,128)(2,1)S(1)} %after_frames.1.refs_1_), channel_id=1, source_target_pairs={{0,1},{1,0},{2,3},{3,2},{4,5},{5,4},{6,7},{7,6},{8,9},{9,8},{10,11... | collective-permute-start | bytes 1019912 | tf_op jit(solution)/shard_map/ppermute | solution.py:666
  18.3 5.7 %collective-permute-start.2 = (bf16[768,128]{1,0:T(8,128)(2,1)S(1)}, bf16[768,128]{1,0:T(8,128)(2,1)S(1)}, u32[]{:S(2)}, u32[]{:S(2)}) collective-permute-start(bf16[768,128]{1,0:T(8,128)(2,1)S(1)} %collective-permute-done.1.refs_4_), channel_id=1, source_target_pairs={{0,4},{2,6},{4,0},{6,2},{8,12},{10,14},{12,8},{14,10},{16,20},{18,... | collective-permute-start | bytes 589832 | tf_op jit(solution)/shard_map/ppermute | solution.py:666
  24.0 9.2 %collective-permute-start.9 = (bf16[1536,128]{1,0:T(8,128)(2,1)S(1)}, bf16[1536,128]{1,0:T(8,128)(2,1)S(1)}, u32[]{:S(2)}, u32[]{:S(2)}) collective-permute-start(bf16[1536,128]{1,0:T(8,128)(2,1)S(1)} %after_one.1), channel_id=1, source_target_pairs={{0,1},{1,0},{2,3},{3,2},{4,5},{5,4},{6,7},{7,6},{8,9},{9,8},{10,11... | collective-permute-start | bytes 1179656 | tf_op jit(solution)/shard_map/ppermute | solution.py:666
  26.1 7.8 %collective-permute-start.6 = (bf16[1328,128]{1,0:T(8,128)(2,1)S(1)}, bf16[1328,128]{1,0:T(8,128)(2,1)S(1)}, u32[]{:S(2)}, u32[]{:S(2)}) collective-permute-start(bf16[1328,128]{1,0:T(8,128)(2,1)S(1)} %collective-permute-done.5.refs_7_.refs_4_), channel_id=1, source_target_pairs={{0,4},{2,6},{4,0},{6,2},{8,12},{10,14},{12,8},{14,10},{16,20},{18,... | collective-permute-start | bytes 1019912 | tf_op jit(solution)/shard_map/ppermute | solution.py:666
  34.0 20.2 %collective-permute-start.13 = (bf16[624,768]{1,0:T(8,128)(2,1)S(1)}, bf16[624,768]{1,0:T(8,128)(2,1)S(1)}, u32[]{:S(2)}, u32[]{:S(2)}) collective-permute-start(bf16[624,768]{1,0:T(8,128)(2,1)S(1)} %after_two.1), channel_id=1, source_target_pairs={{0,1},{1,0},{2,3},{3,2},{4,5},{5,4},{6,7},{7,6},{8,9},{9,8},{10,11... | collective-permute-start | bytes 2875400 | tf_op jit(solution)/shard_map/ppermute | solution.py:666
  35.5 8.0 %collective-permute-start.10 = (bf16[1536,128]{1,0:T(8,128)(2,1)S(1)}, bf16[1536,128]{1,0:T(8,128)(2,1)S(1)}, u32[]{:S(2)}, u32[]{:S(2)}) collective-permute-start(bf16[1536,128]{1,0:T(8,128)(2,1)S(1)} %collective-permute-done.9.refs_11_.refs_1_.refs_8_), channel_id=1, source_target_pairs={{0,4},{2,6},{4,0},{6,2},{8,12},{10,14},{12,8},{14,10},{16,20},{18,... | collective-permute-start | bytes 1179656 | tf_op jit(solution)/shard_map/ppermute | solution.py:666
  37.0 1.4 collective-permute-start.3
  37.0 1.7 %collective-permute-start.4 = (bf16[768,128]{1,0:T(8,128)(2,1)S(1)}, bf16[768,128]{1,0:T(8,128)(2,1)S(1)}, u32[]{:S(2)}, u32[]{:S(2)}) collective-permute-start(bf16[768,128]{1,0:T(8,128)(2,1)S(1)} %collective-permute-done.2.refs_5_.refs_2_), channel_id=1, source_target_pairs={{0,2},{2,0},{4,6},{6,4},{8,10},{10,8},{12,14},{14,12},{16,18},{18,... | collective-permute-start | bytes 589832 | tf_op jit(solution)/shard_map/ppermute | solution.py:666
  43.0 2.8 %collective-permute-start.11 = (bf16[1536,128]{1,0:T(8,128)(2,1)S(1)}, bf16[1536,128]{1,0:T(8,128)(2,1)S(1)}, u32[]{:S(2)}, u32[]{:S(2)}) collective-permute-start(bf16[1536,128]{1,0:T(8,128)(2,1)S(1)} %collective-permute-done.9.refs_11_.refs_1_.refs_8_), channel_id=1, source_target_pairs={{0,2},{2,0},{4,6},{6,4},{8,10},{10,8},{12,14},{14,12},{16,18},{18,... | collective-permute-start | bytes 1179656 | tf_op jit(solution)/shard_map/ppermute | solution.py:666
  43.5 2.8 %collective-permute-start.12 = (bf16[1536,128]{1,0:T(8,128)(2,1)S(1)}, bf16[1536,128]{1,0:T(8,128)(2,1)S(1)}, u32[]{:S(2)}, u32[]{:S(2)}) collective-permute-start(bf16[1536,128]{1,0:T(8,128)(2,1)S(1)} %after_attend.1.refs_12_.refs_9_), channel_id=1, source_target_pairs={{0,2},{2,0},{4,6},{6,4},{8,10},{10,8},{12,14},{14,12},{16,18},{18,... | collective-permute-start | bytes 1179656 | tf_op jit(solution)/shard_map/ppermute | solution.py:666
  43.7 2.2 %collective-permute-start.7 = (bf16[1328,128]{1,0:T(8,128)(2,1)S(1)}, bf16[1328,128]{1,0:T(8,128)(2,1)S(1)}, u32[]{:S(2)}, u32[]{:S(2)}) collective-permute-start(bf16[1328,128]{1,0:T(8,128)(2,1)S(1)} %collective-permute-done.5.refs_7_.refs_4_), channel_id=1, source_target_pairs={{0,2},{2,0},{4,6},{6,4},{8,10},{10,8},{12,14},{14,12},{16,18},{18,... | collective-permute-start | bytes 1019912 | tf_op jit(solution)/shard_map/ppermute | solution.py:666
  44.1 2.2 %collective-permute-start.8 = (bf16[1328,128]{1,0:T(8,128)(2,1)S(1)}, bf16[1328,128]{1,0:T(8,128)(2,1)S(1)}, u32[]{:S(2)}, u32[]{:S(2)}) collective-permute-start(bf16[1328,128]{1,0:T(8,128)(2,1)S(1)} %collective-permute-done.6.refs_8_.refs_2_.refs_5_), channel_id=1, source_target_pairs={{0,2},{2,0},{4,6},{6,4},{8,10},{10,8},{12,14},{14,12},{16,18},{18,... | collective-permute-start | bytes 1019912 | tf_op jit(solution)/shard_map/ppermute | solution.py:666
  64.6 3.9 %collective-permute-start.14 = (bf16[4,1792,128]{2,1,0:T(8,128)(2,1)S(1)}, bf16[4,1792,128]{2,1,0:T(8,128)(2,1)S(1)}, u32[]{:S(2)}, u32[]{:S(2)}) collective-permute-start(bf16[4,1792,128]{2,1,0:T(8,128)(2,1)S(1)} %get-tuple-element.140.refs_2_), channel_id=1, source_target_pairs={{0,2},{2,0},{4,6},{6,4},{8,10},{10,8},{12,14},{14,12},{16,18},{18,... | collective-permute-start | bytes 5505032 | tf_op jit(solution)/shard_map/ppermute | solution.py:666
  67.1 9.5 %collective-permute-start.15 = (bf16[4,1024,128]{2,1,0:T(8,128)(2,1)S(1)}, bf16[4,1024,128]{2,1,0:T(8,128)(2,1)S(1)}, u32[]{:S(2)}, u32[]{:S(2)}) collective-permute-start(bf16[4,1024,128]{2,1,0:T(8,128)(2,1)S(1)} %get-tuple-element.142.refs_2_), channel_id=1, source_target_pairs={{0,2},{2,0},{4,6},{6,4},{8,10},{10,8},{12,14},{14,12},{16,18},{18,... | collective-permute-start | bytes 3145736 | tf_op jit(solution)/shard_map/ppermute | solution.py:666
  69.3 22.5 %collective-permute-start.17 = (bf16[1792,128]{1,0:T(8,128)(2,1)S(1)}, bf16[1792,128]{1,0:T(8,128)(2,1)S(1)}, u32[]{:S(2)}, u32[]{:S(2)}) collective-permute-start(bf16[1792,128]{1,0:T(8,128)(2,1)S(1)} %get-tuple-element.153), channel_id=1, source_target_pairs={{0,1},{1,0},{2,3},{3,2},{4,5},{5,4},{6,7},{7,6},{8,9},{9,8},{10,11... | collective-permute-start | bytes 1376264 | tf_op jit(solution)/shard_map/ppermute | solution.py:666
  71.1 22.4 %collective-permute-start.18 = (bf16[1792,128]{1,0:T(8,128)(2,1)S(1)}, bf16[1792,128]{1,0:T(8,128)(2,1)S(1)}, u32[]{:S(2)}, u32[]{:S(2)}) collective-permute-start(bf16[1792,128]{1,0:T(8,128)(2,1)S(1)} %get-tuple-element.154), channel_id=1, source_target_pairs={{0,5},{1,4},{2,7},{3,6},{4,1},{5,0},{6,3},{7,2},{8,13},{9,12},{10,... | collective-permute-start | bytes 1376264 | tf_op jit(solution)/shard_map/ppermute | solution.py:666
  72.3 22.4 %collective-permute-start.16 = (bf16[1792,128]{1,0:T(8,128)(2,1)S(1)}, bf16[1792,128]{1,0:T(8,128)(2,1)S(1)}, u32[]{:S(2)}, u32[]{:S(2)}) collective-permute-start(bf16[1792,128]{1,0:T(8,128)(2,1)S(1)} %get-tuple-element.143.refs_4_), channel_id=1, source_target_pairs={{0,4},{2,6},{4,0},{6,2},{8,12},{10,14},{12,8},{14,10},{16,20},{18,... | collective-permute-start | bytes 1376264 | tf_op jit(solution)/shard_map/ppermute | solution.py:666
  77.4 29.1 %collective-permute-start.22 = (bf16[1024,128]{1,0:T(8,128)(2,1)S(1)}, bf16[1024,128]{1,0:T(8,128)(2,1)S(1)}, u32[]{:S(2)}, u32[]{:S(2)}) collective-permute-start(bf16[1024,128]{1,0:T(8,128)(2,1)S(1)} %get-tuple-element.146.refs_4_), channel_id=1, source_target_pairs={{0,4},{2,6},{4,0},{6,2},{8,12},{10,14},{12,8},{14,10},{16,20},{18,... | collective-permute-start | bytes 786440 | tf_op jit(solution)/shard_map/ppermute | solution.py:666
  84.9 12.4 %collective-permute-start.20 = (bf16[4,768,128]{2,1,0:T(8,128)(2,1)S(1)}, bf16[4,768,128]{2,1,0:T(8,128)(2,1)S(1)}, u32[]{:S(2)}, u32[]{:S(2)}) collective-permute-start(bf16[4,768,128]{2,1,0:T(8,128)(2,1)S(1)} %get-tuple-element.150.refs_8_), channel_id=1, source_target_pairs={{0,2},{2,0},{4,6},{6,4},{8,10},{10,8},{12,14},{14,12},{16,18},{18,... | collective-permute-start | bytes 2359304 | tf_op jit(solution)/shard_map/ppermute | solution.py:666
  91.8 13.5 %collective-permute-start.23 = (bf16[1024,128]{1,0:T(8,128)(2,1)S(1)}, bf16[1024,128]{1,0:T(8,128)(2,1)S(1)}, u32[]{:S(2)}, u32[]{:S(2)}) collective-permute-start(bf16[1024,128]{1,0:T(8,128)(2,1)S(1)} %get-tuple-element.165), channel_id=1, source_target_pairs={{0,1},{1,0},{2,3},{3,2},{4,5},{5,4},{6,7},{7,6},{8,9},{9,8},{10,11... | collective-permute-start | bytes 786440 | tf_op jit(solution)/shard_map/ppermute | solution.py:666
  93.5 13.0 %collective-permute-start.24 = (bf16[1024,128]{1,0:T(8,128)(2,1)S(1)}, bf16[1024,128]{1,0:T(8,128)(2,1)S(1)}, u32[]{:S(2)}, u32[]{:S(2)}) collective-permute-start(bf16[1024,128]{1,0:T(8,128)(2,1)S(1)} %get-tuple-element.166), channel_id=1, source_target_pairs={{0,5},{1,4},{2,7},{3,6},{4,1},{5,0},{6,3},{7,2},{8,13},{9,12},{10,... | collective-permute-start | bytes 786440 | tf_op jit(solution)/shard_map/ppermute | solution.py:666
  95.6 6.3 %collective-permute-start.19 = (bf16[896,128]{1,0:T(8,128)(2,1)S(1)}, bf16[896,128]{1,0:T(8,128)(2,1)S(1)}, u32[]{:S(2)}, u32[]{:S(2)}) collective-permute-start(bf16[896,128]{1,0:T(8,128)(2,1)S(1)} %get-tuple-element.157), channel_id=1, source_target_pairs={{0,8},{2,10},{4,12},{6,14},{8,0},{10,2},{12,4},{14,6},{16,24},{18,... | collective-permute-start | bytes 688136 | tf_op jit(solution)/shard_map/ppermute | solution.py:666
  98.1 20.7 %collective-permute-start.28 = (bf16[832,128]{1,0:T(8,128)(2,1)S(1)}, bf16[832,128]{1,0:T(8,128)(2,1)S(1)}, u32[]{:S(2)}, u32[]{:S(2)}) collective-permute-start(bf16[832,128]{1,0:T(8,128)(2,1)S(1)} %get-tuple-element.163.refs_2_), channel_id=1, source_target_pairs={{0,4},{2,6},{4,0},{6,2},{8,12},{10,14},{12,8},{14,10},{16,20},{18,... | collective-permute-start | bytes 638984 | tf_op jit(solution)/shard_map/ppermute | solution.py:666
  102.6 11.3 %collective-permute-start.21 = (bf16[896,128]{1,0:T(8,128)(2,1)S(1)}, bf16[896,128]{1,0:T(8,128)(2,1)S(1)}, u32[]{:S(2)}, u32[]{:S(2)}) collective-permute-start(bf16[896,128]{1,0:T(8,128)(2,1)S(1)} %up_2.1.refs_4_.refs_0_), channel_id=1, source_target_pairs={{0,16},{2,18},{4,20},{6,22},{8,24},{10,26},{12,28},{14,30},{16,0},... | collective-permute-start | bytes 688136 | tf_op jit(solution)/shard_map/ppermute | solution.py:666
  107.2 13.3 %collective-permute-start.27 = (bf16[512,128]{1,0:T(8,128)(2,1)S(1)}, bf16[512,128]{1,0:T(8,128)(2,1)S(1)}, u32[]{:S(2)}, u32[]{:S(2)}) collective-permute-start(bf16[512,128]{1,0:T(8,128)(2,1)S(1)} %get-tuple-element.172), channel_id=1, source_target_pairs={{0,8},{2,10},{4,12},{6,14},{8,0},{10,2},{12,4},{14,6},{16,24},{18,... | collective-permute-start | bytes 393224 | tf_op jit(solution)/shard_map/ppermute | solution.py:666
  108.9 9.4 %collective-permute-start.29 = (bf16[832,128]{1,0:T(8,128)(2,1)S(1)}, bf16[832,128]{1,0:T(8,128)(2,1)S(1)}, u32[]{:S(2)}, u32[]{:S(2)}) collective-permute-start(bf16[832,128]{1,0:T(8,128)(2,1)S(1)} %get-tuple-element.174), channel_id=1, source_target_pairs={{0,1},{1,0},{2,3},{3,2},{4,5},{5,4},{6,7},{7,6},{8,9},{9,8},{10,11... | collective-permute-start | bytes 638984 | tf_op jit(solution)/shard_map/ppermute | solution.py:666
  109.4 9.4 %collective-permute-start.30 = (bf16[832,128]{1,0:T(8,128)(2,1)S(1)}, bf16[832,128]{1,0:T(8,128)(2,1)S(1)}, u32[]{:S(2)}, u32[]{:S(2)}) collective-permute-start(bf16[832,128]{1,0:T(8,128)(2,1)S(1)} %get-tuple-element.175), channel_id=1, source_target_pairs={{0,5},{1,4},{2,7},{3,6},{4,1},{5,0},{6,3},{7,2},{8,13},{9,12},{10,... | collective-permute-start | bytes 638984 | tf_op jit(solution)/shard_map/ppermute | solution.py:666
  114.5 8.8 %collective-permute-start.26 = (bf16[896,128]{1,0:T(8,128)(2,1)S(1)}, bf16[896,128]{1,0:T(8,128)(2,1)S(1)}, u32[]{:S(2)}, u32[]{:S(2)}) collective-permute-start(bf16[896,128]{1,0:T(8,128)(2,1)S(1)} %up_3.1.refs_7_.refs_0_), channel_id=1, source_target_pairs={{0,8},{2,10},{4,12},{6,14},{8,0},{10,2},{12,4},{14,6},{16,24},{18,... | collective-permute-start | bytes 688136 | tf_op jit(solution)/shard_map/ppermute | solution.py:666
  118.3 28.8 %collective-permute-start.25 = (bf16[624,1024]{1,0:T(8,128)(2,1)S(1)}, bf16[624,1024]{1,0:T(8,128)(2,1)S(1)}, u32[]{:S(2)}, u32[]{:S(2)}) collective-permute-start(bf16[624,1024]{1,0:T(8,128)(2,1)S(1)} %get-tuple-element.169.refs_4_), channel_id=1, source_target_pairs={{0,1},{1,0},{2,3},{3,2},{4,5},{5,4},{6,7},{7,6},{8,9},{9,8},{10,11... | collective-permute-start | bytes 3833864 | tf_op jit(solution)/shard_map/ppermute | solution.py:666
  119.5 6.0 %collective-permute-start.34 = (bf16[416,128]{1,0:T(8,128)(2,1)S(1)}, bf16[416,128]{1,0:T(8,128)(2,1)S(1)}, u32[]{:S(2)}, u32[]{:S(2)}) collective-permute-start(bf16[416,128]{1,0:T(8,128)(2,1)S(1)} %get-tuple-element.177), channel_id=1, source_target_pairs={{0,8},{2,10},{4,12},{6,14},{8,0},{10,2},{12,4},{14,6},{16,24},{18,... | collective-permute-start | bytes 319496 | tf_op jit(solution)/shard_map/ppermute | solution.py:666
  121.1 7.6 %collective-permute-start.36 = (bf16[512,128]{1,0:T(8,128)(2,1)S(1)}, bf16[512,128]{1,0:T(8,128)(2,1)S(1)}, u32[]{:S(2)}, u32[]{:S(2)}) collective-permute-start(bf16[512,128]{1,0:T(8,128)(2,1)S(1)} %late_2.1.refs_2_.refs_0_), channel_id=1, source_target_pairs={{0,16},{2,18},{4,20},{6,22},{8,24},{10,26},{12,28},{14,30},{16,0},... | collective-permute-start | bytes 393224 | tf_op jit(solution)/shard_map/ppermute | solution.py:666
  123.9 11.9 %collective-permute-start.32 = (bf16[1792,128]{1,0:T(8,128)(2,1)S(1)}, bf16[1792,128]{1,0:T(8,128)(2,1)S(1)}, u32[]{:S(2)}, u32[]{:S(2)}) collective-permute-start(bf16[1792,128]{1,0:T(8,128)(2,1)S(1)} %up_4.1.refs_2_.refs_0_), channel_id=1, source_target_pairs={{0,2},{2,0},{4,6},{6,4},{8,10},{10,8},{12,14},{14,12},{16,18},{18,... | collective-permute-start | bytes 1376264 | tf_op jit(solution)/shard_map/ppermute | solution.py:666
  124.0 12.9 %collective-permute-start.31 = (bf16[1792,128]{1,0:T(8,128)(2,1)S(1)}, bf16[1792,128]{1,0:T(8,128)(2,1)S(1)}, u32[]{:S(2)}, u32[]{:S(2)}) collective-permute-start(bf16[1792,128]{1,0:T(8,128)(2,1)S(1)} %up_4.1.refs_2_.refs_0_), channel_id=1, source_target_pairs={{0,4},{2,6},{4,0},{6,2},{8,12},{10,14},{12,8},{14,10},{16,20},{18,... | collective-permute-start | bytes 1376264 | tf_op jit(solution)/shard_map/ppermute | solution.py:666
  126.1 8.4 %collective-permute-start.35 = (bf16[416,128]{1,0:T(8,128)(2,1)S(1)}, bf16[416,128]{1,0:T(8,128)(2,1)S(1)}, u32[]{:S(2)}, u32[]{:S(2)}) collective-permute-start(bf16[416,128]{1,0:T(8,128)(2,1)S(1)} %early_2.1.refs_2_.refs_0_), channel_id=1, source_target_pairs={{0,16},{2,18},{4,20},{6,22},{8,24},{10,26},{12,28},{14,30},{16,0},... | collective-permute-start | bytes 319496 | tf_op jit(solution)/shard_map/ppermute | solution.py:666
  129.2 6.5 %collective-permute-start.38 = (bf16[512,128]{1,0:T(8,128)(2,1)S(1)}, bf16[512,128]{1,0:T(8,128)(2,1)S(1)}, u32[]{:S(2)}, u32[]{:S(2)}) collective-permute-start(bf16[512,128]{1,0:T(8,128)(2,1)S(1)} %late_3.1.refs_2_.refs_0_), channel_id=1, source_target_pairs={{0,8},{2,10},{4,12},{6,14},{8,0},{10,2},{12,4},{14,6},{16,24},{18,... | collective-permute-start | bytes 393224 | tf_op jit(solution)/shard_map/ppermute | solution.py:666
  135.0 4.8 %collective-permute-start.37 = (bf16[416,128]{1,0:T(8,128)(2,1)S(1)}, bf16[416,128]{1,0:T(8,128)(2,1)S(1)}, u32[]{:S(2)}, u32[]{:S(2)}) collective-permute-start(bf16[416,128]{1,0:T(8,128)(2,1)S(1)} %early_3.1.refs_2_.refs_0_), channel_id=1, source_target_pairs={{0,8},{2,10},{4,12},{6,14},{8,0},{10,2},{12,4},{14,6},{16,24},{18,... | collective-permute-start | bytes 319496 | tf_op jit(solution)/shard_map/ppermute | solution.py:666
  136.3 15.5 %collective-permute-start.43 = (bf16[1024,128]{1,0:T(8,128)(2,1)S(1)}, bf16[1024,128]{1,0:T(8,128)(2,1)S(1)}, u32[]{:S(2)}, u32[]{:S(2)}) collective-permute-start(bf16[1024,128]{1,0:T(8,128)(2,1)S(1)} %late_4.1.refs_2_.refs_4_), channel_id=1, source_target_pairs={{0,2},{2,0},{4,6},{6,4},{8,10},{10,8},{12,14},{14,12},{16,18},{18,... | collective-permute-start | bytes 786440 | tf_op jit(solution)/shard_map/ppermute | solution.py:666
  136.4 13.5 %collective-permute-start.42 = (bf16[1024,128]{1,0:T(8,128)(2,1)S(1)}, bf16[1024,128]{1,0:T(8,128)(2,1)S(1)}, u32[]{:S(2)}, u32[]{:S(2)}) collective-permute-start(bf16[1024,128]{1,0:T(8,128)(2,1)S(1)} %late_4.1.refs_2_.refs_4_), channel_id=1, source_target_pairs={{0,4},{2,6},{4,0},{6,2},{8,12},{10,14},{12,8},{14,10},{16,20},{18,... | collective-permute-start | bytes 786440 | tf_op jit(solution)/shard_map/ppermute | solution.py:666
  136.9 4.1 %collective-permute-start.33 = (bf16[1792,128]{1,0:T(8,128)(2,1)S(1)}, bf16[1792,128]{1,0:T(8,128)(2,1)S(1)}, u32[]{:S(2)}, u32[]{:S(2)}) collective-permute-start(bf16[1792,128]{1,0:T(8,128)(2,1)S(1)} %collective-permute-done.31.refs_1_), channel_id=1, source_target_pairs={{0,2},{2,0},{4,6},{6,4},{8,10},{10,8},{12,14},{14,12},{16,18},{18,... | collective-permute-start | bytes 1376264 | tf_op jit(solution)/shard_map/ppermute | solution.py:666
  140.4 10.1 %collective-permute-start.39 = (bf16[832,128]{1,0:T(8,128)(2,1)S(1)}, bf16[832,128]{1,0:T(8,128)(2,1)S(1)}, u32[]{:S(2)}, u32[]{:S(2)}) collective-permute-start(bf16[832,128]{1,0:T(8,128)(2,1)S(1)} %early_4.1.refs_4_.refs_0_), channel_id=1, source_target_pairs={{0,4},{2,6},{4,0},{6,2},{8,12},{10,14},{12,8},{14,10},{16,20},{18,... | collective-permute-start | bytes 638984 | tf_op jit(solution)/shard_map/ppermute | solution.py:666
  149.9 2.2 %collective-permute-start.44 = (bf16[1024,128]{1,0:T(8,128)(2,1)S(1)}, bf16[1024,128]{1,0:T(8,128)(2,1)S(1)}, u32[]{:S(2)}, u32[]{:S(2)}) collective-permute-start(bf16[1024,128]{1,0:T(8,128)(2,1)S(1)} %after_rows.1.refs_5_), channel_id=1, source_target_pairs={{0,2},{2,0},{4,6},{6,4},{8,10},{10,8},{12,14},{14,12},{16,18},{18,... | collective-permute-start | bytes 786440 | tf_op jit(solution)/shard_map/ppermute | solution.py:666
  150.0 1.8 %collective-permute-start.40 = (bf16[832,128]{1,0:T(8,128)(2,1)S(1)}, bf16[832,128]{1,0:T(8,128)(2,1)S(1)}, u32[]{:S(2)}, u32[]{:S(2)}) collective-permute-start(bf16[832,128]{1,0:T(8,128)(2,1)S(1)} %early_4.1.refs_4_.refs_0_), channel_id=1, source_target_pairs={{0,2},{2,0},{4,6},{6,4},{8,10},{10,8},{12,14},{14,12},{16,18},{18,... | collective-permute-start | bytes 638984 | tf_op jit(solution)/shard_map/ppermute | solution.py:666
  150.5 1.6 %collective-permute-start.41 = (bf16[832,128]{1,0:T(8,128)(2,1)S(1)}, bf16[832,128]{1,0:T(8,128)(2,1)S(1)}, u32[]{:S(2)}, u32[]{:S(2)}) collective-permute-start(bf16[832,128]{1,0:T(8,128)(2,1)S(1)} %after_up.1.refs_1_), channel_id=1, source_target_pairs={{0,2},{2,0},{4,6},{6,4},{8,10},{10,8},{12,14},{14,12},{16,18},{18,... | collective-permute-start | bytes 638984 | tf_op jit(solution)/shard_map/ppermute | solution.py:666
